TPU v7x, 32 devices: a whole 2x2x4 slice. The times are simulated.
32 devices in a mesh: node: 16 (over z, y, x), freq: 2 (over core).
Axes of the slice: x: 2, y: 2, z: 4, core: 2. Of those that a mesh axis runs over, the one named last changes fastest.
Arguments:
- excitation: float32 [2, 8, 16384], P(None, 'freq', 'node')
- g_blocks: float32 [128, 8, 128, 128], P('node', 'freq')
- c_blocks: float32 [128, 8, 128, 128], P('node', 'freq')
- pattern: int32 [128, 8], P('node'), may hold values from 0 to 127, as said below
- counts: int32 [128], P('node'), may hold values from 1 to 8, as said below
- freq_ids: int32 [8], P('freq'), may hold values from 0 to 999
Outputs:
- solution: float32 [2, 8, 16384], P(None, 'freq', 'node')
- residual_norm: float32 [8], P('freq')
Inputs may be any that keep to these rules, and one draw needn't show every extreme that they name: `pattern`: slot 0 of row block b names b itself; the other slots name any row block, repeats allowed. `counts`: slots at or past a row block's count are padding and add nothing.
All inputs are finite; a program needn't handle non-finite values.
Results may differ from a plain program's by a relative error of at most 0.0001.
Values sent between devices are 32-bit elements; how exact they have to be, the bound alone decides.
No kernel may reach another device: no remote copies, remote signals or barrier semaphores. Data moves between devices by JAX's collectives and lax.ppermute only.
A program may use at most 64 MiB of HBM per device.

v0:
```python
import math

import jax
import jax.numpy as jnp
from jax import lax
from jax.sharding import PartitionSpec as P

ITERS = 3


def projected(first_vec, second_vec):
    return jnp.sum(first_vec * second_vec, axis=(0, 2))


def shards(excitation, g_blocks, c_blocks, pattern, counts, freq_ids):
    angular = 0.2 * jnp.exp(freq_ids.astype(jnp.float32) * (math.log(8.0) / 1000.0))
    row_blocks = pattern.shape[0]
    slot_count = pattern.shape[1]
    block_rows = g_blocks.shape[2]
    freq_count = excitation.shape[1]
    in_use = jnp.arange(slot_count)[None, :] < counts[:, None]
    g_whole, c_whole = (
        lax.all_gather(g_blocks, "freq", axis=1, tiled=True),
        lax.all_gather(c_blocks, "freq", axis=1, tiled=True),
    )
    initial_norm = jnp.sqrt(lax.psum(projected(excitation, excitation), "node"))
    krylov = [excitation / initial_norm[None, :, None]]
    columns = []
    for iteration in range(ITERS):
        portion = lax.all_gather(krylov[iteration], "node", axis=2, tiled=True)
        portion_blocks = portion.shape[2] // block_rows
        local_rows = portion.reshape(2, freq_count, portion_blocks, block_rows)
        block_ids = jnp.arange(portion_blocks, dtype=jnp.int32)
        select = ((pattern[:, :, None] == block_ids[None, None, :]) & in_use[:, :, None]).astype(
            jnp.float32
        )
        picked = jnp.einsum("bkp,cfpj->bkcfj", select, local_rows, precision=lax.Precision.HIGHEST)
        g_total = jnp.einsum("bkij,bkcfj->cfbi", g_whole, picked, precision=lax.Precision.HIGHEST)
        c_total = jnp.einsum("bkij,bkcfj->cfbi", c_whole, picked, precision=lax.Precision.HIGHEST)
        gsum = g_total
        csum = c_total
        gsum = gsum.reshape(2, freq_count, row_blocks * block_rows)
        csum = csum.reshape(2, freq_count, row_blocks * block_rows)
        scaled = angular[:, None]
        applied = jnp.stack([gsum[0] - scaled * csum[1], gsum[1] + scaled * csum[0]])
        coeffs = []
        for vector in krylov:
            weight = lax.psum(projected(vector, applied), "node")
            applied = applied - weight[None, :, None] * vector
            coeffs.append(weight)
        height = jnp.sqrt(lax.psum(projected(applied, applied), "node"))
        entries = coeffs + [height] + [jnp.zeros_like(height)] * (ITERS - 1 - iteration)
        columns.append(jnp.stack(entries, axis=1))
        if iteration + 1 < ITERS:
            krylov.append(applied / height[None, :, None])
    hessen = jnp.stack(columns, axis=2)
    normal = jnp.einsum("fim,fin->fmn", hessen, hessen, precision=lax.Precision.HIGHEST)
    right_side = initial_norm[:, None] * hessen[:, 0, :]
    factor = jnp.linalg.cholesky(normal)
    middle = jax.scipy.linalg.solve_triangular(factor, right_side[:, :, None], lower=True)
    coef_y = jax.scipy.linalg.solve_triangular(factor, middle, lower=True, trans=1)[:, :, 0]
    target = jnp.zeros((freq_count, ITERS + 1), jnp.float32).at[:, 0].set(initial_norm)
    misfit = target - jnp.einsum("fim,fm->fi", hessen, coef_y, precision=lax.Precision.HIGHEST)
    residual_norm = jnp.sqrt(jnp.sum(misfit * misfit, axis=1))
    solution = jnp.zeros_like(excitation)
    for iteration in range(ITERS):
        solution = solution + coef_y[:, iteration][None, :, None] * krylov[iteration]
    return (solution, residual_norm)


def solution(mesh):
    in_specs = (
        P(None, "freq", "node"),
        P("node", "freq", None, None),
        P("node", "freq", None, None),
        P("node", None),
        P("node"),
        P("freq"),
    )
    out_specs = (P(None, "freq", "node"), P("freq"))
    return jax.shard_map(shards, mesh=mesh, in_specs=in_specs, out_specs=out_specs, check_vma=False)
```

profile of v0, /device:TPU:0, one launch (start us, length us, event | category | flops | bytes accessed | tf_op | source)
XLA Modules:
  0.0 557.5 jit_solution(5128182396016504641)
XLA Ops:
  7.2 0.7 all-gather.5.cloned.1.call-update
  8.0 0.7 all-gather.3.cloned.1.call-update
  8.7 0.1 multiply_reduce_fusion.9
  8.8 43.5 %psum.70 = f32[4]{0:T(128)S(1)} all-reduce(f32[4]{0:T(128)S(1)} %multiply_reduce_fusion.9), channel_id=1, replica_groups=mesh['node'=16,'freq'=2] {'node'}, use_global_device_ids=true, to_apply=%region_1.0 | all-reduce | flops 4 | bytes 32 | tf_op jit(solution)/shard_map/psum | solution.py:26
  52.3 0.6 compare_reduce_fusion
  52.9 0.7 fusion.66
  53.7 38.3 %all_gather.15 = f32[2,4,16384]{2,1,0:T(4,128)S(1)} all-gather(f32[2,4,1024]{2,1,0:T(4,128)S(1)} %broadcast_divide_fusion.2), channel_id=1, replica_groups=mesh['node'=16,'freq'=2] {'node'}, dimensions={2}, use_global_device_ids=true | all-gather | bytes 557056 | tf_op jit(solution)/shard_map/all_gather | solution.py:30
  91.9 0.4 reshape.356
  92.4 0.3 fusion.42
  92.8 5.4 fusion.21
  98.3 5.4 fusion.12
  103.8 0.2 multiply_reduce_fusion.8
  104.0 38.7 %psum.71 = f32[4]{0:T(128)S(1)} all-reduce(f32[4]{0:T(128)S(1)} %multiply_reduce_fusion.8), channel_id=1, replica_groups=mesh['node'=16,'freq'=2] {'node'}, use_global_device_ids=true, to_apply=%region_3.0 | all-reduce | flops 4 | bytes 32 | tf_op jit(solution)/shard_map/psum | solution.py:48
  142.6 0.2 multiply_reduce_fusion.7
  142.8 36.6 %psum.72 = f32[4]{0:T(128)S(1)} all-reduce(f32[4]{0:T(128)S(1)} %get-tuple-element.18), channel_id=1, replica_groups=mesh['node'=16,'freq'=2] {'node'}, use_global_device_ids=true, to_apply=%region_5.0 | all-reduce | flops 4 | bytes 32 | tf_op jit(solution)/shard_map/psum | solution.py:51
  179.5 40.5 %all_gather.18 = f32[2,4,16384]{2,1,0:T(4,128)S(1)} all-gather(f32[2,4,1024]{2,1,0:T(4,128)S(1)} %broadcast_divide_fusion.1), channel_id=1, replica_groups=mesh['node'=16,'freq'=2] {'node'}, dimensions={2}, use_global_device_ids=true | all-gather | bytes 557056 | tf_op jit(solution)/shard_map/all_gather | solution.py:30
  220.0 0.4 reshape.361
  220.4 0.3 fusion.40
  220.8 5.6 %fusion.24 = f32[2,4,8,128]{3,1,0,2:T(4,128)S(1)} fusion(f32[8,8,128,128]{3,2,1,0:T(8,128)} %all-gather.5.cloned.1.call-done, f32[8,8,2,4,128]{4,1,3,2,0:T(8,128)S(1)} %fusion.40), kind=kOutput, calls=%fused_computation.16 | convolution fusion | flops 100663296 | bytes 4489216 | tf_op jit(solution)/shard_map/bkij,bkcfj->cfbi/dot_general | solution.py:39
  226.4 3.8 fusion.15
  230.2 0.2 multiply_reduce_fusion.6
  230.4 36.6 %psum.73 = f32[4]{0:T(128)S(1)} all-reduce(f32[4]{0:T(128)S(1)} %multiply_reduce_fusion.6), channel_id=1, replica_groups=mesh['node'=16,'freq'=2] {'node'}, use_global_device_ids=true, to_apply=%region_7.0 | all-reduce | flops 4 | bytes 32 | tf_op jit(solution)/shard_map/psum | solution.py:48
  267.0 0.2 multiply_reduce_fusion.5
  267.2 38.6 %psum.74 = f32[4]{0:T(128)S(1)} all-reduce(f32[4]{0:T(128)S(1)} %get-tuple-element.16), channel_id=1, replica_groups=mesh['node'=16,'freq'=2] {'node'}, use_global_device_ids=true, to_apply=%region_9.0 | all-reduce | flops 4 | bytes 32 | tf_op jit(solution)/shard_map/psum | solution.py:48
  305.8 0.2 multiply_reduce_fusion.4
  306.0 36.7 %psum.75 = f32[4]{0:T(128)S(1)} all-reduce(f32[4]{0:T(128)S(1)} %multiply_reduce_fusion.4), channel_id=1, replica_groups=mesh['node'=16,'freq'=2] {'node'}, use_global_device_ids=true, to_apply=%region_11.0 | all-reduce | flops 4 | bytes 32 | tf_op jit(solution)/shard_map/psum | solution.py:51
  342.8 40.5 %all_gather.19 = f32[2,4,16384]{2,1,0:T(4,128)S(1)} all-gather(f32[2,4,1024]{2,1,0:T(4,128)S(1)} %broadcast_divide_fusion), channel_id=1, replica_groups=mesh['node'=16,'freq'=2] {'node'}, dimensions={2}, use_global_device_ids=true | all-gather | bytes 557056 | tf_op jit(solution)/shard_map/all_gather | solution.py:30
  383.3 0.4 reshape.364
  383.6 0.3 fusion.38
  384.0 5.6 %fusion.27 = f32[2,4,8,128]{3,1,0,2:T(4,128)S(1)} fusion(f32[8,8,128,128]{3,2,1,0:T(8,128)} %all-gather.5.cloned.1.call-done, f32[8,8,2,4,128]{4,1,3,2,0:T(8,128)S(1)} %fusion.38), kind=kOutput, calls=%fused_computation.17 | convolution fusion | flops 100663296 | bytes 4489216 | tf_op jit(solution)/shard_map/bkij,bkcfj->cfbi/dot_general | solution.py:39
  389.6 3.8 fusion.18
  393.5 0.2 multiply_reduce_fusion.3
  393.7 36.7 %psum.76 = f32[4]{0:T(128)S(1)} all-reduce(f32[4]{0:T(128)S(1)} %multiply_reduce_fusion.3), channel_id=1, replica_groups=mesh['node'=16,'freq'=2] {'node'}, use_global_device_ids=true, to_apply=%region_13.0 | all-reduce | flops 4 | bytes 32 | tf_op jit(solution)/shard_map/psum | solution.py:48
  430.3 0.2 multiply_reduce_fusion.2
  430.6 38.5 %psum.77 = f32[4]{0:T(128)S(1)} all-reduce(f32[4]{0:T(128)S(1)} %get-tuple-element.14), channel_id=1, replica_groups=mesh['node'=16,'freq'=2] {'node'}, use_global_device_ids=true, to_apply=%region_15.0 | all-reduce | flops 4 | bytes 32 | tf_op jit(solution)/shard_map/psum | solution.py:48
  469.0 0.2 multiply_reduce_fusion.1
  469.3 36.6 %psum.78 = f32[4]{0:T(128)S(1)} all-reduce(f32[4]{0:T(128)S(1)} %multiply_reduce_fusion.1), channel_id=1, replica_groups=mesh['node'=16,'freq'=2] {'node'}, use_global_device_ids=true, to_apply=%region_17.0 | all-reduce | flops 4 | bytes 32 | tf_op jit(solution)/shard_map/psum | solution.py:48
  505.9 0.2 multiply_reduce_fusion
  506.2 38.4 %psum.79 = f32[4]{0:T(128)S(1)} all-reduce(f32[4]{0:T(128)S(1)} %multiply_reduce_fusion), channel_id=1, replica_groups=mesh['node'=16,'freq'=2] {'node'}, use_global_device_ids=true, to_apply=%region_19.0 | all-reduce | flops 4 | bytes 32 | tf_op jit(solution)/shard_map/psum | solution.py:51
  545.3 0.1 copy.36
  545.5 0.2 fusion.68
  545.8 1.1 custom-call.11
  547.0 0.1 compare_reduce_fusion.1
  547.2 1.0 custom-call.12
  548.4 0.2 fusion.62
  548.9 0.2 multiply_reduce_fusion.10
  549.4 0.5 sqrt.19
  549.9 0.7 multiply_add_fusion
  (55 shorter events, 2.6 us)
Async XLA Ops:
  7.2 1.5 copy-start.2
  7.2 85.1 %copy-start.4 = (s32[4]{0:T(128)S(1)}, s32[4]{0:T(128)}, u32[]{:S(2)}) copy-start(s32[4]{0:T(128)} %param.13) | copy-start | bytes 52
  7.2 85.1 %copy-start.5 = (s32[8]{0:T(128)S(1)}, s32[8]{0:T(128)}, u32[]{:S(2)}) copy-start(s32[8]{0:T(128)} %param.12) | copy-start | bytes 100
  7.2 85.2 %copy-start.3 = (s32[8,8]{1,0:T(8,128)S(1)}, s32[8,8]{1,0:T(8,128)}, u32[]{:S(2)}) copy-start(s32[8,8]{1,0:T(8,128)} %param.11) | copy-start | bytes 772
  7.2 85.6 %all-gather.5.cloned.1.call-start = ((), (), s32[]{:S(2)}) async-start(), calls=%async_computation.1 | async-start | bytes 6291456 | tf_op jit(solution)/shard_map/all_gather | solution.py:24
  7.9 90.3 %all-gather.3.cloned.1.call-start = ((), (), s32[]{:S(2)}) async-start(), calls=%async_computation | async-start | bytes 6291456 | tf_op jit(solution)/shard_map/all_gather | solution.py:23
  220.4 6.0 %copy-start = (f32[8,8,128,128]{3,2,1,0:T(8,128)S(1)}, f32[8,8,128,128]{3,2,1,0:T(8,128)}, u32[]{:S(2)}) copy-start(f32[8,8,128,128]{3,2,1,0:T(8,128)} %all-gather.3.cloned.1.call-done) | copy-start | bytes 12582916
  383.6 6.0 %copy-start.1 = (f32[8,8,128,128]{3,2,1,0:T(8,128)S(1)}, f32[8,8,128,128]{3,2,1,0:T(8,128)}, u32[]{:S(2)}) copy-start(f32[8,8,128,128]{3,2,1,0:T(8,128)} %all-gather.3.cloned.1.call-done) | copy-start | bytes 12582916
Sparse Core Ops, SparseCore 0:
  9.6 16.3 all-gather.4
  27.5 14.8 all-gather.2
where the time goes:
time: 558 us; the launch traced here: 557 us
  blocking collectives  500 us (90%)
  matrix products  31 us (6%)
  between operations  14.3 us (3%)
  other arithmetic  7.55 us (1%)
    psum x6, blocking collectives, shards(): weight = lax.psum(projected(vector, applied), 'node')  226 us
    all_gather x3, blocking collectives, shards(): portion = lax.all_gather(krylov[iteration], 'node', axis=2, tiled=True)  119 us
    psum x3, blocking collectives, shards(): height = jnp.sqrt(lax.psum(projected(applied, applied), 'node'))  112 us
    psum x1, blocking collectives, shards(): initial_norm = jnp.sqrt(lax.psum(projected(excitation, excitation), 'node'))  43.5 us
    dot_general x3, matrix products, shards(): jnp.einsum('bkij,bkcfj->cfbi', c_whole, picked, precision=lax.Precision.H...  16.6 us
    dot_general x3, matrix products, shards(): jnp.einsum('bkij,bkcfj->cfbi', g_whole, picked, precision=lax.Precision.H...  12.9 us
  transfers between devices with their start and end apart: 2, of which 0 were waited for; matrix products, arithmetic and copies ran while one was open for 1% of the time, Pallas kernels for 0%

commit v1 on v0

v1 whole, which is shorter than its diff:
```python
import functools
import math

import jax
import jax.numpy as jnp
from jax import lax
from jax.experimental import pallas as pl
from jax.experimental.pallas import tpu as pltpu
from jax.sharding import PartitionSpec as P

ITERS = 3
LANES = 128
GROUP = 8
VMEM_LIMIT = 40 * 1024 * 1024
SIDE = 2


def split_nodes(nodes):
    plane = 4 if nodes % 4 == 0 else 1
    return nodes // plane, plane


def gather_rows(rows, nodes, parts):
    line, plane = split_nodes(nodes)
    held = [rows]
    for d in range(1, line):
        perm = [(i, (i + d * plane) % nodes) for i in range(nodes)]
        held.append(lax.ppermute(rows, "node", perm))
    whole_line = jnp.stack(held).reshape(line, parts, rows.shape[-1])
    held = [whole_line]
    for d in range(1, plane):
        perm = [(i, (i // plane) * plane + ((i % plane) ^ d)) for i in range(nodes)]
        held.append(lax.ppermute(whole_line, "node", perm))
    return held


def gathered_place(owner, node, nodes):
    line, plane = split_nodes(nodes)
    far = lax.rem(node // plane - owner // plane + line, line)
    return ((node % plane) ^ (owner % plane)) * line + far


def work_list(pattern, counts, node, freq, nodes, freqs):
    row_blocks, slots = pattern.shape
    own_slots = slots // freqs
    total = row_blocks * slots
    place = gathered_place(pattern // row_blocks, node, nodes) * row_blocks + pattern % row_blocks
    b = lax.broadcasted_iota(jnp.int32, (row_blocks, slots), 0)
    k = lax.broadcasted_iota(jnp.int32, (row_blocks, slots), 1)
    away = lax.rem(freq - k // own_slots + freqs, freqs)
    stored = (away * row_blocks + b) * own_slots + k % own_slots
    counts = jnp.clip(counts, 0, slots)
    before = jnp.sum(
        jnp.where(jnp.arange(row_blocks)[None, :] < jnp.arange(row_blocks)[:, None], counts[None, :], 0), axis=1
    )
    spot = jnp.where(k < counts[:, None], before[:, None] + k, total).reshape(-1)
    used = jnp.sum(counts)
    order = jnp.arange(total)
    values = jnp.stack([place, stored, b]).reshape(3, total)
    hit = spot[None, None, :] == order[None, :, None]
    packed = jnp.sum(jnp.where(hit, values[:, None, :], 0), axis=2)
    empty = jnp.where(order >= used, nodes * row_blocks, 0)
    groups = jnp.full((1, total), (used + GROUP - 1) // GROUP, jnp.int32)
    return jnp.concatenate([packed.at[0].add(empty), groups]).astype(jnp.int32)


def prepare_kernel(g_ref, c_ref, *rest):
    out_ref = rest[-1]
    size = g_ref.shape[-1]
    for slot in range(g_ref.shape[1]):
        for m, ref in enumerate((g_ref, c_ref)):
            x = ref[0, slot]
            high = x.astype(jnp.bfloat16)
            low = (x - high.astype(jnp.float32)).astype(jnp.bfloat16)
            out_ref[0, 0, slot, m * size : (m + 1) * size, :size] = high
            out_ref[0, 0, slot, m * size : (m + 1) * size, size:] = low


def prepare(g_part, c_part, away, freqs, into):
    row_blocks, own_slots, size, _ = g_part.shape
    shape = (freqs, row_blocks, own_slots, 2 * size, SIDE * size)
    block = pl.BlockSpec((1, own_slots, size, size), lambda b: (b, 0, 0, 0))
    operands, in_specs, aliases = [g_part, c_part], [block, block], {}
    if into is not None:
        operands.append(into)
        in_specs.append(pl.BlockSpec(memory_space=pl.ANY))
        aliases = {2: 0}
    return pl.pallas_call(
        prepare_kernel,
        grid=(row_blocks,),
        in_specs=in_specs,
        out_specs=pl.BlockSpec((1, 1) + shape[2:], lambda b: (away, b, 0, 0, 0)),
        out_shape=jax.ShapeDtypeStruct(shape, jnp.bfloat16),
        input_output_aliases=aliases,
        cost_estimate=pl.CostEstimate(
            flops=8 * g_part.size, bytes_accessed=16 * g_part.size, transcendentals=0
        ),
        name=f"prepare_{away}",
    )(*operands)


def lane_sum(x):
    return jnp.sum(x, axis=1, keepdims=True)


def with_other_part(column):
    wide = jnp.broadcast_to(column, (column.shape[0], LANES))
    return wide + pltpu.roll(wide, column.shape[0] // 2, 0)


def put_lane(tile, lane, column):
    at = lax.broadcasted_iota(jnp.int32, tile.shape, 1) == lane
    return jnp.where(at, column, tile)


def step_kernel(step, plane, line, items_ref, turn_ref, info_in_ref, *refs):
    lines = refs[:plane]
    prev = refs[plane : plane + step]
    w_ref, z_ref, own_ref, local_ref, info_ref, tile_ref, split_ref, acc_ref, held_ref, sems = refs[plane + step :]
    nodes = plane * line
    parts, rows = local_ref.shape
    row_blocks = acc_ref.shape[0]
    size = rows // row_blocks
    groups = items_ref[3, 0]

    def fetch(t):
        return pltpu.make_async_copy(w_ref.at[items_ref[1, t]], held_ref.at[t], sems.at[t])

    @pl.loop(0, groups * GROUP)
    def _(t):
        fetch(t).start()

    split_ref[nodes * row_blocks] = jnp.zeros(split_ref.shape[1:], split_ref.dtype)
    acc_ref[...] = jnp.zeros_like(acc_ref)

    def chunks(body, carry):
        for q in range(plane):
            carry = lax.fori_loop(
                0, line, lambda i, c, q=q: body(q, i, q * line + i, c), carry, unroll=line <= 4
            )
        return carry

    zero = jnp.zeros((parts, rows), jnp.float32)
    info = info_in_ref[...]
    if step == 0:

        def square(q, i, at, total):
            x = lines[q][i]
            return total + x * x

        height = jnp.sqrt(with_other_part(lane_sum(chunks(square, zero))))
        info = put_lane(info, 0, height)
        source = lambda q, i, at: lines[q][i]
    else:

        def dot(q, i, at, totals):
            x = lines[q][i]
            return tuple(s + p[at] * x for s, p in zip(totals, prev))

        sums = chunks(dot, (zero,) * step)
        coeffs = [with_other_part(lane_sum(s)) for s in sums]
        first = 1 if step == 1 else 3
        for i, coeff in enumerate(coeffs):
            info = put_lane(info, first + i, coeff)
        wide = [jnp.tile(coeff, (1, rows // LANES)) for coeff in coeffs]

        def subtract(q, i, at, total):
            x = lines[q][i]
            for coeff, p in zip(wide, prev):
                x = x - coeff * p[at]
            z_ref[at] = x
            return total + x * x

        height = jnp.sqrt(with_other_part(lane_sum(chunks(subtract, zero))))
        info = put_lane(info, first + step, height)
        source = lambda q, i, at: z_ref[at]
    info_ref[...] = info
    height = jnp.tile(height, (1, rows // LANES))

    def spread(q, i, at, carry):
        z = source(q, i, at) / height
        z_ref[at] = z
        high = z.astype(jnp.bfloat16).astype(jnp.float32)
        both = jnp.concatenate([high, z - high], axis=0).astype(jnp.bfloat16)
        for b in range(row_blocks):
            split_ref[at * row_blocks + b] = both[:, b * size : (b + 1) * size]
        return carry

    chunks(spread, 0)
    own_ref[...] = z_ref[0]

    @pl.loop(0, groups)
    def _(group):
        for u in range(GROUP):
            t = group * GROUP + u
            fetch(t).wait()
        for u in range(GROUP):
            t = group * GROUP + u
            v = split_ref[items_ref[0, t]]
            v = jnp.concatenate([v, v], axis=1)
            product = lax.dot_general(
                v, held_ref[t], (((1,), (1,)), ((), ())), preferred_element_type=jnp.float32
            )
            acc_ref[items_ref[2, t]] += product

    turn = turn_ref[...]
    for b in range(row_blocks):
        total = acc_ref[b]
        total = total[:parts] + total[parts:]
        other = pltpu.roll(total[:, size:], parts // 2, 0)
        local_ref[:, b * size : (b + 1) * size] = total[:, :size] + turn * other

    tile = jnp.zeros((parts, LANES), jnp.float32)
    if step == ITERS - 1:
        w = local_ref[...]
        zs = [p[0] for p in prev] + [z_ref[0]]
        values = [lane_sum(z * w) for z in zs]
        gram = [[lane_sum(zs[i] * zs[j]) for j in range(i + 1)] for i in range(ITERS)]
        shares = []
        for i, z in enumerate(zs):
            along = lane_sum(z * w) if i else values[0]
            share = jnp.where(gram[i][i] > 0.0, along / gram[i][i], 0.0)
            shares.append(share)
            w = w - share * z
        values += shares + [lane_sum(z * w) for z in zs] + [lane_sum(w * w)]
        values += [gram[i][j] for i in range(ITERS) for j in range(i + 1)]
        for lane, value in enumerate(values):
            tile = put_lane(tile, lane, value)
    tile_ref[...] = tile


def run_step(step, items, turn, info, lines, prev, blocks, row_blocks):
    plane = len(lines)
    line, parts, rows = lines[0].shape
    nodes = plane * line
    size = rows // row_blocks
    total = items.shape[1]
    vmem = pl.BlockSpec(memory_space=pltpu.VMEM)
    tile = jax.ShapeDtypeStruct((parts, LANES), jnp.float32)
    return pl.pallas_call(
        functools.partial(step_kernel, step, plane, line),
        in_specs=[pl.BlockSpec(memory_space=pltpu.SMEM)]
        + [vmem] * (2 + plane + step)
        + [pl.BlockSpec(memory_space=pl.ANY)],
        out_specs=[vmem] * 5,
        out_shape=[
            jax.ShapeDtypeStruct((nodes, parts, rows), jnp.float32),
            jax.ShapeDtypeStruct((parts, rows), jnp.float32),
            jax.ShapeDtypeStruct((parts, rows), jnp.float32),
            tile,
            tile,
        ],
        scratch_shapes=[
            pltpu.VMEM((nodes * row_blocks + 1, SIDE * parts, size), jnp.bfloat16),
            pltpu.VMEM((row_blocks, SIDE * parts, 2 * size), jnp.float32),
            pltpu.VMEM((total, 2 * size, SIDE * size), jnp.bfloat16),
            pltpu.SemaphoreType.DMA((total,)),
        ],
        compiler_params=pltpu.CompilerParams(vmem_limit_bytes=VMEM_LIMIT),
        cost_estimate=pl.CostEstimate(
            flops=2 * total * SIDE * parts * 2 * size * SIDE * size,
            bytes_accessed=blocks.size * 2,
            transcendentals=0,
        ),
        name=f"step_{step}",
    )(items, turn, info, *lines, *prev, blocks)


def final_kernel(plane, line, info_ref, *refs):
    tiles = refs[:plane]
    krylov = refs[plane : plane + ITERS]
    out_ref, residual_ref = refs[plane + ITERS :]
    parts = info_ref.shape[0]
    fit = LANES // parts
    stacked = [tiles[q][i] for q in range(plane) for i in range(line)]
    sets = [
        jnp.transpose(jnp.concatenate(stacked[at : at + fit], axis=0)) for at in range(0, len(stacked), fit)
    ]
    info = jnp.transpose(jnp.concatenate([info_ref[...]] * fit, axis=0))

    def all_devices(shares):
        total = sum(shares[1:], shares[0])
        step = parts // 2
        while step < LANES:
            total = total + pltpu.roll(total, step, 1)
            step *= 2
        return total

    def row(table, at):
        return jnp.broadcast_to(table[at : at + 1], (8, LANES))

    zero = jnp.zeros((8, LANES), jnp.float32)
    norm, h00, h10, h01, h11, h21 = [row(info, i) for i in range(6)]
    last = [all_devices([row(s, i) for s in sets]) for i in range(ITERS)]
    shares = []
    for s in sets:
        off = [last[i] - row(s, ITERS + i) for i in range(ITERS)]
        square = row(s, 3 * ITERS)
        at = 3 * ITERS + 1
        for i in range(ITERS):
            square = square - 2.0 * off[i] * row(s, 2 * ITERS + i)
            for j in range(i + 1):
                square = square + (1.0 if i == j else 2.0) * off[i] * off[j] * row(s, at)
                at += 1
        shares.append(square)
    height = jnp.sqrt(jnp.maximum(all_devices(shares), 0.0))
    hessen = [[h00, h01, last[0]], [h10, h11, last[1]], [zero, h21, last[2]], [zero, zero, height]]
    normal = [[sum(h[m] * h[n] for h in hessen) for n in range(ITERS)] for m in range(ITERS)]
    low = [[None] * ITERS for _ in range(ITERS)]
    middle = []
    for m in range(ITERS):
        for n in range(m):
            rest = normal[m][n] - sum((low[m][k] * low[n][k] for k in range(n)), zero)
            low[m][n] = rest / low[n][n]
        low[m][m] = jnp.sqrt(normal[m][m] - sum((low[m][k] * low[m][k] for k in range(m)), zero))
        rest = norm * hessen[0][m] - sum((low[m][k] * middle[k] for k in range(m)), zero)
        middle.append(rest / low[m][m])
    coef_y = [None] * ITERS
    for m in reversed(range(ITERS)):
        rest = middle[m] - sum((low[k][m] * coef_y[k] for k in range(m + 1, ITERS)), zero)
        coef_y[m] = rest / low[m][m]
    total = zero
    for i, h in enumerate(hessen):
        misfit = (norm if i == 0 else zero) - sum(h[m] * coef_y[m] for m in range(ITERS))
        total = total + misfit * misfit
    residual_ref[...] = jnp.sqrt(total)
    columns = jnp.transpose(
        jnp.concatenate([y for y in coef_y] + [jnp.zeros((LANES - 8 * ITERS, LANES), jnp.float32)], axis=0)
    )[:parts]
    x = sum(columns[:, 8 * m : 8 * m + 1] * krylov[m][...] for m in range(ITERS))
    out_ref[0] = x[: parts // 2]
    out_ref[1] = x[parts // 2 :]


def run_final(info, tiles, krylov):
    plane = len(tiles)
    line, parts, _ = tiles[0].shape
    rows = krylov[0].shape[-1]
    vmem = pl.BlockSpec(memory_space=pltpu.VMEM)
    return pl.pallas_call(
        functools.partial(final_kernel, plane, line),
        in_specs=[vmem] * (1 + plane + ITERS),
        out_specs=[vmem] * 2,
        out_shape=[
            jax.ShapeDtypeStruct((2, parts // 2, rows), jnp.float32),
            jax.ShapeDtypeStruct((8, LANES), jnp.float32),
        ],
        name="final",
    )(info, *tiles, *krylov)


def make_shards(nodes, freqs):
    def shards(excitation, g_blocks, c_blocks, pattern, counts, freq_ids):
        angular = 0.2 * jnp.exp(freq_ids.astype(jnp.float32) * (math.log(8.0) / 1000.0))
        row_blocks, slots = pattern.shape
        size = g_blocks.shape[2]
        own_slots = g_blocks.shape[1]
        freq_count = excitation.shape[1]
        parts = 2 * freq_count
        node = lax.axis_index("node")
        freq = lax.axis_index("freq")
        blocks = None
        for d in range(freqs):
            perm = [(i, (i + d) % freqs) for i in range(freqs)]
            g_part = lax.ppermute(g_blocks, "freq", perm) if d else g_blocks
            c_part = lax.ppermute(c_blocks, "freq", perm) if d else c_blocks
            blocks = prepare(g_part, c_part, d, freqs, blocks)
        blocks = blocks.reshape(freqs * row_blocks * own_slots, 2 * size, SIDE * size)
        items = work_list(pattern, counts, node, freq, nodes, freqs)
        turn = jnp.broadcast_to(jnp.concatenate([-angular, angular])[:, None], (parts, LANES))
        info = jnp.zeros((parts, LANES), jnp.float32)
        krylov, own = [], []
        rows = excitation
        for step in range(ITERS):
            lines = gather_rows(rows, nodes, parts)
            z, mine, rows, info, tile = run_step(step, items, turn, info, lines, krylov, blocks, row_blocks)
            krylov.append(z)
            own.append(mine)
        tiles = gather_rows(tile, nodes, parts)
        answer, residual = run_final(info, tiles, own)
        return answer, residual[0, :freq_count]

    return shards


def solution(mesh):
    in_specs = (
        P(None, "freq", "node"),
        P("node", "freq", None, None),
        P("node", "freq", None, None),
        P("node", None),
        P("node"),
        P("freq"),
    )
    out_specs = (P(None, "freq", "node"), P("freq"))
    shards = make_shards(mesh.shape["node"], mesh.shape["freq"])
    return jax.shard_map(shards, mesh=mesh, in_specs=in_specs, out_specs=out_specs, check_vma=False)
```

time: 558 us -> 123 us (0.22)
  blocking collectives: 500 us -> 0 us
  Pallas kernels: 0 us -> 50.2 us
  starting transfers between devices: 0.08 us -> 35.7 us
  matrix products: 31 us -> 0 us
  waiting for transfers between devices: 1.42 us -> 21.3 us
  between operations: 14.3 us -> 1.58 us
    psum x10 -> x0, blocking collectives: 381 us -> none  [the longest x6 226 us: shards(): weight = lax.psum(projected(vector, applied), 'node')]
    all_gather x3 -> x0, blocking collectives: 119 us -> none  [shards(): portion = lax.all_gather(krylov[iteration], 'node', axis=2, tiled=True)]
    pallas_call x0 -> x6, Pallas kernels: none -> 50.2 us  [the longest x3 34.2 us: run_step(): pl.pallas_call(functools.partial(step_kernel, step, plane, line), in_spec...]
    ppermute x0 -> x26, starting transfers between devices: none -> 35.7 us  [the longest x12 20.6 us: gather_rows(): held.append(lax.ppermute(rows, 'node', perm))]
    dot_general x10 -> x0, matrix products: 30.9 us -> none  [the longest x3 16.6 us: shards(): jnp.einsum('bkij,bkcfj->cfbi', c_whole, picked, precision=lax.Precision.H...]
    ppermute x0 -> x26, waiting for transfers between devices: none -> 21.3 us  [the longest x12 13.2 us: gather_rows(): held.append(lax.ppermute(whole_line, 'node', perm))]
  transfers between devices with their start and end apart: 2 -> 26, of which waited for: 0 -> 16; matrix products, arithmetic and copies ran while one was open for 1% -> 4% of each run, Pallas kernels for 0% -> 11%
where the time goes in v1:
time: 123 us; the launch traced here: 121 us
  Pallas kernels  50.2 us (41%)
  starting transfers between devices  35.7 us (29%)
  waiting for transfers between devices  21.3 us (17%)
  local copies, waits for them, and re-layouts  8.59 us (7%)
  other arithmetic  3.83 us (3%)
  between operations  1.58 us (1%)
    pallas_call x3, Pallas kernels, run_step(): pl.pallas_call(functools.partial(step_kernel, step, plane, line), in_spec...  34.2 us
    ppermute x12, starting transfers between devices, gather_rows(): held.append(lax.ppermute(rows, 'node', perm))  20.6 us
    ppermute x12, starting transfers between devices, gather_rows(): held.append(lax.ppermute(whole_line, 'node', perm))  14.6 us
    pallas_call x2, Pallas kernels, prepare(): pl.pallas_call(prepare_kernel, grid=(row_blocks,), in_specs=in_specs, out...  13.5 us
    ppermute x12, waiting for transfers between devices, gather_rows(): held.append(lax.ppermute(whole_line, 'node', perm))  13.2 us
    ppermute x12, waiting for transfers between devices, gather_rows(): held.append(lax.ppermute(rows, 'node', perm))  8.08 us
    unnamed x24, local copies, waits for them, and re-layouts  5.96 us
  transfers between devices with their start and end apart: 26, of which 16 were waited for; matrix products, arithmetic and copies ran while one was open for 4% of the time, Pallas kernels for 11%

profile of v1, /device:TPU:0, one launch (start us, length us, event | category | flops | bytes accessed | tf_op | source)
XLA Modules:
  0.0 121.2 jit_solution(7230228765134410490)
XLA Ops:
  0.6 3.1 %collective-permute-start = (f32[2,4,1024]{2,1,0:T(4,128)}, f32[2,4,1024]{2,1,0:T(4,128)S(1)}, u32[]{:S(2)}, u32[]{:S(2)}) collective-permute-start(f32[2,4,1024]{2,1,0:T(4,128)} %param.8), channel_id=1, source_target_pairs={{0,8},{2,10},{4,12},{6,14},{8,16},{10,18},{12,20},{14,22},{16,24},... | collective-permute-start | bytes 98312 | tf_op jit(solution)/shard_map/ppermute | solution.py:28
  3.7 2.6 %collective-permute-start.1 = (f32[2,4,1024]{2,1,0:T(4,128)}, f32[2,4,1024]{2,1,0:T(4,128)S(1)}, u32[]{:S(2)}, u32[]{:S(2)}) collective-permute-start(f32[2,4,1024]{2,1,0:T(4,128)} %param.8), channel_id=1, source_target_pairs={{0,16},{2,18},{4,20},{6,22},{8,24},{10,26},{12,28},{14,30},{16,0},... | collective-permute-start | bytes 98312 | tf_op jit(solution)/shard_map/ppermute | solution.py:28
  6.3 1.3 %collective-permute-start.2 = (f32[2,4,1024]{2,1,0:T(4,128)}, f32[2,4,1024]{2,1,0:T(4,128)S(1)}, u32[]{:S(2)}, u32[]{:S(2)}) collective-permute-start(f32[2,4,1024]{2,1,0:T(4,128)} %param.8), channel_id=1, source_target_pairs={{0,24},{2,26},{4,28},{6,30},{8,0},{10,2},{12,4},{14,6},{16,8},{18,... | collective-permute-start | bytes 98312 | tf_op jit(solution)/shard_map/ppermute | solution.py:28
  8.5 0.7 fusion.4
  9.2 0.8 stack.73
  10.2 1.3 %fusion.18 = (s32[]{:T(128)}, s32[8]{0:T(128)S(1)}) fusion(s32[8]{0:T(128)} %param.12), kind=kLoop, calls=%fused_computation.64 | loop fusion | flops 15 | bytes 68 | tf_op jit(solution)/shard_map/reduce_sum | solution.py:57
  11.9 0.7 fusion.14
  12.7 1.6 %collective-permute-start.3 = (f32[4,8,1024]{2,1,0:T(8,128)S(1)}, f32[4,8,1024]{2,1,0:T(8,128)S(1)}, u32[]{:S(2)}, u32[]{:S(2)}) collective-permute-start(f32[4,8,1024]{2,1,0:T(8,128)S(1)} %constant_dynamic-update-slice_fusion.refs_0_), channel_id=1, source_target_pairs={{0,2},{2,0},{4,6},{6,4},{8,10},{10,8},{12,14},{14,12},{16,18},{18,... | collective-permute-start | bytes 393224 | tf_op jit(solution)/shard_map/ppermute | solution.py:33
  14.3 1.5 %collective-permute-start.4 = (f32[4,8,1024]{2,1,0:T(8,128)S(1)}, f32[4,8,1024]{2,1,0:T(8,128)S(1)}, u32[]{:S(2)}, u32[]{:S(2)}) collective-permute-start(f32[4,8,1024]{2,1,0:T(8,128)S(1)} %constant_dynamic-update-slice_fusion.refs_0_), channel_id=1, source_target_pairs={{0,4},{2,6},{4,0},{6,2},{8,12},{10,14},{12,8},{14,10},{16,20},{18,... | collective-permute-start | bytes 393224 | tf_op jit(solution)/shard_map/ppermute | solution.py:33
  16.3 0.7 fusion.19
  17.7 6.8 %prepare_0.1.rest_0_ = bf16[2,8,4,256,256]{4,3,2,1,0:T(8,128)(2,1)} custom-call(f32[8,4,128,128]{3,2,1,0:T(8,128)} %g_ref.1, f32[8,4,128,128]{3,2,1,0:T(8,128)} %c_ref.1), custom_call_target="tpu_custom_call" | custom-call | flops 4194304 | bytes 8388608 | tf_op jit(solution)/shard_map/prepare_0/pallas_call | solution.py:88
  24.5 1.4 %copy-done.5 = f32[8,4,128,128]{3,2,1,0:T(8,128)} copy-done((f32[8,4,128,128]{3,2,1,0:T(8,128)}, f32[8,4,128,128]{3,2,1,0:T(8,128)S(1)}, u32[]{:S(2)}) %copy-start.5) | copy-done | bytes 2097176
  25.9 6.8 %prepare_1.1 = bf16[2,8,4,256,256]{4,3,2,1,0:T(8,128)(2,1)} custom-call(f32[8,4,128,128]{3,2,1,0:T(8,128)} %copy-done.5, f32[8,4,128,128]{3,2,1,0:T(8,128)} %collective-permute-done.7.c_ref, bf16[2,8,4,256,256]{4,3,2,1,0:T(8,128)(2,1)} %prepare_0.1.rest_0_), custom_call_target="tpu_custom_call", output_to_operand_aliasing={{}: (2, {})} | custom-call | flops 4194304 | bytes 8388608 | tf_op jit(solution)/shard_map/prepare_1/pallas_call | solution.py:88
  32.7 3.4 %copy-done = bf16[2,8,4,256,256]{4,3,2,1,0:T(8,128)(2,1)S(1)} copy-done((bf16[2,8,4,256,256]{4,3,2,1,0:T(8,128)(2,1)S(1)}, bf16[2,8,4,256,256]{4,3,2,1,0:T(8,128)(2,1)}, u32[]{:S(2)}) %copy-start) | copy-done | bytes 8388632
  36.1 11.2 %step_0.1 = (f32[16,8,1024]{2,1,0:T(8,128)S(1)}, f32[8,1024]{1,0:T(8,128)S(1)}, f32[8,1024]{1,0:T(8,128)S(1)}, f32[8,128]{1,0:T(8,128)S(1)}, f32[8,128]{1,0:T(8,128)}) custom-call(s32[4,64]{1,0:T(4,128)S(1)} %concatenate.10.items_ref, f32[8,128]{1,0:T(8,128)S(1)} %broadcast_in_dim.71.turn_ref, f32[8,128]{1,0:T(8,128)S(1)} %broadcast_in_dim.72.info_in_ref, ...), custom_call_target="tpu_custom_call" | custom-call | flops 134217728 | bytes 8388608 | tf_op jit(solution)/shard_map/step_0/pallas_call | solution.py:240
  47.3 0.7 collective-permute-start.8
  48.0 0.8 collective-permute-start.9
  48.8 2.4 %collective-permute-start.10 = (f32[8,1024]{1,0:T(8,128)S(1)}, f32[8,1024]{1,0:T(8,128)S(1)}, u32[]{:S(2)}, u32[]{:S(2)}) collective-permute-start(f32[8,1024]{1,0:T(8,128)S(1)} %get-tuple-element.28), channel_id=1, source_target_pairs={{0,24},{2,26},{4,28},{6,30},{8,0},{10,2},{12,4},{14,6},{16,8},{18,... | collective-permute-start | bytes 98312 | tf_op jit(solution)/shard_map/ppermute | solution.py:28
  51.2 2.0 %collective-permute-done.8 = f32[8,1024]{1,0:T(8,128)S(1)} collective-permute-done((f32[8,1024]{1,0:T(8,128)S(1)}, f32[8,1024]{1,0:T(8,128)S(1)}, u32[]{:S(2)}, u32[]{:S(2)}) %collective-permute-start.8) | collective-permute-done | bytes 32800 | tf_op jit(solution)/shard_map/ppermute | solution.py:28
  53.2 0.7 collective-permute-done.9
  53.9 1.4 %collective-permute-start.11 = (f32[4,8,1024]{2,1,0:T(8,128)S(1)}, f32[4,8,1024]{2,1,0:T(8,128)S(1)}, u32[]{:S(2)}, u32[]{:S(2)}) collective-permute-start(f32[4,8,1024]{2,1,0:T(8,128)S(1)} %pad_maximum_fusion.refs_0_), channel_id=1, source_target_pairs={{0,2},{2,0},{4,6},{6,4},{8,10},{10,8},{12,14},{14,12},{16,18},{18,... | collective-permute-start | bytes 393224 | tf_op jit(solution)/shard_map/ppermute | solution.py:33
  55.2 2.6 %collective-permute-start.12 = (f32[4,8,1024]{2,1,0:T(8,128)S(1)}, f32[4,8,1024]{2,1,0:T(8,128)S(1)}, u32[]{:S(2)}, u32[]{:S(2)}) collective-permute-start(f32[4,8,1024]{2,1,0:T(8,128)S(1)} %pad_maximum_fusion.refs_0_), channel_id=1, source_target_pairs={{0,4},{2,6},{4,0},{6,2},{8,12},{10,14},{12,8},{14,10},{16,20},{18,... | collective-permute-start | bytes 393224 | tf_op jit(solution)/shard_map/ppermute | solution.py:33
  57.8 2.4 %collective-permute-done.11.refs_1_ = f32[4,8,1024]{2,1,0:T(8,128)S(1)} collective-permute-done((f32[4,8,1024]{2,1,0:T(8,128)S(1)}, f32[4,8,1024]{2,1,0:T(8,128)S(1)}, u32[]{:S(2)}, u32[]{:S(2)}) %collective-permute-start.11) | collective-permute-done | bytes 131104 | tf_op jit(solution)/shard_map/ppermute | solution.py:33
  60.2 1.6 %collective-permute-done.12.refs_2_ = f32[4,8,1024]{2,1,0:T(8,128)S(1)} collective-permute-done((f32[4,8,1024]{2,1,0:T(8,128)S(1)}, f32[4,8,1024]{2,1,0:T(8,128)S(1)}, u32[]{:S(2)}, u32[]{:S(2)}) %collective-permute-start.12) | collective-permute-done | bytes 131104 | tf_op jit(solution)/shard_map/ppermute | solution.py:33
  61.9 1.8 %collective-permute-done.13.refs_3_ = f32[4,8,1024]{2,1,0:T(8,128)S(1)} collective-permute-done((f32[4,8,1024]{2,1,0:T(8,128)S(1)}, f32[4,8,1024]{2,1,0:T(8,128)S(1)}, u32[]{:S(2)}, u32[]{:S(2)}) %collective-permute-start.13) | collective-permute-done | bytes 131104 | tf_op jit(solution)/shard_map/ppermute | solution.py:33
  63.7 11.4 %step_1.1 = (f32[16,8,1024]{2,1,0:T(8,128)S(1)}, f32[8,1024]{1,0:T(8,128)S(1)}, f32[8,1024]{1,0:T(8,128)S(1)}, f32[8,128]{1,0:T(8,128)S(1)}, f32[8,128]{1,0:T(8,128)}) custom-call(s32[4,64]{1,0:T(4,128)S(1)} %concatenate.10.items_ref, f32[8,128]{1,0:T(8,128)S(1)} %broadcast_in_dim.71.turn_ref, f32[8,128]{1,0:T(8,128)S(1)} %get-tuple-element.27.info_in_ref, ...), custom_call_target="tpu_custom_call" | custom-call | flops 134217728 | bytes 8388608 | tf_op jit(solution)/shard_map/step_1/pallas_call | solution.py:240
  75.1 1.0 collective-permute-start.14
  76.0 3.0 %collective-permute-start.15 = (f32[8,1024]{1,0:T(8,128)S(1)}, f32[8,1024]{1,0:T(8,128)S(1)}, u32[]{:S(2)}, u32[]{:S(2)}) collective-permute-start(f32[8,1024]{1,0:T(8,128)S(1)} %get-tuple-element.31), channel_id=1, source_target_pairs={{0,16},{2,18},{4,20},{6,22},{8,24},{10,26},{12,28},{14,30},{16,0},... | collective-permute-start | bytes 98312 | tf_op jit(solution)/shard_map/ppermute | solution.py:28
  79.0 1.0 collective-permute-start.16
  80.1 0.8 collective-permute-done.14
  81.2 1.7 %collective-permute-done.16 = f32[8,1024]{1,0:T(8,128)S(1)} collective-permute-done((f32[8,1024]{1,0:T(8,128)S(1)}, f32[8,1024]{1,0:T(8,128)S(1)}, u32[]{:S(2)}, u32[]{:S(2)}) %collective-permute-start.16) | collective-permute-done | bytes 32800 | tf_op jit(solution)/shard_map/ppermute | solution.py:28
  83.1 1.1 collective-permute-start.18
  84.1 2.4 %collective-permute-start.19 = (f32[4,8,1024]{2,1,0:T(8,128)S(1)}, f32[4,8,1024]{2,1,0:T(8,128)S(1)}, u32[]{:S(2)}, u32[]{:S(2)}) collective-permute-start(f32[4,8,1024]{2,1,0:T(8,128)S(1)} %pad_maximum_fusion.1.refs_0_), channel_id=1, source_target_pairs={{0,6},{2,4},{4,2},{6,0},{8,14},{10,12},{12,10},{14,8},{16,22},{18,... | collective-permute-start | bytes 393224 | tf_op jit(solution)/shard_map/ppermute | solution.py:33
  86.5 1.5 %collective-permute-done.17.refs_1_ = f32[4,8,1024]{2,1,0:T(8,128)S(1)} collective-permute-done((f32[4,8,1024]{2,1,0:T(8,128)S(1)}, f32[4,8,1024]{2,1,0:T(8,128)S(1)}, u32[]{:S(2)}, u32[]{:S(2)}) %collective-permute-start.17) | collective-permute-done | bytes 131104 | tf_op jit(solution)/shard_map/ppermute | solution.py:33
  88.1 2.0 %collective-permute-done.19.refs_3_ = f32[4,8,1024]{2,1,0:T(8,128)S(1)} collective-permute-done((f32[4,8,1024]{2,1,0:T(8,128)S(1)}, f32[4,8,1024]{2,1,0:T(8,128)S(1)}, u32[]{:S(2)}, u32[]{:S(2)}) %collective-permute-start.19) | collective-permute-done | bytes 131104 | tf_op jit(solution)/shard_map/ppermute | solution.py:33
  90.0 11.7 %step_2.1 = (f32[16,8,1024]{2,1,0:T(8,128)}, f32[8,1024]{1,0:T(8,128)S(1)}, f32[8,1024]{1,0:T(8,128)}, f32[8,128]{1,0:T(8,128)S(1)}, f32[8,128]{1,0:T(8,128)S(1)}) custom-call(s32[4,64]{1,0:T(4,128)S(1)} %concatenate.10.items_ref, f32[8,128]{1,0:T(8,128)S(1)} %broadcast_in_dim.71.turn_ref, f32[8,128]{1,0:T(8,128)S(1)} %get-tuple-element.30.info_in_ref, ...), custom_call_target="tpu_custom_call" | custom-call | flops 134217728 | bytes 8388608 | tf_op jit(solution)/shard_map/step_2/pallas_call | solution.py:240
  102.3 0.7 collective-permute-start.20
  103.0 3.0 %collective-permute-start.21 = (f32[8,128]{1,0:T(8,128)S(1)}, f32[8,128]{1,0:T(8,128)S(1)}, u32[]{:S(2)}, u32[]{:S(2)}) collective-permute-start(f32[8,128]{1,0:T(8,128)S(1)} %get-tuple-element.34), channel_id=1, source_target_pairs={{0,16},{2,18},{4,20},{6,22},{8,24},{10,26},{12,28},{14,30},{16,0},... | collective-permute-start | bytes 12296 | tf_op jit(solution)/shard_map/ppermute | solution.py:28
  106.0 1.0 collective-permute-start.22
  107.0 0.7 collective-permute-done.20
  107.7 1.9 %collective-permute-done.22 = f32[8,128]{1,0:T(8,128)S(1)} collective-permute-done((f32[8,128]{1,0:T(8,128)S(1)}, f32[8,128]{1,0:T(8,128)S(1)}, u32[]{:S(2)}, u32[]{:S(2)}) %collective-permute-start.22) | collective-permute-done | bytes 4128 | tf_op jit(solution)/shard_map/ppermute | solution.py:28
  109.6 1.2 collective-permute-start.23
  110.8 1.5 %collective-permute-start.24 = (f32[4,8,128]{2,1,0:T(8,128)S(1)}, f32[4,8,128]{2,1,0:T(8,128)S(1)}, u32[]{:S(2)}, u32[]{:S(2)}) collective-permute-start(f32[4,8,128]{2,1,0:T(8,128)S(1)} %pad_maximum_fusion.2.refs_0_), channel_id=1, source_target_pairs={{0,4},{2,6},{4,0},{6,2},{8,12},{10,14},{12,8},{14,10},{16,20},{18,... | collective-permute-start | bytes 49160 | tf_op jit(solution)/shard_map/ppermute | solution.py:33
  112.3 0.8 collective-permute-start.25
  113.4 1.1 collective-permute-done.24.refs_2_
  114.5 2.4 %collective-permute-done.25.refs_3_ = f32[4,8,128]{2,1,0:T(8,128)S(1)} collective-permute-done((f32[4,8,128]{2,1,0:T(8,128)S(1)}, f32[4,8,128]{2,1,0:T(8,128)S(1)}, u32[]{:S(2)}, u32[]{:S(2)}) %collective-permute-start.25) | collective-permute-done | bytes 16416 | tf_op jit(solution)/shard_map/ppermute | solution.py:33
  117.5 2.4 %final.1 = (f32[2,4,1024]{2,1,0:T(4,128)}, f32[8,128]{1,0:T(8,128)}) custom-call(f32[8,128]{1,0:T(8,128)} %copy-done.4, f32[4,8,128]{2,1,0:T(8,128)} %copy-done.6, f32[4,8,128]{2,1,0:T(8,128)} %copy-done.7, f32[4,8,128]{2,1,0:T(8,128)} %copy-done.8, f32[4,8,128]{2,1,0:T(8,128)} %copy-done.9, f32[8,1024]{1,0:T(8,128)} %copy-done.1, f32[8,1024]{1,0:T(8,128)} %copy-done.2, ...), custom_call_target="tpu_custom_call" | custom-call | tf_op jit(solution)/shard_map/final/pallas_call | solution.py:340
  120.0 1.2 slice_bitcast_fusion
  (72 shorter events, 4.2 us)
Async XLA Ops:
  0.6 11.9 %collective-permute-start = (f32[2,4,1024]{2,1,0:T(4,128)}, f32[2,4,1024]{2,1,0:T(4,128)S(1)}, u32[]{:S(2)}, u32[]{:S(2)}) collective-permute-start(f32[2,4,1024]{2,1,0:T(4,128)} %param.8), channel_id=1, source_target_pairs={{0,8},{2,10},{4,12},{6,14},{8,16},{10,18},{12,20},{14,22},{16,24},... | collective-permute-start | bytes 98312 | tf_op jit(solution)/shard_map/ppermute | solution.py:28
  3.7 8.9 %collective-permute-start.1 = (f32[2,4,1024]{2,1,0:T(4,128)}, f32[2,4,1024]{2,1,0:T(4,128)S(1)}, u32[]{:S(2)}, u32[]{:S(2)}) collective-permute-start(f32[2,4,1024]{2,1,0:T(4,128)} %param.8), channel_id=1, source_target_pairs={{0,16},{2,18},{4,20},{6,22},{8,24},{10,26},{12,28},{14,30},{16,0},... | collective-permute-start | bytes 98312 | tf_op jit(solution)/shard_map/ppermute | solution.py:28
  6.3 6.3 %collective-permute-start.2 = (f32[2,4,1024]{2,1,0:T(4,128)}, f32[2,4,1024]{2,1,0:T(4,128)S(1)}, u32[]{:S(2)}, u32[]{:S(2)}) collective-permute-start(f32[2,4,1024]{2,1,0:T(4,128)} %param.8), channel_id=1, source_target_pairs={{0,24},{2,26},{4,28},{6,30},{8,0},{10,2},{12,4},{14,6},{16,8},{18,... | collective-permute-start | bytes 98312 | tf_op jit(solution)/shard_map/ppermute | solution.py:28
  7.6 16.9 %collective-permute-start.6 = (f32[8,4,128,128]{3,2,1,0:T(8,128)}, f32[8,4,128,128]{3,2,1,0:T(8,128)S(1)}, u32[]{:S(2)}, u32[]{:S(2)}) collective-permute-start(f32[8,4,128,128]{3,2,1,0:T(8,128)} %g_ref.1), channel_id=1, source_target_pairs={{0,1},{1,0},{2,3},{3,2},{4,5},{5,4},{6,7},{7,6},{8,9},{9,8},{10,11... | collective-permute-start | bytes 6291464 | tf_op jit(solution)/shard_map/ppermute | solution.py:365
  7.6 16.9 %collective-permute-start.7 = (f32[8,4,128,128]{3,2,1,0:T(8,128)}, f32[8,4,128,128]{3,2,1,0:T(8,128)}, u32[]{:S(2)}, u32[]{:S(2)}) collective-permute-start(f32[8,4,128,128]{3,2,1,0:T(8,128)} %c_ref.1), channel_id=1, source_target_pairs={{0,1},{1,0},{2,3},{3,2},{4,5},{5,4},{6,7},{7,6},{8,9},{9,8},{10,11... | collective-permute-start | bytes 6291464 | tf_op jit(solution)/shard_map/ppermute | solution.py:366
  12.7 19.9 %collective-permute-start.3 = (f32[4,8,1024]{2,1,0:T(8,128)S(1)}, f32[4,8,1024]{2,1,0:T(8,128)S(1)}, u32[]{:S(2)}, u32[]{:S(2)}) collective-permute-start(f32[4,8,1024]{2,1,0:T(8,128)S(1)} %constant_dynamic-update-slice_fusion.refs_0_), channel_id=1, source_target_pairs={{0,2},{2,0},{4,6},{6,4},{8,10},{10,8},{12,14},{14,12},{16,18},{18,... | collective-permute-start | bytes 393224 | tf_op jit(solution)/shard_map/ppermute | solution.py:33
  14.3 18.4 %collective-permute-start.4 = (f32[4,8,1024]{2,1,0:T(8,128)S(1)}, f32[4,8,1024]{2,1,0:T(8,128)S(1)}, u32[]{:S(2)}, u32[]{:S(2)}) collective-permute-start(f32[4,8,1024]{2,1,0:T(8,128)S(1)} %constant_dynamic-update-slice_fusion.refs_0_), channel_id=1, source_target_pairs={{0,4},{2,6},{4,0},{6,2},{8,12},{10,14},{12,8},{14,10},{16,20},{18,... | collective-permute-start | bytes 393224 | tf_op jit(solution)/shard_map/ppermute | solution.py:33
  15.8 16.9 %collective-permute-start.5 = (f32[4,8,1024]{2,1,0:T(8,128)S(1)}, f32[4,8,1024]{2,1,0:T(8,128)S(1)}, u32[]{:S(2)}, u32[]{:S(2)}) collective-permute-start(f32[4,8,1024]{2,1,0:T(8,128)S(1)} %constant_dynamic-update-slice_fusion.refs_0_), channel_id=1, source_target_pairs={{0,6},{2,4},{4,2},{6,0},{8,14},{10,12},{12,10},{14,8},{16,22},{18,... | collective-permute-start | bytes 393224 | tf_op jit(solution)/shard_map/ppermute | solution.py:33
  24.5 1.4 %copy-start.5 = (f32[8,4,128,128]{3,2,1,0:T(8,128)}, f32[8,4,128,128]{3,2,1,0:T(8,128)S(1)}, u32[]{:S(2)}) copy-start(f32[8,4,128,128]{3,2,1,0:T(8,128)S(1)} %collective-permute-done.6.g_ref) | copy-start | bytes 6291460
  32.7 3.4 %copy-start = (bf16[2,8,4,256,256]{4,3,2,1,0:T(8,128)(2,1)S(1)}, bf16[2,8,4,256,256]{4,3,2,1,0:T(8,128)(2,1)}, u32[]{:S(2)}) copy-start(bf16[2,8,4,256,256]{4,3,2,1,0:T(8,128)(2,1)} %prepare_1.1) | copy-start | bytes 25165828
  47.3 27.7 %copy-start.1 = (f32[8,1024]{1,0:T(8,128)}, f32[8,1024]{1,0:T(8,128)S(1)}, u32[]{:S(2)}) copy-start(f32[8,1024]{1,0:T(8,128)S(1)} %get-tuple-element.35.refs_4_) | copy-start | bytes 98308
  47.3 5.9 %collective-permute-start.8 = (f32[8,1024]{1,0:T(8,128)S(1)}, f32[8,1024]{1,0:T(8,128)S(1)}, u32[]{:S(2)}, u32[]{:S(2)}) collective-permute-start(f32[8,1024]{1,0:T(8,128)S(1)} %get-tuple-element.28), channel_id=1, source_target_pairs={{0,8},{2,10},{4,12},{6,14},{8,16},{10,18},{12,20},{14,22},{16,24},... | collective-permute-start | bytes 98312 | tf_op jit(solution)/shard_map/ppermute | solution.py:28
  48.0 5.8 %collective-permute-start.9 = (f32[8,1024]{1,0:T(8,128)S(1)}, f32[8,1024]{1,0:T(8,128)S(1)}, u32[]{:S(2)}, u32[]{:S(2)}) collective-permute-start(f32[8,1024]{1,0:T(8,128)S(1)} %get-tuple-element.28), channel_id=1, source_target_pairs={{0,16},{2,18},{4,20},{6,22},{8,24},{10,26},{12,28},{14,30},{16,0},... | collective-permute-start | bytes 98312 | tf_op jit(solution)/shard_map/ppermute | solution.py:28
  48.8 5.0 %collective-permute-start.10 = (f32[8,1024]{1,0:T(8,128)S(1)}, f32[8,1024]{1,0:T(8,128)S(1)}, u32[]{:S(2)}, u32[]{:S(2)}) collective-permute-start(f32[8,1024]{1,0:T(8,128)S(1)} %get-tuple-element.28), channel_id=1, source_target_pairs={{0,24},{2,26},{4,28},{6,30},{8,0},{10,2},{12,4},{14,6},{16,8},{18,... | collective-permute-start | bytes 98312 | tf_op jit(solution)/shard_map/ppermute | solution.py:28
  53.9 6.4 %collective-permute-start.11 = (f32[4,8,1024]{2,1,0:T(8,128)S(1)}, f32[4,8,1024]{2,1,0:T(8,128)S(1)}, u32[]{:S(2)}, u32[]{:S(2)}) collective-permute-start(f32[4,8,1024]{2,1,0:T(8,128)S(1)} %pad_maximum_fusion.refs_0_), channel_id=1, source_target_pairs={{0,2},{2,0},{4,6},{6,4},{8,10},{10,8},{12,14},{14,12},{16,18},{18,... | collective-permute-start | bytes 393224 | tf_op jit(solution)/shard_map/ppermute | solution.py:33
  55.2 6.7 %collective-permute-start.12 = (f32[4,8,1024]{2,1,0:T(8,128)S(1)}, f32[4,8,1024]{2,1,0:T(8,128)S(1)}, u32[]{:S(2)}, u32[]{:S(2)}) collective-permute-start(f32[4,8,1024]{2,1,0:T(8,128)S(1)} %pad_maximum_fusion.refs_0_), channel_id=1, source_target_pairs={{0,4},{2,6},{4,0},{6,2},{8,12},{10,14},{12,8},{14,10},{16,20},{18,... | collective-permute-start | bytes 393224 | tf_op jit(solution)/shard_map/ppermute | solution.py:33
  57.8 5.9 %collective-permute-start.13 = (f32[4,8,1024]{2,1,0:T(8,128)S(1)}, f32[4,8,1024]{2,1,0:T(8,128)S(1)}, u32[]{:S(2)}, u32[]{:S(2)}) collective-permute-start(f32[4,8,1024]{2,1,0:T(8,128)S(1)} %pad_maximum_fusion.refs_0_), channel_id=1, source_target_pairs={{0,6},{2,4},{4,2},{6,0},{8,14},{10,12},{12,10},{14,8},{16,22},{18,... | collective-permute-start | bytes 393224 | tf_op jit(solution)/shard_map/ppermute | solution.py:33
  75.1 26.6 %copy-start.2 = (f32[8,1024]{1,0:T(8,128)}, f32[8,1024]{1,0:T(8,128)S(1)}, u32[]{:S(2)}) copy-start(f32[8,1024]{1,0:T(8,128)S(1)} %get-tuple-element.36.refs_5_) | copy-start | bytes 98308
  75.1 5.8 %collective-permute-start.14 = (f32[8,1024]{1,0:T(8,128)S(1)}, f32[8,1024]{1,0:T(8,128)S(1)}, u32[]{:S(2)}, u32[]{:S(2)}) collective-permute-start(f32[8,1024]{1,0:T(8,128)S(1)} %get-tuple-element.31), channel_id=1, source_target_pairs={{0,8},{2,10},{4,12},{6,14},{8,16},{10,18},{12,20},{14,22},{16,24},... | collective-permute-start | bytes 98312 | tf_op jit(solution)/shard_map/ppermute | solution.py:28
  76.0 5.2 %collective-permute-start.15 = (f32[8,1024]{1,0:T(8,128)S(1)}, f32[8,1024]{1,0:T(8,128)S(1)}, u32[]{:S(2)}, u32[]{:S(2)}) collective-permute-start(f32[8,1024]{1,0:T(8,128)S(1)} %get-tuple-element.31), channel_id=1, source_target_pairs={{0,16},{2,18},{4,20},{6,22},{8,24},{10,26},{12,28},{14,30},{16,0},... | collective-permute-start | bytes 98312 | tf_op jit(solution)/shard_map/ppermute | solution.py:28
  79.0 3.9 %collective-permute-start.16 = (f32[8,1024]{1,0:T(8,128)S(1)}, f32[8,1024]{1,0:T(8,128)S(1)}, u32[]{:S(2)}, u32[]{:S(2)}) collective-permute-start(f32[8,1024]{1,0:T(8,128)S(1)} %get-tuple-element.31), channel_id=1, source_target_pairs={{0,24},{2,26},{4,28},{6,30},{8,0},{10,2},{12,4},{14,6},{16,8},{18,... | collective-permute-start | bytes 98312 | tf_op jit(solution)/shard_map/ppermute | solution.py:28
  82.9 5.0 %collective-permute-start.17 = (f32[4,8,1024]{2,1,0:T(8,128)S(1)}, f32[4,8,1024]{2,1,0:T(8,128)S(1)}, u32[]{:S(2)}, u32[]{:S(2)}) collective-permute-start(f32[4,8,1024]{2,1,0:T(8,128)S(1)} %pad_maximum_fusion.1.refs_0_), channel_id=1, source_target_pairs={{0,2},{2,0},{4,6},{6,4},{8,10},{10,8},{12,14},{14,12},{16,18},{18,... | collective-permute-start | bytes 393224 | tf_op jit(solution)/shard_map/ppermute | solution.py:33
  83.1 5.0 %collective-permute-start.18 = (f32[4,8,1024]{2,1,0:T(8,128)S(1)}, f32[4,8,1024]{2,1,0:T(8,128)S(1)}, u32[]{:S(2)}, u32[]{:S(2)}) collective-permute-start(f32[4,8,1024]{2,1,0:T(8,128)S(1)} %pad_maximum_fusion.1.refs_0_), channel_id=1, source_target_pairs={{0,4},{2,6},{4,0},{6,2},{8,12},{10,14},{12,8},{14,10},{16,20},{18,... | collective-permute-start | bytes 393224 | tf_op jit(solution)/shard_map/ppermute | solution.py:33
  84.1 5.9 %collective-permute-start.19 = (f32[4,8,1024]{2,1,0:T(8,128)S(1)}, f32[4,8,1024]{2,1,0:T(8,128)S(1)}, u32[]{:S(2)}, u32[]{:S(2)}) collective-permute-start(f32[4,8,1024]{2,1,0:T(8,128)S(1)} %pad_maximum_fusion.1.refs_0_), channel_id=1, source_target_pairs={{0,6},{2,4},{4,2},{6,0},{8,14},{10,12},{12,10},{14,8},{16,22},{18,... | collective-permute-start | bytes 393224 | tf_op jit(solution)/shard_map/ppermute | solution.py:33
  101.7 0.6 copy-start.3
  102.3 7.3 %copy-start.4 = (f32[8,128]{1,0:T(8,128)}, f32[8,128]{1,0:T(8,128)S(1)}, u32[]{:S(2)}) copy-start(f32[8,128]{1,0:T(8,128)S(1)} %get-tuple-element.33.info_ref) | copy-start | bytes 12292
  102.3 5.4 %collective-permute-start.20 = (f32[8,128]{1,0:T(8,128)S(1)}, f32[8,128]{1,0:T(8,128)S(1)}, u32[]{:S(2)}, u32[]{:S(2)}) collective-permute-start(f32[8,128]{1,0:T(8,128)S(1)} %get-tuple-element.34), channel_id=1, source_target_pairs={{0,8},{2,10},{4,12},{6,14},{8,16},{10,18},{12,20},{14,22},{16,24},... | collective-permute-start | bytes 12296 | tf_op jit(solution)/shard_map/ppermute | solution.py:28
  103.0 4.7 %collective-permute-start.21 = (f32[8,128]{1,0:T(8,128)S(1)}, f32[8,128]{1,0:T(8,128)S(1)}, u32[]{:S(2)}, u32[]{:S(2)}) collective-permute-start(f32[8,128]{1,0:T(8,128)S(1)} %get-tuple-element.34), channel_id=1, source_target_pairs={{0,16},{2,18},{4,20},{6,22},{8,24},{10,26},{12,28},{14,30},{16,0},... | collective-permute-start | bytes 12296 | tf_op jit(solution)/shard_map/ppermute | solution.py:28
  106.0 3.6 %collective-permute-start.22 = (f32[8,128]{1,0:T(8,128)S(1)}, f32[8,128]{1,0:T(8,128)S(1)}, u32[]{:S(2)}, u32[]{:S(2)}) collective-permute-start(f32[8,128]{1,0:T(8,128)S(1)} %get-tuple-element.34), channel_id=1, source_target_pairs={{0,24},{2,26},{4,28},{6,30},{8,0},{10,2},{12,4},{14,6},{16,8},{18,... | collective-permute-start | bytes 12296 | tf_op jit(solution)/shard_map/ppermute | solution.py:28
  109.6 7.4 %copy-start.6 = (f32[4,8,128]{2,1,0:T(8,128)}, f32[4,8,128]{2,1,0:T(8,128)S(1)}, u32[]{:S(2)}) copy-start(f32[4,8,128]{2,1,0:T(8,128)S(1)} %pad_maximum_fusion.2.refs_0_) | copy-start | bytes 49156
  109.6 3.8 %collective-permute-start.23 = (f32[4,8,128]{2,1,0:T(8,128)S(1)}, f32[4,8,128]{2,1,0:T(8,128)S(1)}, u32[]{:S(2)}, u32[]{:S(2)}) collective-permute-start(f32[4,8,128]{2,1,0:T(8,128)S(1)} %pad_maximum_fusion.2.refs_0_), channel_id=1, source_target_pairs={{0,2},{2,0},{4,6},{6,4},{8,10},{10,8},{12,14},{14,12},{16,18},{18,... | collective-permute-start | bytes 49160 | tf_op jit(solution)/shard_map/ppermute | solution.py:33
  110.8 3.7 %collective-permute-start.24 = (f32[4,8,128]{2,1,0:T(8,128)S(1)}, f32[4,8,128]{2,1,0:T(8,128)S(1)}, u32[]{:S(2)}, u32[]{:S(2)}) collective-permute-start(f32[4,8,128]{2,1,0:T(8,128)S(1)} %pad_maximum_fusion.2.refs_0_), channel_id=1, source_target_pairs={{0,4},{2,6},{4,0},{6,2},{8,12},{10,14},{12,8},{14,10},{16,20},{18,... | collective-permute-start | bytes 49160 | tf_op jit(solution)/shard_map/ppermute | solution.py:33
  112.3 4.6 %collective-permute-start.25 = (f32[4,8,128]{2,1,0:T(8,128)S(1)}, f32[4,8,128]{2,1,0:T(8,128)S(1)}, u32[]{:S(2)}, u32[]{:S(2)}) collective-permute-start(f32[4,8,128]{2,1,0:T(8,128)S(1)} %pad_maximum_fusion.2.refs_0_), channel_id=1, source_target_pairs={{0,6},{2,4},{4,2},{6,0},{8,14},{10,12},{12,10},{14,8},{16,22},{18,... | collective-permute-start | bytes 49160 | tf_op jit(solution)/shard_map/ppermute | solution.py:33
  113.4 3.6 %copy-start.7 = (f32[4,8,128]{2,1,0:T(8,128)}, f32[4,8,128]{2,1,0:T(8,128)S(1)}, u32[]{:S(2)}) copy-start(f32[4,8,128]{2,1,0:T(8,128)S(1)} %collective-permute-done.23.refs_1_) | copy-start | bytes 49156
  114.5 2.4 %copy-start.8 = (f32[4,8,128]{2,1,0:T(8,128)}, f32[4,8,128]{2,1,0:T(8,128)S(1)}, u32[]{:S(2)}) copy-start(f32[4,8,128]{2,1,0:T(8,128)S(1)} %collective-permute-done.24.refs_2_) | copy-start | bytes 49156
  116.9 0.6 copy-start.9

commit v2 on v1

v2 whole, which is shorter than its diff:
```python
import functools
import math

import jax
import jax.numpy as jnp
from jax import lax
from jax.experimental import pallas as pl
from jax.experimental.pallas import tpu as pltpu
from jax.sharding import PartitionSpec as P

ITERS = 3
LANES = 128
GROUP = 4
VMEM_LIMIT = 20 * 1024 * 1024


def split_nodes(nodes):
    plane = 4 if nodes % 4 == 0 else 1
    return nodes // plane, plane


def gather_rows(rows, nodes, parts):
    line, plane = split_nodes(nodes)
    held = [rows]
    for d in range(1, line):
        perm = [(i, (i + d * plane) % nodes) for i in range(nodes)]
        held.append(lax.ppermute(rows, "node", perm))
    whole_line = jnp.stack(held).reshape(line, parts, rows.shape[-1])
    held = [whole_line]
    for d in range(1, plane):
        perm = [(i, (i // plane) * plane + ((i % plane) ^ d)) for i in range(nodes)]
        held.append(lax.ppermute(whole_line, "node", perm))
    return held


def gathered_place(owner, node, nodes):
    line, plane = split_nodes(nodes)
    far = lax.rem(node // plane - owner // plane + line, line)
    return ((node % plane) ^ (owner % plane)) * line + far


def work_list(pattern, counts, node, freq, nodes, freqs):
    row_blocks, slots = pattern.shape
    own_slots = slots // freqs
    total = row_blocks * own_slots
    place = gathered_place(pattern // row_blocks, node, nodes) * row_blocks + pattern % row_blocks
    slot = jnp.arange(slots)
    places = jnp.where(slot[None, :] < counts[:, None], place, nodes * row_blocks).T
    order = jnp.arange(total)
    b = jnp.arange(row_blocks)
    tables = []
    for d in range(freqs):
        first = lax.rem(freq - d + freqs, freqs) * own_slots
        here = jnp.clip(counts - first, 0, own_slots)
        start = jnp.sum(jnp.where(b[None, :] < b[:, None], here[None, :], 0), axis=1)
        inside = order[:, None] - start[None, :]
        hit = (inside >= 0) & (inside < here[None, :])
        inside = jnp.sum(jnp.where(hit, inside, 0), axis=1)
        used = jnp.sum(here)
        block = jnp.sum(jnp.where(hit, b[None, :], 0), axis=1)
        groups = jnp.full((total,), (used + GROUP - 1) // GROUP)
        stored = block * own_slots + inside
        block = jnp.where(order < used, block, row_blocks)
        tables += [first + inside, block, stored, groups]
    return jnp.stack(tables).astype(jnp.int32), places.astype(jnp.int32)


def lane_sum(x):
    return jnp.sum(x, axis=1, keepdims=True)


def with_other_part(column):
    wide = jnp.broadcast_to(column, (column.shape[0], LANES))
    return wide + pltpu.roll(wide, column.shape[0] // 2, 0)


def put_lane(tile, lane, column):
    at = lax.broadcasted_iota(jnp.int32, tile.shape, 1) == lane
    return jnp.where(at, column, tile)


def split(x):
    high = x.astype(jnp.bfloat16)
    return high, (x - high.astype(jnp.float32)).astype(jnp.bfloat16)


def step_kernel(step, plane, line, freqs, items_ref, places_ref, turn_ref, info_in_ref, *refs):
    lines = refs[:plane]
    refs = refs[plane:]
    prev = refs[:step]
    g_refs = refs[step : step + freqs]
    c_refs = refs[step + freqs : step + 2 * freqs]
    z_ref, own_ref, local_ref, info_ref, tile_ref, layer_ref, mask_ref, acc_ref = refs[step + 2 * freqs :]
    nodes = plane * line
    parts, rows = local_ref.shape
    slots, row_blocks = places_ref.shape
    size = rows // row_blocks

    lane = lax.broadcasted_iota(jnp.int32, (size, LANES), 1)
    for b in range(row_blocks):
        mask_ref[b] = jnp.where((lane // parts) % row_blocks == b, 1.0, 0.0).astype(jnp.bfloat16)
    mask_ref[row_blocks] = jnp.zeros((size, LANES), jnp.bfloat16)
    acc_ref[...] = jnp.zeros_like(acc_ref)
    z_ref[nodes * row_blocks] = jnp.zeros((parts, size), jnp.float32)

    def blocks(body, carry):
        for q in range(plane):

            def chunk(i, carry, q=q):
                x = lines[q][i]
                for b in range(row_blocks):
                    carry = body(b, x[:, b * size : (b + 1) * size], (q * line + i) * row_blocks + b, carry)
                return carry

            if line <= 4:
                for i in range(line):
                    carry = chunk(i, carry)
            else:
                carry = lax.fori_loop(0, line, chunk, carry)
        return carry

    def add(sums, b, term):
        return sums[:b] + (sums[b] + term,) + sums[b + 1 :]

    def whole(sums):
        while len(sums) > 1:
            sums = tuple(x + y for x, y in zip(sums[::2], sums[1::2])) + sums[len(sums) // 2 * 2 :]
        return with_other_part(lane_sum(sums[0]))

    none = (jnp.zeros((parts, size), jnp.float32),) * row_blocks
    info = info_in_ref[...]
    if step == 0:
        height = jnp.sqrt(whole(blocks(lambda b, x, at, sums: add(sums, b, x * x), none)))
        info = put_lane(info, 0, height)

        def normal(b, x, at, carry):
            z_ref[at] = x / height
            return carry
    else:
        first = 1 if step == 1 else 3

        def dot(b, x, at, sums):
            return tuple(add(s, b, p[at] * x) for s, p in zip(sums, prev))

        coeffs = [whole(s) for s in blocks(dot, (none,) * step)]
        for i, coeff in enumerate(coeffs):
            info = put_lane(info, first + i, coeff)

        def subtract(b, x, at, sums):
            for coeff, p in zip(coeffs, prev):
                x = x - coeff * p[at]
            z_ref[at] = x
            return add(sums, b, x * x)

        height = jnp.sqrt(whole(blocks(subtract, none)))
        info = put_lane(info, first + step, height)

        def normal(b, x, at, carry):
            z_ref[at] = z_ref[at] / height
            return carry

    info_ref[...] = info
    blocks(normal, 0)
    own_ref[...] = jnp.concatenate([z_ref[b] for b in range(row_blocks)], axis=1)

    for k in range(slots):
        chosen = jnp.concatenate([z_ref[places_ref[k, b]] for b in range(row_blocks)], axis=0)
        high = chosen.astype(jnp.bfloat16).astype(jnp.float32)
        layer_ref[k] = jnp.transpose(jnp.concatenate([high, chosen - high], axis=0)).astype(jnp.bfloat16)

    for d in range(freqs):

        @pl.loop(0, items_ref[4 * d + 3, 0])
        def _(group):
            total = acc_ref[...]
            for u in range(GROUP):
                t = group * GROUP + u
                stored = items_ref[4 * d + 2, t]
                right = layer_ref[items_ref[4 * d, t]] * mask_ref[items_ref[4 * d + 1, t]]
                right = jnp.concatenate([right, right], axis=0)
                high, low = split(jnp.concatenate([g_refs[d][stored], c_refs[d][stored]], axis=0))
                left = jnp.concatenate([high, low], axis=1)
                total = total + jnp.dot(left, right, preferred_element_type=jnp.float32)
            acc_ref[...] = total

    half = row_blocks * parts
    gsum, csum = jnp.transpose(acc_ref[:size]), jnp.transpose(acc_ref[size:])
    gsum, csum = gsum[:half] + gsum[half:], csum[:half] + csum[half:]
    turn = turn_ref[...]
    for b in range(row_blocks):
        at = slice(b * parts, (b + 1) * parts)
        other = pltpu.roll(csum[at], parts // 2, 0)
        local_ref[:, b * size : (b + 1) * size] = gsum[at] + turn * other

    tile = jnp.zeros((parts, LANES), jnp.float32)
    if step == ITERS - 1:
        w = local_ref[...]
        zs = [jnp.concatenate([p[b] for b in range(row_blocks)], axis=1) for p in prev] + [own_ref[...]]
        values = [lane_sum(z * w) for z in zs]
        gram = [[lane_sum(zs[i] * zs[j]) for j in range(i + 1)] for i in range(ITERS)]
        shares = []
        for i, z in enumerate(zs):
            along = lane_sum(z * w) if i else values[0]
            share = jnp.where(gram[i][i] > 0.0, along / gram[i][i], 0.0)
            shares.append(share)
            w = w - share * z
        values += shares + [lane_sum(z * w) for z in zs] + [lane_sum(w * w)]
        values += [gram[i][j] for i in range(ITERS) for j in range(i + 1)]
        for lane_at, value in enumerate(values):
            tile = put_lane(tile, lane_at, value)
    tile_ref[...] = tile


def run_step(step, items, places, turn, info, lines, prev, g_parts, c_parts):
    plane, freqs = len(lines), len(g_parts)
    line, parts, rows = lines[0].shape
    slots, row_blocks = places.shape
    size = g_parts[0].shape[-1]
    vmem = pl.BlockSpec(memory_space=pltpu.VMEM)
    tile = jax.ShapeDtypeStruct((parts, LANES), jnp.float32)
    own = jax.ShapeDtypeStruct((parts, rows), jnp.float32)
    return pl.pallas_call(
        functools.partial(step_kernel, step, plane, line, freqs),
        in_specs=[pl.BlockSpec(memory_space=pltpu.SMEM)] * 2 + [vmem] * (2 + plane + step + 2 * freqs),
        out_specs=[vmem] * 5,
        out_shape=[
            jax.ShapeDtypeStruct((plane * line * row_blocks + 1, parts, size), jnp.float32),
            own,
            own,
            tile,
            tile,
        ],
        scratch_shapes=[
            pltpu.VMEM((slots, size, LANES), jnp.bfloat16),
            pltpu.VMEM((row_blocks + 1, size, LANES), jnp.bfloat16),
            pltpu.VMEM((2 * size, LANES), jnp.float32),
        ],
        compiler_params=pltpu.CompilerParams(vmem_limit_bytes=VMEM_LIMIT),
        name=f"step_{step}",
    )(items, places, turn, info, *lines, *prev, *g_parts, *c_parts)


def final_kernel(plane, line, info_ref, *refs):
    tiles = refs[:plane]
    krylov = refs[plane : plane + ITERS]
    out_ref, residual_ref = refs[plane + ITERS :]
    parts = info_ref.shape[0]
    fit = LANES // parts
    stacked = [tiles[q][i] for q in range(plane) for i in range(line)]
    sets = [
        jnp.transpose(jnp.concatenate(stacked[at : at + fit], axis=0)) for at in range(0, len(stacked), fit)
    ]
    info = jnp.transpose(jnp.concatenate([info_ref[...]] * fit, axis=0))

    def all_devices(shares):
        total = sum(shares[1:], shares[0])
        step = parts // 2
        while step < LANES:
            total = total + pltpu.roll(total, step, 1)
            step *= 2
        return total

    def row(table, at):
        return jnp.broadcast_to(table[at : at + 1], (8, LANES))

    zero = jnp.zeros((8, LANES), jnp.float32)
    norm, h00, h10, h01, h11, h21 = [row(info, i) for i in range(6)]
    last = [all_devices([row(s, i) for s in sets]) for i in range(ITERS)]
    shares = []
    for s in sets:
        off = [last[i] - row(s, ITERS + i) for i in range(ITERS)]
        square = row(s, 3 * ITERS)
        at = 3 * ITERS + 1
        for i in range(ITERS):
            square = square - 2.0 * off[i] * row(s, 2 * ITERS + i)
            for j in range(i + 1):
                square = square + (1.0 if i == j else 2.0) * off[i] * off[j] * row(s, at)
                at += 1
        shares.append(square)
    height = jnp.sqrt(jnp.maximum(all_devices(shares), 0.0))
    hessen = [[h00, h01, last[0]], [h10, h11, last[1]], [zero, h21, last[2]], [zero, zero, height]]
    normal = [[sum(h[m] * h[n] for h in hessen) for n in range(ITERS)] for m in range(ITERS)]
    low = [[None] * ITERS for _ in range(ITERS)]
    middle = []
    for m in range(ITERS):
        for n in range(m):
            rest = normal[m][n] - sum((low[m][k] * low[n][k] for k in range(n)), zero)
            low[m][n] = rest / low[n][n]
        low[m][m] = jnp.sqrt(normal[m][m] - sum((low[m][k] * low[m][k] for k in range(m)), zero))
        rest = norm * hessen[0][m] - sum((low[m][k] * middle[k] for k in range(m)), zero)
        middle.append(rest / low[m][m])
    coef_y = [None] * ITERS
    for m in reversed(range(ITERS)):
        rest = middle[m] - sum((low[k][m] * coef_y[k] for k in range(m + 1, ITERS)), zero)
        coef_y[m] = rest / low[m][m]
    total = zero
    for i, h in enumerate(hessen):
        misfit = (norm if i == 0 else zero) - sum(h[m] * coef_y[m] for m in range(ITERS))
        total = total + misfit * misfit
    residual_ref[...] = jnp.sqrt(total)
    columns = jnp.transpose(
        jnp.concatenate([y for y in coef_y] + [jnp.zeros((LANES - 8 * ITERS, LANES), jnp.float32)], axis=0)
    )[:parts]
    x = sum(columns[:, 8 * m : 8 * m + 1] * krylov[m][...] for m in range(ITERS))
    out_ref[0] = x[: parts // 2]
    out_ref[1] = x[parts // 2 :]


def run_final(info, tiles, krylov):
    plane = len(tiles)
    line, parts, _ = tiles[0].shape
    rows = krylov[0].shape[-1]
    vmem = pl.BlockSpec(memory_space=pltpu.VMEM)
    return pl.pallas_call(
        functools.partial(final_kernel, plane, line),
        in_specs=[vmem] * (1 + plane + ITERS),
        out_specs=[vmem] * 2,
        out_shape=[
            jax.ShapeDtypeStruct((2, parts // 2, rows), jnp.float32),
            jax.ShapeDtypeStruct((8, LANES), jnp.float32),
        ],
        name="final",
    )(info, *tiles, *krylov)


def make_shards(nodes, freqs):
    def shards(excitation, g_blocks, c_blocks, pattern, counts, freq_ids):
        angular = 0.2 * jnp.exp(freq_ids.astype(jnp.float32) * (math.log(8.0) / 1000.0))
        row_blocks, slots = pattern.shape
        size = g_blocks.shape[2]
        own_slots = g_blocks.shape[1]
        freq_count = excitation.shape[1]
        parts = 2 * freq_count
        node = lax.axis_index("node")
        freq = lax.axis_index("freq")
        stored = (row_blocks * own_slots, size, size)
        g_parts, c_parts = [], []
        for d in range(freqs):
            perm = [(i, (i + d) % freqs) for i in range(freqs)]
            g_part = lax.ppermute(g_blocks, "freq", perm) if d else g_blocks
            c_part = lax.ppermute(c_blocks, "freq", perm) if d else c_blocks
            g_parts.append(g_part.reshape(stored))
            c_parts.append(c_part.reshape(stored))
        items, places = work_list(pattern, counts, node, freq, nodes, freqs)
        turn = jnp.broadcast_to(jnp.concatenate([-angular, angular])[:, None], (parts, LANES))
        info = jnp.zeros((parts, LANES), jnp.float32)
        krylov, own = [], []
        rows = excitation
        for step in range(ITERS):
            lines = gather_rows(rows, nodes, parts)
            z, mine, rows, info, tile = run_step(
                step, items, places, turn, info, lines, krylov, g_parts, c_parts
            )
            krylov.append(z)
            own.append(mine)
        tiles = gather_rows(tile, nodes, parts)
        answer, residual = run_final(info, tiles, own)
        return answer, residual[0, :freq_count]

    return shards


def solution(mesh):
    in_specs = (
        P(None, "freq", "node"),
        P("node", "freq", None, None),
        P("node", "freq", None, None),
        P("node", None),
        P("node"),
        P("freq"),
    )
    out_specs = (P(None, "freq", "node"), P("freq"))
    shards = make_shards(mesh.shape["node"], mesh.shape["freq"])
    return jax.shard_map(shards, mesh=mesh, in_specs=in_specs, out_specs=out_specs, check_vma=False)
```

time: 123 us -> 92.1 us (0.75); the launches traced: 121 us -> 91.9 us
  Pallas kernels: 50.2 us -> 22.3 us
  starting transfers between devices: 35.7 us -> 29.2 us
  waiting for transfers between devices: 21.3 us -> 26.6 us
  local copies, waits for them, and re-layouts: 8.59 us -> 7.32 us
    pallas_call x5 -> x3, Pallas kernels: 47.8 us -> 19.9 us  [run_step(): pl.pallas_call(functools.partial(step_kernel, step, plane, line, freqs),...]
    ppermute x12, starting transfers between devices: 20.6 us -> 14.3 us  [gather_rows(): held.append(lax.ppermute(rows, 'node', perm))]
    ppermute x12, waiting for transfers between devices: 8.08 us -> 12.2 us  [gather_rows(): held.append(lax.ppermute(rows, 'node', perm))]
    ppermute x12, waiting for transfers between devices: 13.2 us -> 14.4 us  [gather_rows(): held.append(lax.ppermute(whole_line, 'node', perm))]
    unnamed x24 -> x28, local copies, waits for them, and re-layouts: 5.96 us -> 5.17 us
  transfers between devices with their start and end apart: 26 -> 26, of which waited for: 16 -> 19; matrix products, arithmetic and copies ran while one was open for 4% -> 6% of each run, Pallas kernels for 11% -> 0%
where the time goes in v2:
time: 92.1 us; the launch traced here: 91.9 us
  starting transfers between devices  29.2 us (32%)
  waiting for transfers between devices  26.6 us (29%)
  Pallas kernels  22.3 us (24%)
  local copies, waits for them, and re-layouts  7.32 us (8%)
  other arithmetic  4.3 us (5%)
  between operations  2.17 us (2%)
    pallas_call x3, Pallas kernels, run_step(): pl.pallas_call(functools.partial(step_kernel, step, plane, line, freqs),...  19.9 us
    ppermute x12, waiting for transfers between devices, gather_rows(): held.append(lax.ppermute(whole_line, 'node', perm))  14.4 us
    ppermute x12, starting transfers between devices, gather_rows(): held.append(lax.ppermute(rows, 'node', perm))  14.3 us
    ppermute x12, starting transfers between devices, gather_rows(): held.append(lax.ppermute(whole_line, 'node', perm))  14.3 us
    ppermute x12, waiting for transfers between devices, gather_rows(): held.append(lax.ppermute(rows, 'node', perm))  12.2 us
    unnamed x28, local copies, waits for them, and re-layouts  5.17 us
    pallas_call x1, Pallas kernels, run_final(): pl.pallas_call(functools.partial(final_kernel, plane, line), in_specs=[vm...  2.43 us
  transfers between devices with their start and end apart: 26, of which 19 were waited for; matrix products, arithmetic and copies ran while one was open for 6% of the time, Pallas kernels for 0%

profile of v2, /device:TPU:0, one launch (start us, length us, event | category | flops | bytes accessed | tf_op | source)
XLA Modules:
  0.0 91.9 jit_solution(12085817937014741670)
XLA Ops:
  1.2 3.0 %collective-permute-start = (f32[2,4,1024]{2,1,0:T(4,128)}, f32[2,4,1024]{2,1,0:T(4,128)S(1)}, u32[]{:S(2)}, u32[]{:S(2)}) collective-permute-start(f32[2,4,1024]{2,1,0:T(4,128)} %param.6), channel_id=1, source_target_pairs={{0,8},{2,10},{4,12},{6,14},{8,16},{10,18},{12,20},{14,22},{16,24},... | collective-permute-start | bytes 98312 | tf_op jit(solution)/shard_map/ppermute | solution.py:27
  4.2 2.0 %collective-permute-start.2 = (f32[2,4,1024]{2,1,0:T(4,128)}, f32[2,4,1024]{2,1,0:T(4,128)S(1)}, u32[]{:S(2)}, u32[]{:S(2)}) collective-permute-start(f32[2,4,1024]{2,1,0:T(4,128)} %param.6), channel_id=1, source_target_pairs={{0,24},{2,26},{4,28},{6,30},{8,0},{10,2},{12,4},{14,6},{16,8},{18,... | collective-permute-start | bytes 98312 | tf_op jit(solution)/shard_map/ppermute | solution.py:27
  6.3 1.0 %collective-permute-start.1 = (f32[2,4,1024]{2,1,0:T(4,128)}, f32[2,4,1024]{2,1,0:T(4,128)S(1)}, u32[]{:S(2)}, u32[]{:S(2)}) collective-permute-start(f32[2,4,1024]{2,1,0:T(4,128)} %param.6), channel_id=1, source_target_pairs={{0,16},{2,18},{4,20},{6,22},{8,24},{10,26},{12,28},{14,30},{16,0},... | collective-permute-start | bytes 98312 | tf_op jit(solution)/shard_map/ppermute | solution.py:27
  7.3 0.8 stack.70
  8.1 0.8 copy.12
  8.9 1.3 %fusion.25 = (s32[]{:T(128)}, s32[8]{0:T(128)S(1)}, s32[]{:T(128)}, s32[8]{0:T(128)S(1)}) fusion(s32[8]{0:T(128)} %param.10, s32[]{:T(128)S(6)} %mul.41, s32[]{:T(128)S(6)} %mul.39), kind=kLoop, calls=%fused_computation.67 | loop fusion | flops 46 | bytes 112 | tf_op jit(solution)/shard_map/reduce_sum | solution.py:59
  10.4 0.6 fusion.22
  11.1 0.7 fusion.23
  11.7 0.7 fusion.6.places_ref
  12.6 2.5 %collective-permute-start.5 = (f32[4,8,1024]{2,1,0:T(8,128)S(1)}, f32[4,8,1024]{2,1,0:T(8,128)S(1)}, u32[]{:S(2)}, u32[]{:S(2)}) collective-permute-start(f32[4,8,1024]{2,1,0:T(8,128)S(1)} %constant_dynamic-update-slice_fusion.refs_0_), channel_id=1, source_target_pairs={{0,6},{2,4},{4,2},{6,0},{8,14},{10,12},{12,10},{14,8},{16,22},{18,... | collective-permute-start | bytes 393224 | tf_op jit(solution)/shard_map/ppermute | solution.py:32
  16.1 0.7 fusion.24
  18.2 1.0 %collective-permute-done.5.refs_3_ = f32[4,8,1024]{2,1,0:T(8,128)S(1)} collective-permute-done((f32[4,8,1024]{2,1,0:T(8,128)S(1)}, f32[4,8,1024]{2,1,0:T(8,128)S(1)}, u32[]{:S(2)}, u32[]{:S(2)}) %collective-permute-start.5) | collective-permute-done | bytes 131104 | tf_op jit(solution)/shard_map/ppermute | solution.py:32
  19.2 1.8 %collective-permute-done.4.refs_2_ = f32[4,8,1024]{2,1,0:T(8,128)S(1)} collective-permute-done((f32[4,8,1024]{2,1,0:T(8,128)S(1)}, f32[4,8,1024]{2,1,0:T(8,128)S(1)}, u32[]{:S(2)}, u32[]{:S(2)}) %collective-permute-start.4) | collective-permute-done | bytes 131104 | tf_op jit(solution)/shard_map/ppermute | solution.py:32
  21.1 1.6 %copy-done = f32[8,4,128,128]{3,2,1,0:T(8,128)S(1)} copy-done((f32[8,4,128,128]{3,2,1,0:T(8,128)S(1)}, f32[8,4,128,128]{3,2,1,0:T(8,128)}, u32[]{:S(2)}) %copy-start) | copy-done | bytes 2097176
  22.7 1.6 %copy-done.2 = f32[8,4,128,128]{3,2,1,0:T(8,128)S(1)} copy-done((f32[8,4,128,128]{3,2,1,0:T(8,128)S(1)}, f32[8,4,128,128]{3,2,1,0:T(8,128)}, u32[]{:S(2)}) %copy-start.2) | copy-done | bytes 2097176
  24.3 6.5 %step_0.1 = (f32[129,8,128]{2,1,0:T(8,128)S(1)}, f32[8,1024]{1,0:T(8,128)S(1)}, f32[8,1024]{1,0:T(8,128)S(1)}, f32[8,128]{1,0:T(8,128)S(1)}, f32[8,128]{1,0:T(8,128)}) custom-call(s32[8,32]{1,0:T(8,128)S(1)} %stack.69.items_ref, s32[8,8]{1,0:T(8,128)S(1)} %fusion.6.places_ref, f32[8,128]{1,0:T(8,128)S(1)} %broadcast_in_dim.78.turn_ref, ...), custom_call_target="tpu_custom_call" | custom-call | tf_op jit(solution)/shard_map/step_0/pallas_call | solution.py:222
  31.3 1.4 %collective-permute-start.9 = (f32[8,1024]{1,0:T(8,128)S(1)}, f32[8,1024]{1,0:T(8,128)S(1)}, u32[]{:S(2)}, u32[]{:S(2)}) collective-permute-start(f32[8,1024]{1,0:T(8,128)S(1)} %get-tuple-element.16), channel_id=1, source_target_pairs={{0,16},{2,18},{4,20},{6,22},{8,24},{10,26},{12,28},{14,30},{16,0},... | collective-permute-start | bytes 98312 | tf_op jit(solution)/shard_map/ppermute | solution.py:27
  32.7 2.0 %collective-permute-start.8 = (f32[8,1024]{1,0:T(8,128)S(1)}, f32[8,1024]{1,0:T(8,128)S(1)}, u32[]{:S(2)}, u32[]{:S(2)}) collective-permute-start(f32[8,1024]{1,0:T(8,128)S(1)} %get-tuple-element.16), channel_id=1, source_target_pairs={{0,8},{2,10},{4,12},{6,14},{8,16},{10,18},{12,20},{14,22},{16,24},... | collective-permute-start | bytes 98312 | tf_op jit(solution)/shard_map/ppermute | solution.py:27
  34.8 1.4 %collective-permute-done.9 = f32[8,1024]{1,0:T(8,128)S(1)} collective-permute-done((f32[8,1024]{1,0:T(8,128)S(1)}, f32[8,1024]{1,0:T(8,128)S(1)}, u32[]{:S(2)}, u32[]{:S(2)}) %collective-permute-start.9) | collective-permute-done | bytes 32800 | tf_op jit(solution)/shard_map/ppermute | solution.py:27
  36.1 2.3 %collective-permute-done.8 = f32[8,1024]{1,0:T(8,128)S(1)} collective-permute-done((f32[8,1024]{1,0:T(8,128)S(1)}, f32[8,1024]{1,0:T(8,128)S(1)}, u32[]{:S(2)}, u32[]{:S(2)}) %collective-permute-start.8) | collective-permute-done | bytes 32800 | tf_op jit(solution)/shard_map/ppermute | solution.py:27
  38.5 1.7 %collective-permute-start.13 = (f32[4,8,1024]{2,1,0:T(8,128)S(1)}, f32[4,8,1024]{2,1,0:T(8,128)S(1)}, u32[]{:S(2)}, u32[]{:S(2)}) collective-permute-start(f32[4,8,1024]{2,1,0:T(8,128)S(1)} %pad_maximum_fusion.refs_0_), channel_id=1, source_target_pairs={{0,6},{2,4},{4,2},{6,0},{8,14},{10,12},{12,10},{14,8},{16,22},{18,... | collective-permute-start | bytes 393224 | tf_op jit(solution)/shard_map/ppermute | solution.py:32
  40.1 1.6 %collective-permute-start.12 = (f32[4,8,1024]{2,1,0:T(8,128)S(1)}, f32[4,8,1024]{2,1,0:T(8,128)S(1)}, u32[]{:S(2)}, u32[]{:S(2)}) collective-permute-start(f32[4,8,1024]{2,1,0:T(8,128)S(1)} %pad_maximum_fusion.refs_0_), channel_id=1, source_target_pairs={{0,4},{2,6},{4,0},{6,2},{8,12},{10,14},{12,8},{14,10},{16,20},{18,... | collective-permute-start | bytes 393224 | tf_op jit(solution)/shard_map/ppermute | solution.py:32
  42.0 2.4 %collective-permute-done.13.refs_3_ = f32[4,8,1024]{2,1,0:T(8,128)S(1)} collective-permute-done((f32[4,8,1024]{2,1,0:T(8,128)S(1)}, f32[4,8,1024]{2,1,0:T(8,128)S(1)}, u32[]{:S(2)}, u32[]{:S(2)}) %collective-permute-start.13) | collective-permute-done | bytes 131104 | tf_op jit(solution)/shard_map/ppermute | solution.py:32
  44.5 1.3 %collective-permute-done.12.refs_2_ = f32[4,8,1024]{2,1,0:T(8,128)S(1)} collective-permute-done((f32[4,8,1024]{2,1,0:T(8,128)S(1)}, f32[4,8,1024]{2,1,0:T(8,128)S(1)}, u32[]{:S(2)}, u32[]{:S(2)}) %collective-permute-start.12) | collective-permute-done | bytes 131104 | tf_op jit(solution)/shard_map/ppermute | solution.py:32
  45.8 0.9 collective-permute-done.11.refs_1_
  46.7 6.6 %step_1.1 = (f32[129,8,128]{2,1,0:T(8,128)S(1)}, f32[8,1024]{1,0:T(8,128)S(1)}, f32[8,1024]{1,0:T(8,128)S(1)}, f32[8,128]{1,0:T(8,128)S(1)}, f32[8,128]{1,0:T(8,128)}) custom-call(s32[8,32]{1,0:T(8,128)S(1)} %stack.69.items_ref, s32[8,8]{1,0:T(8,128)S(1)} %fusion.6.places_ref, f32[8,128]{1,0:T(8,128)S(1)} %broadcast_in_dim.78.turn_ref, ...), custom_call_target="tpu_custom_call" | custom-call | tf_op jit(solution)/shard_map/step_1/pallas_call | solution.py:222
  53.4 1.9 %collective-permute-start.14 = (f32[8,1024]{1,0:T(8,128)S(1)}, f32[8,1024]{1,0:T(8,128)S(1)}, u32[]{:S(2)}, u32[]{:S(2)}) collective-permute-start(f32[8,1024]{1,0:T(8,128)S(1)} %get-tuple-element.19), channel_id=1, source_target_pairs={{0,8},{2,10},{4,12},{6,14},{8,16},{10,18},{12,20},{14,22},{16,24},... | collective-permute-start | bytes 98312 | tf_op jit(solution)/shard_map/ppermute | solution.py:27
  55.3 1.9 %collective-permute-done.16 = f32[8,1024]{1,0:T(8,128)S(1)} collective-permute-done((f32[8,1024]{1,0:T(8,128)S(1)}, f32[8,1024]{1,0:T(8,128)S(1)}, u32[]{:S(2)}, u32[]{:S(2)}) %collective-permute-start.16) | collective-permute-done | bytes 32800 | tf_op jit(solution)/shard_map/ppermute | solution.py:27
  57.2 1.0 %collective-permute-done.15 = f32[8,1024]{1,0:T(8,128)S(1)} collective-permute-done((f32[8,1024]{1,0:T(8,128)S(1)}, f32[8,1024]{1,0:T(8,128)S(1)}, u32[]{:S(2)}, u32[]{:S(2)}) %collective-permute-start.15) | collective-permute-done | bytes 32800 | tf_op jit(solution)/shard_map/ppermute | solution.py:27
  58.2 1.7 %collective-permute-done.14 = f32[8,1024]{1,0:T(8,128)S(1)} collective-permute-done((f32[8,1024]{1,0:T(8,128)S(1)}, f32[8,1024]{1,0:T(8,128)S(1)}, u32[]{:S(2)}, u32[]{:S(2)}) %collective-permute-start.14) | collective-permute-done | bytes 32800 | tf_op jit(solution)/shard_map/ppermute | solution.py:27
  60.3 1.3 %collective-permute-start.18 = (f32[4,8,1024]{2,1,0:T(8,128)S(1)}, f32[4,8,1024]{2,1,0:T(8,128)S(1)}, u32[]{:S(2)}, u32[]{:S(2)}) collective-permute-start(f32[4,8,1024]{2,1,0:T(8,128)S(1)} %pad_maximum_fusion.1.refs_0_), channel_id=1, source_target_pairs={{0,4},{2,6},{4,0},{6,2},{8,12},{10,14},{12,8},{14,10},{16,20},{18,... | collective-permute-start | bytes 393224 | tf_op jit(solution)/shard_map/ppermute | solution.py:32
  61.6 1.9 %collective-permute-start.17 = (f32[4,8,1024]{2,1,0:T(8,128)S(1)}, f32[4,8,1024]{2,1,0:T(8,128)S(1)}, u32[]{:S(2)}, u32[]{:S(2)}) collective-permute-start(f32[4,8,1024]{2,1,0:T(8,128)S(1)} %pad_maximum_fusion.1.refs_0_), channel_id=1, source_target_pairs={{0,2},{2,0},{4,6},{6,4},{8,10},{10,8},{12,14},{14,12},{16,18},{18,... | collective-permute-start | bytes 393224 | tf_op jit(solution)/shard_map/ppermute | solution.py:32
  63.5 2.5 %collective-permute-done.19.refs_3_ = f32[4,8,1024]{2,1,0:T(8,128)S(1)} collective-permute-done((f32[4,8,1024]{2,1,0:T(8,128)S(1)}, f32[4,8,1024]{2,1,0:T(8,128)S(1)}, u32[]{:S(2)}, u32[]{:S(2)}) %collective-permute-start.19) | collective-permute-done | bytes 131104 | tf_op jit(solution)/shard_map/ppermute | solution.py:32
  66.0 0.7 collective-permute-done.18.refs_2_
  66.7 6.8 %step_2.1 = (f32[129,8,128]{2,1,0:T(8,128)}, f32[8,1024]{1,0:T(8,128)S(1)}, f32[8,1024]{1,0:T(8,128)}, f32[8,128]{1,0:T(8,128)S(1)}, f32[8,128]{1,0:T(8,128)S(1)}) custom-call(s32[8,32]{1,0:T(8,128)S(1)} %stack.69.items_ref, s32[8,8]{1,0:T(8,128)S(1)} %fusion.6.places_ref, f32[8,128]{1,0:T(8,128)S(1)} %broadcast_in_dim.78.turn_ref, ...), custom_call_target="tpu_custom_call" | custom-call | tf_op jit(solution)/shard_map/step_2/pallas_call | solution.py:222
  73.5 0.6 copy-done.6
  74.1 0.8 collective-permute-start.22
  74.9 1.5 %collective-permute-start.20 = (f32[8,128]{1,0:T(8,128)S(1)}, f32[8,128]{1,0:T(8,128)S(1)}, u32[]{:S(2)}, u32[]{:S(2)}) collective-permute-start(f32[8,128]{1,0:T(8,128)S(1)} %get-tuple-element.22), channel_id=1, source_target_pairs={{0,8},{2,10},{4,12},{6,14},{8,16},{10,18},{12,20},{14,22},{16,24},... | collective-permute-start | bytes 12296 | tf_op jit(solution)/shard_map/ppermute | solution.py:27
  76.5 1.3 %collective-permute-done.22 = f32[8,128]{1,0:T(8,128)S(1)} collective-permute-done((f32[8,128]{1,0:T(8,128)S(1)}, f32[8,128]{1,0:T(8,128)S(1)}, u32[]{:S(2)}, u32[]{:S(2)}) %collective-permute-start.22) | collective-permute-done | bytes 4128 | tf_op jit(solution)/shard_map/ppermute | solution.py:27
  77.7 1.7 %collective-permute-done.21 = f32[8,128]{1,0:T(8,128)S(1)} collective-permute-done((f32[8,128]{1,0:T(8,128)S(1)}, f32[8,128]{1,0:T(8,128)S(1)}, u32[]{:S(2)}, u32[]{:S(2)}) %collective-permute-start.21) | collective-permute-done | bytes 4128 | tf_op jit(solution)/shard_map/ppermute | solution.py:27
  79.4 0.9 collective-permute-done.20
  80.3 1.0 %collective-permute-start.25 = (f32[4,8,128]{2,1,0:T(8,128)S(1)}, f32[4,8,128]{2,1,0:T(8,128)S(1)}, u32[]{:S(2)}, u32[]{:S(2)}) collective-permute-start(f32[4,8,128]{2,1,0:T(8,128)S(1)} %pad_maximum_fusion.2.refs_0_), channel_id=1, source_target_pairs={{0,6},{2,4},{4,2},{6,0},{8,14},{10,12},{12,10},{14,8},{16,22},{18,... | collective-permute-start | bytes 49160 | tf_op jit(solution)/shard_map/ppermute | solution.py:32
  81.3 2.6 %collective-permute-start.24 = (f32[4,8,128]{2,1,0:T(8,128)S(1)}, f32[4,8,128]{2,1,0:T(8,128)S(1)}, u32[]{:S(2)}, u32[]{:S(2)}) collective-permute-start(f32[4,8,128]{2,1,0:T(8,128)S(1)} %pad_maximum_fusion.2.refs_0_), channel_id=1, source_target_pairs={{0,4},{2,6},{4,0},{6,2},{8,12},{10,14},{12,8},{14,10},{16,20},{18,... | collective-permute-start | bytes 49160 | tf_op jit(solution)/shard_map/ppermute | solution.py:32
  83.9 1.1 %collective-permute-done.25.refs_3_ = f32[4,8,128]{2,1,0:T(8,128)S(1)} collective-permute-done((f32[4,8,128]{2,1,0:T(8,128)S(1)}, f32[4,8,128]{2,1,0:T(8,128)S(1)}, u32[]{:S(2)}, u32[]{:S(2)}) %collective-permute-start.25) | collective-permute-done | bytes 16416 | tf_op jit(solution)/shard_map/ppermute | solution.py:32
  85.0 0.6 collective-permute-done.24.refs_2_
  85.7 2.0 %collective-permute-done.23.refs_1_ = f32[4,8,128]{2,1,0:T(8,128)S(1)} collective-permute-done((f32[4,8,128]{2,1,0:T(8,128)S(1)}, f32[4,8,128]{2,1,0:T(8,128)S(1)}, u32[]{:S(2)}, u32[]{:S(2)}) %collective-permute-start.23) | collective-permute-done | bytes 16416 | tf_op jit(solution)/shard_map/ppermute | solution.py:32
  88.3 2.4 %final.1 = (f32[2,4,1024]{2,1,0:T(4,128)}, f32[8,128]{1,0:T(8,128)}) custom-call(f32[8,128]{1,0:T(8,128)} %copy-done.7, f32[4,8,128]{2,1,0:T(8,128)} %copy-done.8, f32[4,8,128]{2,1,0:T(8,128)} %copy-done.11, f32[4,8,128]{2,1,0:T(8,128)} %copy-done.10, f32[4,8,128]{2,1,0:T(8,128)} %copy-done.9, f32[8,1024]{1,0:T(8,128)} %copy-done.4, f32[8,1024]{1,0:T(8,128)} %copy-done.5, ...), custom_call_target="tpu_custom_call" | custom-call | tf_op jit(solution)/shard_map/final/pallas_call | solution.py:314
  90.7 1.2 %slice_bitcast_fusion = f32[4]{0:T(128)} fusion(f32[8,128]{1,0:T(8,128)} %get-tuple-element.27), kind=kLoop, calls=%fused_computation.62 | loop fusion | bytes 32 | tf_op jit(solution)/shard_map/squeeze | solution.py:358
  (59 shorter events, 4.1 us)
Async XLA Ops:
  0.6 20.4 %collective-permute-start.6 = (f32[8,4,128,128]{3,2,1,0:T(8,128)}, f32[8,4,128,128]{3,2,1,0:T(8,128)S(1)}, u32[]{:S(2)}, u32[]{:S(2)}) collective-permute-start(f32[8,4,128,128]{3,2,1,0:T(8,128)} %param.7), channel_id=1, source_target_pairs={{0,1},{1,0},{2,3},{3,2},{4,5},{5,4},{6,7},{7,6},{8,9},{9,8},{10,11... | collective-permute-start | bytes 6291464 | tf_op jit(solution)/shard_map/ppermute | solution.py:340
  1.1 19.9 %collective-permute-start.7 = (f32[8,4,128,128]{3,2,1,0:T(8,128)}, f32[8,4,128,128]{3,2,1,0:T(8,128)}, u32[]{:S(2)}, u32[]{:S(2)}) collective-permute-start(f32[8,4,128,128]{3,2,1,0:T(8,128)} %param.8), channel_id=1, source_target_pairs={{0,1},{1,0},{2,3},{3,2},{4,5},{5,4},{6,7},{7,6},{8,9},{9,8},{10,11... | collective-permute-start | bytes 6291464 | tf_op jit(solution)/shard_map/ppermute | solution.py:341
  1.2 11.2 %collective-permute-start = (f32[2,4,1024]{2,1,0:T(4,128)}, f32[2,4,1024]{2,1,0:T(4,128)S(1)}, u32[]{:S(2)}, u32[]{:S(2)}) collective-permute-start(f32[2,4,1024]{2,1,0:T(4,128)} %param.6), channel_id=1, source_target_pairs={{0,8},{2,10},{4,12},{6,14},{8,16},{10,18},{12,20},{14,22},{16,24},... | collective-permute-start | bytes 98312 | tf_op jit(solution)/shard_map/ppermute | solution.py:27
  4.2 8.2 %collective-permute-start.2 = (f32[2,4,1024]{2,1,0:T(4,128)}, f32[2,4,1024]{2,1,0:T(4,128)S(1)}, u32[]{:S(2)}, u32[]{:S(2)}) collective-permute-start(f32[2,4,1024]{2,1,0:T(4,128)} %param.6), channel_id=1, source_target_pairs={{0,24},{2,26},{4,28},{6,30},{8,0},{10,2},{12,4},{14,6},{16,8},{18,... | collective-permute-start | bytes 98312 | tf_op jit(solution)/shard_map/ppermute | solution.py:27
  6.3 6.2 %collective-permute-start.1 = (f32[2,4,1024]{2,1,0:T(4,128)}, f32[2,4,1024]{2,1,0:T(4,128)S(1)}, u32[]{:S(2)}, u32[]{:S(2)}) collective-permute-start(f32[2,4,1024]{2,1,0:T(4,128)} %param.6), channel_id=1, source_target_pairs={{0,16},{2,18},{4,20},{6,22},{8,24},{10,26},{12,28},{14,30},{16,0},... | collective-permute-start | bytes 98312 | tf_op jit(solution)/shard_map/ppermute | solution.py:27
  12.6 6.7 %collective-permute-start.5 = (f32[4,8,1024]{2,1,0:T(8,128)S(1)}, f32[4,8,1024]{2,1,0:T(8,128)S(1)}, u32[]{:S(2)}, u32[]{:S(2)}) collective-permute-start(f32[4,8,1024]{2,1,0:T(8,128)S(1)} %constant_dynamic-update-slice_fusion.refs_0_), channel_id=1, source_target_pairs={{0,6},{2,4},{4,2},{6,0},{8,14},{10,12},{12,10},{14,8},{16,22},{18,... | collective-permute-start | bytes 393224 | tf_op jit(solution)/shard_map/ppermute | solution.py:32
  15.1 5.9 %collective-permute-start.4 = (f32[4,8,1024]{2,1,0:T(8,128)S(1)}, f32[4,8,1024]{2,1,0:T(8,128)S(1)}, u32[]{:S(2)}, u32[]{:S(2)}) collective-permute-start(f32[4,8,1024]{2,1,0:T(8,128)S(1)} %constant_dynamic-update-slice_fusion.refs_0_), channel_id=1, source_target_pairs={{0,4},{2,6},{4,0},{6,2},{8,12},{10,14},{12,8},{14,10},{16,20},{18,... | collective-permute-start | bytes 393224 | tf_op jit(solution)/shard_map/ppermute | solution.py:32
  15.6 5.5 %collective-permute-start.3 = (f32[4,8,1024]{2,1,0:T(8,128)S(1)}, f32[4,8,1024]{2,1,0:T(8,128)S(1)}, u32[]{:S(2)}, u32[]{:S(2)}) collective-permute-start(f32[4,8,1024]{2,1,0:T(8,128)S(1)} %constant_dynamic-update-slice_fusion.refs_0_), channel_id=1, source_target_pairs={{0,2},{2,0},{4,6},{6,4},{8,10},{10,8},{12,14},{14,12},{16,18},{18,... | collective-permute-start | bytes 393224 | tf_op jit(solution)/shard_map/ppermute | solution.py:32
  21.1 1.6 %copy-start = (f32[8,4,128,128]{3,2,1,0:T(8,128)S(1)}, f32[8,4,128,128]{3,2,1,0:T(8,128)}, u32[]{:S(2)}) copy-start(f32[8,4,128,128]{3,2,1,0:T(8,128)} %param.7) | copy-start | bytes 6291460
  22.7 1.6 %copy-start.2 = (f32[8,4,128,128]{3,2,1,0:T(8,128)S(1)}, f32[8,4,128,128]{3,2,1,0:T(8,128)}, u32[]{:S(2)}) copy-start(f32[8,4,128,128]{3,2,1,0:T(8,128)} %param.8) | copy-start | bytes 6291460
  24.3 22.4 %copy-start.1 = (f32[8,4,128,128]{3,2,1,0:T(8,128)S(1)}, f32[8,4,128,128]{3,2,1,0:T(8,128)}, u32[]{:S(2)}) copy-start(f32[8,4,128,128]{3,2,1,0:T(8,128)} %param.7) | copy-start | bytes 6291460
  24.3 22.4 %copy-start.3 = (f32[8,4,128,128]{3,2,1,0:T(8,128)S(1)}, f32[8,4,128,128]{3,2,1,0:T(8,128)}, u32[]{:S(2)}) copy-start(f32[8,4,128,128]{3,2,1,0:T(8,128)} %param.8) | copy-start | bytes 6291460
  30.8 22.4 %copy-start.4 = (f32[8,1024]{1,0:T(8,128)}, f32[8,1024]{1,0:T(8,128)S(1)}, u32[]{:S(2)}) copy-start(f32[8,1024]{1,0:T(8,128)S(1)} %get-tuple-element.23.refs_4_) | copy-start | bytes 98308
  30.8 3.9 %collective-permute-start.10 = (f32[8,1024]{1,0:T(8,128)S(1)}, f32[8,1024]{1,0:T(8,128)S(1)}, u32[]{:S(2)}, u32[]{:S(2)}) collective-permute-start(f32[8,1024]{1,0:T(8,128)S(1)} %get-tuple-element.16), channel_id=1, source_target_pairs={{0,24},{2,26},{4,28},{6,30},{8,0},{10,2},{12,4},{14,6},{16,8},{18,... | collective-permute-start | bytes 98312 | tf_op jit(solution)/shard_map/ppermute | solution.py:27
  31.3 4.8 %collective-permute-start.9 = (f32[8,1024]{1,0:T(8,128)S(1)}, f32[8,1024]{1,0:T(8,128)S(1)}, u32[]{:S(2)}, u32[]{:S(2)}) collective-permute-start(f32[8,1024]{1,0:T(8,128)S(1)} %get-tuple-element.16), channel_id=1, source_target_pairs={{0,16},{2,18},{4,20},{6,22},{8,24},{10,26},{12,28},{14,30},{16,0},... | collective-permute-start | bytes 98312 | tf_op jit(solution)/shard_map/ppermute | solution.py:27
  32.7 5.7 %collective-permute-start.8 = (f32[8,1024]{1,0:T(8,128)S(1)}, f32[8,1024]{1,0:T(8,128)S(1)}, u32[]{:S(2)}, u32[]{:S(2)}) collective-permute-start(f32[8,1024]{1,0:T(8,128)S(1)} %get-tuple-element.16), channel_id=1, source_target_pairs={{0,8},{2,10},{4,12},{6,14},{8,16},{10,18},{12,20},{14,22},{16,24},... | collective-permute-start | bytes 98312 | tf_op jit(solution)/shard_map/ppermute | solution.py:27
  38.5 6.0 %collective-permute-start.13 = (f32[4,8,1024]{2,1,0:T(8,128)S(1)}, f32[4,8,1024]{2,1,0:T(8,128)S(1)}, u32[]{:S(2)}, u32[]{:S(2)}) collective-permute-start(f32[4,8,1024]{2,1,0:T(8,128)S(1)} %pad_maximum_fusion.refs_0_), channel_id=1, source_target_pairs={{0,6},{2,4},{4,2},{6,0},{8,14},{10,12},{12,10},{14,8},{16,22},{18,... | collective-permute-start | bytes 393224 | tf_op jit(solution)/shard_map/ppermute | solution.py:32
  40.1 5.7 %collective-permute-start.12 = (f32[4,8,1024]{2,1,0:T(8,128)S(1)}, f32[4,8,1024]{2,1,0:T(8,128)S(1)}, u32[]{:S(2)}, u32[]{:S(2)}) collective-permute-start(f32[4,8,1024]{2,1,0:T(8,128)S(1)} %pad_maximum_fusion.refs_0_), channel_id=1, source_target_pairs={{0,4},{2,6},{4,0},{6,2},{8,12},{10,14},{12,8},{14,10},{16,20},{18,... | collective-permute-start | bytes 393224 | tf_op jit(solution)/shard_map/ppermute | solution.py:32
  41.7 5.0 %collective-permute-start.11 = (f32[4,8,1024]{2,1,0:T(8,128)S(1)}, f32[4,8,1024]{2,1,0:T(8,128)S(1)}, u32[]{:S(2)}, u32[]{:S(2)}) collective-permute-start(f32[4,8,1024]{2,1,0:T(8,128)S(1)} %pad_maximum_fusion.refs_0_), channel_id=1, source_target_pairs={{0,2},{2,0},{4,6},{6,4},{8,10},{10,8},{12,14},{14,12},{16,18},{18,... | collective-permute-start | bytes 393224 | tf_op jit(solution)/shard_map/ppermute | solution.py:32
  53.3 20.2 %copy-start.5 = (f32[8,1024]{1,0:T(8,128)}, f32[8,1024]{1,0:T(8,128)S(1)}, u32[]{:S(2)}) copy-start(f32[8,1024]{1,0:T(8,128)S(1)} %get-tuple-element.24.refs_5_) | copy-start | bytes 98308
  53.3 3.9 %collective-permute-start.16 = (f32[8,1024]{1,0:T(8,128)S(1)}, f32[8,1024]{1,0:T(8,128)S(1)}, u32[]{:S(2)}, u32[]{:S(2)}) collective-permute-start(f32[8,1024]{1,0:T(8,128)S(1)} %get-tuple-element.19), channel_id=1, source_target_pairs={{0,24},{2,26},{4,28},{6,30},{8,0},{10,2},{12,4},{14,6},{16,8},{18,... | collective-permute-start | bytes 98312 | tf_op jit(solution)/shard_map/ppermute | solution.py:27
  53.3 4.9 %collective-permute-start.15 = (f32[8,1024]{1,0:T(8,128)S(1)}, f32[8,1024]{1,0:T(8,128)S(1)}, u32[]{:S(2)}, u32[]{:S(2)}) collective-permute-start(f32[8,1024]{1,0:T(8,128)S(1)} %get-tuple-element.19), channel_id=1, source_target_pairs={{0,16},{2,18},{4,20},{6,22},{8,24},{10,26},{12,28},{14,30},{16,0},... | collective-permute-start | bytes 98312 | tf_op jit(solution)/shard_map/ppermute | solution.py:27
  53.4 6.5 %collective-permute-start.14 = (f32[8,1024]{1,0:T(8,128)S(1)}, f32[8,1024]{1,0:T(8,128)S(1)}, u32[]{:S(2)}, u32[]{:S(2)}) collective-permute-start(f32[8,1024]{1,0:T(8,128)S(1)} %get-tuple-element.19), channel_id=1, source_target_pairs={{0,8},{2,10},{4,12},{6,14},{8,16},{10,18},{12,20},{14,22},{16,24},... | collective-permute-start | bytes 98312 | tf_op jit(solution)/shard_map/ppermute | solution.py:27
  59.9 6.0 %collective-permute-start.19 = (f32[4,8,1024]{2,1,0:T(8,128)S(1)}, f32[4,8,1024]{2,1,0:T(8,128)S(1)}, u32[]{:S(2)}, u32[]{:S(2)}) collective-permute-start(f32[4,8,1024]{2,1,0:T(8,128)S(1)} %pad_maximum_fusion.1.refs_0_), channel_id=1, source_target_pairs={{0,6},{2,4},{4,2},{6,0},{8,14},{10,12},{12,10},{14,8},{16,22},{18,... | collective-permute-start | bytes 393224 | tf_op jit(solution)/shard_map/ppermute | solution.py:32
  60.3 6.4 %collective-permute-start.18 = (f32[4,8,1024]{2,1,0:T(8,128)S(1)}, f32[4,8,1024]{2,1,0:T(8,128)S(1)}, u32[]{:S(2)}, u32[]{:S(2)}) collective-permute-start(f32[4,8,1024]{2,1,0:T(8,128)S(1)} %pad_maximum_fusion.1.refs_0_), channel_id=1, source_target_pairs={{0,4},{2,6},{4,0},{6,2},{8,12},{10,14},{12,8},{14,10},{16,20},{18,... | collective-permute-start | bytes 393224 | tf_op jit(solution)/shard_map/ppermute | solution.py:32
  61.6 5.1 %collective-permute-start.17 = (f32[4,8,1024]{2,1,0:T(8,128)S(1)}, f32[4,8,1024]{2,1,0:T(8,128)S(1)}, u32[]{:S(2)}, u32[]{:S(2)}) collective-permute-start(f32[4,8,1024]{2,1,0:T(8,128)S(1)} %pad_maximum_fusion.1.refs_0_), channel_id=1, source_target_pairs={{0,2},{2,0},{4,6},{6,4},{8,10},{10,8},{12,14},{14,12},{16,18},{18,... | collective-permute-start | bytes 393224 | tf_op jit(solution)/shard_map/ppermute | solution.py:32
  73.5 0.6 copy-start.6
  74.1 6.2 %copy-start.7 = (f32[8,128]{1,0:T(8,128)}, f32[8,128]{1,0:T(8,128)S(1)}, u32[]{:S(2)}) copy-start(f32[8,128]{1,0:T(8,128)S(1)} %get-tuple-element.21.info_ref) | copy-start | bytes 12292
  74.1 3.6 %collective-permute-start.22 = (f32[8,128]{1,0:T(8,128)S(1)}, f32[8,128]{1,0:T(8,128)S(1)}, u32[]{:S(2)}, u32[]{:S(2)}) collective-permute-start(f32[8,128]{1,0:T(8,128)S(1)} %get-tuple-element.22), channel_id=1, source_target_pairs={{0,24},{2,26},{4,28},{6,30},{8,0},{10,2},{12,4},{14,6},{16,8},{18,... | collective-permute-start | bytes 12296 | tf_op jit(solution)/shard_map/ppermute | solution.py:27
  74.9 4.5 %collective-permute-start.21 = (f32[8,128]{1,0:T(8,128)S(1)}, f32[8,128]{1,0:T(8,128)S(1)}, u32[]{:S(2)}, u32[]{:S(2)}) collective-permute-start(f32[8,128]{1,0:T(8,128)S(1)} %get-tuple-element.22), channel_id=1, source_target_pairs={{0,16},{2,18},{4,20},{6,22},{8,24},{10,26},{12,28},{14,30},{16,0},... | collective-permute-start | bytes 12296 | tf_op jit(solution)/shard_map/ppermute | solution.py:27
  74.9 5.4 %collective-permute-start.20 = (f32[8,128]{1,0:T(8,128)S(1)}, f32[8,128]{1,0:T(8,128)S(1)}, u32[]{:S(2)}, u32[]{:S(2)}) collective-permute-start(f32[8,128]{1,0:T(8,128)S(1)} %get-tuple-element.22), channel_id=1, source_target_pairs={{0,8},{2,10},{4,12},{6,14},{8,16},{10,18},{12,20},{14,22},{16,24},... | collective-permute-start | bytes 12296 | tf_op jit(solution)/shard_map/ppermute | solution.py:27
  80.3 7.4 %copy-start.8 = (f32[4,8,128]{2,1,0:T(8,128)}, f32[4,8,128]{2,1,0:T(8,128)S(1)}, u32[]{:S(2)}) copy-start(f32[4,8,128]{2,1,0:T(8,128)S(1)} %pad_maximum_fusion.2.refs_0_) | copy-start | bytes 49156
  80.3 4.7 %collective-permute-start.25 = (f32[4,8,128]{2,1,0:T(8,128)S(1)}, f32[4,8,128]{2,1,0:T(8,128)S(1)}, u32[]{:S(2)}, u32[]{:S(2)}) collective-permute-start(f32[4,8,128]{2,1,0:T(8,128)S(1)} %pad_maximum_fusion.2.refs_0_), channel_id=1, source_target_pairs={{0,6},{2,4},{4,2},{6,0},{8,14},{10,12},{12,10},{14,8},{16,22},{18,... | collective-permute-start | bytes 49160 | tf_op jit(solution)/shard_map/ppermute | solution.py:32
  81.3 4.3 %collective-permute-start.24 = (f32[4,8,128]{2,1,0:T(8,128)S(1)}, f32[4,8,128]{2,1,0:T(8,128)S(1)}, u32[]{:S(2)}, u32[]{:S(2)}) collective-permute-start(f32[4,8,128]{2,1,0:T(8,128)S(1)} %pad_maximum_fusion.2.refs_0_), channel_id=1, source_target_pairs={{0,4},{2,6},{4,0},{6,2},{8,12},{10,14},{12,8},{14,10},{16,20},{18,... | collective-permute-start | bytes 49160 | tf_op jit(solution)/shard_map/ppermute | solution.py:32
  83.9 3.7 %collective-permute-start.23 = (f32[4,8,128]{2,1,0:T(8,128)S(1)}, f32[4,8,128]{2,1,0:T(8,128)S(1)}, u32[]{:S(2)}, u32[]{:S(2)}) collective-permute-start(f32[4,8,128]{2,1,0:T(8,128)S(1)} %pad_maximum_fusion.2.refs_0_), channel_id=1, source_target_pairs={{0,2},{2,0},{4,6},{6,4},{8,10},{10,8},{12,14},{14,12},{16,18},{18,... | collective-permute-start | bytes 49160 | tf_op jit(solution)/shard_map/ppermute | solution.py:32
  85.0 2.6 %copy-start.9 = (f32[4,8,128]{2,1,0:T(8,128)}, f32[4,8,128]{2,1,0:T(8,128)S(1)}, u32[]{:S(2)}) copy-start(f32[4,8,128]{2,1,0:T(8,128)S(1)} %collective-permute-done.25.refs_3_) | copy-start | bytes 49156
  85.7 2.0 %copy-start.10 = (f32[4,8,128]{2,1,0:T(8,128)}, f32[4,8,128]{2,1,0:T(8,128)S(1)}, u32[]{:S(2)}) copy-start(f32[4,8,128]{2,1,0:T(8,128)S(1)} %collective-permute-done.24.refs_2_) | copy-start | bytes 49156
  87.7 0.6 copy-start.11

commit v3 on v2

v3 whole, which is shorter than its diff:
```python
import functools
import math

import jax
import jax.numpy as jnp
from jax import lax
from jax.experimental import pallas as pl
from jax.experimental.pallas import tpu as pltpu
from jax.sharding import Mesh
from jax.sharding import PartitionSpec as P

ITERS = 3
LANES = 128
GROUP = 4
SHIFT = 256
VMEM_LIMIT = 20 * 1024 * 1024


def split_nodes(nodes):
    plane = 4 if nodes % 4 == 0 else 1
    return nodes // plane, plane


def gather_rows(rows, line, plane):
    shape = rows.shape
    whole_line = lax.all_to_all(jnp.broadcast_to(rows[None], (line,) + shape), "line", 0, 0)
    copies = jnp.broadcast_to(whole_line[None], (plane, line) + shape)
    gathered = lax.all_to_all(copies, "place", 0, 0)
    return gathered.reshape((plane * line,) + shape)


def lane_sum(x):
    return jnp.sum(x, axis=1, keepdims=True)


def with_other_part(column):
    wide = jnp.broadcast_to(column, (column.shape[0], LANES))
    return wide + pltpu.roll(wide, column.shape[0] // 2, 0)


def put_lane(tile, lane, column):
    at = lax.broadcasted_iota(jnp.int32, tile.shape, 1) == lane
    return jnp.where(at, column, tile)


def split(x):
    high = x.astype(jnp.bfloat16)
    return high, (x - high.astype(jnp.float32)).astype(jnp.bfloat16)


def step_kernel(step, plane, line, freqs, pattern_ref, counts_ref, where_ref, turn_ref, info_in_ref, *refs):
    lines_ref, refs = refs[0], refs[1:]
    prev = refs[:step]
    g_refs = list(refs[step : step + freqs])
    c_refs = list(refs[step + freqs : step + 2 * freqs])
    z_ref, own_ref, local_ref, info_ref, tile_ref, layer_ref, mask_ref, acc_ref, list_ref = refs[
        step + 2 * freqs : step + 2 * freqs + 9
    ]
    nodes = plane * line
    parts, rows = local_ref.shape
    row_blocks, slots = pattern_ref.shape
    own_slots = slots // freqs
    size = rows // row_blocks
    own_place = (where_ref[1] * line + where_ref[0]) * row_blocks

    arrivals = []
    if step == 0:
        kept, sems = refs[step + 2 * freqs + 9 :]
        for m, held in enumerate((g_refs, c_refs)):
            arrivals.append(pltpu.make_async_copy(held[0], kept.at[m], sems.at[m]))
            arrivals[-1].start()
            held[0] = kept.at[m]

    used = []
    for d in range(freqs):
        first = lax.rem(where_ref[2] + (freqs - d), freqs) * own_slots
        filled = jnp.int32(0)
        for b in range(row_blocks):
            for kk in range(own_slots):
                stored = b * own_slots + kk
                list_ref[d, filled] = (first + kk) * SHIFT + (b * SHIFT * SHIFT + stored)
                filled += (first + kk < counts_ref[b]).astype(jnp.int32)
        for u in range(GROUP):
            list_ref[d, filled + u] = row_blocks * SHIFT * SHIFT
        used.append(filled)

    def block_place(b, k):
        p = pattern_ref[b, k]
        owner = lax.div(p, row_blocks)
        place = lax.rem(owner, plane) * line + lax.div(owner, plane)
        return jnp.where(k < counts_ref[b], place * row_blocks + lax.rem(p, row_blocks), nodes * row_blocks)

    lane = lax.broadcasted_iota(jnp.int32, (size, LANES), 1)
    for b in range(row_blocks):
        mask_ref[b] = jnp.where((lane // parts) % row_blocks == b, 1.0, 0.0).astype(jnp.bfloat16)
    mask_ref[row_blocks] = jnp.zeros((size, LANES), jnp.bfloat16)
    acc_ref[...] = jnp.zeros_like(acc_ref)
    z_ref[nodes * row_blocks] = jnp.zeros((parts, size), jnp.float32)

    def blocks(body, carry):
        def chunk(i, carry):
            x = lines_ref[i]
            for b in range(row_blocks):
                carry = body(b, x[:, b * size : (b + 1) * size], i * row_blocks + b, carry)
            return carry

        if nodes > 16:
            return lax.fori_loop(0, nodes, chunk, carry)
        for i in range(nodes):
            carry = chunk(i, carry)
        return carry

    def add(sums, b, term):
        return sums[:b] + (sums[b] + term,) + sums[b + 1 :]

    def whole(sums):
        while len(sums) > 1:
            sums = tuple(x + y for x, y in zip(sums[::2], sums[1::2])) + sums[len(sums) // 2 * 2 :]
        return with_other_part(lane_sum(sums[0]))

    none = (jnp.zeros((parts, size), jnp.float32),) * row_blocks
    info = info_in_ref[...]
    if step == 0:
        height = jnp.sqrt(whole(blocks(lambda b, x, at, sums: add(sums, b, x * x), none)))
        info = put_lane(info, 0, height)

        def normal(b, x, at, carry):
            z_ref[at] = x / height
            return carry
    else:
        first = 1 if step == 1 else 3

        def dot(b, x, at, sums):
            return tuple(add(s, b, p[at] * x) for s, p in zip(sums, prev))

        coeffs = [whole(s) for s in blocks(dot, (none,) * step)]
        for i, coeff in enumerate(coeffs):
            info = put_lane(info, first + i, coeff)

        def subtract(b, x, at, sums):
            for coeff, p in zip(coeffs, prev):
                x = x - coeff * p[at]
            z_ref[at] = x
            return add(sums, b, x * x)

        height = jnp.sqrt(whole(blocks(subtract, none)))
        info = put_lane(info, first + step, height)

        def normal(b, x, at, carry):
            z_ref[at] = z_ref[at] / height
            return carry

    info_ref[...] = info
    blocks(normal, 0)
    own_ref[...] = jnp.concatenate([z_ref[own_place + b] for b in range(row_blocks)], axis=1)

    for k in range(slots):
        chosen = jnp.concatenate([z_ref[block_place(b, k)] for b in range(row_blocks)], axis=0)
        high = chosen.astype(jnp.bfloat16).astype(jnp.float32)
        layer_ref[k] = jnp.transpose(jnp.concatenate([high, chosen - high], axis=0)).astype(jnp.bfloat16)

    for d in reversed(range(freqs)):
        if d == 0:
            for arrival in arrivals:
                arrival.wait()

        @pl.loop(0, lax.div(used[d] + (GROUP - 1), GROUP))
        def _(group):
            total = acc_ref[...]
            for u in range(GROUP):
                item = list_ref[d, group * GROUP + u]
                stored = lax.rem(item, SHIFT)
                layer = lax.rem(lax.div(item, SHIFT), SHIFT)
                right = layer_ref[layer] * mask_ref[lax.div(item, SHIFT * SHIFT)]
                right = jnp.concatenate([right, right], axis=0)
                high, low = split(jnp.concatenate([g_refs[d][stored], c_refs[d][stored]], axis=0))
                left = jnp.concatenate([high, low], axis=1)
                total = total + jnp.dot(left, right, preferred_element_type=jnp.float32)
            acc_ref[...] = total

    half = row_blocks * parts
    gsum, csum = jnp.transpose(acc_ref[:size]), jnp.transpose(acc_ref[size:])
    gsum, csum = gsum[:half] + gsum[half:], csum[:half] + csum[half:]
    turn = turn_ref[...]
    for b in range(row_blocks):
        at = slice(b * parts, (b + 1) * parts)
        other = pltpu.roll(csum[at], parts // 2, 0)
        local_ref[:, b * size : (b + 1) * size] = gsum[at] + turn * other

    tile = jnp.zeros((parts, LANES), jnp.float32)
    if step == ITERS - 1:
        w = local_ref[...]
        zs = [jnp.concatenate([p[own_place + b] for b in range(row_blocks)], axis=1) for p in prev] + [own_ref[...]]
        values = [lane_sum(z * w) for z in zs]
        gram = [[lane_sum(zs[i] * zs[j]) for j in range(i + 1)] for i in range(ITERS)]
        shares = []
        for i, z in enumerate(zs):
            along = lane_sum(z * w) if i else values[0]
            share = jnp.where(gram[i][i] > 0.0, along / gram[i][i], 0.0)
            shares.append(share)
            w = w - share * z
        values += shares + [lane_sum(z * w) for z in zs] + [lane_sum(w * w)]
        values += [gram[i][j] for i in range(ITERS) for j in range(i + 1)]
        for lane_at, value in enumerate(values):
            tile = put_lane(tile, lane_at, value)
    tile_ref[...] = tile


def run_step(step, plane, pattern, counts, where, turn, info, lines, prev, g_parts, c_parts):
    freqs = len(g_parts)
    nodes, parts, rows = lines.shape
    row_blocks, slots = pattern.shape
    stored, size, _ = g_parts[0].shape
    vmem = pl.BlockSpec(memory_space=pltpu.VMEM)
    in_specs = [pl.BlockSpec(memory_space=pltpu.SMEM)] * 3 + [vmem] * (3 + step + 2 * freqs)
    scratch_shapes = [
        pltpu.VMEM((slots, size, LANES), jnp.bfloat16),
        pltpu.VMEM((row_blocks + 1, size, LANES), jnp.bfloat16),
        pltpu.VMEM((2 * size, LANES), jnp.float32),
        pltpu.SMEM((freqs, stored + GROUP), jnp.int32),
    ]
    if step == 0:
        in_specs[6] = in_specs[6 + freqs] = pl.BlockSpec(memory_space=pltpu.HBM)
        scratch_shapes += [pltpu.VMEM((2, stored, size, size), jnp.float32), pltpu.SemaphoreType.DMA((2,))]
    tile = jax.ShapeDtypeStruct((parts, LANES), jnp.float32)
    own = jax.ShapeDtypeStruct((parts, rows), jnp.float32)
    return pl.pallas_call(
        functools.partial(step_kernel, step, plane, nodes // plane, freqs),
        in_specs=in_specs,
        out_specs=[vmem] * 5,
        out_shape=[
            jax.ShapeDtypeStruct((nodes * row_blocks + 1, parts, size), jnp.float32),
            own,
            own,
            tile,
            tile,
        ],
        scratch_shapes=scratch_shapes,
        compiler_params=pltpu.CompilerParams(vmem_limit_bytes=VMEM_LIMIT),
        name=f"step_{step}",
    )(pattern, counts, where, turn, info, lines, *prev, *g_parts, *c_parts)


def final_kernel(info_ref, tiles_ref, *refs):
    krylov = refs[:ITERS]
    out_ref, residual_ref = refs[ITERS:]
    parts = info_ref.shape[0]
    fit = LANES // parts
    stacked = [tiles_ref[i] for i in range(tiles_ref.shape[0])]
    sets = [
        jnp.transpose(jnp.concatenate(stacked[at : at + fit], axis=0)) for at in range(0, len(stacked), fit)
    ]
    info = jnp.transpose(jnp.concatenate([info_ref[...]] * fit, axis=0))

    def all_devices(shares):
        total = sum(shares[1:], shares[0])
        step = parts // 2
        while step < LANES:
            total = total + pltpu.roll(total, step, 1)
            step *= 2
        return total

    def row(table, at):
        return jnp.broadcast_to(table[at : at + 1], (8, LANES))

    zero = jnp.zeros((8, LANES), jnp.float32)
    norm, h00, h10, h01, h11, h21 = [row(info, i) for i in range(6)]
    last = [all_devices([row(s, i) for s in sets]) for i in range(ITERS)]
    shares = []
    for s in sets:
        off = [last[i] - row(s, ITERS + i) for i in range(ITERS)]
        square = row(s, 3 * ITERS)
        at = 3 * ITERS + 1
        for i in range(ITERS):
            square = square - 2.0 * off[i] * row(s, 2 * ITERS + i)
            for j in range(i + 1):
                square = square + (1.0 if i == j else 2.0) * off[i] * off[j] * row(s, at)
                at += 1
        shares.append(square)
    height = jnp.sqrt(jnp.maximum(all_devices(shares), 0.0))
    hessen = [[h00, h01, last[0]], [h10, h11, last[1]], [zero, h21, last[2]], [zero, zero, height]]
    normal = [[sum(h[m] * h[n] for h in hessen) for n in range(ITERS)] for m in range(ITERS)]
    low = [[None] * ITERS for _ in range(ITERS)]
    middle = []
    for m in range(ITERS):
        for n in range(m):
            rest = normal[m][n] - sum((low[m][k] * low[n][k] for k in range(n)), zero)
            low[m][n] = rest / low[n][n]
        low[m][m] = jnp.sqrt(normal[m][m] - sum((low[m][k] * low[m][k] for k in range(m)), zero))
        rest = norm * hessen[0][m] - sum((low[m][k] * middle[k] for k in range(m)), zero)
        middle.append(rest / low[m][m])
    coef_y = [None] * ITERS
    for m in reversed(range(ITERS)):
        rest = middle[m] - sum((low[k][m] * coef_y[k] for k in range(m + 1, ITERS)), zero)
        coef_y[m] = rest / low[m][m]
    total = zero
    for i, h in enumerate(hessen):
        misfit = (norm if i == 0 else zero) - sum(h[m] * coef_y[m] for m in range(ITERS))
        total = total + misfit * misfit
    residual_ref[...] = jnp.sqrt(total)[:1, : parts // 2]
    columns = jnp.transpose(
        jnp.concatenate([y for y in coef_y] + [jnp.zeros((LANES - 8 * ITERS, LANES), jnp.float32)], axis=0)
    )[:parts]
    x = sum(columns[:, 8 * m : 8 * m + 1] * krylov[m][...] for m in range(ITERS))
    out_ref[0] = x[: parts // 2]
    out_ref[1] = x[parts // 2 :]


def run_final(info, tiles, krylov):
    parts, rows = krylov[0].shape
    vmem = pl.BlockSpec(memory_space=pltpu.VMEM)
    return pl.pallas_call(
        final_kernel,
        in_specs=[vmem] * (2 + ITERS),
        out_specs=[vmem] * 2,
        out_shape=[
            jax.ShapeDtypeStruct((2, parts // 2, rows), jnp.float32),
            jax.ShapeDtypeStruct((1, parts // 2), jnp.float32),
        ],
        name="final",
    )(info, tiles, *krylov)


def make_shards(line, plane, freqs):
    def shards(excitation, g_blocks, c_blocks, pattern, counts, freq_ids):
        angular = 0.2 * jnp.exp(freq_ids.astype(jnp.float32) * (math.log(8.0) / 1000.0))
        row_blocks, own_slots, size, _ = g_blocks.shape
        freq_count = excitation.shape[1]
        parts = 2 * freq_count
        where = jnp.stack([lax.axis_index(name) for name in ("line", "place", "freq")]).astype(jnp.int32)
        stored = (row_blocks * own_slots, size, size)
        g_parts, c_parts = [], []
        for d in range(freqs):
            perm = [(i, (i + d) % freqs) for i in range(freqs)]
            g_part = lax.ppermute(g_blocks, "freq", perm) if d else g_blocks
            c_part = lax.ppermute(c_blocks, "freq", perm) if d else c_blocks
            g_parts.append(g_part.reshape(stored))
            c_parts.append(c_part.reshape(stored))
        turn = jnp.broadcast_to(jnp.concatenate([-angular, angular])[:, None], (parts, LANES))
        info = jnp.zeros((parts, LANES), jnp.float32)
        krylov, own = [], []
        rows = excitation.reshape(parts, row_blocks * size)
        for step in range(ITERS):
            lines = gather_rows(rows, line, plane)
            z, mine, rows, info, tile = run_step(
                step, plane, pattern, counts, where, turn, info, lines, krylov, g_parts, c_parts
            )
            krylov.append(z)
            own.append(mine)
        tiles = gather_rows(tile, line, plane)
        answer, residual = run_final(info, tiles, own)
        return answer, residual.reshape(freq_count)

    return shards


def solution(mesh):
    line, plane = split_nodes(mesh.shape["node"])
    freqs = mesh.shape["freq"]
    fine = Mesh(mesh.devices.reshape(line, plane, freqs), ("line", "place", "freq"))
    node = ("line", "place")
    in_specs = (
        P(None, "freq", node),
        P(node, "freq", None, None),
        P(node, "freq", None, None),
        P(node, None),
        P(node),
        P("freq"),
    )
    out_specs = (P(None, "freq", node), P("freq"))
    shards = make_shards(line, plane, freqs)
    return jax.shard_map(shards, mesh=fine, in_specs=in_specs, out_specs=out_specs, check_vma=False)
```

time: 92.1 us -> 109 us (1.18)
  blocking collectives: 0 us -> 52 us
  starting transfers between devices: 29.2 us -> 10.6 us
  waiting for transfers between devices: 26.6 us -> 12.6 us
  other arithmetic: 4.3 us -> 0.16 us
  Pallas kernels: 22.3 us -> 26 us
  between operations: 2.17 us -> 0.74 us
  local copies, waits for them, and re-layouts: 7.32 us -> 5.93 us
    all_to_all x0 -> x6, blocking collectives: none -> 52 us  [the longest x3 27.1 us: gather_rows(): gathered = lax.all_to_all(copies, 'place', 0, 0)]
    ppermute x24 -> x0, starting transfers between devices: 28.6 us -> none  [the longest x12 14.3 us: gather_rows(): held.append(lax.ppermute(rows, 'node', perm))]
    ppermute x24 -> x0, waiting for transfers between devices: 26.6 us -> none  [the longest x12 14.4 us: gather_rows(): held.append(lax.ppermute(whole_line, 'node', perm))]
    all_to_all x0 -> x2, waiting for transfers between devices: none -> 12.6 us  [the longest x1 6.53 us: gather_rows(): gathered = lax.all_to_all(copies, 'place', 0, 0)]
    all_to_all x0 -> x2, starting transfers between devices: none -> 10 us  [the longest x1 6.32 us: gather_rows(): lax.all_to_all(jnp.broadcast_to(rows[None], (line,) + shape), 'line', 0, 0)]
    pallas_call x4, Pallas kernels: 22.3 us -> 26 us  [the longest x3 23.6 us: run_step(): pl.pallas_call(functools.partial(step_kernel, step, plane, nodes // plane...]
    broadcast_in_dim x0 -> x9, local copies, waits for them, and re-layouts: none -> 2.44 us  [the longest x5 1.49 us: gather_rows(): jnp.broadcast_to(rows[None], (line,) + shape)]
    unnamed x28 -> x20, local copies, waits for them, and re-layouts: 5.17 us -> 3.43 us
  transfers between devices with their start and end apart: 26 -> 4, of which waited for: 19 -> 2; matrix products, arithmetic and copies ran while one was open for 6% -> 2% of each run, Pallas kernels for 0% -> 0%
where the time goes in v3:
time: 109 us; the launch traced here: 108 us
  blocking collectives  52 us (48%)
  Pallas kernels  26 us (24%)
  waiting for transfers between devices  12.6 us (12%)
  starting transfers between devices  10.6 us (10%)
  local copies, waits for them, and re-layouts  5.93 us (5%)
    all_to_all x3, blocking collectives, gather_rows(): gathered = lax.all_to_all(copies, 'place', 0, 0)  27.1 us
    all_to_all x3, blocking collectives, gather_rows(): lax.all_to_all(jnp.broadcast_to(rows[None], (line,) + shape), 'line', 0, 0)  24.9 us
    pallas_call x3, Pallas kernels, run_step(): pl.pallas_call(functools.partial(step_kernel, step, plane, nodes // plane...  23.6 us
    all_to_all x1, waiting for transfers between devices, gather_rows(): gathered = lax.all_to_all(copies, 'place', 0, 0)  6.53 us
    all_to_all x1, starting transfers between devices, gather_rows(): lax.all_to_all(jnp.broadcast_to(rows[None], (line,) + shape), 'line', 0, 0)  6.32 us
    all_to_all x1, waiting for transfers between devices, gather_rows(): lax.all_to_all(jnp.broadcast_to(rows[None], (line,) + shape), 'line', 0, 0)  6.09 us
    all_to_all x1, starting transfers between devices, gather_rows(): gathered = lax.all_to_all(copies, 'place', 0, 0)  3.72 us
    unnamed x20, local copies, waits for them, and re-layouts  3.43 us
  transfers between devices with their start and end apart: 4, of which 2 were waited for; matrix products, arithmetic and copies ran while one was open for 2% of the time, Pallas kernels for 0%

profile of v3, /device:TPU:0, one launch (start us, length us, event | category | flops | bytes accessed | tf_op | source)
XLA Modules:
  0.0 108.1 jit_solution(15687224653839243696)
XLA Ops:
  0.6 0.0 copy-start
  0.6 0.0 copy-start.9
  0.7 0.0 copy-start.7
  0.7 0.0 copy-start.3
  0.7 0.5 collective-permute-start
  1.2 0.1 collective-permute-start.1
  1.3 0.8 broadcast_in_dim.24
  2.1 0.7 broadcast_in_dim.25
  2.7 6.3 %all-to-all-start = ((f32[4,8,1024]{2,1,0:T(8,128)}), f32[4,8,1024]{2,1,0:T(8,128)S(1)}, u32[]{:S(2)}, u32[]{:S(2)}) async-start(f32[4,8,1024]{2,1,0:T(8,128)} %broadcast_in_dim.25), calls=%async_computation | async-start | bytes 262144 | tf_op jit(solution)/shard_map/all_to_all | solution.py:26
  9.1 6.1 %all-to-all-done = f32[4,8,1024]{2,1,0:T(8,128)S(1)} async-done(((f32[4,8,1024]{2,1,0:T(8,128)}), f32[4,8,1024]{2,1,0:T(8,128)S(1)}, u32[]{:S(2)}, u32[]{:S(2)}) %all-to-all-start) | async-done | bytes 131104 | tf_op jit(solution)/shard_map/all_to_all | solution.py:26
  15.2 0.9 broadcast_in_dim.26
  16.0 3.7 %all-to-all-start.1 = ((f32[4,4,8,1024]{3,2,1,0:T(8,128)}), f32[4,4,8,1024]{3,2,1,0:T(8,128)S(1)}, u32[]{:S(2)}, u32[]{:S(2)}) async-start(f32[4,4,8,1024]{3,2,1,0:T(8,128)} %broadcast_in_dim.26), calls=%async_computation.1 | async-start | bytes 1048576 | tf_op jit(solution)/shard_map/all_to_all | solution.py:28
  19.7 0.0 copy-done.9
  19.7 0.1 pad_maximum_fusion
  19.8 0.1 pad_add_fusion.where_ref
  19.9 6.5 %all-to-all-done.1 = f32[4,4,8,1024]{3,2,1,0:T(8,128)S(1)} async-done(((f32[4,4,8,1024]{3,2,1,0:T(8,128)}), f32[4,4,8,1024]{3,2,1,0:T(8,128)S(1)}, u32[]{:S(2)}, u32[]{:S(2)}) %all-to-all-start.1) | async-done | bytes 524320 | tf_op jit(solution)/shard_map/all_to_all | solution.py:28
  26.4 0.0 collective-permute-done
  26.4 0.0 collective-permute-done.1
  26.4 0.1 broadcast_in_dim.22.turn_ref
  26.5 0.0 copy-done
  26.5 0.0 copy-done.7
  26.5 0.0 copy-done.3
  26.5 0.0 copy-start.1
  26.5 1.6 %copy-done.1 = f32[8,4,128,128]{3,2,1,0:T(8,128)S(1)} copy-done((f32[8,4,128,128]{3,2,1,0:T(8,128)S(1)}, f32[8,4,128,128]{3,2,1,0:T(8,128)}, u32[]{:S(2)}) %copy-start.1) | copy-done | bytes 2097176
  28.1 7.9 %step_0.1 = (f32[129,8,128]{2,1,0:T(8,128)S(1)}, f32[8,1024]{1,0:T(8,128)S(1)}, f32[8,1024]{1,0:T(8,128)S(1)}, f32[8,128]{1,0:T(8,128)S(1)}, f32[8,128]{1,0:T(8,128)}) custom-call(s32[8,8]{1,0:T(8,128)S(1)} %copy-done.3, s32[8]{0:T(128)S(1)} %copy-done.7, s32[3]{0:T(128)S(1)} %pad_add_fusion.where_ref, f32[8,128]{1,0:T(8,128)S(1)} %broadcast_in_dim.22.turn_ref, ...), custom_call_target="tpu_custom_call" | custom-call | tf_op jit(solution)/shard_map/step_0/pallas_call | solution.py:227
  36.0 0.0 copy-start.4
  36.0 0.6 copy-done.4
  36.6 0.0 copy-start.2
  36.6 8.7 %all_to_all.40 = f32[4,8,1024]{2,1,0:T(8,128)S(1)} all-to-all(f32[4,8,1024]{2,1,0:T(8,128)S(1)} %broadcast_in_dim.27), channel_id=1, replica_groups=mesh['line'=4,'place'=4,'freq'=2] {'line'}, dimensions={0} | all-to-all | bytes 262144 | tf_op jit(solution)/shard_map/all_to_all | solution.py:26
  45.4 9.7 %all_to_all.41 = f32[4,4,8,1024]{3,2,1,0:T(8,128)S(1)} all-to-all(f32[4,4,8,1024]{3,2,1,0:T(8,128)S(1)} %broadcast_in_dim.28), channel_id=1, replica_groups=mesh['line'=4,'place'=4,'freq'=2] {'place'}, dimensions={0} | all-to-all | bytes 1048576 | tf_op jit(solution)/shard_map/all_to_all | solution.py:28
  55.0 0.0 copy-done.2
  55.0 7.7 %step_1.1 = (f32[129,8,128]{2,1,0:T(8,128)S(1)}, f32[8,1024]{1,0:T(8,128)S(1)}, f32[8,1024]{1,0:T(8,128)S(1)}, f32[8,128]{1,0:T(8,128)S(1)}, f32[8,128]{1,0:T(8,128)}) custom-call(s32[8,8]{1,0:T(8,128)S(1)} %copy-done.3, s32[8]{0:T(128)S(1)} %copy-done.7, s32[3]{0:T(128)S(1)} %pad_add_fusion.where_ref, f32[8,128]{1,0:T(8,128)S(1)} %broadcast_in_dim.22.turn_ref, ...), custom_call_target="tpu_custom_call" | custom-call | tf_op jit(solution)/shard_map/step_1/pallas_call | solution.py:227
  62.7 0.0 copy-start.5
  62.7 8.3 %all_to_all.42 = f32[4,8,1024]{2,1,0:T(8,128)S(1)} all-to-all(f32[4,8,1024]{2,1,0:T(8,128)S(1)} %broadcast_in_dim.29), channel_id=1, replica_groups=mesh['line'=4,'place'=4,'freq'=2] {'line'}, dimensions={0} | all-to-all | bytes 262144 | tf_op jit(solution)/shard_map/all_to_all | solution.py:26
  71.1 9.5 %all_to_all.43 = f32[4,4,8,1024]{3,2,1,0:T(8,128)S(1)} all-to-all(f32[4,4,8,1024]{3,2,1,0:T(8,128)S(1)} %broadcast_in_dim.30), channel_id=1, replica_groups=mesh['line'=4,'place'=4,'freq'=2] {'place'}, dimensions={0} | all-to-all | bytes 1048576 | tf_op jit(solution)/shard_map/all_to_all | solution.py:28
  80.6 8.0 %step_2.1 = (f32[129,8,128]{2,1,0:T(8,128)}, f32[8,1024]{1,0:T(8,128)S(1)}, f32[8,1024]{1,0:T(8,128)}, f32[8,128]{1,0:T(8,128)S(1)}, f32[8,128]{1,0:T(8,128)S(1)}) custom-call(s32[8,8]{1,0:T(8,128)S(1)} %copy-done.3, s32[8]{0:T(128)S(1)} %copy-done.7, s32[3]{0:T(128)S(1)} %pad_add_fusion.where_ref, f32[8,128]{1,0:T(8,128)S(1)} %broadcast_in_dim.22.turn_ref, ...), custom_call_target="tpu_custom_call" | custom-call | tf_op jit(solution)/shard_map/step_2/pallas_call | solution.py:227
  88.6 0.0 copy-done.5
  88.6 0.0 copy-start.6
  88.6 0.6 copy-done.6
  89.2 0.0 copy-start.8
  89.2 0.6 copy-done.8
  89.8 8.0 %all_to_all.44 = f32[4,8,128]{2,1,0:T(8,128)S(1)} all-to-all(f32[4,8,128]{2,1,0:T(8,128)S(1)} %broadcast_in_dim.31), channel_id=1, replica_groups=mesh['line'=4,'place'=4,'freq'=2] {'line'}, dimensions={0} | all-to-all | bytes 32768 | tf_op jit(solution)/shard_map/all_to_all | solution.py:26
  97.8 7.9 %all_to_all.45 = f32[4,4,8,128]{3,2,1,0:T(8,128)} all-to-all(f32[4,4,8,128]{3,2,1,0:T(8,128)S(1)} %broadcast_in_dim.32), channel_id=1, replica_groups=mesh['line'=4,'place'=4,'freq'=2] {'place'}, dimensions={0} | all-to-all | bytes 131072 | tf_op jit(solution)/shard_map/all_to_all | solution.py:28
  105.7 2.4 %final.1 = (f32[2,4,1024]{2,1,0:T(4,128)}, f32[1,4]{1,0:T(1,128)}) custom-call(f32[8,128]{1,0:T(8,128)} %copy-done.8, f32[16,8,128]{2,1,0:T(8,128)} %bitcast.21, f32[8,1024]{1,0:T(8,128)} %copy-done.4, f32[8,1024]{1,0:T(8,128)} %copy-done.5, f32[8,1024]{1,0:T(8,128)} %copy-done.6), custom_call_target="tpu_custom_call" | custom-call | tf_op jit(solution)/shard_map/final/pallas_call | solution.py:312
  (8 shorter events, 0.1 us)
Async XLA Ops:
  0.6 25.9 %copy-start = (f32[8,4,128,128]{3,2,1,0:T(8,128)S(1)}, f32[8,4,128,128]{3,2,1,0:T(8,128)}, u32[]{:S(2)}) copy-start(f32[8,4,128,128]{3,2,1,0:T(8,128)} %param.7) | copy-start | bytes 6291460
  0.6 19.1 %copy-start.9 = (s32[4]{0:T(128)S(1)}, s32[4]{0:T(128)}, u32[]{:S(2)}) copy-start(s32[4]{0:T(128)} %param.11) | copy-start | bytes 52
  0.7 25.8 %copy-start.7 = (s32[8]{0:T(128)S(1)}, s32[8]{0:T(128)}, u32[]{:S(2)}) copy-start(s32[8]{0:T(128)} %counts_ref.5) | copy-start | bytes 100
  0.7 25.8 %copy-start.3 = (s32[8,8]{1,0:T(8,128)S(1)}, s32[8,8]{1,0:T(8,128)}, u32[]{:S(2)}) copy-start(s32[8,8]{1,0:T(8,128)} %pattern_ref.5) | copy-start | bytes 772
  0.7 25.7 %collective-permute-start = (f32[8,4,128,128]{3,2,1,0:T(8,128)}, f32[8,4,128,128]{3,2,1,0:T(8,128)}, u32[]{:S(2)}, u32[]{:S(2)}) collective-permute-start(f32[8,4,128,128]{3,2,1,0:T(8,128)} %param.7), channel_id=1, source_target_pairs={{0,1},{1,0},{2,3},{3,2},{4,5},{5,4},{6,7},{7,6},{8,9},{9,8},{10,11... | collective-permute-start | bytes 6291464 | tf_op jit(solution)/shard_map/ppermute | solution.py:335
  1.2 25.2 %collective-permute-start.1 = (f32[8,4,128,128]{3,2,1,0:T(8,128)}, f32[8,4,128,128]{3,2,1,0:T(8,128)}, u32[]{:S(2)}, u32[]{:S(2)}) collective-permute-start(f32[8,4,128,128]{3,2,1,0:T(8,128)} %param.8), channel_id=1, source_target_pairs={{0,1},{1,0},{2,3},{3,2},{4,5},{5,4},{6,7},{7,6},{8,9},{9,8},{10,11... | collective-permute-start | bytes 6291464 | tf_op jit(solution)/shard_map/ppermute | solution.py:336
  2.7 12.4 %all-to-all-start = ((f32[4,8,1024]{2,1,0:T(8,128)}), f32[4,8,1024]{2,1,0:T(8,128)S(1)}, u32[]{:S(2)}, u32[]{:S(2)}) async-start(f32[4,8,1024]{2,1,0:T(8,128)} %broadcast_in_dim.25), calls=%async_computation | async-start | bytes 262144 | tf_op jit(solution)/shard_map/all_to_all | solution.py:26
  16.0 10.4 %all-to-all-start.1 = ((f32[4,4,8,1024]{3,2,1,0:T(8,128)}), f32[4,4,8,1024]{3,2,1,0:T(8,128)S(1)}, u32[]{:S(2)}, u32[]{:S(2)}) async-start(f32[4,4,8,1024]{3,2,1,0:T(8,128)} %broadcast_in_dim.26), calls=%async_computation.1 | async-start | bytes 1048576 | tf_op jit(solution)/shard_map/all_to_all | solution.py:28
  26.5 1.6 %copy-start.1 = (f32[8,4,128,128]{3,2,1,0:T(8,128)S(1)}, f32[8,4,128,128]{3,2,1,0:T(8,128)}, u32[]{:S(2)}) copy-start(f32[8,4,128,128]{3,2,1,0:T(8,128)} %param.8) | copy-start | bytes 6291460
  36.0 0.6 copy-start.4
  36.6 18.4 %copy-start.2 = (f32[8,4,128,128]{3,2,1,0:T(8,128)S(1)}, f32[8,4,128,128]{3,2,1,0:T(8,128)}, u32[]{:S(2)}) copy-start(f32[8,4,128,128]{3,2,1,0:T(8,128)} %param.8) | copy-start | bytes 6291460
  62.7 25.9 %copy-start.5 = (f32[8,1024]{1,0:T(8,128)}, f32[8,1024]{1,0:T(8,128)S(1)}, u32[]{:S(2)}) copy-start(f32[8,1024]{1,0:T(8,128)S(1)} %get-tuple-element.24.refs_1_) | copy-start | bytes 98308
  88.6 0.6 copy-start.6
  89.2 0.6 copy-start.8

commit v4 on v3

--- a/solution.py
+++ b/solution.py
@@ -13,6 +13,7 @@
 LANES = 128
 GROUP = 4
 SHIFT = 256
+SHARES = 16
 VMEM_LIMIT = 20 * 1024 * 1024
 
 
@@ -21,57 +22,28 @@
     return nodes // plane, plane
 
 
+def partner_steps(size):
+    if size & (size - 1) == 0:
+        return [[(i, i ^ d) for i in range(size)] for d in range(1, size)]
+    return [[(i, (i + d) % size) for i in range(size)] for d in range(1, size)]
+
+
+def distance(me, other, size):
+    if size & (size - 1) == 0:
+        return me ^ other
+    return lax.rem(me - other + size, size)
+
+
 def gather_rows(rows, line, plane):
-    shape = rows.shape
-    whole_line = lax.all_to_all(jnp.broadcast_to(rows[None], (line,) + shape), "line", 0, 0)
-    copies = jnp.broadcast_to(whole_line[None], (plane, line) + shape)
-    gathered = lax.all_to_all(copies, "place", 0, 0)
-    return gathered.reshape((plane * line,) + shape)
-
-
-def lane_sum(x):
-    return jnp.sum(x, axis=1, keepdims=True)
-
-
-def with_other_part(column):
-    wide = jnp.broadcast_to(column, (column.shape[0], LANES))
-    return wide + pltpu.roll(wide, column.shape[0] // 2, 0)
-
-
-def put_lane(tile, lane, column):
-    at = lax.broadcasted_iota(jnp.int32, tile.shape, 1) == lane
-    return jnp.where(at, column, tile)
-
-
-def split(x):
-    high = x.astype(jnp.bfloat16)
-    return high, (x - high.astype(jnp.float32)).astype(jnp.bfloat16)
-
-
-def step_kernel(step, plane, line, freqs, pattern_ref, counts_ref, where_ref, turn_ref, info_in_ref, *refs):
-    lines_ref, refs = refs[0], refs[1:]
-    prev = refs[:step]
-    g_refs = list(refs[step : step + freqs])
-    c_refs = list(refs[step + freqs : step + 2 * freqs])
-    z_ref, own_ref, local_ref, info_ref, tile_ref, layer_ref, mask_ref, acc_ref, list_ref = refs[
-        step + 2 * freqs : step + 2 * freqs + 9
-    ]
-    nodes = plane * line
-    parts, rows = local_ref.shape
+    parts = rows.size // rows.shape[-1]
+    held = [rows] + [lax.ppermute(rows, "line", perm) for perm in partner_steps(line)]
+    whole_line = jnp.stack(held).reshape(line, parts, rows.shape[-1])
+    return [whole_line] + [lax.ppermute(whole_line, "place", perm) for perm in partner_steps(plane)]
+
+
+def list_kernel(line, plane, freqs, pattern_ref, counts_ref, where_ref, list_ref, places_ref, used_ref):
     row_blocks, slots = pattern_ref.shape
     own_slots = slots // freqs
-    size = rows // row_blocks
-    own_place = (where_ref[1] * line + where_ref[0]) * row_blocks
-
-    arrivals = []
-    if step == 0:
-        kept, sems = refs[step + 2 * freqs + 9 :]
-        for m, held in enumerate((g_refs, c_refs)):
-            arrivals.append(pltpu.make_async_copy(held[0], kept.at[m], sems.at[m]))
-            arrivals[-1].start()
-            held[0] = kept.at[m]
-
-    used = []
     for d in range(freqs):
         first = lax.rem(where_ref[2] + (freqs - d), freqs) * own_slots
         filled = jnp.int32(0)
@@ -82,13 +54,69 @@
                 filled += (first + kk < counts_ref[b]).astype(jnp.int32)
         for u in range(GROUP):
             list_ref[d, filled + u] = row_blocks * SHIFT * SHIFT
-        used.append(filled)
-
-    def block_place(b, k):
-        p = pattern_ref[b, k]
-        owner = lax.div(p, row_blocks)
-        place = lax.rem(owner, plane) * line + lax.div(owner, plane)
-        return jnp.where(k < counts_ref[b], place * row_blocks + lax.rem(p, row_blocks), nodes * row_blocks)
+        used_ref[d] = lax.div(filled + (GROUP - 1), GROUP)
+    for b in range(row_blocks):
+        for k in range(slots):
+            p = pattern_ref[b, k]
+            owner = lax.div(p, row_blocks)
+            far = distance(where_ref[0], lax.div(owner, plane), line)
+            place = distance(where_ref[1], lax.rem(owner, plane), plane) * line + far
+            place = place * row_blocks + lax.rem(p, row_blocks)
+            places_ref[k, b] = jnp.where(k < counts_ref[b], place, line * plane * row_blocks)
+
+
+def work_list(pattern, counts, where, line, plane, freqs):
+    row_blocks, slots = pattern.shape
+    smem = pl.BlockSpec(memory_space=pltpu.SMEM)
+    return pl.pallas_call(
+        functools.partial(list_kernel, line, plane, freqs),
+        in_specs=[smem] * 3,
+        out_specs=[smem] * 3,
+        out_shape=[
+            jax.ShapeDtypeStruct((freqs, row_blocks * slots // freqs + GROUP), jnp.int32),
+            jax.ShapeDtypeStruct((slots, row_blocks), jnp.int32),
+            jax.ShapeDtypeStruct((freqs,), jnp.int32),
+        ],
+        name="work_list",
+    )(pattern, counts, where)
+
+
+def lane_sum(x):
+    return jnp.sum(x, axis=1, keepdims=True)
+
+
+def with_other_part(column):
+    wide = jnp.broadcast_to(column, (column.shape[0], LANES))
+    return wide + pltpu.roll(wide, column.shape[0] // 2, 0)
+
+
+def put_lane(tile, lane, column):
+    at = lax.broadcasted_iota(jnp.int32, tile.shape, 1) == lane
+    return jnp.where(at, column, tile)
+
+
+def split(x):
+    high = x.astype(jnp.bfloat16)
+    return high, (x - high.astype(jnp.float32)).astype(jnp.bfloat16)
+
+
+def step_kernel(step, plane, line, freqs, list_ref, places_ref, used_ref, turn_ref, info_in_ref, *refs):
+    lines, refs = refs[:plane], refs[plane:]
+    prev, refs = refs[:step], refs[step:]
+    g_refs, c_refs = list(refs[:freqs]), list(refs[freqs : 2 * freqs])
+    z_ref, own_ref, local_ref, info_ref, layer_ref, mask_ref, acc_ref = refs[2 * freqs : 2 * freqs + 7]
+    nodes = plane * line
+    parts, rows = own_ref.shape
+    slots, row_blocks = places_ref.shape
+    size = rows // row_blocks
+
+    arrivals = []
+    if step == 0:
+        kept, sems = refs[2 * freqs + 7 :]
+        for m, held in enumerate((g_refs, c_refs)):
+            arrivals.append(pltpu.make_async_copy(held[0], kept.at[m], sems.at[m]))
+            arrivals[-1].start()
+            held[0] = kept.at[m]
 
     lane = lax.broadcasted_iota(jnp.int32, (size, LANES), 1)
     for b in range(row_blocks):
@@ -98,16 +126,19 @@
     z_ref[nodes * row_blocks] = jnp.zeros((parts, size), jnp.float32)
 
     def blocks(body, carry):
-        def chunk(i, carry):
-            x = lines_ref[i]
-            for b in range(row_blocks):
-                carry = body(b, x[:, b * size : (b + 1) * size], i * row_blocks + b, carry)
-            return carry
-
-        if nodes > 16:
-            return lax.fori_loop(0, nodes, chunk, carry)
-        for i in range(nodes):
-            carry = chunk(i, carry)
+        for q in range(plane):
+
+            def chunk(i, carry, q=q):
+                x = lines[q][i]
+                for b in range(row_blocks):
+                    carry = body(b, x[:, b * size : (b + 1) * size], (q * line + i) * row_blocks + b, carry)
+                return carry
+
+            if line <= 4:
+                for i in range(line):
+                    carry = chunk(i, carry)
+            else:
+                carry = lax.fori_loop(0, line, chunk, carry)
         return carry
 
     def add(sums, b, term):
@@ -150,12 +181,11 @@
             z_ref[at] = z_ref[at] / height
             return carry
 
-    info_ref[...] = info
     blocks(normal, 0)
-    own_ref[...] = jnp.concatenate([z_ref[own_place + b] for b in range(row_blocks)], axis=1)
+    own_ref[...] = jnp.concatenate([z_ref[b] for b in range(row_blocks)], axis=1)
 
     for k in range(slots):
-        chosen = jnp.concatenate([z_ref[block_place(b, k)] for b in range(row_blocks)], axis=0)
+        chosen = jnp.concatenate([z_ref[places_ref[k, b]] for b in range(row_blocks)], axis=0)
         high = chosen.astype(jnp.bfloat16).astype(jnp.float32)
         layer_ref[k] = jnp.transpose(jnp.concatenate([high, chosen - high], axis=0)).astype(jnp.bfloat16)
 
@@ -164,7 +194,7 @@
             for arrival in arrivals:
                 arrival.wait()
 
-        @pl.loop(0, lax.div(used[d] + (GROUP - 1), GROUP))
+        @pl.loop(0, used_ref[d])
         def _(group):
             total = acc_ref[...]
             for u in range(GROUP):
@@ -187,10 +217,9 @@
         other = pltpu.roll(csum[at], parts // 2, 0)
         local_ref[:, b * size : (b + 1) * size] = gsum[at] + turn * other
 
-    tile = jnp.zeros((parts, LANES), jnp.float32)
     if step == ITERS - 1:
         w = local_ref[...]
-        zs = [jnp.concatenate([p[own_place + b] for b in range(row_blocks)], axis=1) for p in prev] + [own_ref[...]]
+        zs = [jnp.concatenate([p[b] for b in range(row_blocks)], axis=1) for p in prev] + [own_ref[...]]
         values = [lane_sum(z * w) for z in zs]
         gram = [[lane_sum(zs[i] * zs[j]) for j in range(i + 1)] for i in range(ITERS)]
         shares = []
@@ -202,55 +231,53 @@
         values += shares + [lane_sum(z * w) for z in zs] + [lane_sum(w * w)]
         values += [gram[i][j] for i in range(ITERS) for j in range(i + 1)]
         for lane_at, value in enumerate(values):
-            tile = put_lane(tile, lane_at, value)
-    tile_ref[...] = tile
-
-
-def run_step(step, plane, pattern, counts, where, turn, info, lines, prev, g_parts, c_parts):
-    freqs = len(g_parts)
-    nodes, parts, rows = lines.shape
-    row_blocks, slots = pattern.shape
+            info = put_lane(info, SHARES + lane_at, value)
+    info_ref[...] = info
+
+
+def run_step(step, lists, turn, info, lines, prev, g_parts, c_parts):
+    plane, freqs = len(lines), len(g_parts)
+    line, parts, rows = lines[0].shape
+    slots, row_blocks = lists[1].shape
     stored, size, _ = g_parts[0].shape
     vmem = pl.BlockSpec(memory_space=pltpu.VMEM)
-    in_specs = [pl.BlockSpec(memory_space=pltpu.SMEM)] * 3 + [vmem] * (3 + step + 2 * freqs)
+    in_specs = [pl.BlockSpec(memory_space=pltpu.SMEM)] * 3 + [vmem] * (2 + plane + step + 2 * freqs)
     scratch_shapes = [
         pltpu.VMEM((slots, size, LANES), jnp.bfloat16),
         pltpu.VMEM((row_blocks + 1, size, LANES), jnp.bfloat16),
         pltpu.VMEM((2 * size, LANES), jnp.float32),
-        pltpu.SMEM((freqs, stored + GROUP), jnp.int32),
     ]
     if step == 0:
-        in_specs[6] = in_specs[6 + freqs] = pl.BlockSpec(memory_space=pltpu.HBM)
+        in_specs[5 + plane] = in_specs[5 + plane + freqs] = pl.BlockSpec(memory_space=pltpu.HBM)
         scratch_shapes += [pltpu.VMEM((2, stored, size, size), jnp.float32), pltpu.SemaphoreType.DMA((2,))]
     tile = jax.ShapeDtypeStruct((parts, LANES), jnp.float32)
     own = jax.ShapeDtypeStruct((parts, rows), jnp.float32)
     return pl.pallas_call(
-        functools.partial(step_kernel, step, plane, nodes // plane, freqs),
+        functools.partial(step_kernel, step, plane, line, freqs),
         in_specs=in_specs,
-        out_specs=[vmem] * 5,
+        out_specs=[vmem] * 4,
         out_shape=[
-            jax.ShapeDtypeStruct((nodes * row_blocks + 1, parts, size), jnp.float32),
+            jax.ShapeDtypeStruct((plane * line * row_blocks + 1, parts, size), jnp.float32),
             own,
             own,
-            tile,
             tile,
         ],
         scratch_shapes=scratch_shapes,
         compiler_params=pltpu.CompilerParams(vmem_limit_bytes=VMEM_LIMIT),
         name=f"step_{step}",
-    )(pattern, counts, where, turn, info, lines, *prev, *g_parts, *c_parts)
-
-
-def final_kernel(info_ref, tiles_ref, *refs):
-    krylov = refs[:ITERS]
-    out_ref, residual_ref = refs[ITERS:]
-    parts = info_ref.shape[0]
+    )(*lists, turn, info, *lines, *prev, *g_parts, *c_parts)
+
+
+def final_kernel(plane, *refs):
+    tiles, krylov = refs[:plane], refs[plane : plane + ITERS]
+    out_ref, residual_ref = refs[plane + ITERS :]
+    line, parts, _ = tiles[0].shape
     fit = LANES // parts
-    stacked = [tiles_ref[i] for i in range(tiles_ref.shape[0])]
+    stacked = [tiles[q][i] for q in range(plane) for i in range(line)]
     sets = [
         jnp.transpose(jnp.concatenate(stacked[at : at + fit], axis=0)) for at in range(0, len(stacked), fit)
     ]
-    info = jnp.transpose(jnp.concatenate([info_ref[...]] * fit, axis=0))
+    info = jnp.transpose(jnp.concatenate([tiles[0][0]] * fit, axis=0))
 
     def all_devices(shares):
         total = sum(shares[1:], shares[0])
@@ -265,14 +292,14 @@
 
     zero = jnp.zeros((8, LANES), jnp.float32)
     norm, h00, h10, h01, h11, h21 = [row(info, i) for i in range(6)]
-    last = [all_devices([row(s, i) for s in sets]) for i in range(ITERS)]
+    last = [all_devices([row(s, SHARES + i) for s in sets]) for i in range(ITERS)]
     shares = []
     for s in sets:
-        off = [last[i] - row(s, ITERS + i) for i in range(ITERS)]
-        square = row(s, 3 * ITERS)
-        at = 3 * ITERS + 1
+        off = [last[i] - row(s, SHARES + ITERS + i) for i in range(ITERS)]
+        square = row(s, SHARES + 3 * ITERS)
+        at = SHARES + 3 * ITERS + 1
         for i in range(ITERS):
-            square = square - 2.0 * off[i] * row(s, 2 * ITERS + i)
+            square = square - 2.0 * off[i] * row(s, SHARES + 2 * ITERS + i)
             for j in range(i + 1):
                 square = square + (1.0 if i == j else 2.0) * off[i] * off[j] * row(s, at)
                 at += 1
@@ -306,19 +333,19 @@
     out_ref[1] = x[parts // 2 :]
 
 
-def run_final(info, tiles, krylov):
+def run_final(tiles, krylov):
     parts, rows = krylov[0].shape
     vmem = pl.BlockSpec(memory_space=pltpu.VMEM)
     return pl.pallas_call(
-        final_kernel,
-        in_specs=[vmem] * (2 + ITERS),
+        functools.partial(final_kernel, len(tiles)),
+        in_specs=[vmem] * (len(tiles) + ITERS),
         out_specs=[vmem] * 2,
         out_shape=[
             jax.ShapeDtypeStruct((2, parts // 2, rows), jnp.float32),
             jax.ShapeDtypeStruct((1, parts // 2), jnp.float32),
         ],
         name="final",
-    )(info, tiles, *krylov)
+    )(*tiles, *krylov)
 
 
 def make_shards(line, plane, freqs):
@@ -339,16 +366,14 @@
         turn = jnp.broadcast_to(jnp.concatenate([-angular, angular])[:, None], (parts, LANES))
         info = jnp.zeros((parts, LANES), jnp.float32)
         krylov, own = [], []
-        rows = excitation.reshape(parts, row_blocks * size)
+        lists = work_list(pattern, counts, where, line, plane, freqs)
+        rows = excitation
         for step in range(ITERS):
             lines = gather_rows(rows, line, plane)
-            z, mine, rows, info, tile = run_step(
-                step, plane, pattern, counts, where, turn, info, lines, krylov, g_parts, c_parts
-            )
+            z, mine, rows, info = run_step(step, lists, turn, info, lines, krylov, g_parts, c_parts)
             krylov.append(z)
             own.append(mine)
-        tiles = gather_rows(tile, line, plane)
-        answer, residual = run_final(info, tiles, own)
+        answer, residual = run_final(gather_rows(info, line, plane), own)
         return answer, residual.reshape(freq_count)
 
     return shards

time: 109 us -> 90.3 us (0.83)
  blocking collectives: 52 us -> 0 us
  starting transfers between devices: 10.6 us -> 33.6 us
  waiting for transfers between devices: 12.6 us -> 22.5 us
  Pallas kernels: 26 us -> 23.1 us
  local copies, waits for them, and re-layouts: 5.93 us -> 7.95 us
  other arithmetic: 0.16 us -> 1.36 us
    all_to_all x6 -> x0, blocking collectives: 52 us -> none  [the longest x3 27.1 us: gather_rows(): gathered = lax.all_to_all(copies, 'place', 0, 0)]
    ppermute x0 -> x24, starting transfers between devices: none -> 33 us  [the longest x12 18.8 us: gather_rows(): lax.ppermute(rows, 'line', perm)]
    ppermute x0 -> x24, waiting for transfers between devices: none -> 22.5 us  [the longest x12 13 us: gather_rows(): lax.ppermute(whole_line, 'place', perm)]
    all_to_all x2 -> x0, waiting for transfers between devices: 12.6 us -> none  [the longest x1 6.53 us: gather_rows(): gathered = lax.all_to_all(copies, 'place', 0, 0)]
    all_to_all x2 -> x0, starting transfers between devices: 10 us -> none  [the longest x1 6.32 us: gather_rows(): lax.all_to_all(jnp.broadcast_to(rows[None], (line,) + shape), 'line', 0, 0)]
    unnamed x20 -> x33, local copies, waits for them, and re-layouts: 3.43 us -> 7.02 us
    pallas_call x4 -> x5, Pallas kernels: 26 us -> 23.1 us  [the longest x3 18.7 us: run_step(): pl.pallas_call(functools.partial(step_kernel, step, plane, line, freqs),...]
    broadcast_in_dim x9 -> x0, local copies, waits for them, and re-layouts: 2.44 us -> none  [the longest x5 1.49 us: gather_rows(): jnp.broadcast_to(rows[None], (line,) + shape)]
  transfers between devices with their start and end apart: 4 -> 26, of which waited for: 2 -> 19; matrix products, arithmetic and copies ran while one was open for 2% -> 2% of each run, Pallas kernels for 0% -> 2%
where the time goes in v4:
time: 90.3 us; the launch traced here: 89.2 us
  starting transfers between devices  33.6 us (37%)
  Pallas kernels  23.1 us (26%)
  waiting for transfers between devices  22.5 us (25%)
  local copies, waits for them, and re-layouts  7.95 us (9%)
  other arithmetic  1.36 us (2%)
    ppermute x12, starting transfers between devices, gather_rows(): lax.ppermute(rows, 'line', perm)  18.8 us
    pallas_call x3, Pallas kernels, run_step(): pl.pallas_call(functools.partial(step_kernel, step, plane, line, freqs),...  18.7 us
    ppermute x12, starting transfers between devices, gather_rows(): lax.ppermute(whole_line, 'place', perm)  14.1 us
    ppermute x12, waiting for transfers between devices, gather_rows(): lax.ppermute(whole_line, 'place', perm)  13 us
    ppermute x12, waiting for transfers between devices, gather_rows(): lax.ppermute(rows, 'line', perm)  9.46 us
    unnamed x33, local copies, waits for them, and re-layouts  7.02 us
    pallas_call x1, Pallas kernels, run_final(): pl.pallas_call(functools.partial(final_kernel, len(tiles)), in_specs=[vme...  2.43 us
    pallas_call x1, Pallas kernels, work_list(): pl.pallas_call(functools.partial(list_kernel, line, plane, freqs), in_spe...  1.97 us
  transfers between devices with their start and end apart: 26, of which 19 were waited for; matrix products, arithmetic and copies ran while one was open for 2% of the time, Pallas kernels for 2%

profile of v4, /device:TPU:0, one launch (start us, length us, event | category | flops | bytes accessed | tf_op | source)
XLA Modules:
  0.0 89.2 jit_solution(7830157716989331646)
XLA Ops:
  1.2 3.0 %collective-permute-start = (f32[2,4,1024]{2,1,0:T(4,128)}, f32[2,4,1024]{2,1,0:T(4,128)S(1)}, u32[]{:S(2)}, u32[]{:S(2)}) collective-permute-start(f32[2,4,1024]{2,1,0:T(4,128)} %param.6), channel_id=1, source_target_pairs={{0,8},{8,0},{16,24},{24,16},{1,9},{9,1},{17,25},{25,17},{2,10},{10... | collective-permute-start | bytes 98312 | tf_op jit(solution)/shard_map/ppermute | solution.py:39
  4.2 2.5 %collective-permute-start.2 = (f32[2,4,1024]{2,1,0:T(4,128)}, f32[2,4,1024]{2,1,0:T(4,128)S(1)}, u32[]{:S(2)}, u32[]{:S(2)}) collective-permute-start(f32[2,4,1024]{2,1,0:T(4,128)} %param.6), channel_id=1, source_target_pairs={{0,24},{8,16},{16,8},{24,0},{1,25},{9,17},{17,9},{25,1},{2,26},{10... | collective-permute-start | bytes 98312 | tf_op jit(solution)/shard_map/ppermute | solution.py:39
  6.8 0.8 stack.76
  7.6 0.7 fusion
  8.3 2.0 %collective-permute-done.2 = f32[2,4,1024]{2,1,0:T(4,128)S(1)} collective-permute-done((f32[2,4,1024]{2,1,0:T(4,128)}, f32[2,4,1024]{2,1,0:T(4,128)S(1)}, u32[]{:S(2)}, u32[]{:S(2)}) %collective-permute-start.2) | collective-permute-done | bytes 32800 | tf_op jit(solution)/shard_map/ppermute | solution.py:39
  10.3 1.8 %collective-permute-done.1 = f32[2,4,1024]{2,1,0:T(4,128)S(1)} collective-permute-done((f32[2,4,1024]{2,1,0:T(4,128)}, f32[2,4,1024]{2,1,0:T(4,128)S(1)}, u32[]{:S(2)}, u32[]{:S(2)}) %collective-permute-start.1) | collective-permute-done | bytes 32800 | tf_op jit(solution)/shard_map/ppermute | solution.py:39
  12.1 2.5 %collective-permute-start.5 = (f32[4,8,1024]{2,1,0:T(8,128)S(1)}, f32[4,8,1024]{2,1,0:T(8,128)S(1)}, u32[]{:S(2)}, u32[]{:S(2)}) collective-permute-start(f32[4,8,1024]{2,1,0:T(8,128)S(1)} %constant_dynamic-update-slice_fusion.refs_0_), channel_id=1, source_target_pairs={{0,6},{2,4},{4,2},{6,0},{1,7},{3,5},{5,3},{7,1},{8,14},{10,12},{12... | collective-permute-start | bytes 393224 | tf_op jit(solution)/shard_map/ppermute | solution.py:41
  16.3 2.0 %work_list.1 = (s32[2,36]{1,0:T(2,128)}, s32[8,8]{1,0:T(8,128)}, s32[2]{0:T(128)}) custom-call(s32[8,8]{1,0:T(8,128)} %pattern_ref.1, s32[8]{0:T(128)} %counts_ref.1, s32[3]{0:T(128)} %pad_add_fusion.where_ref), custom_call_target="tpu_custom_call" | custom-call | tf_op jit(solution)/shard_map/work_list/pallas_call | solution.py:71
  18.3 1.1 %collective-permute-done.5.refs_3_ = f32[4,8,1024]{2,1,0:T(8,128)S(1)} collective-permute-done((f32[4,8,1024]{2,1,0:T(8,128)S(1)}, f32[4,8,1024]{2,1,0:T(8,128)S(1)}, u32[]{:S(2)}, u32[]{:S(2)}) %collective-permute-start.5) | collective-permute-done | bytes 131104 | tf_op jit(solution)/shard_map/ppermute | solution.py:41
  19.4 0.8 collective-permute-done.4.refs_2_
  20.3 1.6 %copy-done = f32[8,4,128,128]{3,2,1,0:T(8,128)S(1)} copy-done((f32[8,4,128,128]{3,2,1,0:T(8,128)S(1)}, f32[8,4,128,128]{3,2,1,0:T(8,128)}, u32[]{:S(2)}) %copy-start) | copy-done | bytes 2097176
  21.9 1.6 %copy-done.2 = f32[8,4,128,128]{3,2,1,0:T(8,128)S(1)} copy-done((f32[8,4,128,128]{3,2,1,0:T(8,128)S(1)}, f32[8,4,128,128]{3,2,1,0:T(8,128)}, u32[]{:S(2)}) %copy-start.2) | copy-done | bytes 2097176
  23.5 0.7 copy-done.4
  24.2 0.7 copy-done.8
  24.8 0.7 copy-done.9
  25.5 6.2 %step_0.1 = (f32[129,8,128]{2,1,0:T(8,128)S(1)}, f32[8,1024]{1,0:T(8,128)S(1)}, f32[8,1024]{1,0:T(8,128)S(1)}, f32[8,128]{1,0:T(8,128)S(1)}) custom-call(s32[2,36]{1,0:T(2,128)S(1)} %copy-done.8, s32[8,8]{1,0:T(8,128)S(1)} %copy-done.4, s32[2]{0:T(128)S(1)} %copy-done.9, f32[8,128]{1,0:T(8,128)S(1)} %broadcast_in_dim.4.turn_ref, ...), custom_call_target="tpu_custom_call" | custom-call | tf_op jit(solution)/shard_map/step_0/pallas_call | solution.py:255
  31.7 0.6 copy-done.5
  32.3 0.9 collective-permute-start.10
  33.3 3.4 %collective-permute-start.8 = (f32[8,1024]{1,0:T(8,128)S(1)}, f32[8,1024]{1,0:T(8,128)S(1)}, u32[]{:S(2)}, u32[]{:S(2)}) collective-permute-start(f32[8,1024]{1,0:T(8,128)S(1)} %get-tuple-element.21), channel_id=1, source_target_pairs={{0,8},{8,0},{16,24},{24,16},{1,9},{9,1},{17,25},{25,17},{2,10},{10... | collective-permute-start | bytes 98312 | tf_op jit(solution)/shard_map/ppermute | solution.py:39
  36.7 1.4 %collective-permute-done.10 = f32[8,1024]{1,0:T(8,128)S(1)} collective-permute-done((f32[8,1024]{1,0:T(8,128)S(1)}, f32[8,1024]{1,0:T(8,128)S(1)}, u32[]{:S(2)}, u32[]{:S(2)}) %collective-permute-start.10) | collective-permute-done | bytes 32800 | tf_op jit(solution)/shard_map/ppermute | solution.py:39
  38.1 0.7 collective-permute-done.9
  38.8 1.5 %collective-permute-start.13 = (f32[4,8,1024]{2,1,0:T(8,128)S(1)}, f32[4,8,1024]{2,1,0:T(8,128)S(1)}, u32[]{:S(2)}, u32[]{:S(2)}) collective-permute-start(f32[4,8,1024]{2,1,0:T(8,128)S(1)} %pad_maximum_fusion.refs_0_), channel_id=1, source_target_pairs={{0,6},{2,4},{4,2},{6,0},{1,7},{3,5},{5,3},{7,1},{8,14},{10,12},{12... | collective-permute-start | bytes 393224 | tf_op jit(solution)/shard_map/ppermute | solution.py:41
  40.4 1.2 %collective-permute-start.12 = (f32[4,8,1024]{2,1,0:T(8,128)S(1)}, f32[4,8,1024]{2,1,0:T(8,128)S(1)}, u32[]{:S(2)}, u32[]{:S(2)}) collective-permute-start(f32[4,8,1024]{2,1,0:T(8,128)S(1)} %pad_maximum_fusion.refs_0_), channel_id=1, source_target_pairs={{0,4},{2,6},{4,0},{6,2},{1,5},{3,7},{5,1},{7,3},{8,12},{10,14},{12... | collective-permute-start | bytes 393224 | tf_op jit(solution)/shard_map/ppermute | solution.py:41
  41.5 0.9 collective-permute-start.11
  42.4 2.5 %collective-permute-done.13.refs_3_ = f32[4,8,1024]{2,1,0:T(8,128)S(1)} collective-permute-done((f32[4,8,1024]{2,1,0:T(8,128)S(1)}, f32[4,8,1024]{2,1,0:T(8,128)S(1)}, u32[]{:S(2)}, u32[]{:S(2)}) %collective-permute-start.13) | collective-permute-done | bytes 131104 | tf_op jit(solution)/shard_map/ppermute | solution.py:41
  44.9 1.3 %collective-permute-done.12.refs_2_ = f32[4,8,1024]{2,1,0:T(8,128)S(1)} collective-permute-done((f32[4,8,1024]{2,1,0:T(8,128)S(1)}, f32[4,8,1024]{2,1,0:T(8,128)S(1)}, u32[]{:S(2)}, u32[]{:S(2)}) %collective-permute-start.12) | collective-permute-done | bytes 131104 | tf_op jit(solution)/shard_map/ppermute | solution.py:41
  46.5 5.9 %step_1.1 = (f32[129,8,128]{2,1,0:T(8,128)S(1)}, f32[8,1024]{1,0:T(8,128)S(1)}, f32[8,1024]{1,0:T(8,128)S(1)}, f32[8,128]{1,0:T(8,128)S(1)}) custom-call(s32[2,36]{1,0:T(2,128)S(1)} %copy-done.8, s32[8,8]{1,0:T(8,128)S(1)} %copy-done.4, s32[2]{0:T(128)S(1)} %copy-done.10, f32[8,128]{1,0:T(8,128)S(1)} %broadcast_in_dim.4.turn_ref, ...), custom_call_target="tpu_custom_call" | custom-call | tf_op jit(solution)/shard_map/step_1/pallas_call | solution.py:255
  52.4 0.8 collective-permute-start.16
  53.2 1.4 %collective-permute-start.15 = (f32[8,1024]{1,0:T(8,128)S(1)}, f32[8,1024]{1,0:T(8,128)S(1)}, u32[]{:S(2)}, u32[]{:S(2)}) collective-permute-start(f32[8,1024]{1,0:T(8,128)S(1)} %get-tuple-element.24), channel_id=1, source_target_pairs={{0,16},{8,24},{16,0},{24,8},{1,17},{9,25},{17,1},{25,9},{2,18},{10... | collective-permute-start | bytes 98312 | tf_op jit(solution)/shard_map/ppermute | solution.py:39
  54.6 2.2 %collective-permute-start.14 = (f32[8,1024]{1,0:T(8,128)S(1)}, f32[8,1024]{1,0:T(8,128)S(1)}, u32[]{:S(2)}, u32[]{:S(2)}) collective-permute-start(f32[8,1024]{1,0:T(8,128)S(1)} %get-tuple-element.24), channel_id=1, source_target_pairs={{0,8},{8,0},{16,24},{24,16},{1,9},{9,1},{17,25},{25,17},{2,10},{10... | collective-permute-start | bytes 98312 | tf_op jit(solution)/shard_map/ppermute | solution.py:39
  56.8 1.4 %collective-permute-done.16 = f32[8,1024]{1,0:T(8,128)S(1)} collective-permute-done((f32[8,1024]{1,0:T(8,128)S(1)}, f32[8,1024]{1,0:T(8,128)S(1)}, u32[]{:S(2)}, u32[]{:S(2)}) %collective-permute-start.16) | collective-permute-done | bytes 32800 | tf_op jit(solution)/shard_map/ppermute | solution.py:39
  58.8 1.7 %collective-permute-start.19 = (f32[4,8,1024]{2,1,0:T(8,128)S(1)}, f32[4,8,1024]{2,1,0:T(8,128)S(1)}, u32[]{:S(2)}, u32[]{:S(2)}) collective-permute-start(f32[4,8,1024]{2,1,0:T(8,128)S(1)} %pad_maximum_fusion.1.refs_0_), channel_id=1, source_target_pairs={{0,6},{2,4},{4,2},{6,0},{1,7},{3,5},{5,3},{7,1},{8,14},{10,12},{12... | collective-permute-start | bytes 393224 | tf_op jit(solution)/shard_map/ppermute | solution.py:41
  60.5 0.9 %collective-permute-start.18 = (f32[4,8,1024]{2,1,0:T(8,128)S(1)}, f32[4,8,1024]{2,1,0:T(8,128)S(1)}, u32[]{:S(2)}, u32[]{:S(2)}) collective-permute-start(f32[4,8,1024]{2,1,0:T(8,128)S(1)} %pad_maximum_fusion.1.refs_0_), channel_id=1, source_target_pairs={{0,4},{2,6},{4,0},{6,2},{1,5},{3,7},{5,1},{7,3},{8,12},{10,14},{12... | collective-permute-start | bytes 393224 | tf_op jit(solution)/shard_map/ppermute | solution.py:41
  61.5 0.9 %collective-permute-start.17 = (f32[4,8,1024]{2,1,0:T(8,128)S(1)}, f32[4,8,1024]{2,1,0:T(8,128)S(1)}, u32[]{:S(2)}, u32[]{:S(2)}) collective-permute-start(f32[4,8,1024]{2,1,0:T(8,128)S(1)} %pad_maximum_fusion.1.refs_0_), channel_id=1, source_target_pairs={{0,2},{2,0},{4,6},{6,4},{1,3},{3,1},{5,7},{7,5},{8,10},{10,8},{12,... | collective-permute-start | bytes 393224 | tf_op jit(solution)/shard_map/ppermute | solution.py:41
  62.4 2.4 %collective-permute-done.19.refs_3_ = f32[4,8,1024]{2,1,0:T(8,128)S(1)} collective-permute-done((f32[4,8,1024]{2,1,0:T(8,128)S(1)}, f32[4,8,1024]{2,1,0:T(8,128)S(1)}, u32[]{:S(2)}, u32[]{:S(2)}) %collective-permute-start.19) | collective-permute-done | bytes 131104 | tf_op jit(solution)/shard_map/ppermute | solution.py:41
  64.8 1.3 %collective-permute-done.18.refs_2_ = f32[4,8,1024]{2,1,0:T(8,128)S(1)} collective-permute-done((f32[4,8,1024]{2,1,0:T(8,128)S(1)}, f32[4,8,1024]{2,1,0:T(8,128)S(1)}, u32[]{:S(2)}, u32[]{:S(2)}) %collective-permute-start.18) | collective-permute-done | bytes 131104 | tf_op jit(solution)/shard_map/ppermute | solution.py:41
  66.5 6.6 %step_2.1 = (f32[129,8,128]{2,1,0:T(8,128)}, f32[8,1024]{1,0:T(8,128)S(1)}, f32[8,1024]{1,0:T(8,128)}, f32[8,128]{1,0:T(8,128)S(1)}) custom-call(s32[2,36]{1,0:T(2,128)S(1)} %copy-done.8, s32[8,8]{1,0:T(8,128)S(1)} %copy-done.4, s32[2]{0:T(128)S(1)} %copy-done.10, f32[8,128]{1,0:T(8,128)S(1)} %broadcast_in_dim.4.turn_ref, ...), custom_call_target="tpu_custom_call" | custom-call | tf_op jit(solution)/shard_map/step_2/pallas_call | solution.py:255
  73.1 0.6 copy-done.7
  73.7 0.9 collective-permute-start.22
  74.6 1.3 %collective-permute-start.21 = (f32[8,128]{1,0:T(8,128)S(1)}, f32[8,128]{1,0:T(8,128)S(1)}, u32[]{:S(2)}, u32[]{:S(2)}) collective-permute-start(f32[8,128]{1,0:T(8,128)S(1)} %get-tuple-element.26), channel_id=1, source_target_pairs={{0,16},{8,24},{16,0},{24,8},{1,17},{9,25},{17,1},{25,9},{2,18},{10... | collective-permute-start | bytes 12296 | tf_op jit(solution)/shard_map/ppermute | solution.py:39
  75.9 2.2 %collective-permute-start.20 = (f32[8,128]{1,0:T(8,128)S(1)}, f32[8,128]{1,0:T(8,128)S(1)}, u32[]{:S(2)}, u32[]{:S(2)}) collective-permute-start(f32[8,128]{1,0:T(8,128)S(1)} %get-tuple-element.26), channel_id=1, source_target_pairs={{0,8},{8,0},{16,24},{24,16},{1,9},{9,1},{17,25},{25,17},{2,10},{10... | collective-permute-start | bytes 12296 | tf_op jit(solution)/shard_map/ppermute | solution.py:39
  78.1 1.0 %collective-permute-done.22 = f32[8,128]{1,0:T(8,128)S(1)} collective-permute-done((f32[8,128]{1,0:T(8,128)S(1)}, f32[8,128]{1,0:T(8,128)S(1)}, u32[]{:S(2)}, u32[]{:S(2)}) %collective-permute-start.22) | collective-permute-done | bytes 4128 | tf_op jit(solution)/shard_map/ppermute | solution.py:39
  79.7 1.3 %collective-permute-start.25 = (f32[4,8,128]{2,1,0:T(8,128)S(1)}, f32[4,8,128]{2,1,0:T(8,128)S(1)}, u32[]{:S(2)}, u32[]{:S(2)}) collective-permute-start(f32[4,8,128]{2,1,0:T(8,128)S(1)} %pad_maximum_fusion.2.refs_0_), channel_id=1, source_target_pairs={{0,6},{2,4},{4,2},{6,0},{1,7},{3,5},{5,3},{7,1},{8,14},{10,12},{12... | collective-permute-start | bytes 49160 | tf_op jit(solution)/shard_map/ppermute | solution.py:41
  81.0 1.5 %collective-permute-start.24 = (f32[4,8,128]{2,1,0:T(8,128)S(1)}, f32[4,8,128]{2,1,0:T(8,128)S(1)}, u32[]{:S(2)}, u32[]{:S(2)}) collective-permute-start(f32[4,8,128]{2,1,0:T(8,128)S(1)} %pad_maximum_fusion.2.refs_0_), channel_id=1, source_target_pairs={{0,4},{2,6},{4,0},{6,2},{1,5},{3,7},{5,1},{7,3},{8,12},{10,14},{12... | collective-permute-start | bytes 49160 | tf_op jit(solution)/shard_map/ppermute | solution.py:41
  82.5 0.7 collective-permute-start.23
  83.2 1.1 %collective-permute-done.25.refs_3_ = f32[4,8,128]{2,1,0:T(8,128)S(1)} collective-permute-done((f32[4,8,128]{2,1,0:T(8,128)S(1)}, f32[4,8,128]{2,1,0:T(8,128)S(1)}, u32[]{:S(2)}, u32[]{:S(2)}) %collective-permute-start.25) | collective-permute-done | bytes 16416 | tf_op jit(solution)/shard_map/ppermute | solution.py:41
  84.8 1.5 %collective-permute-done.23.refs_1_ = f32[4,8,128]{2,1,0:T(8,128)S(1)} collective-permute-done((f32[4,8,128]{2,1,0:T(8,128)S(1)}, f32[4,8,128]{2,1,0:T(8,128)S(1)}, u32[]{:S(2)}, u32[]{:S(2)}) %collective-permute-start.23) | collective-permute-done | bytes 16416 | tf_op jit(solution)/shard_map/ppermute | solution.py:41
  86.8 2.4 %final.1 = (f32[2,4,1024]{2,1,0:T(4,128)}, f32[1,4]{1,0:T(1,128)}) custom-call(f32[4,8,128]{2,1,0:T(8,128)} %copy-done.11, f32[4,8,128]{2,1,0:T(8,128)} %copy-done.14, f32[4,8,128]{2,1,0:T(8,128)} %copy-done.13, f32[4,8,128]{2,1,0:T(8,128)} %copy-done.12, f32[8,1024]{1,0:T(8,128)} %copy-done.5, f32[8,1024]{1,0:T(8,128)} %copy-done.6, f32[8,1024]{1,0:T(8,128)} %copy-done.7), custom_call_target="tpu_custom_call" | custom-call | tf_op jit(solution)/shard_map/final/pallas_call | solution.py:339
  (55 shorter events, 5.5 us)
Async XLA Ops:
  0.6 19.6 %collective-permute-start.6 = (f32[8,4,128,128]{3,2,1,0:T(8,128)}, f32[8,4,128,128]{3,2,1,0:T(8,128)S(1)}, u32[]{:S(2)}, u32[]{:S(2)}) collective-permute-start(f32[8,4,128,128]{3,2,1,0:T(8,128)} %param.7), channel_id=1, source_target_pairs={{0,1},{1,0},{2,3},{3,2},{4,5},{5,4},{6,7},{7,6},{8,9},{9,8},{10,11... | collective-permute-start | bytes 6291464 | tf_op jit(solution)/shard_map/ppermute | solution.py:362
  1.1 19.1 %collective-permute-start.7 = (f32[8,4,128,128]{3,2,1,0:T(8,128)}, f32[8,4,128,128]{3,2,1,0:T(8,128)}, u32[]{:S(2)}, u32[]{:S(2)}) collective-permute-start(f32[8,4,128,128]{3,2,1,0:T(8,128)} %param.8), channel_id=1, source_target_pairs={{0,1},{1,0},{2,3},{3,2},{4,5},{5,4},{6,7},{7,6},{8,9},{9,8},{10,11... | collective-permute-start | bytes 6291464 | tf_op jit(solution)/shard_map/ppermute | solution.py:363
  1.2 7.1 %collective-permute-start = (f32[2,4,1024]{2,1,0:T(4,128)}, f32[2,4,1024]{2,1,0:T(4,128)S(1)}, u32[]{:S(2)}, u32[]{:S(2)}) collective-permute-start(f32[2,4,1024]{2,1,0:T(4,128)} %param.6), channel_id=1, source_target_pairs={{0,8},{8,0},{16,24},{24,16},{1,9},{9,1},{17,25},{25,17},{2,10},{10... | collective-permute-start | bytes 98312 | tf_op jit(solution)/shard_map/ppermute | solution.py:39
  4.2 6.1 %collective-permute-start.2 = (f32[2,4,1024]{2,1,0:T(4,128)}, f32[2,4,1024]{2,1,0:T(4,128)S(1)}, u32[]{:S(2)}, u32[]{:S(2)}) collective-permute-start(f32[2,4,1024]{2,1,0:T(4,128)} %param.6), channel_id=1, source_target_pairs={{0,24},{8,16},{16,8},{24,0},{1,25},{9,17},{17,9},{25,1},{2,26},{10... | collective-permute-start | bytes 98312 | tf_op jit(solution)/shard_map/ppermute | solution.py:39
  6.7 5.4 %collective-permute-start.1 = (f32[2,4,1024]{2,1,0:T(4,128)}, f32[2,4,1024]{2,1,0:T(4,128)S(1)}, u32[]{:S(2)}, u32[]{:S(2)}) collective-permute-start(f32[2,4,1024]{2,1,0:T(4,128)} %param.6), channel_id=1, source_target_pairs={{0,16},{8,24},{16,0},{24,8},{1,17},{9,25},{17,1},{25,9},{2,18},{10... | collective-permute-start | bytes 98312 | tf_op jit(solution)/shard_map/ppermute | solution.py:39
  12.1 7.3 %collective-permute-start.5 = (f32[4,8,1024]{2,1,0:T(8,128)S(1)}, f32[4,8,1024]{2,1,0:T(8,128)S(1)}, u32[]{:S(2)}, u32[]{:S(2)}) collective-permute-start(f32[4,8,1024]{2,1,0:T(8,128)S(1)} %constant_dynamic-update-slice_fusion.refs_0_), channel_id=1, source_target_pairs={{0,6},{2,4},{4,2},{6,0},{1,7},{3,5},{5,3},{7,1},{8,14},{10,12},{12... | collective-permute-start | bytes 393224 | tf_op jit(solution)/shard_map/ppermute | solution.py:41
  14.6 5.6 %collective-permute-start.4 = (f32[4,8,1024]{2,1,0:T(8,128)S(1)}, f32[4,8,1024]{2,1,0:T(8,128)S(1)}, u32[]{:S(2)}, u32[]{:S(2)}) collective-permute-start(f32[4,8,1024]{2,1,0:T(8,128)S(1)} %constant_dynamic-update-slice_fusion.refs_0_), channel_id=1, source_target_pairs={{0,4},{2,6},{4,0},{6,2},{1,5},{3,7},{5,1},{7,3},{8,12},{10,14},{12... | collective-permute-start | bytes 393224 | tf_op jit(solution)/shard_map/ppermute | solution.py:41
  15.2 5.1 %collective-permute-start.3 = (f32[4,8,1024]{2,1,0:T(8,128)S(1)}, f32[4,8,1024]{2,1,0:T(8,128)S(1)}, u32[]{:S(2)}, u32[]{:S(2)}) collective-permute-start(f32[4,8,1024]{2,1,0:T(8,128)S(1)} %constant_dynamic-update-slice_fusion.refs_0_), channel_id=1, source_target_pairs={{0,2},{2,0},{4,6},{6,4},{1,3},{3,1},{5,7},{7,5},{8,10},{10,8},{12,... | collective-permute-start | bytes 393224 | tf_op jit(solution)/shard_map/ppermute | solution.py:41
  20.3 1.6 %copy-start = (f32[8,4,128,128]{3,2,1,0:T(8,128)S(1)}, f32[8,4,128,128]{3,2,1,0:T(8,128)}, u32[]{:S(2)}) copy-start(f32[8,4,128,128]{3,2,1,0:T(8,128)} %param.7) | copy-start | bytes 6291460
  21.9 1.6 %copy-start.2 = (f32[8,4,128,128]{3,2,1,0:T(8,128)S(1)}, f32[8,4,128,128]{3,2,1,0:T(8,128)}, u32[]{:S(2)}) copy-start(f32[8,4,128,128]{3,2,1,0:T(8,128)} %param.8) | copy-start | bytes 6291460
  23.5 0.7 copy-start.4
  24.2 0.7 copy-start.8
  24.8 0.7 copy-start.9
  25.5 21.0 %copy-start.1 = (f32[8,4,128,128]{3,2,1,0:T(8,128)S(1)}, f32[8,4,128,128]{3,2,1,0:T(8,128)}, u32[]{:S(2)}) copy-start(f32[8,4,128,128]{3,2,1,0:T(8,128)} %param.7) | copy-start | bytes 6291460
  25.5 21.0 %copy-start.3 = (f32[8,4,128,128]{3,2,1,0:T(8,128)S(1)}, f32[8,4,128,128]{3,2,1,0:T(8,128)}, u32[]{:S(2)}) copy-start(f32[8,4,128,128]{3,2,1,0:T(8,128)} %param.8) | copy-start | bytes 6291460
  25.5 21.0 %copy-start.10 = (s32[2]{0:T(128)S(1)}, s32[2]{0:T(128)}, u32[]{:S(2)}) copy-start(s32[2]{0:T(128)} %get-tuple-element.19.used_ref) | copy-start | bytes 28
  31.7 0.6 copy-start.5
  32.3 5.8 %collective-permute-start.10 = (f32[8,1024]{1,0:T(8,128)S(1)}, f32[8,1024]{1,0:T(8,128)S(1)}, u32[]{:S(2)}, u32[]{:S(2)}) collective-permute-start(f32[8,1024]{1,0:T(8,128)S(1)} %get-tuple-element.21), channel_id=1, source_target_pairs={{0,24},{8,16},{16,8},{24,0},{1,25},{9,17},{17,9},{25,1},{2,26},{10... | collective-permute-start | bytes 98312 | tf_op jit(solution)/shard_map/ppermute | solution.py:39
  33.2 5.6 %collective-permute-start.9 = (f32[8,1024]{1,0:T(8,128)S(1)}, f32[8,1024]{1,0:T(8,128)S(1)}, u32[]{:S(2)}, u32[]{:S(2)}) collective-permute-start(f32[8,1024]{1,0:T(8,128)S(1)} %get-tuple-element.21), channel_id=1, source_target_pairs={{0,16},{8,24},{16,0},{24,8},{1,17},{9,25},{17,1},{25,9},{2,18},{10... | collective-permute-start | bytes 98312 | tf_op jit(solution)/shard_map/ppermute | solution.py:39
  33.3 5.5 %collective-permute-start.8 = (f32[8,1024]{1,0:T(8,128)S(1)}, f32[8,1024]{1,0:T(8,128)S(1)}, u32[]{:S(2)}, u32[]{:S(2)}) collective-permute-start(f32[8,1024]{1,0:T(8,128)S(1)} %get-tuple-element.21), channel_id=1, source_target_pairs={{0,8},{8,0},{16,24},{24,16},{1,9},{9,1},{17,25},{25,17},{2,10},{10... | collective-permute-start | bytes 98312 | tf_op jit(solution)/shard_map/ppermute | solution.py:39
  38.8 6.0 %collective-permute-start.13 = (f32[4,8,1024]{2,1,0:T(8,128)S(1)}, f32[4,8,1024]{2,1,0:T(8,128)S(1)}, u32[]{:S(2)}, u32[]{:S(2)}) collective-permute-start(f32[4,8,1024]{2,1,0:T(8,128)S(1)} %pad_maximum_fusion.refs_0_), channel_id=1, source_target_pairs={{0,6},{2,4},{4,2},{6,0},{1,7},{3,5},{5,3},{7,1},{8,14},{10,12},{12... | collective-permute-start | bytes 393224 | tf_op jit(solution)/shard_map/ppermute | solution.py:41
  40.4 5.8 %collective-permute-start.12 = (f32[4,8,1024]{2,1,0:T(8,128)S(1)}, f32[4,8,1024]{2,1,0:T(8,128)S(1)}, u32[]{:S(2)}, u32[]{:S(2)}) collective-permute-start(f32[4,8,1024]{2,1,0:T(8,128)S(1)} %pad_maximum_fusion.refs_0_), channel_id=1, source_target_pairs={{0,4},{2,6},{4,0},{6,2},{1,5},{3,7},{5,1},{7,3},{8,12},{10,14},{12... | collective-permute-start | bytes 393224 | tf_op jit(solution)/shard_map/ppermute | solution.py:41
  41.5 5.0 %collective-permute-start.11 = (f32[4,8,1024]{2,1,0:T(8,128)S(1)}, f32[4,8,1024]{2,1,0:T(8,128)S(1)}, u32[]{:S(2)}, u32[]{:S(2)}) collective-permute-start(f32[4,8,1024]{2,1,0:T(8,128)S(1)} %pad_maximum_fusion.refs_0_), channel_id=1, source_target_pairs={{0,2},{2,0},{4,6},{6,4},{1,3},{3,1},{5,7},{7,5},{8,10},{10,8},{12,... | collective-permute-start | bytes 393224 | tf_op jit(solution)/shard_map/ppermute | solution.py:41
  52.4 20.7 %copy-start.6 = (f32[8,1024]{1,0:T(8,128)}, f32[8,1024]{1,0:T(8,128)S(1)}, u32[]{:S(2)}) copy-start(f32[8,1024]{1,0:T(8,128)S(1)} %get-tuple-element.28.refs_5_) | copy-start | bytes 98308
  52.4 5.9 %collective-permute-start.16 = (f32[8,1024]{1,0:T(8,128)S(1)}, f32[8,1024]{1,0:T(8,128)S(1)}, u32[]{:S(2)}, u32[]{:S(2)}) collective-permute-start(f32[8,1024]{1,0:T(8,128)S(1)} %get-tuple-element.24), channel_id=1, source_target_pairs={{0,24},{8,16},{16,8},{24,0},{1,25},{9,17},{17,9},{25,1},{2,26},{10... | collective-permute-start | bytes 98312 | tf_op jit(solution)/shard_map/ppermute | solution.py:39
  53.2 5.6 %collective-permute-start.15 = (f32[8,1024]{1,0:T(8,128)S(1)}, f32[8,1024]{1,0:T(8,128)S(1)}, u32[]{:S(2)}, u32[]{:S(2)}) collective-permute-start(f32[8,1024]{1,0:T(8,128)S(1)} %get-tuple-element.24), channel_id=1, source_target_pairs={{0,16},{8,24},{16,0},{24,8},{1,17},{9,25},{17,1},{25,9},{2,18},{10... | collective-permute-start | bytes 98312 | tf_op jit(solution)/shard_map/ppermute | solution.py:39
  54.6 4.2 %collective-permute-start.14 = (f32[8,1024]{1,0:T(8,128)S(1)}, f32[8,1024]{1,0:T(8,128)S(1)}, u32[]{:S(2)}, u32[]{:S(2)}) collective-permute-start(f32[8,1024]{1,0:T(8,128)S(1)} %get-tuple-element.24), channel_id=1, source_target_pairs={{0,8},{8,0},{16,24},{24,16},{1,9},{9,1},{17,25},{25,17},{2,10},{10... | collective-permute-start | bytes 98312 | tf_op jit(solution)/shard_map/ppermute | solution.py:39
  58.8 6.0 %collective-permute-start.19 = (f32[4,8,1024]{2,1,0:T(8,128)S(1)}, f32[4,8,1024]{2,1,0:T(8,128)S(1)}, u32[]{:S(2)}, u32[]{:S(2)}) collective-permute-start(f32[4,8,1024]{2,1,0:T(8,128)S(1)} %pad_maximum_fusion.1.refs_0_), channel_id=1, source_target_pairs={{0,6},{2,4},{4,2},{6,0},{1,7},{3,5},{5,3},{7,1},{8,14},{10,12},{12... | collective-permute-start | bytes 393224 | tf_op jit(solution)/shard_map/ppermute | solution.py:41
  60.5 5.6 %collective-permute-start.18 = (f32[4,8,1024]{2,1,0:T(8,128)S(1)}, f32[4,8,1024]{2,1,0:T(8,128)S(1)}, u32[]{:S(2)}, u32[]{:S(2)}) collective-permute-start(f32[4,8,1024]{2,1,0:T(8,128)S(1)} %pad_maximum_fusion.1.refs_0_), channel_id=1, source_target_pairs={{0,4},{2,6},{4,0},{6,2},{1,5},{3,7},{5,1},{7,3},{8,12},{10,14},{12... | collective-permute-start | bytes 393224 | tf_op jit(solution)/shard_map/ppermute | solution.py:41
  61.5 5.0 %collective-permute-start.17 = (f32[4,8,1024]{2,1,0:T(8,128)S(1)}, f32[4,8,1024]{2,1,0:T(8,128)S(1)}, u32[]{:S(2)}, u32[]{:S(2)}) collective-permute-start(f32[4,8,1024]{2,1,0:T(8,128)S(1)} %pad_maximum_fusion.1.refs_0_), channel_id=1, source_target_pairs={{0,2},{2,0},{4,6},{6,4},{1,3},{3,1},{5,7},{7,5},{8,10},{10,8},{12,... | collective-permute-start | bytes 393224 | tf_op jit(solution)/shard_map/ppermute | solution.py:41
  73.1 0.6 copy-start.7
  73.7 5.4 %collective-permute-start.22 = (f32[8,128]{1,0:T(8,128)S(1)}, f32[8,128]{1,0:T(8,128)S(1)}, u32[]{:S(2)}, u32[]{:S(2)}) collective-permute-start(f32[8,128]{1,0:T(8,128)S(1)} %get-tuple-element.26), channel_id=1, source_target_pairs={{0,24},{8,16},{16,8},{24,0},{1,25},{9,17},{17,9},{25,1},{2,26},{10... | collective-permute-start | bytes 12296 | tf_op jit(solution)/shard_map/ppermute | solution.py:39
  74.6 4.6 %collective-permute-start.21 = (f32[8,128]{1,0:T(8,128)S(1)}, f32[8,128]{1,0:T(8,128)S(1)}, u32[]{:S(2)}, u32[]{:S(2)}) collective-permute-start(f32[8,128]{1,0:T(8,128)S(1)} %get-tuple-element.26), channel_id=1, source_target_pairs={{0,16},{8,24},{16,0},{24,8},{1,17},{9,25},{17,1},{25,9},{2,18},{10... | collective-permute-start | bytes 12296 | tf_op jit(solution)/shard_map/ppermute | solution.py:39
  75.9 3.8 %collective-permute-start.20 = (f32[8,128]{1,0:T(8,128)S(1)}, f32[8,128]{1,0:T(8,128)S(1)}, u32[]{:S(2)}, u32[]{:S(2)}) collective-permute-start(f32[8,128]{1,0:T(8,128)S(1)} %get-tuple-element.26), channel_id=1, source_target_pairs={{0,8},{8,0},{16,24},{24,16},{1,9},{9,1},{17,25},{25,17},{2,10},{10... | collective-permute-start | bytes 12296 | tf_op jit(solution)/shard_map/ppermute | solution.py:39
  79.7 6.5 %copy-start.11 = (f32[4,8,128]{2,1,0:T(8,128)}, f32[4,8,128]{2,1,0:T(8,128)S(1)}, u32[]{:S(2)}) copy-start(f32[4,8,128]{2,1,0:T(8,128)S(1)} %pad_maximum_fusion.2.refs_0_) | copy-start | bytes 49156
  79.7 4.6 %collective-permute-start.25 = (f32[4,8,128]{2,1,0:T(8,128)S(1)}, f32[4,8,128]{2,1,0:T(8,128)S(1)}, u32[]{:S(2)}, u32[]{:S(2)}) collective-permute-start(f32[4,8,128]{2,1,0:T(8,128)S(1)} %pad_maximum_fusion.2.refs_0_), channel_id=1, source_target_pairs={{0,6},{2,4},{4,2},{6,0},{1,7},{3,5},{5,3},{7,1},{8,14},{10,12},{12... | collective-permute-start | bytes 49160 | tf_op jit(solution)/shard_map/ppermute | solution.py:41
  81.0 3.7 %collective-permute-start.24 = (f32[4,8,128]{2,1,0:T(8,128)S(1)}, f32[4,8,128]{2,1,0:T(8,128)S(1)}, u32[]{:S(2)}, u32[]{:S(2)}) collective-permute-start(f32[4,8,128]{2,1,0:T(8,128)S(1)} %pad_maximum_fusion.2.refs_0_), channel_id=1, source_target_pairs={{0,4},{2,6},{4,0},{6,2},{1,5},{3,7},{5,1},{7,3},{8,12},{10,14},{12... | collective-permute-start | bytes 49160 | tf_op jit(solution)/shard_map/ppermute | solution.py:41
  82.5 3.7 %collective-permute-start.23 = (f32[4,8,128]{2,1,0:T(8,128)S(1)}, f32[4,8,128]{2,1,0:T(8,128)S(1)}, u32[]{:S(2)}, u32[]{:S(2)}) collective-permute-start(f32[4,8,128]{2,1,0:T(8,128)S(1)} %pad_maximum_fusion.2.refs_0_), channel_id=1, source_target_pairs={{0,2},{2,0},{4,6},{6,4},{1,3},{3,1},{5,7},{7,5},{8,10},{10,8},{12,... | collective-permute-start | bytes 49160 | tf_op jit(solution)/shard_map/ppermute | solution.py:41
  84.3 1.9 %copy-start.12 = (f32[4,8,128]{2,1,0:T(8,128)}, f32[4,8,128]{2,1,0:T(8,128)S(1)}, u32[]{:S(2)}) copy-start(f32[4,8,128]{2,1,0:T(8,128)S(1)} %collective-permute-done.25.refs_3_) | copy-start | bytes 49156
  84.7 1.5 %copy-start.13 = (f32[4,8,128]{2,1,0:T(8,128)}, f32[4,8,128]{2,1,0:T(8,128)S(1)}, u32[]{:S(2)}) copy-start(f32[4,8,128]{2,1,0:T(8,128)S(1)} %collective-permute-done.24.refs_2_) | copy-start | bytes 49156
  86.2 0.6 copy-start.14

commit v5 on v4

--- a/solution.py
+++ b/solution.py
@@ -12,9 +12,9 @@
 ITERS = 3
 LANES = 128
 GROUP = 4
-SHIFT = 256
+FULL_GROUP = 8
 SHARES = 16
-VMEM_LIMIT = 20 * 1024 * 1024
+VMEM_LIMIT = 16 * 1024 * 1024
 
 
 def split_nodes(nodes):
@@ -41,44 +41,33 @@
     return [whole_line] + [lax.ppermute(whole_line, "place", perm) for perm in partner_steps(plane)]
 
 
-def list_kernel(line, plane, freqs, pattern_ref, counts_ref, where_ref, list_ref, places_ref, used_ref):
-    row_blocks, slots = pattern_ref.shape
-    own_slots = slots // freqs
-    for d in range(freqs):
-        first = lax.rem(where_ref[2] + (freqs - d), freqs) * own_slots
-        filled = jnp.int32(0)
-        for b in range(row_blocks):
-            for kk in range(own_slots):
-                stored = b * own_slots + kk
-                list_ref[d, filled] = (first + kk) * SHIFT + (b * SHIFT * SHIFT + stored)
-                filled += (first + kk < counts_ref[b]).astype(jnp.int32)
-        for u in range(GROUP):
-            list_ref[d, filled + u] = row_blocks * SHIFT * SHIFT
-        used_ref[d] = lax.div(filled + (GROUP - 1), GROUP)
-    for b in range(row_blocks):
-        for k in range(slots):
-            p = pattern_ref[b, k]
-            owner = lax.div(p, row_blocks)
-            far = distance(where_ref[0], lax.div(owner, plane), line)
-            place = distance(where_ref[1], lax.rem(owner, plane), plane) * line + far
-            place = place * row_blocks + lax.rem(p, row_blocks)
-            places_ref[k, b] = jnp.where(k < counts_ref[b], place, line * plane * row_blocks)
-
-
 def work_list(pattern, counts, where, line, plane, freqs):
     row_blocks, slots = pattern.shape
-    smem = pl.BlockSpec(memory_space=pltpu.SMEM)
-    return pl.pallas_call(
-        functools.partial(list_kernel, line, plane, freqs),
-        in_specs=[smem] * 3,
-        out_specs=[smem] * 3,
-        out_shape=[
-            jax.ShapeDtypeStruct((freqs, row_blocks * slots // freqs + GROUP), jnp.int32),
-            jax.ShapeDtypeStruct((slots, row_blocks), jnp.int32),
-            jax.ShapeDtypeStruct((freqs,), jnp.int32),
-        ],
-        name="work_list",
-    )(pattern, counts, where)
+    own_slots = slots // freqs
+    owner = lax.div(pattern, row_blocks)
+    far = distance(where[0], lax.div(owner, plane), line)
+    place = distance(where[1], lax.rem(owner, plane), plane) * line + far
+    place = place * row_blocks + lax.rem(pattern, row_blocks)
+    slot = jnp.arange(slots)
+    places = jnp.where(slot[None, :] < counts[:, None], place, line * plane * row_blocks).T
+    b = jnp.arange(row_blocks)
+    order = jnp.arange(row_blocks * slots)
+    tables = []
+    for d in list(range(freqs)) + [None]:
+        first = 0 if d is None else lax.rem(where[2] + (freqs - d), freqs) * own_slots
+        group = FULL_GROUP if d is None else GROUP
+        here = counts if d is None else jnp.clip(counts - first, 0, own_slots)
+        start = jnp.sum(jnp.where(b[None, :] < b[:, None], here[None, :], 0), axis=1)
+        inside = order[:, None] - start[None, :]
+        hit = (inside >= 0) & (inside < here[None, :])
+        layer = first + jnp.sum(jnp.where(hit, inside, 0), axis=1)
+        block = jnp.sum(jnp.where(hit, b[None, :], 0), axis=1)
+        away = lax.rem(where[2] - lax.div(layer, own_slots) + freqs, freqs)
+        stored = (away * row_blocks + block) * own_slots + lax.rem(layer, own_slots)
+        used = jnp.sum(here)
+        block = jnp.where(order < used, block, row_blocks)
+        tables += [layer, block, stored, jnp.full(order.shape, lax.div(used + (group - 1), group))]
+    return jnp.stack(tables).astype(jnp.int32), places.astype(jnp.int32)
 
 
 def lane_sum(x):
@@ -100,23 +89,20 @@
     return high, (x - high.astype(jnp.float32)).astype(jnp.bfloat16)
 
 
-def step_kernel(step, plane, line, freqs, list_ref, places_ref, used_ref, turn_ref, info_in_ref, *refs):
+def step_kernel(step, plane, line, freqs, items_ref, places_ref, turn_ref, info_in_ref, *refs):
     lines, refs = refs[:plane], refs[plane:]
     prev, refs = refs[:step], refs[step:]
-    g_refs, c_refs = list(refs[:freqs]), list(refs[freqs : 2 * freqs])
-    z_ref, own_ref, local_ref, info_ref, layer_ref, mask_ref, acc_ref = refs[2 * freqs : 2 * freqs + 7]
+    slots, row_blocks = places_ref.shape
     nodes = plane * line
-    parts, rows = own_ref.shape
-    slots, row_blocks = places_ref.shape
+    if step == 0:
+        g_refs, c_refs = refs[:freqs], refs[freqs : 2 * freqs]
+        z_ref, local_ref, info_ref, split_ref, layer_ref, mask_ref, acc_ref = refs[2 * freqs :]
+    elif step < ITERS - 1:
+        split_ref, z_ref, local_ref, info_ref, layer_ref, mask_ref, acc_ref = refs
+    else:
+        split_ref, own_ref, info_ref, layer_ref, mask_ref, acc_ref, z_ref, local_ref = refs
+    parts, rows = local_ref.shape
     size = rows // row_blocks
-
-    arrivals = []
-    if step == 0:
-        kept, sems = refs[2 * freqs + 7 :]
-        for m, held in enumerate((g_refs, c_refs)):
-            arrivals.append(pltpu.make_async_copy(held[0], kept.at[m], sems.at[m]))
-            arrivals[-1].start()
-            held[0] = kept.at[m]
 
     lane = lax.broadcasted_iota(jnp.int32, (size, LANES), 1)
     for b in range(row_blocks):
@@ -182,30 +168,40 @@
             return carry
 
     blocks(normal, 0)
-    own_ref[...] = jnp.concatenate([z_ref[b] for b in range(row_blocks)], axis=1)
 
     for k in range(slots):
         chosen = jnp.concatenate([z_ref[places_ref[k, b]] for b in range(row_blocks)], axis=0)
         high = chosen.astype(jnp.bfloat16).astype(jnp.float32)
         layer_ref[k] = jnp.transpose(jnp.concatenate([high, chosen - high], axis=0)).astype(jnp.bfloat16)
 
-    for d in reversed(range(freqs)):
-        if d == 0:
-            for arrival in arrivals:
-                arrival.wait()
-
-        @pl.loop(0, used_ref[d])
+    def product(table, t, left):
+        right = layer_ref[items_ref[table, t]] * mask_ref[items_ref[table + 1, t]]
+        right = jnp.concatenate([right, right], axis=0)
+        return jnp.dot(left, right, preferred_element_type=jnp.float32)
+
+    if step == 0:
+        for d in range(freqs):
+
+            @pl.loop(0, items_ref[4 * d + 3, 0])
+            def _(group):
+                total = acc_ref[...]
+                for u in range(GROUP):
+                    t = group * GROUP + u
+                    stored = items_ref[4 * d + 2, t]
+                    here = stored - d * g_refs[d].shape[0]
+                    high, low = split(jnp.concatenate([g_refs[d][here], c_refs[d][here]], axis=0))
+                    left = jnp.concatenate([high, low], axis=1)
+                    split_ref[stored] = left
+                    total = total + product(4 * d, t, left)
+                acc_ref[...] = total
+    else:
+
+        @pl.loop(0, items_ref[4 * freqs + 3, 0])
         def _(group):
             total = acc_ref[...]
-            for u in range(GROUP):
-                item = list_ref[d, group * GROUP + u]
-                stored = lax.rem(item, SHIFT)
-                layer = lax.rem(lax.div(item, SHIFT), SHIFT)
-                right = layer_ref[layer] * mask_ref[lax.div(item, SHIFT * SHIFT)]
-                right = jnp.concatenate([right, right], axis=0)
-                high, low = split(jnp.concatenate([g_refs[d][stored], c_refs[d][stored]], axis=0))
-                left = jnp.concatenate([high, low], axis=1)
-                total = total + jnp.dot(left, right, preferred_element_type=jnp.float32)
+            for u in range(FULL_GROUP):
+                t = group * FULL_GROUP + u
+                total = total + product(4 * freqs, t, split_ref[items_ref[4 * freqs + 2, t]])
             acc_ref[...] = total
 
     half = row_blocks * parts
@@ -219,7 +215,8 @@
 
     if step == ITERS - 1:
         w = local_ref[...]
-        zs = [jnp.concatenate([p[b] for b in range(row_blocks)], axis=1) for p in prev] + [own_ref[...]]
+        zs = [jnp.concatenate([p[b] for b in range(row_blocks)], axis=1) for p in (*prev, z_ref)]
+        own_ref[...] = zs[-1]
         values = [lane_sum(z * w) for z in zs]
         gram = [[lane_sum(zs[i] * zs[j]) for j in range(i + 1)] for i in range(ITERS)]
         shares = []
@@ -235,37 +232,35 @@
     info_ref[...] = info
 
 
-def run_step(step, lists, turn, info, lines, prev, g_parts, c_parts):
-    plane, freqs = len(lines), len(g_parts)
+def run_step(step, lists, turn, info, lines, prev, blocks, freqs):
+    plane = len(lines)
     line, parts, rows = lines[0].shape
     slots, row_blocks = lists[1].shape
-    stored, size, _ = g_parts[0].shape
+    size = rows // row_blocks
     vmem = pl.BlockSpec(memory_space=pltpu.VMEM)
-    in_specs = [pl.BlockSpec(memory_space=pltpu.SMEM)] * 3 + [vmem] * (2 + plane + step + 2 * freqs)
+    in_specs = [pl.BlockSpec(memory_space=pltpu.SMEM)] * 2 + [vmem] * (2 + plane + step + len(blocks))
+    z = (plane * line * row_blocks + 1, parts, size)
+    tile = jax.ShapeDtypeStruct((parts, LANES), jnp.float32)
+    own = jax.ShapeDtypeStruct((parts, rows), jnp.float32)
+    out_shape = [own, tile] if step == ITERS - 1 else [jax.ShapeDtypeStruct(z, jnp.float32), own, tile]
     scratch_shapes = [
         pltpu.VMEM((slots, size, LANES), jnp.bfloat16),
         pltpu.VMEM((row_blocks + 1, size, LANES), jnp.bfloat16),
         pltpu.VMEM((2 * size, LANES), jnp.float32),
     ]
     if step == 0:
-        in_specs[5 + plane] = in_specs[5 + plane + freqs] = pl.BlockSpec(memory_space=pltpu.HBM)
-        scratch_shapes += [pltpu.VMEM((2, stored, size, size), jnp.float32), pltpu.SemaphoreType.DMA((2,))]
-    tile = jax.ShapeDtypeStruct((parts, LANES), jnp.float32)
-    own = jax.ShapeDtypeStruct((parts, rows), jnp.float32)
+        out_shape.append(jax.ShapeDtypeStruct((row_blocks * slots, 2 * size, 2 * size), jnp.bfloat16))
+    if step == ITERS - 1:
+        scratch_shapes += [pltpu.VMEM(z, jnp.float32), pltpu.VMEM((parts, rows), jnp.float32)]
     return pl.pallas_call(
         functools.partial(step_kernel, step, plane, line, freqs),
         in_specs=in_specs,
-        out_specs=[vmem] * 4,
-        out_shape=[
-            jax.ShapeDtypeStruct((plane * line * row_blocks + 1, parts, size), jnp.float32),
-            own,
-            own,
-            tile,
-        ],
+        out_specs=[vmem] * len(out_shape),
+        out_shape=out_shape,
         scratch_shapes=scratch_shapes,
         compiler_params=pltpu.CompilerParams(vmem_limit_bytes=VMEM_LIMIT),
         name=f"step_{step}",
-    )(*lists, turn, info, *lines, *prev, *g_parts, *c_parts)
+    )(*lists, turn, info, *lines, *prev, *blocks)
 
 
 def final_kernel(plane, *refs):
@@ -328,13 +323,17 @@
     columns = jnp.transpose(
         jnp.concatenate([y for y in coef_y] + [jnp.zeros((LANES - 8 * ITERS, LANES), jnp.float32)], axis=0)
     )[:parts]
-    x = sum(columns[:, 8 * m : 8 * m + 1] * krylov[m][...] for m in range(ITERS))
-    out_ref[0] = x[: parts // 2]
-    out_ref[1] = x[parts // 2 :]
+    size = krylov[0].shape[-1]
+    wide = [jnp.broadcast_to(columns[:, 8 * m : 8 * m + 1], (parts, size)) for m in range(ITERS)]
+    for b in range(out_ref.shape[-1] // size):
+        at = slice(b * size, (b + 1) * size)
+        x = wide[-1] * krylov[-1][:, at] + sum(y * z[b] for y, z in zip(wide[:-1], krylov[:-1]))
+        out_ref[0, :, at] = x[: parts // 2]
+        out_ref[1, :, at] = x[parts // 2 :]
 
 
 def run_final(tiles, krylov):
-    parts, rows = krylov[0].shape
+    parts, rows = krylov[-1].shape
     vmem = pl.BlockSpec(memory_space=pltpu.VMEM)
     return pl.pallas_call(
         functools.partial(final_kernel, len(tiles)),
@@ -356,24 +355,35 @@
         parts = 2 * freq_count
         where = jnp.stack([lax.axis_index(name) for name in ("line", "place", "freq")]).astype(jnp.int32)
         stored = (row_blocks * own_slots, size, size)
+        slot = lax.axis_index("freq") * own_slots + jnp.arange(own_slots)
+        in_use = (slot[None, :] < counts[:, None])[:, :, None, None]
         g_parts, c_parts = [], []
         for d in range(freqs):
             perm = [(i, (i + d) % freqs) for i in range(freqs)]
-            g_part = lax.ppermute(g_blocks, "freq", perm) if d else g_blocks
-            c_part = lax.ppermute(c_blocks, "freq", perm) if d else c_blocks
+            g_part = lax.ppermute(g_blocks, "freq", perm) if d else jnp.where(in_use, g_blocks, 0.0)
+            c_part = lax.ppermute(c_blocks, "freq", perm) if d else jnp.where(in_use, c_blocks, 0.0)
             g_parts.append(g_part.reshape(stored))
             c_parts.append(c_part.reshape(stored))
         turn = jnp.broadcast_to(jnp.concatenate([-angular, angular])[:, None], (parts, LANES))
         info = jnp.zeros((parts, LANES), jnp.float32)
-        krylov, own = [], []
         lists = work_list(pattern, counts, where, line, plane, freqs)
+        krylov = []
         rows = excitation
+        blocks = g_parts + c_parts
         for step in range(ITERS):
             lines = gather_rows(rows, line, plane)
-            z, mine, rows, info = run_step(step, lists, turn, info, lines, krylov, g_parts, c_parts)
-            krylov.append(z)
-            own.append(mine)
-        answer, residual = run_final(gather_rows(info, line, plane), own)
+            result = run_step(step, lists, turn, info, lines, krylov, blocks, freqs)
+            if step == ITERS - 1:
+                rows, info = result
+                krylov.append(rows)
+            elif step == 0:
+                z, rows, info, tiles = result
+                blocks = [tiles]
+                krylov.append(z)
+            else:
+                z, rows, info = result
+                krylov.append(z)
+        answer, residual = run_final(gather_rows(info, line, plane), krylov)
         return answer, residual.reshape(freq_count)
 
     return shards

time: 90.3 us -> 91.2 us (level)
  other arithmetic: 1.36 us -> 10.2 us
  Pallas kernels: 23.1 us -> 17.3 us
  local copies, waits for them, and re-layouts: 7.95 us -> 4.52 us
  between operations: 0.76 us -> 2.8 us
    pallas_call x3, Pallas kernels: 18.7 us -> 14.5 us  [run_step(): pl.pallas_call(functools.partial(step_kernel, step, plane, line, freqs),...]
    select_n x0 -> x1, other arithmetic: none -> 4.15 us  [shards(): jnp.where(in_use, c_blocks, 0.0)]
    unnamed x33 -> x22, local copies, waits for them, and re-layouts: 7.02 us -> 3.57 us
    reduce_sum x0 -> x6, other arithmetic: none -> 2.49 us  [the longest x1 1.4 us: work_list(): used = jnp.sum(here)]
    pallas_call x1 -> x0, Pallas kernels: 1.97 us -> none  [work_list(): pl.pallas_call(functools.partial(list_kernel, line, plane, freqs), in_spe...]
    add x0 -> x3, other arithmetic: none -> 1.96 us  [the longest x2 1.96 us: work_list(): stored = (away * row_blocks + block) * own_slots + lax.rem(layer, own_slots)]
    ppermute x12, waiting for transfers between devices: 9.46 us -> 8.03 us  [gather_rows(): lax.ppermute(rows, 'line', perm)]
  transfers between devices with their start and end apart: 26 -> 26, of which waited for: 19 -> 18; matrix products, arithmetic and copies ran while one was open for 2% -> 13% of each run, Pallas kernels for 2% -> 0%
where the time goes in v5:
time: 91.2 us; the launch traced here: 90.3 us
  starting transfers between devices  33.6 us (37%)
  waiting for transfers between devices  21.7 us (24%)
  Pallas kernels  17.3 us (19%)
  other arithmetic  10.2 us (11%)
  local copies, waits for them, and re-layouts  4.52 us (5%)
  between operations  2.8 us (3%)
    ppermute x12, starting transfers between devices, gather_rows(): lax.ppermute(rows, 'line', perm)  19 us
    pallas_call x3, Pallas kernels, run_step(): pl.pallas_call(functools.partial(step_kernel, step, plane, line, freqs),...  14.5 us
    ppermute x12, starting transfers between devices, gather_rows(): lax.ppermute(whole_line, 'place', perm)  14.1 us
    ppermute x12, waiting for transfers between devices, gather_rows(): lax.ppermute(whole_line, 'place', perm)  13.7 us
    ppermute x12, waiting for transfers between devices, gather_rows(): lax.ppermute(rows, 'line', perm)  8.03 us
    select_n x1, other arithmetic, shards(): jnp.where(in_use, c_blocks, 0.0)  4.15 us
    unnamed x22, local copies, waits for them, and re-layouts  3.57 us
    pallas_call x1, Pallas kernels, run_final(): pl.pallas_call(functools.partial(final_kernel, len(tiles)), in_specs=[vme...  2.84 us
  transfers between devices with their start and end apart: 26, of which 18 were waited for; matrix products, arithmetic and copies ran while one was open for 13% of the time, Pallas kernels for 0%

profile of v5, /device:TPU:0, one launch (start us, length us, event | category | flops | bytes accessed | tf_op | source)
XLA Modules:
  0.0 90.3 jit_solution(4035838631481534769)
XLA Ops:
  0.6 3.1 %collective-permute-start = (f32[2,4,1024]{2,1,0:T(4,128)}, f32[2,4,1024]{2,1,0:T(4,128)S(1)}, u32[]{:S(2)}, u32[]{:S(2)}) collective-permute-start(f32[2,4,1024]{2,1,0:T(4,128)} %param.6), channel_id=1, source_target_pairs={{0,8},{8,0},{16,24},{24,16},{1,9},{9,1},{17,25},{25,17},{2,10},{10... | collective-permute-start | bytes 98312 | tf_op jit(solution)/shard_map/ppermute | solution.py:39
  3.7 2.5 %collective-permute-start.2 = (f32[2,4,1024]{2,1,0:T(4,128)}, f32[2,4,1024]{2,1,0:T(4,128)S(1)}, u32[]{:S(2)}, u32[]{:S(2)}) collective-permute-start(f32[2,4,1024]{2,1,0:T(4,128)} %param.6), channel_id=1, source_target_pairs={{0,24},{8,16},{16,8},{24,0},{1,25},{9,17},{17,9},{25,1},{2,26},{10... | collective-permute-start | bytes 98312 | tf_op jit(solution)/shard_map/ppermute | solution.py:39
  6.8 0.8 stack.76
  7.6 1.4 %fusion.31 = (s32[]{:T(128)}, s32[8]{0:T(128)S(1)}, s32[]{:T(128)}, s32[]{:T(128)}, s32[8]{0:T(128)S(1)}) fusion(s32[8]{0:T(128)} %param.10, s32[]{:T(128)S(6)} %mul.84, s32[]{:T(128)S(6)} %mul.81), kind=kLoop, calls=%fused_computation.86 | loop fusion | flops 53 | bytes 116 | tf_op jit(solution)/shard_map/reduce_sum | solution.py:67
  9.4 0.8 copy.11
  10.1 0.8 fusion.6
  10.9 0.7 select_reduce_fusion
  11.7 0.7 broadcast_compare_fusion
  12.4 0.7 fusion.20
  13.1 1.3 %fusion.18 = (s32[1,64]{1,0:T(1,128)S(1)}, s32[1,64]{1,0:T(1,128)S(1)}, s32[1,64]{1,0:T(1,128)S(1)}, s32[1,64]{1,0:T(1,128)S(1)}, s32[1,64]{1,0:T(1,128)S(1)}, /*index=5*/s32[1,64]{1,0:T(1,128)S(1)}) fusion(s32[64]{0:T(128)S(1)} %get-tuple-element.28, s32[]{:T(128)S(6)} %axis_index.36, s32[64]{0:T(128)S(1)} %get-tuple-element.29, s32[]{:T(128)S(6)} %mul.81, ...), kind=kLoop, calls=%fused_computation.66 | loop fusion | flops 3072 | bytes 2580 | tf_op jit(solution)/shard_map/add | solution.py:66
  14.4 4.1 %broadcast_select_fusion = (f32[8,4,128,128]{3,2,1,0:T(8,128)S(1)}, f32[8,4,128,128]{3,2,1,0:T(8,128)}) fusion(f32[8,4,128,128]{3,2,1,0:T(8,128)} %param.8, pred[8,4]{1,0:T(8,128)(4,1)S(1)} %broadcast_compare_fusion, f32[8,4,128,128]{3,2,1,0:T(8,128)} %param.7), kind=kLoop, calls=%fused_computation | loop fusion | flops 1048576 | bytes 8388640 | tf_op jit(solution)/shard_map/jit(_where)/select_n | solution.py:364
  18.7 2.5 %collective-permute-start.5 = (f32[4,8,1024]{2,1,0:T(8,128)S(1)}, f32[4,8,1024]{2,1,0:T(8,128)S(1)}, u32[]{:S(2)}, u32[]{:S(2)}) collective-permute-start(f32[4,8,1024]{2,1,0:T(8,128)S(1)} %constant_dynamic-update-slice_fusion.refs_0_), channel_id=1, source_target_pairs={{0,6},{2,4},{4,2},{6,0},{1,7},{3,5},{5,3},{7,1},{8,14},{10,12},{12... | collective-permute-start | bytes 393224 | tf_op jit(solution)/shard_map/ppermute | solution.py:41
  24.3 1.0 %collective-permute-done.5.refs_3_ = f32[4,8,1024]{2,1,0:T(8,128)S(1)} collective-permute-done((f32[4,8,1024]{2,1,0:T(8,128)S(1)}, f32[4,8,1024]{2,1,0:T(8,128)S(1)}, u32[]{:S(2)}, u32[]{:S(2)}) %collective-permute-start.5) | collective-permute-done | bytes 131104 | tf_op jit(solution)/shard_map/ppermute | solution.py:41
  25.3 2.5 %collective-permute-done.4.refs_2_ = f32[4,8,1024]{2,1,0:T(8,128)S(1)} collective-permute-done((f32[4,8,1024]{2,1,0:T(8,128)S(1)}, f32[4,8,1024]{2,1,0:T(8,128)S(1)}, u32[]{:S(2)}, u32[]{:S(2)}) %collective-permute-start.4) | collective-permute-done | bytes 131104 | tf_op jit(solution)/shard_map/ppermute | solution.py:41
  28.0 1.6 %copy-done = f32[8,4,128,128]{3,2,1,0:T(8,128)S(1)} copy-done((f32[8,4,128,128]{3,2,1,0:T(8,128)S(1)}, f32[8,4,128,128]{3,2,1,0:T(8,128)}, u32[]{:S(2)}) %copy-start) | copy-done | bytes 2097176
  29.6 6.2 %step_0.1 = (f32[129,8,128]{2,1,0:T(8,128)S(1)}, f32[8,1024]{1,0:T(8,128)S(1)}, f32[8,128]{1,0:T(8,128)S(1)}, bf16[64,256,256]{2,1,0:T(8,128)(2,1)S(1)}) custom-call(s32[12,64]{1,0:T(8,128)S(1)} %stack.75.items_ref, s32[8,8]{1,0:T(8,128)S(1)} %get-tuple-element.42.places_ref, f32[8,128]{1,0:T(8,128)S(1)} %broadcast_in_dim.120.turn_ref, ...), custom_call_target="tpu_custom_call" | custom-call | tf_op jit(solution)/shard_map/step_0/pallas_call | solution.py:255
  35.8 3.0 %collective-permute-start.10 = (f32[8,1024]{1,0:T(8,128)S(1)}, f32[8,1024]{1,0:T(8,128)S(1)}, u32[]{:S(2)}, u32[]{:S(2)}) collective-permute-start(f32[8,1024]{1,0:T(8,128)S(1)} %get-tuple-element.14), channel_id=1, source_target_pairs={{0,24},{8,16},{16,8},{24,0},{1,25},{9,17},{17,9},{25,1},{2,26},{10... | collective-permute-start | bytes 98312 | tf_op jit(solution)/shard_map/ppermute | solution.py:39
  38.8 0.7 collective-permute-start.9
  39.4 0.8 collective-permute-start.8
  40.2 1.4 %collective-permute-done.10 = f32[8,1024]{1,0:T(8,128)S(1)} collective-permute-done((f32[8,1024]{1,0:T(8,128)S(1)}, f32[8,1024]{1,0:T(8,128)S(1)}, u32[]{:S(2)}, u32[]{:S(2)}) %collective-permute-start.10) | collective-permute-done | bytes 32800 | tf_op jit(solution)/shard_map/ppermute | solution.py:39
  41.7 2.0 %collective-permute-done.9 = f32[8,1024]{1,0:T(8,128)S(1)} collective-permute-done((f32[8,1024]{1,0:T(8,128)S(1)}, f32[8,1024]{1,0:T(8,128)S(1)}, u32[]{:S(2)}, u32[]{:S(2)}) %collective-permute-start.9) | collective-permute-done | bytes 32800 | tf_op jit(solution)/shard_map/ppermute | solution.py:39
  43.7 0.8 collective-permute-start.13
  44.5 1.3 %collective-permute-start.12 = (f32[4,8,1024]{2,1,0:T(8,128)S(1)}, f32[4,8,1024]{2,1,0:T(8,128)S(1)}, u32[]{:S(2)}, u32[]{:S(2)}) collective-permute-start(f32[4,8,1024]{2,1,0:T(8,128)S(1)} %pad_maximum_fusion.refs_0_), channel_id=1, source_target_pairs={{0,4},{2,6},{4,0},{6,2},{1,5},{3,7},{5,1},{7,3},{8,12},{10,14},{12... | collective-permute-start | bytes 393224 | tf_op jit(solution)/shard_map/ppermute | solution.py:41
  45.7 1.5 %collective-permute-start.11 = (f32[4,8,1024]{2,1,0:T(8,128)S(1)}, f32[4,8,1024]{2,1,0:T(8,128)S(1)}, u32[]{:S(2)}, u32[]{:S(2)}) collective-permute-start(f32[4,8,1024]{2,1,0:T(8,128)S(1)} %pad_maximum_fusion.refs_0_), channel_id=1, source_target_pairs={{0,2},{2,0},{4,6},{6,4},{1,3},{3,1},{5,7},{7,5},{8,10},{10,8},{12,... | collective-permute-start | bytes 393224 | tf_op jit(solution)/shard_map/ppermute | solution.py:41
  47.3 3.1 %collective-permute-done.13.refs_3_ = f32[4,8,1024]{2,1,0:T(8,128)S(1)} collective-permute-done((f32[4,8,1024]{2,1,0:T(8,128)S(1)}, f32[4,8,1024]{2,1,0:T(8,128)S(1)}, u32[]{:S(2)}, u32[]{:S(2)}) %collective-permute-start.13) | collective-permute-done | bytes 131104 | tf_op jit(solution)/shard_map/ppermute | solution.py:41
  51.4 3.9 %step_1.1 = (f32[129,8,128]{2,1,0:T(8,128)S(1)}, f32[8,1024]{1,0:T(8,128)S(1)}, f32[8,128]{1,0:T(8,128)S(1)}) custom-call(s32[12,64]{1,0:T(8,128)S(1)} %stack.75.items_ref, s32[8,8]{1,0:T(8,128)S(1)} %get-tuple-element.42.places_ref, f32[8,128]{1,0:T(8,128)S(1)} %broadcast_in_dim.120.turn_ref, f32[8,128]{1,0:T(8,128)S(1)} %get-tuple-element.13.info_in_ref, ...), custom_call_target="tpu_custom_call" | custom-call | tf_op jit(solution)/shard_map/step_1/pallas_call | solution.py:255
  55.3 1.5 %collective-permute-start.16 = (f32[8,1024]{1,0:T(8,128)S(1)}, f32[8,1024]{1,0:T(8,128)S(1)}, u32[]{:S(2)}, u32[]{:S(2)}) collective-permute-start(f32[8,1024]{1,0:T(8,128)S(1)} %get-tuple-element.18), channel_id=1, source_target_pairs={{0,24},{8,16},{16,8},{24,0},{1,25},{9,17},{17,9},{25,1},{2,26},{10... | collective-permute-start | bytes 98312 | tf_op jit(solution)/shard_map/ppermute | solution.py:39
  57.4 2.4 %collective-permute-start.14 = (f32[8,1024]{1,0:T(8,128)S(1)}, f32[8,1024]{1,0:T(8,128)S(1)}, u32[]{:S(2)}, u32[]{:S(2)}) collective-permute-start(f32[8,1024]{1,0:T(8,128)S(1)} %get-tuple-element.18), channel_id=1, source_target_pairs={{0,8},{8,0},{16,24},{24,16},{1,9},{9,1},{17,25},{25,17},{2,10},{10... | collective-permute-start | bytes 98312 | tf_op jit(solution)/shard_map/ppermute | solution.py:39
  59.8 1.3 %collective-permute-done.16 = f32[8,1024]{1,0:T(8,128)S(1)} collective-permute-done((f32[8,1024]{1,0:T(8,128)S(1)}, f32[8,1024]{1,0:T(8,128)S(1)}, u32[]{:S(2)}, u32[]{:S(2)}) %collective-permute-start.16) | collective-permute-done | bytes 32800 | tf_op jit(solution)/shard_map/ppermute | solution.py:39
  61.1 0.6 collective-permute-done.15
  62.0 1.0 %collective-permute-start.19 = (f32[4,8,1024]{2,1,0:T(8,128)S(1)}, f32[4,8,1024]{2,1,0:T(8,128)S(1)}, u32[]{:S(2)}, u32[]{:S(2)}) collective-permute-start(f32[4,8,1024]{2,1,0:T(8,128)S(1)} %pad_maximum_fusion.1.refs_0_), channel_id=1, source_target_pairs={{0,6},{2,4},{4,2},{6,0},{1,7},{3,5},{5,3},{7,1},{8,14},{10,12},{12... | collective-permute-start | bytes 393224 | tf_op jit(solution)/shard_map/ppermute | solution.py:41
  63.0 1.4 %collective-permute-start.18 = (f32[4,8,1024]{2,1,0:T(8,128)S(1)}, f32[4,8,1024]{2,1,0:T(8,128)S(1)}, u32[]{:S(2)}, u32[]{:S(2)}) collective-permute-start(f32[4,8,1024]{2,1,0:T(8,128)S(1)} %pad_maximum_fusion.1.refs_0_), channel_id=1, source_target_pairs={{0,4},{2,6},{4,0},{6,2},{1,5},{3,7},{5,1},{7,3},{8,12},{10,14},{12... | collective-permute-start | bytes 393224 | tf_op jit(solution)/shard_map/ppermute | solution.py:41
  64.4 1.2 %collective-permute-start.17 = (f32[4,8,1024]{2,1,0:T(8,128)S(1)}, f32[4,8,1024]{2,1,0:T(8,128)S(1)}, u32[]{:S(2)}, u32[]{:S(2)}) collective-permute-start(f32[4,8,1024]{2,1,0:T(8,128)S(1)} %pad_maximum_fusion.1.refs_0_), channel_id=1, source_target_pairs={{0,2},{2,0},{4,6},{6,4},{1,3},{3,1},{5,7},{7,5},{8,10},{10,8},{12,... | collective-permute-start | bytes 393224 | tf_op jit(solution)/shard_map/ppermute | solution.py:41
  65.6 2.5 %collective-permute-done.19.refs_3_ = f32[4,8,1024]{2,1,0:T(8,128)S(1)} collective-permute-done((f32[4,8,1024]{2,1,0:T(8,128)S(1)}, f32[4,8,1024]{2,1,0:T(8,128)S(1)}, u32[]{:S(2)}, u32[]{:S(2)}) %collective-permute-start.19) | collective-permute-done | bytes 131104 | tf_op jit(solution)/shard_map/ppermute | solution.py:41
  68.1 1.3 %collective-permute-done.18.refs_2_ = f32[4,8,1024]{2,1,0:T(8,128)S(1)} collective-permute-done((f32[4,8,1024]{2,1,0:T(8,128)S(1)}, f32[4,8,1024]{2,1,0:T(8,128)S(1)}, u32[]{:S(2)}, u32[]{:S(2)}) %collective-permute-start.18) | collective-permute-done | bytes 131104 | tf_op jit(solution)/shard_map/ppermute | solution.py:41
  69.4 4.4 %step_2.1 = (f32[8,1024]{1,0:T(8,128)S(1)}, f32[8,128]{1,0:T(8,128)S(1)}) custom-call(s32[12,64]{1,0:T(8,128)S(1)} %stack.75.items_ref, s32[8,8]{1,0:T(8,128)S(1)} %get-tuple-element.42.places_ref, f32[8,128]{1,0:T(8,128)S(1)} %broadcast_in_dim.120.turn_ref, f32[8,128]{1,0:T(8,128)S(1)} %get-tuple-element.17.info_in_ref, ...), custom_call_target="tpu_custom_call" | custom-call | tf_op jit(solution)/shard_map/step_2/pallas_call | solution.py:255
  73.8 0.6 copy-done.3
  74.4 1.9 %collective-permute-start.22 = (f32[8,128]{1,0:T(8,128)S(1)}, f32[8,128]{1,0:T(8,128)S(1)}, u32[]{:S(2)}, u32[]{:S(2)}) collective-permute-start(f32[8,128]{1,0:T(8,128)S(1)} %get-tuple-element.20), channel_id=1, source_target_pairs={{0,24},{8,16},{16,8},{24,0},{1,25},{9,17},{17,9},{25,1},{2,26},{10... | collective-permute-start | bytes 12296 | tf_op jit(solution)/shard_map/ppermute | solution.py:39
  76.3 1.2 %collective-permute-start.21 = (f32[8,128]{1,0:T(8,128)S(1)}, f32[8,128]{1,0:T(8,128)S(1)}, u32[]{:S(2)}, u32[]{:S(2)}) collective-permute-start(f32[8,128]{1,0:T(8,128)S(1)} %get-tuple-element.20), channel_id=1, source_target_pairs={{0,16},{8,24},{16,0},{24,8},{1,17},{9,25},{17,1},{25,9},{2,18},{10... | collective-permute-start | bytes 12296 | tf_op jit(solution)/shard_map/ppermute | solution.py:39
  77.5 1.3 %collective-permute-start.20 = (f32[8,128]{1,0:T(8,128)S(1)}, f32[8,128]{1,0:T(8,128)S(1)}, u32[]{:S(2)}, u32[]{:S(2)}) collective-permute-start(f32[8,128]{1,0:T(8,128)S(1)} %get-tuple-element.20), channel_id=1, source_target_pairs={{0,8},{8,0},{16,24},{24,16},{1,9},{9,1},{17,25},{25,17},{2,10},{10... | collective-permute-start | bytes 12296 | tf_op jit(solution)/shard_map/ppermute | solution.py:39
  78.8 1.0 %collective-permute-done.22 = f32[8,128]{1,0:T(8,128)S(1)} collective-permute-done((f32[8,128]{1,0:T(8,128)S(1)}, f32[8,128]{1,0:T(8,128)S(1)}, u32[]{:S(2)}, u32[]{:S(2)}) %collective-permute-start.22) | collective-permute-done | bytes 4128 | tf_op jit(solution)/shard_map/ppermute | solution.py:39
  79.8 1.0 %collective-permute-done.21 = f32[8,128]{1,0:T(8,128)S(1)} collective-permute-done((f32[8,128]{1,0:T(8,128)S(1)}, f32[8,128]{1,0:T(8,128)S(1)}, u32[]{:S(2)}, u32[]{:S(2)}) %collective-permute-start.21) | collective-permute-done | bytes 4128 | tf_op jit(solution)/shard_map/ppermute | solution.py:39
  81.1 0.7 collective-permute-start.25
  81.8 1.3 %collective-permute-start.24 = (f32[4,8,128]{2,1,0:T(8,128)S(1)}, f32[4,8,128]{2,1,0:T(8,128)S(1)}, u32[]{:S(2)}, u32[]{:S(2)}) collective-permute-start(f32[4,8,128]{2,1,0:T(8,128)S(1)} %pad_maximum_fusion.2.refs_0_), channel_id=1, source_target_pairs={{0,4},{2,6},{4,0},{6,2},{1,5},{3,7},{5,1},{7,3},{8,12},{10,14},{12... | collective-permute-start | bytes 49160 | tf_op jit(solution)/shard_map/ppermute | solution.py:41
  83.1 1.5 %collective-permute-start.23 = (f32[4,8,128]{2,1,0:T(8,128)S(1)}, f32[4,8,128]{2,1,0:T(8,128)S(1)}, u32[]{:S(2)}, u32[]{:S(2)}) collective-permute-start(f32[4,8,128]{2,1,0:T(8,128)S(1)} %pad_maximum_fusion.2.refs_0_), channel_id=1, source_target_pairs={{0,2},{2,0},{4,6},{6,4},{1,3},{3,1},{5,7},{7,5},{8,10},{10,8},{12,... | collective-permute-start | bytes 49160 | tf_op jit(solution)/shard_map/ppermute | solution.py:41
  84.6 1.1 %collective-permute-done.25.refs_3_ = f32[4,8,128]{2,1,0:T(8,128)S(1)} collective-permute-done((f32[4,8,128]{2,1,0:T(8,128)S(1)}, f32[4,8,128]{2,1,0:T(8,128)S(1)}, u32[]{:S(2)}, u32[]{:S(2)}) %collective-permute-start.25) | collective-permute-done | bytes 16416 | tf_op jit(solution)/shard_map/ppermute | solution.py:41
  85.8 1.1 %collective-permute-done.23.refs_1_ = f32[4,8,128]{2,1,0:T(8,128)S(1)} collective-permute-done((f32[4,8,128]{2,1,0:T(8,128)S(1)}, f32[4,8,128]{2,1,0:T(8,128)S(1)}, u32[]{:S(2)}, u32[]{:S(2)}) %collective-permute-start.23) | collective-permute-done | bytes 16416 | tf_op jit(solution)/shard_map/ppermute | solution.py:41
  87.4 2.8 %final.1 = (f32[2,4,1024]{2,1,0:T(4,128)}, f32[1,4]{1,0:T(1,128)}) custom-call(f32[4,8,128]{2,1,0:T(8,128)} %copy-done.4, f32[4,8,128]{2,1,0:T(8,128)} %copy-done.7, f32[4,8,128]{2,1,0:T(8,128)} %copy-done.6, f32[4,8,128]{2,1,0:T(8,128)} %copy-done.5, f32[129,8,128]{2,1,0:T(8,128)} %copy-done.1, f32[129,8,128]{2,1,0:T(8,128)} %copy-done.2, f32[8,1024]{1,0:T(8,128)} %copy-done.3), custom_call_target="tpu_custom_call" | custom-call | tf_op jit(solution)/shard_map/final/pallas_call | solution.py:338
  (58 shorter events, 5.2 us)
Async XLA Ops:
  0.6 17.9 %collective-permute-start = (f32[2,4,1024]{2,1,0:T(4,128)}, f32[2,4,1024]{2,1,0:T(4,128)S(1)}, u32[]{:S(2)}, u32[]{:S(2)}) collective-permute-start(f32[2,4,1024]{2,1,0:T(4,128)} %param.6), channel_id=1, source_target_pairs={{0,8},{8,0},{16,24},{24,16},{1,9},{9,1},{17,25},{25,17},{2,10},{10... | collective-permute-start | bytes 98312 | tf_op jit(solution)/shard_map/ppermute | solution.py:39
  3.7 14.8 %collective-permute-start.2 = (f32[2,4,1024]{2,1,0:T(4,128)}, f32[2,4,1024]{2,1,0:T(4,128)S(1)}, u32[]{:S(2)}, u32[]{:S(2)}) collective-permute-start(f32[2,4,1024]{2,1,0:T(4,128)} %param.6), channel_id=1, source_target_pairs={{0,24},{8,16},{16,8},{24,0},{1,25},{9,17},{17,9},{25,1},{2,26},{10... | collective-permute-start | bytes 98312 | tf_op jit(solution)/shard_map/ppermute | solution.py:39
  6.2 12.4 %collective-permute-start.1 = (f32[2,4,1024]{2,1,0:T(4,128)}, f32[2,4,1024]{2,1,0:T(4,128)S(1)}, u32[]{:S(2)}, u32[]{:S(2)}) collective-permute-start(f32[2,4,1024]{2,1,0:T(4,128)} %param.6), channel_id=1, source_target_pairs={{0,16},{8,24},{16,0},{24,8},{1,17},{9,25},{17,1},{25,9},{2,18},{10... | collective-permute-start | bytes 98312 | tf_op jit(solution)/shard_map/ppermute | solution.py:39
  6.3 21.6 %collective-permute-start.6 = (f32[8,4,128,128]{3,2,1,0:T(8,128)}, f32[8,4,128,128]{3,2,1,0:T(8,128)}, u32[]{:S(2)}, u32[]{:S(2)}) collective-permute-start(f32[8,4,128,128]{3,2,1,0:T(8,128)} %param.7), channel_id=1, source_target_pairs={{0,1},{1,0},{2,3},{3,2},{4,5},{5,4},{6,7},{7,6},{8,9},{9,8},{10,11... | collective-permute-start | bytes 6291464 | tf_op jit(solution)/shard_map/ppermute | solution.py:363
  6.3 21.6 %collective-permute-start.7 = (f32[8,4,128,128]{3,2,1,0:T(8,128)}, f32[8,4,128,128]{3,2,1,0:T(8,128)}, u32[]{:S(2)}, u32[]{:S(2)}) collective-permute-start(f32[8,4,128,128]{3,2,1,0:T(8,128)} %param.8), channel_id=1, source_target_pairs={{0,1},{1,0},{2,3},{3,2},{4,5},{5,4},{6,7},{7,6},{8,9},{9,8},{10,11... | collective-permute-start | bytes 6291464 | tf_op jit(solution)/shard_map/ppermute | solution.py:364
  14.4 7.8 %copy-start.8 = (s32[4]{0:T(128)S(1)}, s32[4]{0:T(128)}, u32[]{:S(2)}) copy-start(s32[4]{0:T(128)} %param.11) | copy-start | bytes 52
  18.7 6.7 %collective-permute-start.5 = (f32[4,8,1024]{2,1,0:T(8,128)S(1)}, f32[4,8,1024]{2,1,0:T(8,128)S(1)}, u32[]{:S(2)}, u32[]{:S(2)}) collective-permute-start(f32[4,8,1024]{2,1,0:T(8,128)S(1)} %constant_dynamic-update-slice_fusion.refs_0_), channel_id=1, source_target_pairs={{0,6},{2,4},{4,2},{6,0},{1,7},{3,5},{5,3},{7,1},{8,14},{10,12},{12... | collective-permute-start | bytes 393224 | tf_op jit(solution)/shard_map/ppermute | solution.py:41
  21.2 6.7 %collective-permute-start.4 = (f32[4,8,1024]{2,1,0:T(8,128)S(1)}, f32[4,8,1024]{2,1,0:T(8,128)S(1)}, u32[]{:S(2)}, u32[]{:S(2)}) collective-permute-start(f32[4,8,1024]{2,1,0:T(8,128)S(1)} %constant_dynamic-update-slice_fusion.refs_0_), channel_id=1, source_target_pairs={{0,4},{2,6},{4,0},{6,2},{1,5},{3,7},{5,1},{7,3},{8,12},{10,14},{12... | collective-permute-start | bytes 393224 | tf_op jit(solution)/shard_map/ppermute | solution.py:41
  21.7 6.2 %collective-permute-start.3 = (f32[4,8,1024]{2,1,0:T(8,128)S(1)}, f32[4,8,1024]{2,1,0:T(8,128)S(1)}, u32[]{:S(2)}, u32[]{:S(2)}) collective-permute-start(f32[4,8,1024]{2,1,0:T(8,128)S(1)} %constant_dynamic-update-slice_fusion.refs_0_), channel_id=1, source_target_pairs={{0,2},{2,0},{4,6},{6,4},{1,3},{3,1},{5,7},{7,5},{8,10},{10,8},{12,... | collective-permute-start | bytes 393224 | tf_op jit(solution)/shard_map/ppermute | solution.py:41
  28.0 1.6 %copy-start = (f32[8,4,128,128]{3,2,1,0:T(8,128)S(1)}, f32[8,4,128,128]{3,2,1,0:T(8,128)}, u32[]{:S(2)}) copy-start(f32[8,4,128,128]{3,2,1,0:T(8,128)} %get-tuple-element.39) | copy-start | bytes 6291460
  35.8 33.6 %copy-start.1 = (f32[129,8,128]{2,1,0:T(8,128)}, f32[129,8,128]{2,1,0:T(8,128)S(1)}, u32[]{:S(2)}) copy-start(f32[129,8,128]{2,1,0:T(8,128)S(1)} %get-tuple-element.15.refs_4_) | copy-start | bytes 1585156
  35.8 5.9 %collective-permute-start.10 = (f32[8,1024]{1,0:T(8,128)S(1)}, f32[8,1024]{1,0:T(8,128)S(1)}, u32[]{:S(2)}, u32[]{:S(2)}) collective-permute-start(f32[8,1024]{1,0:T(8,128)S(1)} %get-tuple-element.14), channel_id=1, source_target_pairs={{0,24},{8,16},{16,8},{24,0},{1,25},{9,17},{17,9},{25,1},{2,26},{10... | collective-permute-start | bytes 98312 | tf_op jit(solution)/shard_map/ppermute | solution.py:39
  38.8 4.9 %collective-permute-start.9 = (f32[8,1024]{1,0:T(8,128)S(1)}, f32[8,1024]{1,0:T(8,128)S(1)}, u32[]{:S(2)}, u32[]{:S(2)}) collective-permute-start(f32[8,1024]{1,0:T(8,128)S(1)} %get-tuple-element.14), channel_id=1, source_target_pairs={{0,16},{8,24},{16,0},{24,8},{1,17},{9,25},{17,1},{25,9},{2,18},{10... | collective-permute-start | bytes 98312 | tf_op jit(solution)/shard_map/ppermute | solution.py:39
  39.4 4.3 %collective-permute-start.8 = (f32[8,1024]{1,0:T(8,128)S(1)}, f32[8,1024]{1,0:T(8,128)S(1)}, u32[]{:S(2)}, u32[]{:S(2)}) collective-permute-start(f32[8,1024]{1,0:T(8,128)S(1)} %get-tuple-element.14), channel_id=1, source_target_pairs={{0,8},{8,0},{16,24},{24,16},{1,9},{9,1},{17,25},{25,17},{2,10},{10... | collective-permute-start | bytes 98312 | tf_op jit(solution)/shard_map/ppermute | solution.py:39
  43.7 6.7 %collective-permute-start.13 = (f32[4,8,1024]{2,1,0:T(8,128)S(1)}, f32[4,8,1024]{2,1,0:T(8,128)S(1)}, u32[]{:S(2)}, u32[]{:S(2)}) collective-permute-start(f32[4,8,1024]{2,1,0:T(8,128)S(1)} %pad_maximum_fusion.refs_0_), channel_id=1, source_target_pairs={{0,6},{2,4},{4,2},{6,0},{1,7},{3,5},{5,3},{7,1},{8,14},{10,12},{12... | collective-permute-start | bytes 393224 | tf_op jit(solution)/shard_map/ppermute | solution.py:41
  44.5 6.4 %collective-permute-start.12 = (f32[4,8,1024]{2,1,0:T(8,128)S(1)}, f32[4,8,1024]{2,1,0:T(8,128)S(1)}, u32[]{:S(2)}, u32[]{:S(2)}) collective-permute-start(f32[4,8,1024]{2,1,0:T(8,128)S(1)} %pad_maximum_fusion.refs_0_), channel_id=1, source_target_pairs={{0,4},{2,6},{4,0},{6,2},{1,5},{3,7},{5,1},{7,3},{8,12},{10,14},{12... | collective-permute-start | bytes 393224 | tf_op jit(solution)/shard_map/ppermute | solution.py:41
  45.7 5.6 %collective-permute-start.11 = (f32[4,8,1024]{2,1,0:T(8,128)S(1)}, f32[4,8,1024]{2,1,0:T(8,128)S(1)}, u32[]{:S(2)}, u32[]{:S(2)}) collective-permute-start(f32[4,8,1024]{2,1,0:T(8,128)S(1)} %pad_maximum_fusion.refs_0_), channel_id=1, source_target_pairs={{0,2},{2,0},{4,6},{6,4},{1,3},{3,1},{5,7},{7,5},{8,10},{10,8},{12,... | collective-permute-start | bytes 393224 | tf_op jit(solution)/shard_map/ppermute | solution.py:41
  55.3 18.5 %copy-start.2 = (f32[129,8,128]{2,1,0:T(8,128)}, f32[129,8,128]{2,1,0:T(8,128)S(1)}, u32[]{:S(2)}) copy-start(f32[129,8,128]{2,1,0:T(8,128)S(1)} %get-tuple-element.19.refs_5_) | copy-start | bytes 1585156
  55.3 5.8 %collective-permute-start.16 = (f32[8,1024]{1,0:T(8,128)S(1)}, f32[8,1024]{1,0:T(8,128)S(1)}, u32[]{:S(2)}, u32[]{:S(2)}) collective-permute-start(f32[8,1024]{1,0:T(8,128)S(1)} %get-tuple-element.18), channel_id=1, source_target_pairs={{0,24},{8,16},{16,8},{24,0},{1,25},{9,17},{17,9},{25,1},{2,26},{10... | collective-permute-start | bytes 98312 | tf_op jit(solution)/shard_map/ppermute | solution.py:39
  56.9 4.8 %collective-permute-start.15 = (f32[8,1024]{1,0:T(8,128)S(1)}, f32[8,1024]{1,0:T(8,128)S(1)}, u32[]{:S(2)}, u32[]{:S(2)}) collective-permute-start(f32[8,1024]{1,0:T(8,128)S(1)} %get-tuple-element.18), channel_id=1, source_target_pairs={{0,16},{8,24},{16,0},{24,8},{1,17},{9,25},{17,1},{25,9},{2,18},{10... | collective-permute-start | bytes 98312 | tf_op jit(solution)/shard_map/ppermute | solution.py:39
  57.4 4.7 %collective-permute-start.14 = (f32[8,1024]{1,0:T(8,128)S(1)}, f32[8,1024]{1,0:T(8,128)S(1)}, u32[]{:S(2)}, u32[]{:S(2)}) collective-permute-start(f32[8,1024]{1,0:T(8,128)S(1)} %get-tuple-element.18), channel_id=1, source_target_pairs={{0,8},{8,0},{16,24},{24,16},{1,9},{9,1},{17,25},{25,17},{2,10},{10... | collective-permute-start | bytes 98312 | tf_op jit(solution)/shard_map/ppermute | solution.py:39
  62.0 6.0 %collective-permute-start.19 = (f32[4,8,1024]{2,1,0:T(8,128)S(1)}, f32[4,8,1024]{2,1,0:T(8,128)S(1)}, u32[]{:S(2)}, u32[]{:S(2)}) collective-permute-start(f32[4,8,1024]{2,1,0:T(8,128)S(1)} %pad_maximum_fusion.1.refs_0_), channel_id=1, source_target_pairs={{0,6},{2,4},{4,2},{6,0},{1,7},{3,5},{5,3},{7,1},{8,14},{10,12},{12... | collective-permute-start | bytes 393224 | tf_op jit(solution)/shard_map/ppermute | solution.py:41
  63.0 6.3 %collective-permute-start.18 = (f32[4,8,1024]{2,1,0:T(8,128)S(1)}, f32[4,8,1024]{2,1,0:T(8,128)S(1)}, u32[]{:S(2)}, u32[]{:S(2)}) collective-permute-start(f32[4,8,1024]{2,1,0:T(8,128)S(1)} %pad_maximum_fusion.1.refs_0_), channel_id=1, source_target_pairs={{0,4},{2,6},{4,0},{6,2},{1,5},{3,7},{5,1},{7,3},{8,12},{10,14},{12... | collective-permute-start | bytes 393224 | tf_op jit(solution)/shard_map/ppermute | solution.py:41
  64.4 5.0 %collective-permute-start.17 = (f32[4,8,1024]{2,1,0:T(8,128)S(1)}, f32[4,8,1024]{2,1,0:T(8,128)S(1)}, u32[]{:S(2)}, u32[]{:S(2)}) collective-permute-start(f32[4,8,1024]{2,1,0:T(8,128)S(1)} %pad_maximum_fusion.1.refs_0_), channel_id=1, source_target_pairs={{0,2},{2,0},{4,6},{6,4},{1,3},{3,1},{5,7},{7,5},{8,10},{10,8},{12,... | collective-permute-start | bytes 393224 | tf_op jit(solution)/shard_map/ppermute | solution.py:41
  73.8 0.6 copy-start.3
  74.4 5.4 %collective-permute-start.22 = (f32[8,128]{1,0:T(8,128)S(1)}, f32[8,128]{1,0:T(8,128)S(1)}, u32[]{:S(2)}, u32[]{:S(2)}) collective-permute-start(f32[8,128]{1,0:T(8,128)S(1)} %get-tuple-element.20), channel_id=1, source_target_pairs={{0,24},{8,16},{16,8},{24,0},{1,25},{9,17},{17,9},{25,1},{2,26},{10... | collective-permute-start | bytes 12296 | tf_op jit(solution)/shard_map/ppermute | solution.py:39
  76.3 4.5 %collective-permute-start.21 = (f32[8,128]{1,0:T(8,128)S(1)}, f32[8,128]{1,0:T(8,128)S(1)}, u32[]{:S(2)}, u32[]{:S(2)}) collective-permute-start(f32[8,128]{1,0:T(8,128)S(1)} %get-tuple-element.20), channel_id=1, source_target_pairs={{0,16},{8,24},{16,0},{24,8},{1,17},{9,25},{17,1},{25,9},{2,18},{10... | collective-permute-start | bytes 12296 | tf_op jit(solution)/shard_map/ppermute | solution.py:39
  77.5 3.6 %collective-permute-start.20 = (f32[8,128]{1,0:T(8,128)S(1)}, f32[8,128]{1,0:T(8,128)S(1)}, u32[]{:S(2)}, u32[]{:S(2)}) collective-permute-start(f32[8,128]{1,0:T(8,128)S(1)} %get-tuple-element.20), channel_id=1, source_target_pairs={{0,8},{8,0},{16,24},{24,16},{1,9},{9,1},{17,25},{25,17},{2,10},{10... | collective-permute-start | bytes 12296 | tf_op jit(solution)/shard_map/ppermute | solution.py:39
  81.1 5.7 %copy-start.4 = (f32[4,8,128]{2,1,0:T(8,128)}, f32[4,8,128]{2,1,0:T(8,128)S(1)}, u32[]{:S(2)}) copy-start(f32[4,8,128]{2,1,0:T(8,128)S(1)} %pad_maximum_fusion.2.refs_0_) | copy-start | bytes 49156
  81.1 4.6 %collective-permute-start.25 = (f32[4,8,128]{2,1,0:T(8,128)S(1)}, f32[4,8,128]{2,1,0:T(8,128)S(1)}, u32[]{:S(2)}, u32[]{:S(2)}) collective-permute-start(f32[4,8,128]{2,1,0:T(8,128)S(1)} %pad_maximum_fusion.2.refs_0_), channel_id=1, source_target_pairs={{0,6},{2,4},{4,2},{6,0},{1,7},{3,5},{5,3},{7,1},{8,14},{10,12},{12... | collective-permute-start | bytes 49160 | tf_op jit(solution)/shard_map/ppermute | solution.py:41
  81.8 3.9 %collective-permute-start.24 = (f32[4,8,128]{2,1,0:T(8,128)S(1)}, f32[4,8,128]{2,1,0:T(8,128)S(1)}, u32[]{:S(2)}, u32[]{:S(2)}) collective-permute-start(f32[4,8,128]{2,1,0:T(8,128)S(1)} %pad_maximum_fusion.2.refs_0_), channel_id=1, source_target_pairs={{0,4},{2,6},{4,0},{6,2},{1,5},{3,7},{5,1},{7,3},{8,12},{10,14},{12... | collective-permute-start | bytes 49160 | tf_op jit(solution)/shard_map/ppermute | solution.py:41
  83.1 3.7 %collective-permute-start.23 = (f32[4,8,128]{2,1,0:T(8,128)S(1)}, f32[4,8,128]{2,1,0:T(8,128)S(1)}, u32[]{:S(2)}, u32[]{:S(2)}) collective-permute-start(f32[4,8,128]{2,1,0:T(8,128)S(1)} %pad_maximum_fusion.2.refs_0_), channel_id=1, source_target_pairs={{0,2},{2,0},{4,6},{6,4},{1,3},{3,1},{5,7},{7,5},{8,10},{10,8},{12,... | collective-permute-start | bytes 49160 | tf_op jit(solution)/shard_map/ppermute | solution.py:41
  85.8 1.1 %copy-start.5 = (f32[4,8,128]{2,1,0:T(8,128)}, f32[4,8,128]{2,1,0:T(8,128)S(1)}, u32[]{:S(2)}) copy-start(f32[4,8,128]{2,1,0:T(8,128)S(1)} %collective-permute-done.25.refs_3_) | copy-start | bytes 49156
  85.8 1.1 %copy-start.6 = (f32[4,8,128]{2,1,0:T(8,128)}, f32[4,8,128]{2,1,0:T(8,128)S(1)}, u32[]{:S(2)}) copy-start(f32[4,8,128]{2,1,0:T(8,128)S(1)} %collective-permute-done.24.refs_2_) | copy-start | bytes 49156
  86.8 0.6 copy-start.7

commit v6 on v5

--- a/solution.py
+++ b/solution.py
@@ -41,33 +41,89 @@
     return [whole_line] + [lax.ppermute(whole_line, "place", perm) for perm in partner_steps(plane)]
 
 
-def work_list(pattern, counts, where, line, plane, freqs):
-    row_blocks, slots = pattern.shape
+def setup_kernel(
+    line, plane, freqs, pattern_ref, counts_ref, where_ref, ids_ref, g_ref, c_ref,
+    items_ref, places_ref, turn_ref, g_out_ref, c_out_ref, sems,
+):
+    row_blocks, slots = pattern_ref.shape
     own_slots = slots // freqs
+    pieces = sems.shape[1]
+    part = g_ref.shape[0] // pieces
+    copies = []
+    for m, (source, target) in enumerate(((g_ref, g_out_ref), (c_ref, c_out_ref))):
+        for i in range(pieces):
+            at = pl.ds(i * part, part)
+            copies.append(pltpu.make_async_copy(source.at[at], target.at[at], sems.at[m, i]))
+            copies[-1].start()
+
+    order = lax.broadcasted_iota(jnp.int32, (8, LANES), 1)
+    freq = where_ref[2]
+    for table, d in enumerate(list(range(freqs)) + [None]):
+        first = 0 if d is None else lax.rem(freq + (freqs - d), freqs) * own_slots
+        group = FULL_GROUP if d is None else GROUP
+        layer = jnp.zeros((8, LANES), jnp.int32) + first
+        block = jnp.full((8, LANES), row_blocks, jnp.int32)
+        home = jnp.zeros((8, LANES), jnp.int32)
+        used = jnp.int32(0)
+        for b in range(row_blocks):
+            here = counts_ref[b] if d is None else jnp.clip(counts_ref[b] - first, 0, own_slots)
+            inside = order - used
+            hit = (inside >= 0) & (inside < here)
+            layer = jnp.where(hit, first + inside, layer)
+            block = jnp.where(hit, b, block)
+            home = jnp.where(hit, b, home)
+            used = used + here
+        away = freq - lax.div(layer, own_slots)
+        away = jnp.where(away < 0, away + freqs, away)
+        stored = (away * row_blocks + home) * own_slots + lax.rem(layer, own_slots)
+        groups = jnp.zeros((8, LANES), jnp.int32) + lax.div(used + (group - 1), group)
+        for i, values in enumerate((layer, block, stored, groups)):
+            items_ref[4 * table + i : 4 * table + i + 1, :] = values[:1]
+
+    pattern = pattern_ref[...]
     owner = lax.div(pattern, row_blocks)
-    far = distance(where[0], lax.div(owner, plane), line)
-    place = distance(where[1], lax.rem(owner, plane), plane) * line + far
+    far = distance(where_ref[0], lax.div(owner, plane), line)
+    place = distance(where_ref[1], lax.rem(owner, plane), plane) * line + far
     place = place * row_blocks + lax.rem(pattern, row_blocks)
-    slot = jnp.arange(slots)
-    places = jnp.where(slot[None, :] < counts[:, None], place, line * plane * row_blocks).T
-    b = jnp.arange(row_blocks)
-    order = jnp.arange(row_blocks * slots)
-    tables = []
-    for d in list(range(freqs)) + [None]:
-        first = 0 if d is None else lax.rem(where[2] + (freqs - d), freqs) * own_slots
-        group = FULL_GROUP if d is None else GROUP
-        here = counts if d is None else jnp.clip(counts - first, 0, own_slots)
-        start = jnp.sum(jnp.where(b[None, :] < b[:, None], here[None, :], 0), axis=1)
-        inside = order[:, None] - start[None, :]
-        hit = (inside >= 0) & (inside < here[None, :])
-        layer = first + jnp.sum(jnp.where(hit, inside, 0), axis=1)
-        block = jnp.sum(jnp.where(hit, b[None, :], 0), axis=1)
-        away = lax.rem(where[2] - lax.div(layer, own_slots) + freqs, freqs)
-        stored = (away * row_blocks + block) * own_slots + lax.rem(layer, own_slots)
-        used = jnp.sum(here)
-        block = jnp.where(order < used, block, row_blocks)
-        tables += [layer, block, stored, jnp.full(order.shape, lax.div(used + (group - 1), group))]
-    return jnp.stack(tables).astype(jnp.int32), places.astype(jnp.int32)
+    b_at = lax.broadcasted_iota(jnp.int32, pattern.shape, 0)
+    k_at = lax.broadcasted_iota(jnp.int32, pattern.shape, 1)
+    count = jnp.zeros(pattern.shape, jnp.int32)
+    for b in range(row_blocks):
+        count = jnp.where(b_at == b, counts_ref[b], count)
+    places_ref[...] = jnp.where(k_at < count, place, line * plane * row_blocks)
+
+    half = turn_ref.shape[0] // 2
+    row_at = lax.broadcasted_iota(jnp.int32, turn_ref.shape, 0)
+    ids = jnp.zeros(turn_ref.shape, jnp.int32)
+    for f in range(half):
+        ids = jnp.where(lax.rem(row_at, half) == f, ids_ref[f], ids)
+    angular = 0.2 * jnp.exp(ids.astype(jnp.float32) * (math.log(8.0) / 1000.0))
+    turn_ref[...] = jnp.where(row_at < half, -angular, angular)
+    for copy in copies:
+        copy.wait()
+
+
+def run_setup(pattern, counts, where, freq_ids, g_own, c_own, line, plane, freqs):
+    smem, vmem = pl.BlockSpec(memory_space=pltpu.SMEM), pl.BlockSpec(memory_space=pltpu.VMEM)
+    far = pl.BlockSpec(memory_space=pl.ANY)
+    blocks = jax.ShapeDtypeStruct(g_own.shape, jnp.float32)
+    pieces = math.gcd(g_own.shape[0], 8)
+    return pl.pallas_call(
+        functools.partial(setup_kernel, line, plane, freqs),
+        in_specs=[vmem, smem, smem, smem, far, far],
+        out_specs=[vmem] * 5,
+        out_shape=[
+            jax.ShapeDtypeStruct((4 * (freqs + 1), LANES), jnp.int32),
+            jax.ShapeDtypeStruct(pattern.shape, jnp.int32),
+            jax.ShapeDtypeStruct((2 * freq_ids.shape[0], LANES), jnp.float32),
+            blocks,
+            blocks,
+        ],
+        scratch_shapes=[pltpu.SemaphoreType.DMA((2, pieces))],
+        compiler_params=pltpu.CompilerParams(vmem_limit_bytes=VMEM_LIMIT),
+        cost_estimate=pl.CostEstimate(flops=0, bytes_accessed=16 * g_own.size, transcendentals=0),
+        name="setup",
+    )(pattern, counts, where, freq_ids, g_own, c_own)
 
 
 def lane_sum(x):
@@ -92,7 +148,7 @@
 def step_kernel(step, plane, line, freqs, items_ref, places_ref, turn_ref, info_in_ref, *refs):
     lines, refs = refs[:plane], refs[plane:]
     prev, refs = refs[:step], refs[step:]
-    slots, row_blocks = places_ref.shape
+    row_blocks, slots = places_ref.shape
     nodes = plane * line
     if step == 0:
         g_refs, c_refs = refs[:freqs], refs[freqs : 2 * freqs]
@@ -170,7 +226,7 @@
     blocks(normal, 0)
 
     for k in range(slots):
-        chosen = jnp.concatenate([z_ref[places_ref[k, b]] for b in range(row_blocks)], axis=0)
+        chosen = jnp.concatenate([z_ref[places_ref[b, k]] for b in range(row_blocks)], axis=0)
         high = chosen.astype(jnp.bfloat16).astype(jnp.float32)
         layer_ref[k] = jnp.transpose(jnp.concatenate([high, chosen - high], axis=0)).astype(jnp.bfloat16)
 
@@ -235,7 +291,7 @@
 def run_step(step, lists, turn, info, lines, prev, blocks, freqs):
     plane = len(lines)
     line, parts, rows = lines[0].shape
-    slots, row_blocks = lists[1].shape
+    row_blocks, slots = lists[1].shape
     size = rows // row_blocks
     vmem = pl.BlockSpec(memory_space=pltpu.VMEM)
     in_specs = [pl.BlockSpec(memory_space=pltpu.SMEM)] * 2 + [vmem] * (2 + plane + step + len(blocks))
@@ -349,24 +405,21 @@
 
 def make_shards(line, plane, freqs):
     def shards(excitation, g_blocks, c_blocks, pattern, counts, freq_ids):
-        angular = 0.2 * jnp.exp(freq_ids.astype(jnp.float32) * (math.log(8.0) / 1000.0))
         row_blocks, own_slots, size, _ = g_blocks.shape
         freq_count = excitation.shape[1]
         parts = 2 * freq_count
         where = jnp.stack([lax.axis_index(name) for name in ("line", "place", "freq")]).astype(jnp.int32)
         stored = (row_blocks * own_slots, size, size)
-        slot = lax.axis_index("freq") * own_slots + jnp.arange(own_slots)
-        in_use = (slot[None, :] < counts[:, None])[:, :, None, None]
-        g_parts, c_parts = [], []
-        for d in range(freqs):
+        g_own, c_own = g_blocks.reshape(stored), c_blocks.reshape(stored)
+        *lists, turn, g_near, c_near = run_setup(
+            pattern, counts, where, freq_ids, g_own, c_own, line, plane, freqs
+        )
+        g_parts, c_parts = [g_near], [c_near]
+        for d in range(1, freqs):
             perm = [(i, (i + d) % freqs) for i in range(freqs)]
-            g_part = lax.ppermute(g_blocks, "freq", perm) if d else jnp.where(in_use, g_blocks, 0.0)
-            c_part = lax.ppermute(c_blocks, "freq", perm) if d else jnp.where(in_use, c_blocks, 0.0)
-            g_parts.append(g_part.reshape(stored))
-            c_parts.append(c_part.reshape(stored))
-        turn = jnp.broadcast_to(jnp.concatenate([-angular, angular])[:, None], (parts, LANES))
+            g_parts.append(lax.ppermute(g_own, "freq", perm))
+            c_parts.append(lax.ppermute(c_own, "freq", perm))
         info = jnp.zeros((parts, LANES), jnp.float32)
-        lists = work_list(pattern, counts, where, line, plane, freqs)
         krylov = []
         rows = excitation
         blocks = g_parts + c_parts

time: 91.2 us -> 82.5 us (0.905)
  other arithmetic: 10.2 us -> 0.1 us
  local copies, waits for them, and re-layouts: 4.52 us -> 7.26 us
  Pallas kernels: 17.3 us -> 19.3 us
  between operations: 2.8 us -> 0.83 us
    select_n x1 -> x0, other arithmetic: 4.15 us -> none  [shards(): jnp.where(in_use, c_blocks, 0.0)]
    unnamed x22 -> x27, local copies, waits for them, and re-layouts: 3.57 us -> 6.4 us
    reduce_sum x6 -> x0, other arithmetic: 2.49 us -> none  [the longest x1 1.4 us: work_list(): used = jnp.sum(here)]
    ppermute x12, waiting for transfers between devices: 13.7 us -> 11.2 us  [gather_rows(): lax.ppermute(whole_line, 'place', perm)]
    ppermute x12, waiting for transfers between devices: 8.03 us -> 10.1 us  [gather_rows(): lax.ppermute(rows, 'line', perm)]
    add x3 -> x0, other arithmetic: 1.96 us -> none  [the longest x2 1.96 us: work_list(): stored = (away * row_blocks + block) * own_slots + lax.rem(layer, own_slots)]
    pallas_call x0 -> x1, Pallas kernels: none -> 1.07 us  [run_setup(): pl.pallas_call(functools.partial(setup_kernel, line, plane, freqs), in_sp...]
  transfers between devices with their start and end apart: 26 -> 26, of which waited for: 18 -> 17; matrix products, arithmetic and copies ran while one was open for 13% -> 1% of each run, Pallas kernels for 0% -> 1%
where the time goes in v6:
time: 82.5 us; the launch traced here: 82.4 us
  starting transfers between devices  33.6 us (41%)
  waiting for transfers between devices  21.3 us (26%)
  Pallas kernels  19.3 us (23%)
  local copies, waits for them, and re-layouts  7.26 us (9%)
  between operations  0.83 us (1%)
    ppermute x12, starting transfers between devices, gather_rows(): lax.ppermute(rows, 'line', perm)  18.9 us
    pallas_call x3, Pallas kernels, run_step(): pl.pallas_call(functools.partial(step_kernel, step, plane, line, freqs),...  15.4 us
    ppermute x12, starting transfers between devices, gather_rows(): lax.ppermute(whole_line, 'place', perm)  14.1 us
    ppermute x12, waiting for transfers between devices, gather_rows(): lax.ppermute(whole_line, 'place', perm)  11.2 us
    ppermute x12, waiting for transfers between devices, gather_rows(): lax.ppermute(rows, 'line', perm)  10.1 us
    unnamed x27, local copies, waits for them, and re-layouts  6.4 us
    pallas_call x1, Pallas kernels, run_final(): pl.pallas_call(functools.partial(final_kernel, len(tiles)), in_specs=[vme...  2.84 us
  transfers between devices with their start and end apart: 26, of which 17 were waited for; matrix products, arithmetic and copies ran while one was open for 1% of the time, Pallas kernels for 1%

profile of v6, /device:TPU:0, one launch (start us, length us, event | category | flops | bytes accessed | tf_op | source)
XLA Modules:
  0.0 82.4 jit_solution(8549444127536439809)
XLA Ops:
  0.6 0.5 collective-permute-start.6
  1.2 3.0 %collective-permute-start = (f32[2,4,1024]{2,1,0:T(4,128)}, f32[2,4,1024]{2,1,0:T(4,128)S(1)}, u32[]{:S(2)}, u32[]{:S(2)}) collective-permute-start(f32[2,4,1024]{2,1,0:T(4,128)} %param.6), channel_id=1, source_target_pairs={{0,8},{8,0},{16,24},{24,16},{1,9},{9,1},{17,25},{25,17},{2,10},{10... | collective-permute-start | bytes 98312 | tf_op jit(solution)/shard_map/ppermute | solution.py:39
  4.2 2.5 %collective-permute-start.2 = (f32[2,4,1024]{2,1,0:T(4,128)}, f32[2,4,1024]{2,1,0:T(4,128)S(1)}, u32[]{:S(2)}, u32[]{:S(2)}) collective-permute-start(f32[2,4,1024]{2,1,0:T(4,128)} %param.6), channel_id=1, source_target_pairs={{0,24},{8,16},{16,8},{24,0},{1,25},{9,17},{17,9},{25,1},{2,26},{10... | collective-permute-start | bytes 98312 | tf_op jit(solution)/shard_map/ppermute | solution.py:39
  6.8 0.8 stack.76
  7.7 2.6 %collective-permute-done.2 = f32[2,4,1024]{2,1,0:T(4,128)S(1)} collective-permute-done((f32[2,4,1024]{2,1,0:T(4,128)}, f32[2,4,1024]{2,1,0:T(4,128)S(1)}, u32[]{:S(2)}, u32[]{:S(2)}) %collective-permute-start.2) | collective-permute-done | bytes 32800 | tf_op jit(solution)/shard_map/ppermute | solution.py:39
  10.3 1.8 %collective-permute-done.1 = f32[2,4,1024]{2,1,0:T(4,128)S(1)} collective-permute-done((f32[2,4,1024]{2,1,0:T(4,128)}, f32[2,4,1024]{2,1,0:T(4,128)S(1)}, u32[]{:S(2)}, u32[]{:S(2)}) %collective-permute-start.1) | collective-permute-done | bytes 32800 | tf_op jit(solution)/shard_map/ppermute | solution.py:39
  12.1 2.5 %collective-permute-start.5 = (f32[4,8,1024]{2,1,0:T(8,128)S(1)}, f32[4,8,1024]{2,1,0:T(8,128)S(1)}, u32[]{:S(2)}, u32[]{:S(2)}) collective-permute-start(f32[4,8,1024]{2,1,0:T(8,128)S(1)} %constant_dynamic-update-slice_fusion.refs_0_), channel_id=1, source_target_pairs={{0,6},{2,4},{4,2},{6,0},{1,7},{3,5},{5,3},{7,1},{8,14},{10,12},{12... | collective-permute-start | bytes 393224 | tf_op jit(solution)/shard_map/ppermute | solution.py:41
  14.6 0.5 collective-permute-start.4
  15.2 0.5 collective-permute-start.3
  15.8 1.6 %copy-done.2 = f32[8,4,128,128]{3,2,1,0:T(8,128)S(1)} copy-done((f32[8,4,128,128]{3,2,1,0:T(8,128)S(1)}, f32[8,4,128,128]{3,2,1,0:T(8,128)}, u32[]{:S(2)}) %copy-start.2) | copy-done | bytes 2097176
  17.4 1.6 %copy-done.3 = f32[8,4,128,128]{3,2,1,0:T(8,128)S(1)} copy-done((f32[8,4,128,128]{3,2,1,0:T(8,128)S(1)}, f32[8,4,128,128]{3,2,1,0:T(8,128)}, u32[]{:S(2)}) %copy-start.3) | copy-done | bytes 2097176
  19.0 0.7 copy-done.5
  19.6 0.7 copy-done.6
  20.3 0.7 copy-done.7
  20.9 1.1 %setup.1 = (s32[12,128]{1,0:T(8,128)S(1)}, s32[8,8]{1,0:T(8,128)S(1)}, f32[8,128]{1,0:T(8,128)S(1)}, f32[32,128,128]{2,1,0:T(8,128)S(1)}, f32[32,128,128]{2,1,0:T(8,128)S(1)}) custom-call(s32[8,8]{1,0:T(8,128)S(1)} %copy-done.5, s32[8]{0:T(128)S(1)} %copy-done.6, s32[3]{0:T(128)S(1)} %pad_add_fusion.where_ref, s32[4]{0:T(128)S(1)} %copy-done.7, ...), custom_call_target="tpu_custom_call" | custom-call | bytes 8388608 | tf_op jit(solution)/shard_map/setup/pallas_call | solution.py:111
  22.1 6.3 %step_0.1 = (f32[129,8,128]{2,1,0:T(8,128)S(1)}, f32[8,1024]{1,0:T(8,128)S(1)}, f32[8,128]{1,0:T(8,128)S(1)}, bf16[64,256,256]{2,1,0:T(8,128)(2,1)S(1)}) custom-call(s32[12,128]{1,0:T(8,128)S(1)} %get-tuple-element.18.items_ref, s32[8,8]{1,0:T(8,128)S(1)} %get-tuple-element.19.places_ref, f32[8,128]{1,0:T(8,128)S(1)} %get-tuple-element.20.turn_ref, ...), custom_call_target="tpu_custom_call" | custom-call | tf_op jit(solution)/shard_map/step_0/pallas_call | solution.py:311
  28.4 0.6 collective-permute-start.10
  29.3 3.5 %collective-permute-start.8 = (f32[8,1024]{1,0:T(8,128)S(1)}, f32[8,1024]{1,0:T(8,128)S(1)}, u32[]{:S(2)}, u32[]{:S(2)}) collective-permute-start(f32[8,1024]{1,0:T(8,128)S(1)} %get-tuple-element.24), channel_id=1, source_target_pairs={{0,8},{8,0},{16,24},{24,16},{1,9},{9,1},{17,25},{25,17},{2,10},{10... | collective-permute-start | bytes 98312 | tf_op jit(solution)/shard_map/ppermute | solution.py:39
  32.8 1.3 %collective-permute-done.10 = f32[8,1024]{1,0:T(8,128)S(1)} collective-permute-done((f32[8,1024]{1,0:T(8,128)S(1)}, f32[8,1024]{1,0:T(8,128)S(1)}, u32[]{:S(2)}, u32[]{:S(2)}) %collective-permute-start.10) | collective-permute-done | bytes 32800 | tf_op jit(solution)/shard_map/ppermute | solution.py:39
  34.2 0.6 collective-permute-done.8
  34.7 2.9 %collective-permute-start.13 = (f32[4,8,1024]{2,1,0:T(8,128)S(1)}, f32[4,8,1024]{2,1,0:T(8,128)S(1)}, u32[]{:S(2)}, u32[]{:S(2)}) collective-permute-start(f32[4,8,1024]{2,1,0:T(8,128)S(1)} %pad_maximum_fusion.refs_0_), channel_id=1, source_target_pairs={{0,6},{2,4},{4,2},{6,0},{1,7},{3,5},{5,3},{7,1},{8,14},{10,12},{12... | collective-permute-start | bytes 393224 | tf_op jit(solution)/shard_map/ppermute | solution.py:41
  37.6 0.7 collective-permute-start.11
  38.3 2.8 %collective-permute-done.13.refs_3_ = f32[4,8,1024]{2,1,0:T(8,128)S(1)} collective-permute-done((f32[4,8,1024]{2,1,0:T(8,128)S(1)}, f32[4,8,1024]{2,1,0:T(8,128)S(1)}, u32[]{:S(2)}, u32[]{:S(2)}) %collective-permute-start.13) | collective-permute-done | bytes 131104 | tf_op jit(solution)/shard_map/ppermute | solution.py:41
  41.1 1.5 %collective-permute-done.12.refs_2_ = f32[4,8,1024]{2,1,0:T(8,128)S(1)} collective-permute-done((f32[4,8,1024]{2,1,0:T(8,128)S(1)}, f32[4,8,1024]{2,1,0:T(8,128)S(1)}, u32[]{:S(2)}, u32[]{:S(2)}) %collective-permute-start.12) | collective-permute-done | bytes 131104 | tf_op jit(solution)/shard_map/ppermute | solution.py:41
  42.6 4.3 %step_1.1 = (f32[129,8,128]{2,1,0:T(8,128)S(1)}, f32[8,1024]{1,0:T(8,128)S(1)}, f32[8,128]{1,0:T(8,128)S(1)}) custom-call(s32[12,128]{1,0:T(8,128)S(1)} %get-tuple-element.18.items_ref, s32[8,8]{1,0:T(8,128)S(1)} %get-tuple-element.19.places_ref, f32[8,128]{1,0:T(8,128)S(1)} %get-tuple-element.20.turn_ref, f32[8,128]{1,0:T(8,128)S(1)} %get-tuple-element.23.info_in_ref, ...), custom_call_target="tpu_custom_call" | custom-call | tf_op jit(solution)/shard_map/step_1/pallas_call | solution.py:311
  46.9 1.2 %collective-permute-start.16 = (f32[8,1024]{1,0:T(8,128)S(1)}, f32[8,1024]{1,0:T(8,128)S(1)}, u32[]{:S(2)}, u32[]{:S(2)}) collective-permute-start(f32[8,1024]{1,0:T(8,128)S(1)} %get-tuple-element.28), channel_id=1, source_target_pairs={{0,24},{8,16},{16,8},{24,0},{1,25},{9,17},{17,9},{25,1},{2,26},{10... | collective-permute-start | bytes 98312 | tf_op jit(solution)/shard_map/ppermute | solution.py:39
  48.1 1.1 %collective-permute-start.15 = (f32[8,1024]{1,0:T(8,128)S(1)}, f32[8,1024]{1,0:T(8,128)S(1)}, u32[]{:S(2)}, u32[]{:S(2)}) collective-permute-start(f32[8,1024]{1,0:T(8,128)S(1)} %get-tuple-element.28), channel_id=1, source_target_pairs={{0,16},{8,24},{16,0},{24,8},{1,17},{9,25},{17,1},{25,9},{2,18},{10... | collective-permute-start | bytes 98312 | tf_op jit(solution)/shard_map/ppermute | solution.py:39
  49.2 2.1 %collective-permute-start.14 = (f32[8,1024]{1,0:T(8,128)S(1)}, f32[8,1024]{1,0:T(8,128)S(1)}, u32[]{:S(2)}, u32[]{:S(2)}) collective-permute-start(f32[8,1024]{1,0:T(8,128)S(1)} %get-tuple-element.28), channel_id=1, source_target_pairs={{0,8},{8,0},{16,24},{24,16},{1,9},{9,1},{17,25},{25,17},{2,10},{10... | collective-permute-start | bytes 98312 | tf_op jit(solution)/shard_map/ppermute | solution.py:39
  51.4 1.3 %collective-permute-done.16 = f32[8,1024]{1,0:T(8,128)S(1)} collective-permute-done((f32[8,1024]{1,0:T(8,128)S(1)}, f32[8,1024]{1,0:T(8,128)S(1)}, u32[]{:S(2)}, u32[]{:S(2)}) %collective-permute-start.16) | collective-permute-done | bytes 32800 | tf_op jit(solution)/shard_map/ppermute | solution.py:39
  52.7 0.8 collective-permute-done.15
  53.6 2.2 %collective-permute-start.19 = (f32[4,8,1024]{2,1,0:T(8,128)S(1)}, f32[4,8,1024]{2,1,0:T(8,128)S(1)}, u32[]{:S(2)}, u32[]{:S(2)}) collective-permute-start(f32[4,8,1024]{2,1,0:T(8,128)S(1)} %pad_maximum_fusion.1.refs_0_), channel_id=1, source_target_pairs={{0,6},{2,4},{4,2},{6,0},{1,7},{3,5},{5,3},{7,1},{8,14},{10,12},{12... | collective-permute-start | bytes 393224 | tf_op jit(solution)/shard_map/ppermute | solution.py:41
  55.8 0.5 collective-permute-start.18
  56.3 0.9 %collective-permute-start.17 = (f32[4,8,1024]{2,1,0:T(8,128)S(1)}, f32[4,8,1024]{2,1,0:T(8,128)S(1)}, u32[]{:S(2)}, u32[]{:S(2)}) collective-permute-start(f32[4,8,1024]{2,1,0:T(8,128)S(1)} %pad_maximum_fusion.1.refs_0_), channel_id=1, source_target_pairs={{0,2},{2,0},{4,6},{6,4},{1,3},{3,1},{5,7},{7,5},{8,10},{10,8},{12,... | collective-permute-start | bytes 393224 | tf_op jit(solution)/shard_map/ppermute | solution.py:41
  57.1 2.4 %collective-permute-done.19.refs_3_ = f32[4,8,1024]{2,1,0:T(8,128)S(1)} collective-permute-done((f32[4,8,1024]{2,1,0:T(8,128)S(1)}, f32[4,8,1024]{2,1,0:T(8,128)S(1)}, u32[]{:S(2)}, u32[]{:S(2)}) %collective-permute-start.19) | collective-permute-done | bytes 131104 | tf_op jit(solution)/shard_map/ppermute | solution.py:41
  59.5 1.4 %collective-permute-done.18.refs_2_ = f32[4,8,1024]{2,1,0:T(8,128)S(1)} collective-permute-done((f32[4,8,1024]{2,1,0:T(8,128)S(1)}, f32[4,8,1024]{2,1,0:T(8,128)S(1)}, u32[]{:S(2)}, u32[]{:S(2)}) %collective-permute-start.18) | collective-permute-done | bytes 131104 | tf_op jit(solution)/shard_map/ppermute | solution.py:41
  61.2 4.8 %step_2.1 = (f32[8,1024]{1,0:T(8,128)S(1)}, f32[8,128]{1,0:T(8,128)S(1)}) custom-call(s32[12,128]{1,0:T(8,128)S(1)} %get-tuple-element.18.items_ref, s32[8,8]{1,0:T(8,128)S(1)} %get-tuple-element.19.places_ref, f32[8,128]{1,0:T(8,128)S(1)} %get-tuple-element.20.turn_ref, f32[8,128]{1,0:T(8,128)S(1)} %get-tuple-element.27.info_in_ref, ...), custom_call_target="tpu_custom_call" | custom-call | tf_op jit(solution)/shard_map/step_2/pallas_call | solution.py:311
  66.0 0.6 copy-done.4
  66.7 1.1 %collective-permute-start.22 = (f32[8,128]{1,0:T(8,128)S(1)}, f32[8,128]{1,0:T(8,128)S(1)}, u32[]{:S(2)}, u32[]{:S(2)}) collective-permute-start(f32[8,128]{1,0:T(8,128)S(1)} %get-tuple-element.30), channel_id=1, source_target_pairs={{0,24},{8,16},{16,8},{24,0},{1,25},{9,17},{17,9},{25,1},{2,26},{10... | collective-permute-start | bytes 12296 | tf_op jit(solution)/shard_map/ppermute | solution.py:39
  67.7 0.9 %collective-permute-start.21 = (f32[8,128]{1,0:T(8,128)S(1)}, f32[8,128]{1,0:T(8,128)S(1)}, u32[]{:S(2)}, u32[]{:S(2)}) collective-permute-start(f32[8,128]{1,0:T(8,128)S(1)} %get-tuple-element.30), channel_id=1, source_target_pairs={{0,16},{8,24},{16,0},{24,8},{1,17},{9,25},{17,1},{25,9},{2,18},{10... | collective-permute-start | bytes 12296 | tf_op jit(solution)/shard_map/ppermute | solution.py:39
  68.6 2.4 %collective-permute-start.20 = (f32[8,128]{1,0:T(8,128)S(1)}, f32[8,128]{1,0:T(8,128)S(1)}, u32[]{:S(2)}, u32[]{:S(2)}) collective-permute-start(f32[8,128]{1,0:T(8,128)S(1)} %get-tuple-element.30), channel_id=1, source_target_pairs={{0,8},{8,0},{16,24},{24,16},{1,9},{9,1},{17,25},{25,17},{2,10},{10... | collective-permute-start | bytes 12296 | tf_op jit(solution)/shard_map/ppermute | solution.py:39
  71.0 1.0 %collective-permute-done.22 = f32[8,128]{1,0:T(8,128)S(1)} collective-permute-done((f32[8,128]{1,0:T(8,128)S(1)}, f32[8,128]{1,0:T(8,128)S(1)}, u32[]{:S(2)}, u32[]{:S(2)}) %collective-permute-start.22) | collective-permute-done | bytes 4128 | tf_op jit(solution)/shard_map/ppermute | solution.py:39
  72.2 0.4 collective-permute-done.20
  72.6 2.6 %collective-permute-start.25 = (f32[4,8,128]{2,1,0:T(8,128)S(1)}, f32[4,8,128]{2,1,0:T(8,128)S(1)}, u32[]{:S(2)}, u32[]{:S(2)}) collective-permute-start(f32[4,8,128]{2,1,0:T(8,128)S(1)} %pad_maximum_fusion.2.refs_0_), channel_id=1, source_target_pairs={{0,6},{2,4},{4,2},{6,0},{1,7},{3,5},{5,3},{7,1},{8,14},{10,12},{12... | collective-permute-start | bytes 49160 | tf_op jit(solution)/shard_map/ppermute | solution.py:41
  75.2 0.9 %collective-permute-start.23 = (f32[4,8,128]{2,1,0:T(8,128)S(1)}, f32[4,8,128]{2,1,0:T(8,128)S(1)}, u32[]{:S(2)}, u32[]{:S(2)}) collective-permute-start(f32[4,8,128]{2,1,0:T(8,128)S(1)} %pad_maximum_fusion.2.refs_0_), channel_id=1, source_target_pairs={{0,2},{2,0},{4,6},{6,4},{1,3},{3,1},{5,7},{7,5},{8,10},{10,8},{12,... | collective-permute-start | bytes 49160 | tf_op jit(solution)/shard_map/ppermute | solution.py:41
  76.1 1.1 %collective-permute-done.25.refs_3_ = f32[4,8,128]{2,1,0:T(8,128)S(1)} collective-permute-done((f32[4,8,128]{2,1,0:T(8,128)S(1)}, f32[4,8,128]{2,1,0:T(8,128)S(1)}, u32[]{:S(2)}, u32[]{:S(2)}) %collective-permute-start.25) | collective-permute-done | bytes 16416 | tf_op jit(solution)/shard_map/ppermute | solution.py:41
  77.3 1.7 %collective-permute-done.24.refs_2_ = f32[4,8,128]{2,1,0:T(8,128)S(1)} collective-permute-done((f32[4,8,128]{2,1,0:T(8,128)S(1)}, f32[4,8,128]{2,1,0:T(8,128)S(1)}, u32[]{:S(2)}, u32[]{:S(2)}) %collective-permute-start.24) | collective-permute-done | bytes 16416 | tf_op jit(solution)/shard_map/ppermute | solution.py:41
  79.0 0.6 copy-done.10
  79.6 2.8 %final.1 = (f32[2,4,1024]{2,1,0:T(4,128)}, f32[1,4]{1,0:T(1,128)}) custom-call(f32[4,8,128]{2,1,0:T(8,128)} %copy-done.8, f32[4,8,128]{2,1,0:T(8,128)} %copy-done.11, f32[4,8,128]{2,1,0:T(8,128)} %copy-done.10, f32[4,8,128]{2,1,0:T(8,128)} %copy-done.9, f32[129,8,128]{2,1,0:T(8,128)} %copy-done, f32[129,8,128]{2,1,0:T(8,128)} %copy-done.1, f32[8,1024]{1,0:T(8,128)} %copy-done.4), custom_call_target="tpu_custom_call" | custom-call | tf_op jit(solution)/shard_map/final/pallas_call | solution.py:394
  (46 shorter events, 1.4 us)
Async XLA Ops:
  0.6 21.4 %collective-permute-start.6 = (f32[32,128,128]{2,1,0:T(8,128)}, f32[32,128,128]{2,1,0:T(8,128)S(1)}, u32[]{:S(2)}, u32[]{:S(2)}) collective-permute-start(f32[32,128,128]{2,1,0:T(8,128)} %bitcast.18), channel_id=1, source_target_pairs={{0,1},{1,0},{2,3},{3,2},{4,5},{5,4},{6,7},{7,6},{8,9},{9,8},{10,11... | collective-permute-start | bytes 6291464 | tf_op jit(solution)/shard_map/ppermute | solution.py:420
  1.1 20.9 %collective-permute-start.7 = (f32[32,128,128]{2,1,0:T(8,128)}, f32[32,128,128]{2,1,0:T(8,128)}, u32[]{:S(2)}, u32[]{:S(2)}) collective-permute-start(f32[32,128,128]{2,1,0:T(8,128)} %bitcast.20), channel_id=1, source_target_pairs={{0,1},{1,0},{2,3},{3,2},{4,5},{5,4},{6,7},{7,6},{8,9},{9,8},{10,11... | collective-permute-start | bytes 6291464 | tf_op jit(solution)/shard_map/ppermute | solution.py:421
  1.2 6.4 %collective-permute-start = (f32[2,4,1024]{2,1,0:T(4,128)}, f32[2,4,1024]{2,1,0:T(4,128)S(1)}, u32[]{:S(2)}, u32[]{:S(2)}) collective-permute-start(f32[2,4,1024]{2,1,0:T(4,128)} %param.6), channel_id=1, source_target_pairs={{0,8},{8,0},{16,24},{24,16},{1,9},{9,1},{17,25},{25,17},{2,10},{10... | collective-permute-start | bytes 98312 | tf_op jit(solution)/shard_map/ppermute | solution.py:39
  4.2 6.1 %collective-permute-start.2 = (f32[2,4,1024]{2,1,0:T(4,128)}, f32[2,4,1024]{2,1,0:T(4,128)S(1)}, u32[]{:S(2)}, u32[]{:S(2)}) collective-permute-start(f32[2,4,1024]{2,1,0:T(4,128)} %param.6), channel_id=1, source_target_pairs={{0,24},{8,16},{16,8},{24,0},{1,25},{9,17},{17,9},{25,1},{2,26},{10... | collective-permute-start | bytes 98312 | tf_op jit(solution)/shard_map/ppermute | solution.py:39
  6.7 5.4 %collective-permute-start.1 = (f32[2,4,1024]{2,1,0:T(4,128)}, f32[2,4,1024]{2,1,0:T(4,128)S(1)}, u32[]{:S(2)}, u32[]{:S(2)}) collective-permute-start(f32[2,4,1024]{2,1,0:T(4,128)} %param.6), channel_id=1, source_target_pairs={{0,16},{8,24},{16,0},{24,8},{1,17},{9,25},{17,1},{25,9},{2,18},{10... | collective-permute-start | bytes 98312 | tf_op jit(solution)/shard_map/ppermute | solution.py:39
  12.1 9.9 %collective-permute-start.5 = (f32[4,8,1024]{2,1,0:T(8,128)S(1)}, f32[4,8,1024]{2,1,0:T(8,128)S(1)}, u32[]{:S(2)}, u32[]{:S(2)}) collective-permute-start(f32[4,8,1024]{2,1,0:T(8,128)S(1)} %constant_dynamic-update-slice_fusion.refs_0_), channel_id=1, source_target_pairs={{0,6},{2,4},{4,2},{6,0},{1,7},{3,5},{5,3},{7,1},{8,14},{10,12},{12... | collective-permute-start | bytes 393224 | tf_op jit(solution)/shard_map/ppermute | solution.py:41
  14.6 7.4 %collective-permute-start.4 = (f32[4,8,1024]{2,1,0:T(8,128)S(1)}, f32[4,8,1024]{2,1,0:T(8,128)S(1)}, u32[]{:S(2)}, u32[]{:S(2)}) collective-permute-start(f32[4,8,1024]{2,1,0:T(8,128)S(1)} %constant_dynamic-update-slice_fusion.refs_0_), channel_id=1, source_target_pairs={{0,4},{2,6},{4,0},{6,2},{1,5},{3,7},{5,1},{7,3},{8,12},{10,14},{12... | collective-permute-start | bytes 393224 | tf_op jit(solution)/shard_map/ppermute | solution.py:41
  15.2 6.9 %collective-permute-start.3 = (f32[4,8,1024]{2,1,0:T(8,128)S(1)}, f32[4,8,1024]{2,1,0:T(8,128)S(1)}, u32[]{:S(2)}, u32[]{:S(2)}) collective-permute-start(f32[4,8,1024]{2,1,0:T(8,128)S(1)} %constant_dynamic-update-slice_fusion.refs_0_), channel_id=1, source_target_pairs={{0,2},{2,0},{4,6},{6,4},{1,3},{3,1},{5,7},{7,5},{8,10},{10,8},{12,... | collective-permute-start | bytes 393224 | tf_op jit(solution)/shard_map/ppermute | solution.py:41
  15.8 1.6 %copy-start.2 = (f32[8,4,128,128]{3,2,1,0:T(8,128)S(1)}, f32[8,4,128,128]{3,2,1,0:T(8,128)}, u32[]{:S(2)}) copy-start(f32[8,4,128,128]{3,2,1,0:T(8,128)} %param.7) | copy-start | bytes 6291460
  17.4 1.6 %copy-start.3 = (f32[8,4,128,128]{3,2,1,0:T(8,128)S(1)}, f32[8,4,128,128]{3,2,1,0:T(8,128)}, u32[]{:S(2)}) copy-start(f32[8,4,128,128]{3,2,1,0:T(8,128)} %param.8) | copy-start | bytes 6291460
  19.0 0.7 copy-start.5
  19.6 0.7 copy-start.6
  20.3 0.7 copy-start.7
  28.4 32.9 %copy-start = (f32[129,8,128]{2,1,0:T(8,128)}, f32[129,8,128]{2,1,0:T(8,128)S(1)}, u32[]{:S(2)}) copy-start(f32[129,8,128]{2,1,0:T(8,128)S(1)} %get-tuple-element.25.refs_4_) | copy-start | bytes 1585156
  28.4 5.8 %collective-permute-start.10 = (f32[8,1024]{1,0:T(8,128)S(1)}, f32[8,1024]{1,0:T(8,128)S(1)}, u32[]{:S(2)}, u32[]{:S(2)}) collective-permute-start(f32[8,1024]{1,0:T(8,128)S(1)} %get-tuple-element.24), channel_id=1, source_target_pairs={{0,24},{8,16},{16,8},{24,0},{1,25},{9,17},{17,9},{25,1},{2,26},{10... | collective-permute-start | bytes 98312 | tf_op jit(solution)/shard_map/ppermute | solution.py:39
  28.9 5.2 %collective-permute-start.9 = (f32[8,1024]{1,0:T(8,128)S(1)}, f32[8,1024]{1,0:T(8,128)S(1)}, u32[]{:S(2)}, u32[]{:S(2)}) collective-permute-start(f32[8,1024]{1,0:T(8,128)S(1)} %get-tuple-element.24), channel_id=1, source_target_pairs={{0,16},{8,24},{16,0},{24,8},{1,17},{9,25},{17,1},{25,9},{2,18},{10... | collective-permute-start | bytes 98312 | tf_op jit(solution)/shard_map/ppermute | solution.py:39
  29.3 5.4 %collective-permute-start.8 = (f32[8,1024]{1,0:T(8,128)S(1)}, f32[8,1024]{1,0:T(8,128)S(1)}, u32[]{:S(2)}, u32[]{:S(2)}) collective-permute-start(f32[8,1024]{1,0:T(8,128)S(1)} %get-tuple-element.24), channel_id=1, source_target_pairs={{0,8},{8,0},{16,24},{24,16},{1,9},{9,1},{17,25},{25,17},{2,10},{10... | collective-permute-start | bytes 98312 | tf_op jit(solution)/shard_map/ppermute | solution.py:39
  34.7 6.4 %collective-permute-start.13 = (f32[4,8,1024]{2,1,0:T(8,128)S(1)}, f32[4,8,1024]{2,1,0:T(8,128)S(1)}, u32[]{:S(2)}, u32[]{:S(2)}) collective-permute-start(f32[4,8,1024]{2,1,0:T(8,128)S(1)} %pad_maximum_fusion.refs_0_), channel_id=1, source_target_pairs={{0,6},{2,4},{4,2},{6,0},{1,7},{3,5},{5,3},{7,1},{8,14},{10,12},{12... | collective-permute-start | bytes 393224 | tf_op jit(solution)/shard_map/ppermute | solution.py:41
  37.6 5.0 %collective-permute-start.12 = (f32[4,8,1024]{2,1,0:T(8,128)S(1)}, f32[4,8,1024]{2,1,0:T(8,128)S(1)}, u32[]{:S(2)}, u32[]{:S(2)}) collective-permute-start(f32[4,8,1024]{2,1,0:T(8,128)S(1)} %pad_maximum_fusion.refs_0_), channel_id=1, source_target_pairs={{0,4},{2,6},{4,0},{6,2},{1,5},{3,7},{5,1},{7,3},{8,12},{10,14},{12... | collective-permute-start | bytes 393224 | tf_op jit(solution)/shard_map/ppermute | solution.py:41
  37.6 5.0 %collective-permute-start.11 = (f32[4,8,1024]{2,1,0:T(8,128)S(1)}, f32[4,8,1024]{2,1,0:T(8,128)S(1)}, u32[]{:S(2)}, u32[]{:S(2)}) collective-permute-start(f32[4,8,1024]{2,1,0:T(8,128)S(1)} %pad_maximum_fusion.refs_0_), channel_id=1, source_target_pairs={{0,2},{2,0},{4,6},{6,4},{1,3},{3,1},{5,7},{7,5},{8,10},{10,8},{12,... | collective-permute-start | bytes 393224 | tf_op jit(solution)/shard_map/ppermute | solution.py:41
  46.9 19.1 %copy-start.1 = (f32[129,8,128]{2,1,0:T(8,128)}, f32[129,8,128]{2,1,0:T(8,128)S(1)}, u32[]{:S(2)}) copy-start(f32[129,8,128]{2,1,0:T(8,128)S(1)} %get-tuple-element.29.refs_5_) | copy-start | bytes 1585156
  46.9 5.8 %collective-permute-start.16 = (f32[8,1024]{1,0:T(8,128)S(1)}, f32[8,1024]{1,0:T(8,128)S(1)}, u32[]{:S(2)}, u32[]{:S(2)}) collective-permute-start(f32[8,1024]{1,0:T(8,128)S(1)} %get-tuple-element.28), channel_id=1, source_target_pairs={{0,24},{8,16},{16,8},{24,0},{1,25},{9,17},{17,9},{25,1},{2,26},{10... | collective-permute-start | bytes 98312 | tf_op jit(solution)/shard_map/ppermute | solution.py:39
  48.1 5.4 %collective-permute-start.15 = (f32[8,1024]{1,0:T(8,128)S(1)}, f32[8,1024]{1,0:T(8,128)S(1)}, u32[]{:S(2)}, u32[]{:S(2)}) collective-permute-start(f32[8,1024]{1,0:T(8,128)S(1)} %get-tuple-element.28), channel_id=1, source_target_pairs={{0,16},{8,24},{16,0},{24,8},{1,17},{9,25},{17,1},{25,9},{2,18},{10... | collective-permute-start | bytes 98312 | tf_op jit(solution)/shard_map/ppermute | solution.py:39
  49.2 4.3 %collective-permute-start.14 = (f32[8,1024]{1,0:T(8,128)S(1)}, f32[8,1024]{1,0:T(8,128)S(1)}, u32[]{:S(2)}, u32[]{:S(2)}) collective-permute-start(f32[8,1024]{1,0:T(8,128)S(1)} %get-tuple-element.28), channel_id=1, source_target_pairs={{0,8},{8,0},{16,24},{24,16},{1,9},{9,1},{17,25},{25,17},{2,10},{10... | collective-permute-start | bytes 98312 | tf_op jit(solution)/shard_map/ppermute | solution.py:39
  53.6 5.9 %collective-permute-start.19 = (f32[4,8,1024]{2,1,0:T(8,128)S(1)}, f32[4,8,1024]{2,1,0:T(8,128)S(1)}, u32[]{:S(2)}, u32[]{:S(2)}) collective-permute-start(f32[4,8,1024]{2,1,0:T(8,128)S(1)} %pad_maximum_fusion.1.refs_0_), channel_id=1, source_target_pairs={{0,6},{2,4},{4,2},{6,0},{1,7},{3,5},{5,3},{7,1},{8,14},{10,12},{12... | collective-permute-start | bytes 393224 | tf_op jit(solution)/shard_map/ppermute | solution.py:41
  55.8 5.2 %collective-permute-start.18 = (f32[4,8,1024]{2,1,0:T(8,128)S(1)}, f32[4,8,1024]{2,1,0:T(8,128)S(1)}, u32[]{:S(2)}, u32[]{:S(2)}) collective-permute-start(f32[4,8,1024]{2,1,0:T(8,128)S(1)} %pad_maximum_fusion.1.refs_0_), channel_id=1, source_target_pairs={{0,4},{2,6},{4,0},{6,2},{1,5},{3,7},{5,1},{7,3},{8,12},{10,14},{12... | collective-permute-start | bytes 393224 | tf_op jit(solution)/shard_map/ppermute | solution.py:41
  56.3 5.0 %collective-permute-start.17 = (f32[4,8,1024]{2,1,0:T(8,128)S(1)}, f32[4,8,1024]{2,1,0:T(8,128)S(1)}, u32[]{:S(2)}, u32[]{:S(2)}) collective-permute-start(f32[4,8,1024]{2,1,0:T(8,128)S(1)} %pad_maximum_fusion.1.refs_0_), channel_id=1, source_target_pairs={{0,2},{2,0},{4,6},{6,4},{1,3},{3,1},{5,7},{7,5},{8,10},{10,8},{12,... | collective-permute-start | bytes 393224 | tf_op jit(solution)/shard_map/ppermute | solution.py:41
  66.0 0.6 copy-start.4
  66.7 5.4 %collective-permute-start.22 = (f32[8,128]{1,0:T(8,128)S(1)}, f32[8,128]{1,0:T(8,128)S(1)}, u32[]{:S(2)}, u32[]{:S(2)}) collective-permute-start(f32[8,128]{1,0:T(8,128)S(1)} %get-tuple-element.30), channel_id=1, source_target_pairs={{0,24},{8,16},{16,8},{24,0},{1,25},{9,17},{17,9},{25,1},{2,26},{10... | collective-permute-start | bytes 12296 | tf_op jit(solution)/shard_map/ppermute | solution.py:39
  67.7 4.5 %collective-permute-start.21 = (f32[8,128]{1,0:T(8,128)S(1)}, f32[8,128]{1,0:T(8,128)S(1)}, u32[]{:S(2)}, u32[]{:S(2)}) collective-permute-start(f32[8,128]{1,0:T(8,128)S(1)} %get-tuple-element.30), channel_id=1, source_target_pairs={{0,16},{8,24},{16,0},{24,8},{1,17},{9,25},{17,1},{25,9},{2,18},{10... | collective-permute-start | bytes 12296 | tf_op jit(solution)/shard_map/ppermute | solution.py:39
  68.6 4.0 %collective-permute-start.20 = (f32[8,128]{1,0:T(8,128)S(1)}, f32[8,128]{1,0:T(8,128)S(1)}, u32[]{:S(2)}, u32[]{:S(2)}) collective-permute-start(f32[8,128]{1,0:T(8,128)S(1)} %get-tuple-element.30), channel_id=1, source_target_pairs={{0,8},{8,0},{16,24},{24,16},{1,9},{9,1},{17,25},{25,17},{2,10},{10... | collective-permute-start | bytes 12296 | tf_op jit(solution)/shard_map/ppermute | solution.py:39
  72.6 6.3 %copy-start.8 = (f32[4,8,128]{2,1,0:T(8,128)}, f32[4,8,128]{2,1,0:T(8,128)S(1)}, u32[]{:S(2)}) copy-start(f32[4,8,128]{2,1,0:T(8,128)S(1)} %pad_maximum_fusion.2.refs_0_) | copy-start | bytes 49156
  72.6 4.6 %collective-permute-start.25 = (f32[4,8,128]{2,1,0:T(8,128)S(1)}, f32[4,8,128]{2,1,0:T(8,128)S(1)}, u32[]{:S(2)}, u32[]{:S(2)}) collective-permute-start(f32[4,8,128]{2,1,0:T(8,128)S(1)} %pad_maximum_fusion.2.refs_0_), channel_id=1, source_target_pairs={{0,6},{2,4},{4,2},{6,0},{1,7},{3,5},{5,3},{7,1},{8,14},{10,12},{12... | collective-permute-start | bytes 49160 | tf_op jit(solution)/shard_map/ppermute | solution.py:41
  75.2 3.7 %collective-permute-start.24 = (f32[4,8,128]{2,1,0:T(8,128)S(1)}, f32[4,8,128]{2,1,0:T(8,128)S(1)}, u32[]{:S(2)}, u32[]{:S(2)}) collective-permute-start(f32[4,8,128]{2,1,0:T(8,128)S(1)} %pad_maximum_fusion.2.refs_0_), channel_id=1, source_target_pairs={{0,4},{2,6},{4,0},{6,2},{1,5},{3,7},{5,1},{7,3},{8,12},{10,14},{12... | collective-permute-start | bytes 49160 | tf_op jit(solution)/shard_map/ppermute | solution.py:41
  75.2 3.7 %collective-permute-start.23 = (f32[4,8,128]{2,1,0:T(8,128)S(1)}, f32[4,8,128]{2,1,0:T(8,128)S(1)}, u32[]{:S(2)}, u32[]{:S(2)}) collective-permute-start(f32[4,8,128]{2,1,0:T(8,128)S(1)} %pad_maximum_fusion.2.refs_0_), channel_id=1, source_target_pairs={{0,2},{2,0},{4,6},{6,4},{1,3},{3,1},{5,7},{7,5},{8,10},{10,8},{12,... | collective-permute-start | bytes 49160 | tf_op jit(solution)/shard_map/ppermute | solution.py:41
  77.3 1.7 %copy-start.9 = (f32[4,8,128]{2,1,0:T(8,128)}, f32[4,8,128]{2,1,0:T(8,128)S(1)}, u32[]{:S(2)}) copy-start(f32[4,8,128]{2,1,0:T(8,128)S(1)} %collective-permute-done.25.refs_3_) | copy-start | bytes 49156
  79.0 0.6 copy-start.10
  79.0 0.6 copy-start.11

commit v7 on v6

--- a/solution.py
+++ b/solution.py
@@ -34,19 +34,30 @@
     return lax.rem(me - other + size, size)
 
 
-def gather_rows(rows, line, plane):
+def gather_rows(rows, line, plane, between=()):
     parts = rows.size // rows.shape[-1]
     held = [rows] + [lax.ppermute(rows, "line", perm) for perm in partner_steps(line)]
     whole_line = jnp.stack(held).reshape(line, parts, rows.shape[-1])
-    return [whole_line] + [lax.ppermute(whole_line, "place", perm) for perm in partner_steps(plane)]
-
-
-def setup_kernel(
-    line, plane, freqs, pattern_ref, counts_ref, where_ref, ids_ref, g_ref, c_ref,
-    items_ref, places_ref, turn_ref, g_out_ref, c_out_ref, sems,
-):
-    row_blocks, slots = pattern_ref.shape
-    own_slots = slots // freqs
+    if between:
+        whole_line, *between = lax.optimization_barrier((whole_line, *between))
+    held = [whole_line] + [lax.ppermute(whole_line, "place", perm) for perm in partner_steps(plane)]
+    return (held, *between) if between else held
+
+
+def gather_tiles(tile, line, plane):
+    if (line & (line - 1)) or (plane & (plane - 1)):
+        return jnp.concatenate(gather_rows(tile, line, plane))
+    tiles = tile[None]
+    for axis, size in (("line", line), ("place", plane)):
+        d = 1
+        while d < size:
+            other = lax.ppermute(tiles, axis, [(i, i ^ d) for i in range(size)])
+            tiles = jnp.concatenate([tiles, other])
+            d *= 2
+    return tiles
+
+
+def near_kernel(g_ref, c_ref, g_out_ref, c_out_ref, sems):
     pieces = sems.shape[1]
     part = g_ref.shape[0] // pieces
     copies = []
@@ -55,7 +66,30 @@
             at = pl.ds(i * part, part)
             copies.append(pltpu.make_async_copy(source.at[at], target.at[at], sems.at[m, i]))
             copies[-1].start()
-
+    for copy in copies:
+        copy.wait()
+
+
+def bring_near(g_own, c_own):
+    vmem, far = pl.BlockSpec(memory_space=pltpu.VMEM), pl.BlockSpec(memory_space=pl.ANY)
+    blocks = jax.ShapeDtypeStruct(g_own.shape, jnp.float32)
+    return pl.pallas_call(
+        near_kernel,
+        in_specs=[far] * 2,
+        out_specs=[vmem] * 2,
+        out_shape=[blocks] * 2,
+        scratch_shapes=[pltpu.SemaphoreType.DMA((2, math.gcd(g_own.shape[0], 8)))],
+        compiler_params=pltpu.CompilerParams(vmem_limit_bytes=VMEM_LIMIT),
+        cost_estimate=pl.CostEstimate(flops=0, bytes_accessed=16 * g_own.size, transcendentals=0),
+        name="near",
+    )(g_own, c_own)
+
+
+def setup_kernel(
+    line, plane, freqs, pattern_ref, counts_ref, where_ref, ids_ref, items_ref, places_ref, turn_ref
+):
+    row_blocks, slots = pattern_ref.shape
+    own_slots = slots // freqs
     order = lax.broadcasted_iota(jnp.int32, (8, LANES), 1)
     freq = where_ref[2]
     for table, d in enumerate(list(range(freqs)) + [None]):
@@ -99,31 +133,21 @@
         ids = jnp.where(lax.rem(row_at, half) == f, ids_ref[f], ids)
     angular = 0.2 * jnp.exp(ids.astype(jnp.float32) * (math.log(8.0) / 1000.0))
     turn_ref[...] = jnp.where(row_at < half, -angular, angular)
-    for copy in copies:
-        copy.wait()
-
-
-def run_setup(pattern, counts, where, freq_ids, g_own, c_own, line, plane, freqs):
+
+
+def run_setup(pattern, counts, where, freq_ids, line, plane, freqs):
     smem, vmem = pl.BlockSpec(memory_space=pltpu.SMEM), pl.BlockSpec(memory_space=pltpu.VMEM)
-    far = pl.BlockSpec(memory_space=pl.ANY)
-    blocks = jax.ShapeDtypeStruct(g_own.shape, jnp.float32)
-    pieces = math.gcd(g_own.shape[0], 8)
     return pl.pallas_call(
         functools.partial(setup_kernel, line, plane, freqs),
-        in_specs=[vmem, smem, smem, smem, far, far],
-        out_specs=[vmem] * 5,
+        in_specs=[vmem, smem, smem, smem],
+        out_specs=[vmem] * 3,
         out_shape=[
             jax.ShapeDtypeStruct((4 * (freqs + 1), LANES), jnp.int32),
             jax.ShapeDtypeStruct(pattern.shape, jnp.int32),
             jax.ShapeDtypeStruct((2 * freq_ids.shape[0], LANES), jnp.float32),
-            blocks,
-            blocks,
         ],
-        scratch_shapes=[pltpu.SemaphoreType.DMA((2, pieces))],
-        compiler_params=pltpu.CompilerParams(vmem_limit_bytes=VMEM_LIMIT),
-        cost_estimate=pl.CostEstimate(flops=0, bytes_accessed=16 * g_own.size, transcendentals=0),
         name="setup",
-    )(pattern, counts, where, freq_ids, g_own, c_own)
+    )(pattern, counts, where, freq_ids)
 
 
 def lane_sum(x):
@@ -272,7 +296,8 @@
     if step == ITERS - 1:
         w = local_ref[...]
         zs = [jnp.concatenate([p[b] for b in range(row_blocks)], axis=1) for p in (*prev, z_ref)]
-        own_ref[...] = zs[-1]
+        for i, z in enumerate(zs):
+            own_ref[i] = z
         values = [lane_sum(z * w) for z in zs]
         gram = [[lane_sum(zs[i] * zs[j]) for j in range(i + 1)] for i in range(ITERS)]
         shares = []
@@ -298,7 +323,8 @@
     z = (plane * line * row_blocks + 1, parts, size)
     tile = jax.ShapeDtypeStruct((parts, LANES), jnp.float32)
     own = jax.ShapeDtypeStruct((parts, rows), jnp.float32)
-    out_shape = [own, tile] if step == ITERS - 1 else [jax.ShapeDtypeStruct(z, jnp.float32), own, tile]
+    owns = jax.ShapeDtypeStruct((ITERS, parts, rows), jnp.float32)
+    out_shape = [owns, tile] if step == ITERS - 1 else [jax.ShapeDtypeStruct(z, jnp.float32), own, tile]
     scratch_shapes = [
         pltpu.VMEM((slots, size, LANES), jnp.bfloat16),
         pltpu.VMEM((row_blocks + 1, size, LANES), jnp.bfloat16),
@@ -319,16 +345,17 @@
     )(*lists, turn, info, *lines, *prev, *blocks)
 
 
-def final_kernel(plane, *refs):
-    tiles, krylov = refs[:plane], refs[plane : plane + ITERS]
-    out_ref, residual_ref = refs[plane + ITERS :]
-    line, parts, _ = tiles[0].shape
+def final_kernel(tiles_ref, own_ref, out_ref, residual_ref):
+    devices, parts, _ = tiles_ref.shape
     fit = LANES // parts
-    stacked = [tiles[q][i] for q in range(plane) for i in range(line)]
-    sets = [
-        jnp.transpose(jnp.concatenate(stacked[at : at + fit], axis=0)) for at in range(0, len(stacked), fit)
-    ]
-    info = jnp.transpose(jnp.concatenate([tiles[0][0]] * fit, axis=0))
+    tiles = [tiles_ref[i] for i in range(devices)]
+    sets = [jnp.transpose(jnp.concatenate(tiles[at : at + fit], axis=0)) for at in range(0, devices, fit)]
+    sums = tiles
+    while len(sums) > 1:
+        sums = [x + y for x, y in zip(sums[::2], sums[1::2])] + sums[len(sums) // 2 * 2 :]
+    total = sums[0] + pltpu.roll(sums[0], parts // 2, 0)
+    lane = lax.broadcasted_iota(jnp.int32, total.shape, 1)
+    info = jnp.transpose(jnp.concatenate([jnp.where(lane < SHARES, tiles[0], total)] * fit, axis=0))
 
     def all_devices(shares):
         total = sum(shares[1:], shares[0])
@@ -343,7 +370,7 @@
 
     zero = jnp.zeros((8, LANES), jnp.float32)
     norm, h00, h10, h01, h11, h21 = [row(info, i) for i in range(6)]
-    last = [all_devices([row(s, SHARES + i) for s in sets]) for i in range(ITERS)]
+    last = [row(info, SHARES + i) for i in range(ITERS)]
     shares = []
     for s in sets:
         off = [last[i] - row(s, SHARES + ITERS + i) for i in range(ITERS)]
@@ -379,28 +406,25 @@
     columns = jnp.transpose(
         jnp.concatenate([y for y in coef_y] + [jnp.zeros((LANES - 8 * ITERS, LANES), jnp.float32)], axis=0)
     )[:parts]
-    size = krylov[0].shape[-1]
-    wide = [jnp.broadcast_to(columns[:, 8 * m : 8 * m + 1], (parts, size)) for m in range(ITERS)]
-    for b in range(out_ref.shape[-1] // size):
-        at = slice(b * size, (b + 1) * size)
-        x = wide[-1] * krylov[-1][:, at] + sum(y * z[b] for y, z in zip(wide[:-1], krylov[:-1]))
-        out_ref[0, :, at] = x[: parts // 2]
-        out_ref[1, :, at] = x[parts // 2 :]
-
-
-def run_final(tiles, krylov):
-    parts, rows = krylov[-1].shape
+    rows = own_ref.shape[-1]
+    x = sum(jnp.broadcast_to(columns[:, 8 * m : 8 * m + 1], (parts, rows)) * own_ref[m] for m in range(ITERS))
+    out_ref[0] = x[: parts // 2]
+    out_ref[1] = x[parts // 2 :]
+
+
+def run_final(tiles, own):
+    _, parts, rows = own.shape
     vmem = pl.BlockSpec(memory_space=pltpu.VMEM)
     return pl.pallas_call(
-        functools.partial(final_kernel, len(tiles)),
-        in_specs=[vmem] * (len(tiles) + ITERS),
+        final_kernel,
+        in_specs=[vmem] * 2,
         out_specs=[vmem] * 2,
         out_shape=[
             jax.ShapeDtypeStruct((2, parts // 2, rows), jnp.float32),
             jax.ShapeDtypeStruct((1, parts // 2), jnp.float32),
         ],
         name="final",
-    )(*tiles, *krylov)
+    )(tiles, own)
 
 
 def make_shards(line, plane, freqs):
@@ -411,9 +435,8 @@
         where = jnp.stack([lax.axis_index(name) for name in ("line", "place", "freq")]).astype(jnp.int32)
         stored = (row_blocks * own_slots, size, size)
         g_own, c_own = g_blocks.reshape(stored), c_blocks.reshape(stored)
-        *lists, turn, g_near, c_near = run_setup(
-            pattern, counts, where, freq_ids, g_own, c_own, line, plane, freqs
-        )
+        *lists, turn = run_setup(pattern, counts, where, freq_ids, line, plane, freqs)
+        first_lines, g_near, c_near = gather_rows(excitation, line, plane, bring_near(g_own, c_own))
         g_parts, c_parts = [g_near], [c_near]
         for d in range(1, freqs):
             perm = [(i, (i + d) % freqs) for i in range(freqs)]
@@ -421,14 +444,12 @@
             c_parts.append(lax.ppermute(c_own, "freq", perm))
         info = jnp.zeros((parts, LANES), jnp.float32)
         krylov = []
-        rows = excitation
         blocks = g_parts + c_parts
         for step in range(ITERS):
-            lines = gather_rows(rows, line, plane)
+            lines = gather_rows(rows, line, plane) if step else first_lines
             result = run_step(step, lists, turn, info, lines, krylov, blocks, freqs)
             if step == ITERS - 1:
-                rows, info = result
-                krylov.append(rows)
+                own, info = result
             elif step == 0:
                 z, rows, info, tiles = result
                 blocks = [tiles]
@@ -436,7 +457,7 @@
             else:
                 z, rows, info = result
                 krylov.append(z)
-        answer, residual = run_final(gather_rows(info, line, plane), krylov)
+        answer, residual = run_final(gather_tiles(info, line, plane), own)
         return answer, residual.reshape(freq_count)
 
     return shards

time: 82.5 us -> 91.8 us (1.11)
  waiting for transfers between devices: 21.3 us -> 30.1 us
  local copies, waits for them, and re-layouts: 7.26 us -> 13.2 us
  starting transfers between devices: 33.6 us -> 28.4 us
  Pallas kernels: 19.3 us -> 17.9 us
    ppermute x0 -> x4, waiting for transfers between devices: none -> 13.5 us  [gather_tiles(): other = lax.ppermute(tiles, axis, [(i, i ^ d) for i in range(size)])]
    unnamed x27 -> x26, local copies, waits for them, and re-layouts: 6.4 us -> 12.4 us
    ppermute x12 -> x9, waiting for transfers between devices: 10.1 us -> 4.74 us  [gather_rows(): lax.ppermute(rows, 'line', perm)]
    ppermute x12 -> x9, starting transfers between devices: 18.9 us -> 14.5 us  [gather_rows(): lax.ppermute(rows, 'line', perm)]
    ppermute x12 -> x9, starting transfers between devices: 14.1 us -> 11 us  [gather_rows(): lax.ppermute(whole_line, 'place', perm)]
    ppermute x0 -> x4, starting transfers between devices: none -> 2.3 us  [gather_tiles(): other = lax.ppermute(tiles, axis, [(i, i ^ d) for i in range(size)])]
    pallas_call x3, Pallas kernels: 15.4 us -> 13.8 us  [run_step(): pl.pallas_call(functools.partial(step_kernel, step, plane, line, freqs),...]
    ppermute x12 -> x9, waiting for transfers between devices: 11.2 us -> 11.9 us  [gather_rows(): lax.ppermute(whole_line, 'place', perm)]
  transfers between devices with their start and end apart: 26 -> 24, of which waited for: 17 -> 17; matrix products, arithmetic and copies ran while one was open for 1% -> 2% of each run, Pallas kernels for 1% -> 2%
where the time goes in v7:
time: 91.8 us; the launch traced here: 91.1 us
  waiting for transfers between devices  30.1 us (33%)
  starting transfers between devices  28.4 us (31%)
  Pallas kernels  17.9 us (19%)
  local copies, waits for them, and re-layouts  13.2 us (14%)
    ppermute x9, starting transfers between devices, gather_rows(): lax.ppermute(rows, 'line', perm)  14.5 us
    pallas_call x3, Pallas kernels, run_step(): pl.pallas_call(functools.partial(step_kernel, step, plane, line, freqs),...  13.8 us
    ppermute x4, waiting for transfers between devices, gather_tiles(): other = lax.ppermute(tiles, axis, [(i, i ^ d) for i in range(size)])  13.5 us
    unnamed x26, local copies, waits for them, and re-layouts  12.4 us
    ppermute x9, waiting for transfers between devices, gather_rows(): lax.ppermute(whole_line, 'place', perm)  11.9 us
    ppermute x9, starting transfers between devices, gather_rows(): lax.ppermute(whole_line, 'place', perm)  11 us
    ppermute x9, waiting for transfers between devices, gather_rows(): lax.ppermute(rows, 'line', perm)  4.74 us
    ppermute x4, starting transfers between devices, gather_tiles(): other = lax.ppermute(tiles, axis, [(i, i ^ d) for i in range(size)])  2.3 us
  transfers between devices with their start and end apart: 24, of which 17 were waited for; matrix products, arithmetic and copies ran while one was open for 2% of the time, Pallas kernels for 2%

profile of v7, /device:TPU:0, one launch (start us, length us, event | category | flops | bytes accessed | tf_op | source)
XLA Modules:
  0.0 91.1 jit_solution(16114738884197309178)
XLA Ops:
  1.2 3.0 %collective-permute-start = (f32[2,4,1024]{2,1,0:T(4,128)}, f32[2,4,1024]{2,1,0:T(4,128)S(1)}, u32[]{:S(2)}, u32[]{:S(2)}) collective-permute-start(f32[2,4,1024]{2,1,0:T(4,128)} %param.6), channel_id=1, source_target_pairs={{0,8},{8,0},{16,24},{24,16},{1,9},{9,1},{17,25},{25,17},{2,10},{10... | collective-permute-start | bytes 98312 | tf_op jit(solution)/shard_map/ppermute | solution.py:39
  4.2 2.5 %collective-permute-start.2 = (f32[2,4,1024]{2,1,0:T(4,128)}, f32[2,4,1024]{2,1,0:T(4,128)S(1)}, u32[]{:S(2)}, u32[]{:S(2)}) collective-permute-start(f32[2,4,1024]{2,1,0:T(4,128)} %param.6), channel_id=1, source_target_pairs={{0,24},{8,16},{16,8},{24,0},{1,25},{9,17},{17,9},{25,1},{2,26},{10... | collective-permute-start | bytes 98312 | tf_op jit(solution)/shard_map/ppermute | solution.py:39
  6.8 0.8 stack.61
  7.6 1.6 %copy-done = f32[8,4,128,128]{3,2,1,0:T(8,128)S(1)} copy-done((f32[8,4,128,128]{3,2,1,0:T(8,128)S(1)}, f32[8,4,128,128]{3,2,1,0:T(8,128)}, u32[]{:S(2)}) %copy-start) | copy-done | bytes 2097176
  9.2 1.6 %copy-done.1 = f32[8,4,128,128]{3,2,1,0:T(8,128)S(1)} copy-done((f32[8,4,128,128]{3,2,1,0:T(8,128)S(1)}, f32[8,4,128,128]{3,2,1,0:T(8,128)}, u32[]{:S(2)}) %copy-start.1) | copy-done | bytes 2097176
  11.3 1.3 %copy-done.2 = f32[32,128,128]{2,1,0:T(8,128)} copy-done((f32[32,128,128]{2,1,0:T(8,128)}, f32[32,128,128]{2,1,0:T(8,128)S(1)}, u32[]{:S(2)}) %copy-start.2) | copy-done | bytes 2097176
  12.6 1.4 %copy-done.4 = f32[32,128,128]{2,1,0:T(8,128)} copy-done((f32[32,128,128]{2,1,0:T(8,128)}, f32[32,128,128]{2,1,0:T(8,128)S(1)}, u32[]{:S(2)}) %copy-start.4) | copy-done | bytes 2097176
  14.1 2.5 %collective-permute-start.5 = (f32[4,8,1024]{2,1,0:T(8,128)S(1)}, f32[4,8,1024]{2,1,0:T(8,128)S(1)}, u32[]{:S(2)}, u32[]{:S(2)}) collective-permute-start(f32[4,8,1024]{2,1,0:T(8,128)S(1)} %pad_maximum_fusion.refs_0_), channel_id=1, source_target_pairs={{0,6},{2,4},{4,2},{6,0},{1,7},{3,5},{5,3},{7,1},{8,14},{10,12},{12... | collective-permute-start | bytes 393224 | tf_op jit(solution)/shard_map/ppermute | solution.py:43
  17.7 0.7 pad_add_fusion.where_ref
  18.3 1.5 %setup.1 = (s32[12,128]{1,0:T(8,128)}, s32[8,8]{1,0:T(8,128)}, f32[8,128]{1,0:T(8,128)}) custom-call(s32[8,8]{1,0:T(8,128)} %pattern_ref.1, s32[8]{0:T(128)} %counts_ref.1, s32[3]{0:T(128)} %pad_add_fusion.where_ref, s32[4]{0:T(128)} %ids_ref.1), custom_call_target="tpu_custom_call" | custom-call | tf_op jit(solution)/shard_map/setup/pallas_call | solution.py:140
  19.8 0.7 collective-permute-done.5.refs_3_
  20.5 2.3 %collective-permute-done.4.refs_2_ = f32[4,8,1024]{2,1,0:T(8,128)S(1)} collective-permute-done((f32[4,8,1024]{2,1,0:T(8,128)S(1)}, f32[4,8,1024]{2,1,0:T(8,128)S(1)}, u32[]{:S(2)}, u32[]{:S(2)}) %collective-permute-start.4) | collective-permute-done | bytes 131104 | tf_op jit(solution)/shard_map/ppermute | solution.py:43
  22.9 1.6 %copy-done.3 = f32[32,128,128]{2,1,0:T(8,128)S(1)} copy-done((f32[32,128,128]{2,1,0:T(8,128)S(1)}, f32[32,128,128]{2,1,0:T(8,128)}, u32[]{:S(2)}) %copy-start.3) | copy-done | bytes 2097176
  24.5 1.6 %copy-done.5 = f32[32,128,128]{2,1,0:T(8,128)S(1)} copy-done((f32[32,128,128]{2,1,0:T(8,128)S(1)}, f32[32,128,128]{2,1,0:T(8,128)}, u32[]{:S(2)}) %copy-start.5) | copy-done | bytes 2097176
  26.1 0.7 copy-done.7
  26.8 0.7 copy-done.8
  27.5 0.7 copy-done.9
  28.1 5.5 %step_0.1 = (f32[129,8,128]{2,1,0:T(8,128)S(1)}, f32[8,1024]{1,0:T(8,128)S(1)}, f32[8,128]{1,0:T(8,128)S(1)}, bf16[64,256,256]{2,1,0:T(8,128)(2,1)S(1)}) custom-call(s32[12,128]{1,0:T(8,128)S(1)} %copy-done.7, s32[8,8]{1,0:T(8,128)S(1)} %copy-done.8, f32[8,128]{1,0:T(8,128)S(1)} %copy-done.9, f32[8,128]{1,0:T(8,128)S(1)} %broadcast_in_dim.6.info_in_ref, ...), custom_call_target="tpu_custom_call" | custom-call | tf_op jit(solution)/shard_map/step_0/pallas_call | solution.py:337
  33.7 2.1 %collective-permute-start.10 = (f32[8,1024]{1,0:T(8,128)S(1)}, f32[8,1024]{1,0:T(8,128)S(1)}, u32[]{:S(2)}, u32[]{:S(2)}) collective-permute-start(f32[8,1024]{1,0:T(8,128)S(1)} %get-tuple-element.30), channel_id=1, source_target_pairs={{0,24},{8,16},{16,8},{24,0},{1,25},{9,17},{17,9},{25,1},{2,26},{10... | collective-permute-start | bytes 98312 | tf_op jit(solution)/shard_map/ppermute | solution.py:39
  35.8 0.7 collective-permute-start.9
  36.4 1.7 %collective-permute-start.8 = (f32[8,1024]{1,0:T(8,128)S(1)}, f32[8,1024]{1,0:T(8,128)S(1)}, u32[]{:S(2)}, u32[]{:S(2)}) collective-permute-start(f32[8,1024]{1,0:T(8,128)S(1)} %get-tuple-element.30), channel_id=1, source_target_pairs={{0,8},{8,0},{16,24},{24,16},{1,9},{9,1},{17,25},{25,17},{2,10},{10... | collective-permute-start | bytes 98312 | tf_op jit(solution)/shard_map/ppermute | solution.py:39
  38.2 1.4 %collective-permute-done.10 = f32[8,1024]{1,0:T(8,128)S(1)} collective-permute-done((f32[8,1024]{1,0:T(8,128)S(1)}, f32[8,1024]{1,0:T(8,128)S(1)}, u32[]{:S(2)}, u32[]{:S(2)}) %collective-permute-start.10) | collective-permute-done | bytes 32800 | tf_op jit(solution)/shard_map/ppermute | solution.py:39
  39.6 1.1 %collective-permute-done.9 = f32[8,1024]{1,0:T(8,128)S(1)} collective-permute-done((f32[8,1024]{1,0:T(8,128)S(1)}, f32[8,1024]{1,0:T(8,128)S(1)}, u32[]{:S(2)}, u32[]{:S(2)}) %collective-permute-start.9) | collective-permute-done | bytes 32800 | tf_op jit(solution)/shard_map/ppermute | solution.py:39
  40.7 2.2 %collective-permute-start.13 = (f32[4,8,1024]{2,1,0:T(8,128)S(1)}, f32[4,8,1024]{2,1,0:T(8,128)S(1)}, u32[]{:S(2)}, u32[]{:S(2)}) collective-permute-start(f32[4,8,1024]{2,1,0:T(8,128)S(1)} %pad_maximum_fusion.1.refs_0_), channel_id=1, source_target_pairs={{0,6},{2,4},{4,2},{6,0},{1,7},{3,5},{5,3},{7,1},{8,14},{10,12},{12... | collective-permute-start | bytes 393224 | tf_op jit(solution)/shard_map/ppermute | solution.py:43
  42.9 1.7 %collective-permute-start.12 = (f32[4,8,1024]{2,1,0:T(8,128)S(1)}, f32[4,8,1024]{2,1,0:T(8,128)S(1)}, u32[]{:S(2)}, u32[]{:S(2)}) collective-permute-start(f32[4,8,1024]{2,1,0:T(8,128)S(1)} %pad_maximum_fusion.1.refs_0_), channel_id=1, source_target_pairs={{0,4},{2,6},{4,0},{6,2},{1,5},{3,7},{5,1},{7,3},{8,12},{10,14},{12... | collective-permute-start | bytes 393224 | tf_op jit(solution)/shard_map/ppermute | solution.py:43
  44.6 3.0 %collective-permute-done.13.refs_3_ = f32[4,8,1024]{2,1,0:T(8,128)S(1)} collective-permute-done((f32[4,8,1024]{2,1,0:T(8,128)S(1)}, f32[4,8,1024]{2,1,0:T(8,128)S(1)}, u32[]{:S(2)}, u32[]{:S(2)}) %collective-permute-start.13) | collective-permute-done | bytes 131104 | tf_op jit(solution)/shard_map/ppermute | solution.py:43
  47.6 1.3 %collective-permute-done.12.refs_2_ = f32[4,8,1024]{2,1,0:T(8,128)S(1)} collective-permute-done((f32[4,8,1024]{2,1,0:T(8,128)S(1)}, f32[4,8,1024]{2,1,0:T(8,128)S(1)}, u32[]{:S(2)}, u32[]{:S(2)}) %collective-permute-start.12) | collective-permute-done | bytes 131104 | tf_op jit(solution)/shard_map/ppermute | solution.py:43
  48.9 0.7 collective-permute-done.11.refs_1_
  49.6 3.9 %step_1.1 = (f32[129,8,128]{2,1,0:T(8,128)S(1)}, f32[8,1024]{1,0:T(8,128)S(1)}, f32[8,128]{1,0:T(8,128)S(1)}) custom-call(s32[12,128]{1,0:T(8,128)S(1)} %copy-done.7, s32[8,8]{1,0:T(8,128)S(1)} %copy-done.8, f32[8,128]{1,0:T(8,128)S(1)} %copy-done.9, f32[8,128]{1,0:T(8,128)S(1)} %get-tuple-element.29.info_in_ref, ...), custom_call_target="tpu_custom_call" | custom-call | tf_op jit(solution)/shard_map/step_1/pallas_call | solution.py:337
  53.5 1.1 %collective-permute-start.16 = (f32[8,1024]{1,0:T(8,128)S(1)}, f32[8,1024]{1,0:T(8,128)S(1)}, u32[]{:S(2)}, u32[]{:S(2)}) collective-permute-start(f32[8,1024]{1,0:T(8,128)S(1)} %get-tuple-element.34), channel_id=1, source_target_pairs={{0,24},{8,16},{16,8},{24,0},{1,25},{9,17},{17,9},{25,1},{2,26},{10... | collective-permute-start | bytes 98312 | tf_op jit(solution)/shard_map/ppermute | solution.py:39
  54.9 3.0 %collective-permute-start.14 = (f32[8,1024]{1,0:T(8,128)S(1)}, f32[8,1024]{1,0:T(8,128)S(1)}, u32[]{:S(2)}, u32[]{:S(2)}) collective-permute-start(f32[8,1024]{1,0:T(8,128)S(1)} %get-tuple-element.34), channel_id=1, source_target_pairs={{0,8},{8,0},{16,24},{24,16},{1,9},{9,1},{17,25},{25,17},{2,10},{10... | collective-permute-start | bytes 98312 | tf_op jit(solution)/shard_map/ppermute | solution.py:39
  57.9 1.3 %collective-permute-done.16 = f32[8,1024]{1,0:T(8,128)S(1)} collective-permute-done((f32[8,1024]{1,0:T(8,128)S(1)}, f32[8,1024]{1,0:T(8,128)S(1)}, u32[]{:S(2)}, u32[]{:S(2)}) %collective-permute-start.16) | collective-permute-done | bytes 32800 | tf_op jit(solution)/shard_map/ppermute | solution.py:39
  59.3 0.8 collective-permute-done.15
  60.2 1.1 %collective-permute-start.19 = (f32[4,8,1024]{2,1,0:T(8,128)S(1)}, f32[4,8,1024]{2,1,0:T(8,128)S(1)}, u32[]{:S(2)}, u32[]{:S(2)}) collective-permute-start(f32[4,8,1024]{2,1,0:T(8,128)S(1)} %pad_maximum_fusion.2.refs_0_), channel_id=1, source_target_pairs={{0,6},{2,4},{4,2},{6,0},{1,7},{3,5},{5,3},{7,1},{8,14},{10,12},{12... | collective-permute-start | bytes 393224 | tf_op jit(solution)/shard_map/ppermute | solution.py:43
  61.2 1.0 %collective-permute-start.18 = (f32[4,8,1024]{2,1,0:T(8,128)S(1)}, f32[4,8,1024]{2,1,0:T(8,128)S(1)}, u32[]{:S(2)}, u32[]{:S(2)}) collective-permute-start(f32[4,8,1024]{2,1,0:T(8,128)S(1)} %pad_maximum_fusion.2.refs_0_), channel_id=1, source_target_pairs={{0,4},{2,6},{4,0},{6,2},{1,5},{3,7},{5,1},{7,3},{8,12},{10,14},{12... | collective-permute-start | bytes 393224 | tf_op jit(solution)/shard_map/ppermute | solution.py:43
  62.3 1.4 %collective-permute-start.17 = (f32[4,8,1024]{2,1,0:T(8,128)S(1)}, f32[4,8,1024]{2,1,0:T(8,128)S(1)}, u32[]{:S(2)}, u32[]{:S(2)}) collective-permute-start(f32[4,8,1024]{2,1,0:T(8,128)S(1)} %pad_maximum_fusion.2.refs_0_), channel_id=1, source_target_pairs={{0,2},{2,0},{4,6},{6,4},{1,3},{3,1},{5,7},{7,5},{8,10},{10,8},{12,... | collective-permute-start | bytes 393224 | tf_op jit(solution)/shard_map/ppermute | solution.py:43
  63.7 2.5 %collective-permute-done.19.refs_3_ = f32[4,8,1024]{2,1,0:T(8,128)S(1)} collective-permute-done((f32[4,8,1024]{2,1,0:T(8,128)S(1)}, f32[4,8,1024]{2,1,0:T(8,128)S(1)}, u32[]{:S(2)}, u32[]{:S(2)}) %collective-permute-start.19) | collective-permute-done | bytes 131104 | tf_op jit(solution)/shard_map/ppermute | solution.py:43
  66.2 1.3 %collective-permute-done.18.refs_2_ = f32[4,8,1024]{2,1,0:T(8,128)S(1)} collective-permute-done((f32[4,8,1024]{2,1,0:T(8,128)S(1)}, f32[4,8,1024]{2,1,0:T(8,128)S(1)}, u32[]{:S(2)}, u32[]{:S(2)}) %collective-permute-start.18) | collective-permute-done | bytes 131104 | tf_op jit(solution)/shard_map/ppermute | solution.py:43
  67.5 4.3 %step_2.1 = (f32[3,8,1024]{2,1,0:T(8,128)S(1)}, f32[8,128]{1,0:T(8,128)S(1)}) custom-call(s32[12,128]{1,0:T(8,128)S(1)} %copy-done.7, s32[8,8]{1,0:T(8,128)S(1)} %copy-done.8, f32[8,128]{1,0:T(8,128)S(1)} %copy-done.9, f32[8,128]{1,0:T(8,128)S(1)} %get-tuple-element.33.info_in_ref, f32[4,8,1024]{2,1,0:T(8,128)S(1)} %pad_maximum_fusion.2.refs_0_, ...), custom_call_target="tpu_custom_call" | custom-call | tf_op jit(solution)/shard_map/step_2/pallas_call | solution.py:337
  71.9 0.6 copy-done.6
  72.5 1.3 %collective-permute-start.20 = (f32[1,8,128]{2,1,0:T(8,128)S(1)}, f32[1,8,128]{2,1,0:T(8,128)S(1)}, u32[]{:S(2)}, u32[]{:S(2)}) collective-permute-start(f32[1,8,128]{2,1,0:T(8,128)S(1)} %bitcast.20), channel_id=1, source_target_pairs={{0,8},{8,0},{16,24},{24,16},{1,9},{9,1},{17,25},{25,17},{2,10},{10... | collective-permute-start | bytes 12296 | tf_op jit(solution)/shard_map/ppermute | solution.py:54
  73.8 2.3 %collective-permute-done.20 = f32[1,8,128]{2,1,0:T(8,128)S(1)} collective-permute-done((f32[1,8,128]{2,1,0:T(8,128)S(1)}, f32[1,8,128]{2,1,0:T(8,128)S(1)}, u32[]{:S(2)}, u32[]{:S(2)}) %collective-permute-start.20) | collective-permute-done | bytes 4128 | tf_op jit(solution)/shard_map/ppermute | solution.py:54
  76.1 0.9 collective-permute-start.21
  76.9 3.7 %collective-permute-done.21 = f32[2,8,128]{2,1,0:T(8,128)S(1)} collective-permute-done((f32[2,8,128]{2,1,0:T(8,128)S(1)}, f32[2,8,128]{2,1,0:T(8,128)S(1)}, u32[]{:S(2)}, u32[]{:S(2)}) %collective-permute-start.21) | collective-permute-done | bytes 8224 | tf_op jit(solution)/shard_map/ppermute | solution.py:54
  80.6 3.7 %collective-permute-done.22 = f32[4,8,128]{2,1,0:T(8,128)S(1)} collective-permute-done((f32[4,8,128]{2,1,0:T(8,128)S(1)}, f32[4,8,128]{2,1,0:T(8,128)S(1)}, u32[]{:S(2)}, u32[]{:S(2)}) %collective-permute-start.22) | collective-permute-done | bytes 16416 | tf_op jit(solution)/shard_map/ppermute | solution.py:54
  84.5 3.8 %collective-permute-done.23 = f32[8,8,128]{2,1,0:T(8,128)S(1)} collective-permute-done((f32[8,8,128]{2,1,0:T(8,128)S(1)}, f32[8,8,128]{2,1,0:T(8,128)S(1)}, u32[]{:S(2)}, u32[]{:S(2)}) %collective-permute-start.23) | collective-permute-done | bytes 32800 | tf_op jit(solution)/shard_map/ppermute | solution.py:54
  88.3 0.6 copy-done.10
  88.9 2.2 %final.1 = (f32[2,4,1024]{2,1,0:T(4,128)}, f32[1,4]{1,0:T(1,128)}) custom-call(f32[16,8,128]{2,1,0:T(8,128)} %copy-done.10, f32[3,8,1024]{2,1,0:T(8,128)} %copy-done.6), custom_call_target="tpu_custom_call" | custom-call | tf_op jit(solution)/shard_map/final/pallas_call | solution.py:418
  (45 shorter events, 3.0 us)
Async XLA Ops:
  0.6 22.3 %collective-permute-start.6 = (f32[32,128,128]{2,1,0:T(8,128)}, f32[32,128,128]{2,1,0:T(8,128)S(1)}, u32[]{:S(2)}, u32[]{:S(2)}) collective-permute-start(f32[32,128,128]{2,1,0:T(8,128)} %bitcast.16), channel_id=1, source_target_pairs={{0,1},{1,0},{2,3},{3,2},{4,5},{5,4},{6,7},{7,6},{8,9},{9,8},{10,11... | collective-permute-start | bytes 6291464 | tf_op jit(solution)/shard_map/ppermute | solution.py:443
  1.1 21.8 %collective-permute-start.7 = (f32[32,128,128]{2,1,0:T(8,128)}, f32[32,128,128]{2,1,0:T(8,128)}, u32[]{:S(2)}, u32[]{:S(2)}) collective-permute-start(f32[32,128,128]{2,1,0:T(8,128)} %bitcast.18), channel_id=1, source_target_pairs={{0,1},{1,0},{2,3},{3,2},{4,5},{5,4},{6,7},{7,6},{8,9},{9,8},{10,11... | collective-permute-start | bytes 6291464 | tf_op jit(solution)/shard_map/ppermute | solution.py:444
  1.2 12.8 %collective-permute-start = (f32[2,4,1024]{2,1,0:T(4,128)}, f32[2,4,1024]{2,1,0:T(4,128)S(1)}, u32[]{:S(2)}, u32[]{:S(2)}) collective-permute-start(f32[2,4,1024]{2,1,0:T(4,128)} %param.6), channel_id=1, source_target_pairs={{0,8},{8,0},{16,24},{24,16},{1,9},{9,1},{17,25},{25,17},{2,10},{10... | collective-permute-start | bytes 98312 | tf_op jit(solution)/shard_map/ppermute | solution.py:39
  4.2 9.8 %collective-permute-start.2 = (f32[2,4,1024]{2,1,0:T(4,128)}, f32[2,4,1024]{2,1,0:T(4,128)S(1)}, u32[]{:S(2)}, u32[]{:S(2)}) collective-permute-start(f32[2,4,1024]{2,1,0:T(4,128)} %param.6), channel_id=1, source_target_pairs={{0,24},{8,16},{16,8},{24,0},{1,25},{9,17},{17,9},{25,1},{2,26},{10... | collective-permute-start | bytes 98312 | tf_op jit(solution)/shard_map/ppermute | solution.py:39
  6.7 7.4 %collective-permute-start.1 = (f32[2,4,1024]{2,1,0:T(4,128)}, f32[2,4,1024]{2,1,0:T(4,128)S(1)}, u32[]{:S(2)}, u32[]{:S(2)}) collective-permute-start(f32[2,4,1024]{2,1,0:T(4,128)} %param.6), channel_id=1, source_target_pairs={{0,16},{8,24},{16,0},{24,8},{1,17},{9,25},{17,1},{25,9},{2,18},{10... | collective-permute-start | bytes 98312 | tf_op jit(solution)/shard_map/ppermute | solution.py:39
  7.6 1.6 %copy-start = (f32[8,4,128,128]{3,2,1,0:T(8,128)S(1)}, f32[8,4,128,128]{3,2,1,0:T(8,128)}, u32[]{:S(2)}) copy-start(f32[8,4,128,128]{3,2,1,0:T(8,128)} %param.7) | copy-start | bytes 6291460
  9.2 1.6 %copy-start.1 = (f32[8,4,128,128]{3,2,1,0:T(8,128)S(1)}, f32[8,4,128,128]{3,2,1,0:T(8,128)}, u32[]{:S(2)}) copy-start(f32[8,4,128,128]{3,2,1,0:T(8,128)} %param.8) | copy-start | bytes 6291460
  11.3 1.3 %copy-start.2 = (f32[32,128,128]{2,1,0:T(8,128)}, f32[32,128,128]{2,1,0:T(8,128)S(1)}, u32[]{:S(2)}) copy-start(f32[32,128,128]{2,1,0:T(8,128)S(1)} %get-tuple-element.27.refs_4_) | copy-start | bytes 6291460
  12.6 1.4 %copy-start.4 = (f32[32,128,128]{2,1,0:T(8,128)}, f32[32,128,128]{2,1,0:T(8,128)S(1)}, u32[]{:S(2)}) copy-start(f32[32,128,128]{2,1,0:T(8,128)S(1)} %get-tuple-element.28.refs_6_) | copy-start | bytes 6291460
  14.1 6.4 %collective-permute-start.5 = (f32[4,8,1024]{2,1,0:T(8,128)S(1)}, f32[4,8,1024]{2,1,0:T(8,128)S(1)}, u32[]{:S(2)}, u32[]{:S(2)}) collective-permute-start(f32[4,8,1024]{2,1,0:T(8,128)S(1)} %pad_maximum_fusion.refs_0_), channel_id=1, source_target_pairs={{0,6},{2,4},{4,2},{6,0},{1,7},{3,5},{5,3},{7,1},{8,14},{10,12},{12... | collective-permute-start | bytes 393224 | tf_op jit(solution)/shard_map/ppermute | solution.py:43
  16.6 6.2 %collective-permute-start.4 = (f32[4,8,1024]{2,1,0:T(8,128)S(1)}, f32[4,8,1024]{2,1,0:T(8,128)S(1)}, u32[]{:S(2)}, u32[]{:S(2)}) collective-permute-start(f32[4,8,1024]{2,1,0:T(8,128)S(1)} %pad_maximum_fusion.refs_0_), channel_id=1, source_target_pairs={{0,4},{2,6},{4,0},{6,2},{1,5},{3,7},{5,1},{7,3},{8,12},{10,14},{12... | collective-permute-start | bytes 393224 | tf_op jit(solution)/shard_map/ppermute | solution.py:43
  17.1 5.8 %collective-permute-start.3 = (f32[4,8,1024]{2,1,0:T(8,128)S(1)}, f32[4,8,1024]{2,1,0:T(8,128)S(1)}, u32[]{:S(2)}, u32[]{:S(2)}) collective-permute-start(f32[4,8,1024]{2,1,0:T(8,128)S(1)} %pad_maximum_fusion.refs_0_), channel_id=1, source_target_pairs={{0,2},{2,0},{4,6},{6,4},{1,3},{3,1},{5,7},{7,5},{8,10},{10,8},{12,... | collective-permute-start | bytes 393224 | tf_op jit(solution)/shard_map/ppermute | solution.py:43
  22.9 1.6 %copy-start.3 = (f32[32,128,128]{2,1,0:T(8,128)S(1)}, f32[32,128,128]{2,1,0:T(8,128)}, u32[]{:S(2)}) copy-start(f32[32,128,128]{2,1,0:T(8,128)} %copy-done.2) | copy-start | bytes 6291460
  24.5 1.6 %copy-start.5 = (f32[32,128,128]{2,1,0:T(8,128)S(1)}, f32[32,128,128]{2,1,0:T(8,128)}, u32[]{:S(2)}) copy-start(f32[32,128,128]{2,1,0:T(8,128)} %copy-done.4) | copy-start | bytes 6291460
  26.1 0.7 copy-start.7
  26.8 0.7 copy-start.8
  27.5 0.7 copy-start.9
  33.7 5.9 %collective-permute-start.10 = (f32[8,1024]{1,0:T(8,128)S(1)}, f32[8,1024]{1,0:T(8,128)S(1)}, u32[]{:S(2)}, u32[]{:S(2)}) collective-permute-start(f32[8,1024]{1,0:T(8,128)S(1)} %get-tuple-element.30), channel_id=1, source_target_pairs={{0,24},{8,16},{16,8},{24,0},{1,25},{9,17},{17,9},{25,1},{2,26},{10... | collective-permute-start | bytes 98312 | tf_op jit(solution)/shard_map/ppermute | solution.py:39
  35.8 4.9 %collective-permute-start.9 = (f32[8,1024]{1,0:T(8,128)S(1)}, f32[8,1024]{1,0:T(8,128)S(1)}, u32[]{:S(2)}, u32[]{:S(2)}) collective-permute-start(f32[8,1024]{1,0:T(8,128)S(1)} %get-tuple-element.30), channel_id=1, source_target_pairs={{0,16},{8,24},{16,0},{24,8},{1,17},{9,25},{17,1},{25,9},{2,18},{10... | collective-permute-start | bytes 98312 | tf_op jit(solution)/shard_map/ppermute | solution.py:39
  36.4 4.3 %collective-permute-start.8 = (f32[8,1024]{1,0:T(8,128)S(1)}, f32[8,1024]{1,0:T(8,128)S(1)}, u32[]{:S(2)}, u32[]{:S(2)}) collective-permute-start(f32[8,1024]{1,0:T(8,128)S(1)} %get-tuple-element.30), channel_id=1, source_target_pairs={{0,8},{8,0},{16,24},{24,16},{1,9},{9,1},{17,25},{25,17},{2,10},{10... | collective-permute-start | bytes 98312 | tf_op jit(solution)/shard_map/ppermute | solution.py:39
  40.7 6.9 %collective-permute-start.13 = (f32[4,8,1024]{2,1,0:T(8,128)S(1)}, f32[4,8,1024]{2,1,0:T(8,128)S(1)}, u32[]{:S(2)}, u32[]{:S(2)}) collective-permute-start(f32[4,8,1024]{2,1,0:T(8,128)S(1)} %pad_maximum_fusion.1.refs_0_), channel_id=1, source_target_pairs={{0,6},{2,4},{4,2},{6,0},{1,7},{3,5},{5,3},{7,1},{8,14},{10,12},{12... | collective-permute-start | bytes 393224 | tf_op jit(solution)/shard_map/ppermute | solution.py:43
  42.9 6.0 %collective-permute-start.12 = (f32[4,8,1024]{2,1,0:T(8,128)S(1)}, f32[4,8,1024]{2,1,0:T(8,128)S(1)}, u32[]{:S(2)}, u32[]{:S(2)}) collective-permute-start(f32[4,8,1024]{2,1,0:T(8,128)S(1)} %pad_maximum_fusion.1.refs_0_), channel_id=1, source_target_pairs={{0,4},{2,6},{4,0},{6,2},{1,5},{3,7},{5,1},{7,3},{8,12},{10,14},{12... | collective-permute-start | bytes 393224 | tf_op jit(solution)/shard_map/ppermute | solution.py:43
  44.6 5.0 %collective-permute-start.11 = (f32[4,8,1024]{2,1,0:T(8,128)S(1)}, f32[4,8,1024]{2,1,0:T(8,128)S(1)}, u32[]{:S(2)}, u32[]{:S(2)}) collective-permute-start(f32[4,8,1024]{2,1,0:T(8,128)S(1)} %pad_maximum_fusion.1.refs_0_), channel_id=1, source_target_pairs={{0,2},{2,0},{4,6},{6,4},{1,3},{3,1},{5,7},{7,5},{8,10},{10,8},{12,... | collective-permute-start | bytes 393224 | tf_op jit(solution)/shard_map/ppermute | solution.py:43
  53.5 5.8 %collective-permute-start.16 = (f32[8,1024]{1,0:T(8,128)S(1)}, f32[8,1024]{1,0:T(8,128)S(1)}, u32[]{:S(2)}, u32[]{:S(2)}) collective-permute-start(f32[8,1024]{1,0:T(8,128)S(1)} %get-tuple-element.34), channel_id=1, source_target_pairs={{0,24},{8,16},{16,8},{24,0},{1,25},{9,17},{17,9},{25,1},{2,26},{10... | collective-permute-start | bytes 98312 | tf_op jit(solution)/shard_map/ppermute | solution.py:39
  54.6 5.5 %collective-permute-start.15 = (f32[8,1024]{1,0:T(8,128)S(1)}, f32[8,1024]{1,0:T(8,128)S(1)}, u32[]{:S(2)}, u32[]{:S(2)}) collective-permute-start(f32[8,1024]{1,0:T(8,128)S(1)} %get-tuple-element.34), channel_id=1, source_target_pairs={{0,16},{8,24},{16,0},{24,8},{1,17},{9,25},{17,1},{25,9},{2,18},{10... | collective-permute-start | bytes 98312 | tf_op jit(solution)/shard_map/ppermute | solution.py:39
  54.9 5.2 %collective-permute-start.14 = (f32[8,1024]{1,0:T(8,128)S(1)}, f32[8,1024]{1,0:T(8,128)S(1)}, u32[]{:S(2)}, u32[]{:S(2)}) collective-permute-start(f32[8,1024]{1,0:T(8,128)S(1)} %get-tuple-element.34), channel_id=1, source_target_pairs={{0,8},{8,0},{16,24},{24,16},{1,9},{9,1},{17,25},{25,17},{2,10},{10... | collective-permute-start | bytes 98312 | tf_op jit(solution)/shard_map/ppermute | solution.py:39
  60.2 6.0 %collective-permute-start.19 = (f32[4,8,1024]{2,1,0:T(8,128)S(1)}, f32[4,8,1024]{2,1,0:T(8,128)S(1)}, u32[]{:S(2)}, u32[]{:S(2)}) collective-permute-start(f32[4,8,1024]{2,1,0:T(8,128)S(1)} %pad_maximum_fusion.2.refs_0_), channel_id=1, source_target_pairs={{0,6},{2,4},{4,2},{6,0},{1,7},{3,5},{5,3},{7,1},{8,14},{10,12},{12... | collective-permute-start | bytes 393224 | tf_op jit(solution)/shard_map/ppermute | solution.py:43
  61.2 6.3 %collective-permute-start.18 = (f32[4,8,1024]{2,1,0:T(8,128)S(1)}, f32[4,8,1024]{2,1,0:T(8,128)S(1)}, u32[]{:S(2)}, u32[]{:S(2)}) collective-permute-start(f32[4,8,1024]{2,1,0:T(8,128)S(1)} %pad_maximum_fusion.2.refs_0_), channel_id=1, source_target_pairs={{0,4},{2,6},{4,0},{6,2},{1,5},{3,7},{5,1},{7,3},{8,12},{10,14},{12... | collective-permute-start | bytes 393224 | tf_op jit(solution)/shard_map/ppermute | solution.py:43
  62.3 5.2 %collective-permute-start.17 = (f32[4,8,1024]{2,1,0:T(8,128)S(1)}, f32[4,8,1024]{2,1,0:T(8,128)S(1)}, u32[]{:S(2)}, u32[]{:S(2)}) collective-permute-start(f32[4,8,1024]{2,1,0:T(8,128)S(1)} %pad_maximum_fusion.2.refs_0_), channel_id=1, source_target_pairs={{0,2},{2,0},{4,6},{6,4},{1,3},{3,1},{5,7},{7,5},{8,10},{10,8},{12,... | collective-permute-start | bytes 393224 | tf_op jit(solution)/shard_map/ppermute | solution.py:43
  71.8 0.6 copy-start.6
  72.5 3.6 %collective-permute-start.20 = (f32[1,8,128]{2,1,0:T(8,128)S(1)}, f32[1,8,128]{2,1,0:T(8,128)S(1)}, u32[]{:S(2)}, u32[]{:S(2)}) collective-permute-start(f32[1,8,128]{2,1,0:T(8,128)S(1)} %bitcast.20), channel_id=1, source_target_pairs={{0,8},{8,0},{16,24},{24,16},{1,9},{9,1},{17,25},{25,17},{2,10},{10... | collective-permute-start | bytes 12296 | tf_op jit(solution)/shard_map/ppermute | solution.py:54
  76.1 4.5 %collective-permute-start.21 = (f32[2,8,128]{2,1,0:T(8,128)S(1)}, f32[2,8,128]{2,1,0:T(8,128)S(1)}, u32[]{:S(2)}, u32[]{:S(2)}) collective-permute-start(f32[2,8,128]{2,1,0:T(8,128)S(1)} %pad_maximum_fusion.5), channel_id=1, source_target_pairs={{0,16},{8,24},{16,0},{24,8},{1,17},{9,25},{17,1},{25,9},{2,18},{10... | collective-permute-start | bytes 24584 | tf_op jit(solution)/shard_map/ppermute | solution.py:54
  80.6 3.7 %collective-permute-start.22 = (f32[4,8,128]{2,1,0:T(8,128)S(1)}, f32[4,8,128]{2,1,0:T(8,128)S(1)}, u32[]{:S(2)}, u32[]{:S(2)}) collective-permute-start(f32[4,8,128]{2,1,0:T(8,128)S(1)} %pad_maximum_fusion.4), channel_id=1, source_target_pairs={{0,2},{2,0},{4,6},{6,4},{1,3},{3,1},{5,7},{7,5},{8,10},{10,8},{12,... | collective-permute-start | bytes 49160 | tf_op jit(solution)/shard_map/ppermute | solution.py:54
  84.4 3.9 %collective-permute-start.23 = (f32[8,8,128]{2,1,0:T(8,128)S(1)}, f32[8,8,128]{2,1,0:T(8,128)S(1)}, u32[]{:S(2)}, u32[]{:S(2)}) collective-permute-start(f32[8,8,128]{2,1,0:T(8,128)S(1)} %pad_maximum_fusion.3), channel_id=1, source_target_pairs={{0,4},{2,6},{4,0},{6,2},{1,5},{3,7},{5,1},{7,3},{8,12},{10,14},{12... | collective-permute-start | bytes 98312 | tf_op jit(solution)/shard_map/ppermute | solution.py:54
  88.3 0.6 copy-start.10

commit v8 on v6

--- a/solution.py
+++ b/solution.py
@@ -42,7 +42,7 @@
 
 
 def setup_kernel(
-    line, plane, freqs, pattern_ref, counts_ref, where_ref, ids_ref, g_ref, c_ref,
+    line, plane, freqs, pattern_ref, scalars_ref, g_ref, c_ref,
     items_ref, places_ref, turn_ref, g_out_ref, c_out_ref, sems,
 ):
     row_blocks, slots = pattern_ref.shape
@@ -57,7 +57,7 @@
             copies[-1].start()
 
     order = lax.broadcasted_iota(jnp.int32, (8, LANES), 1)
-    freq = where_ref[2]
+    freq = scalars_ref[2]
     for table, d in enumerate(list(range(freqs)) + [None]):
         first = 0 if d is None else lax.rem(freq + (freqs - d), freqs) * own_slots
         group = FULL_GROUP if d is None else GROUP
@@ -66,7 +66,7 @@
         home = jnp.zeros((8, LANES), jnp.int32)
         used = jnp.int32(0)
         for b in range(row_blocks):
-            here = counts_ref[b] if d is None else jnp.clip(counts_ref[b] - first, 0, own_slots)
+            here = scalars_ref[3 + b] if d is None else jnp.clip(scalars_ref[3 + b] - first, 0, own_slots)
             inside = order - used
             hit = (inside >= 0) & (inside < here)
             layer = jnp.where(hit, first + inside, layer)
@@ -82,40 +82,40 @@
 
     pattern = pattern_ref[...]
     owner = lax.div(pattern, row_blocks)
-    far = distance(where_ref[0], lax.div(owner, plane), line)
-    place = distance(where_ref[1], lax.rem(owner, plane), plane) * line + far
+    far = distance(scalars_ref[0], lax.div(owner, plane), line)
+    place = distance(scalars_ref[1], lax.rem(owner, plane), plane) * line + far
     place = place * row_blocks + lax.rem(pattern, row_blocks)
     b_at = lax.broadcasted_iota(jnp.int32, pattern.shape, 0)
     k_at = lax.broadcasted_iota(jnp.int32, pattern.shape, 1)
     count = jnp.zeros(pattern.shape, jnp.int32)
     for b in range(row_blocks):
-        count = jnp.where(b_at == b, counts_ref[b], count)
+        count = jnp.where(b_at == b, scalars_ref[3 + b], count)
     places_ref[...] = jnp.where(k_at < count, place, line * plane * row_blocks)
 
     half = turn_ref.shape[0] // 2
     row_at = lax.broadcasted_iota(jnp.int32, turn_ref.shape, 0)
     ids = jnp.zeros(turn_ref.shape, jnp.int32)
     for f in range(half):
-        ids = jnp.where(lax.rem(row_at, half) == f, ids_ref[f], ids)
+        ids = jnp.where(lax.rem(row_at, half) == f, scalars_ref[3 + row_blocks + f], ids)
     angular = 0.2 * jnp.exp(ids.astype(jnp.float32) * (math.log(8.0) / 1000.0))
     turn_ref[...] = jnp.where(row_at < half, -angular, angular)
     for copy in copies:
         copy.wait()
 
 
-def run_setup(pattern, counts, where, freq_ids, g_own, c_own, line, plane, freqs):
+def run_setup(pattern, scalars, freq_count, g_own, c_own, line, plane, freqs):
     smem, vmem = pl.BlockSpec(memory_space=pltpu.SMEM), pl.BlockSpec(memory_space=pltpu.VMEM)
     far = pl.BlockSpec(memory_space=pl.ANY)
     blocks = jax.ShapeDtypeStruct(g_own.shape, jnp.float32)
     pieces = math.gcd(g_own.shape[0], 8)
     return pl.pallas_call(
         functools.partial(setup_kernel, line, plane, freqs),
-        in_specs=[vmem, smem, smem, smem, far, far],
+        in_specs=[vmem, smem, far, far],
         out_specs=[vmem] * 5,
         out_shape=[
             jax.ShapeDtypeStruct((4 * (freqs + 1), LANES), jnp.int32),
             jax.ShapeDtypeStruct(pattern.shape, jnp.int32),
-            jax.ShapeDtypeStruct((2 * freq_ids.shape[0], LANES), jnp.float32),
+            jax.ShapeDtypeStruct((2 * freq_count, LANES), jnp.float32),
             blocks,
             blocks,
         ],
@@ -123,7 +123,7 @@
         compiler_params=pltpu.CompilerParams(vmem_limit_bytes=VMEM_LIMIT),
         cost_estimate=pl.CostEstimate(flops=0, bytes_accessed=16 * g_own.size, transcendentals=0),
         name="setup",
-    )(pattern, counts, where, freq_ids, g_own, c_own)
+    )(pattern, scalars, g_own, c_own)
 
 
 def lane_sum(x):
@@ -272,7 +272,8 @@
     if step == ITERS - 1:
         w = local_ref[...]
         zs = [jnp.concatenate([p[b] for b in range(row_blocks)], axis=1) for p in (*prev, z_ref)]
-        own_ref[...] = zs[-1]
+        for i, z in enumerate(zs):
+            own_ref[i] = z
         values = [lane_sum(z * w) for z in zs]
         gram = [[lane_sum(zs[i] * zs[j]) for j in range(i + 1)] for i in range(ITERS)]
         shares = []
@@ -298,7 +299,8 @@
     z = (plane * line * row_blocks + 1, parts, size)
     tile = jax.ShapeDtypeStruct((parts, LANES), jnp.float32)
     own = jax.ShapeDtypeStruct((parts, rows), jnp.float32)
-    out_shape = [own, tile] if step == ITERS - 1 else [jax.ShapeDtypeStruct(z, jnp.float32), own, tile]
+    owns = jax.ShapeDtypeStruct((ITERS, parts, rows), jnp.float32)
+    out_shape = [owns, tile] if step == ITERS - 1 else [jax.ShapeDtypeStruct(z, jnp.float32), own, tile]
     scratch_shapes = [
         pltpu.VMEM((slots, size, LANES), jnp.bfloat16),
         pltpu.VMEM((row_blocks + 1, size, LANES), jnp.bfloat16),
@@ -319,16 +321,17 @@
     )(*lists, turn, info, *lines, *prev, *blocks)
 
 
-def final_kernel(plane, *refs):
-    tiles, krylov = refs[:plane], refs[plane : plane + ITERS]
-    out_ref, residual_ref = refs[plane + ITERS :]
-    line, parts, _ = tiles[0].shape
+def final_kernel(tiles_ref, own_ref, out_ref, residual_ref):
+    devices, parts, _ = tiles_ref.shape
     fit = LANES // parts
-    stacked = [tiles[q][i] for q in range(plane) for i in range(line)]
-    sets = [
-        jnp.transpose(jnp.concatenate(stacked[at : at + fit], axis=0)) for at in range(0, len(stacked), fit)
-    ]
-    info = jnp.transpose(jnp.concatenate([tiles[0][0]] * fit, axis=0))
+    tiles = [tiles_ref[i] for i in range(devices)]
+    sets = [jnp.transpose(jnp.concatenate(tiles[at : at + fit], axis=0)) for at in range(0, devices, fit)]
+    sums = tiles
+    while len(sums) > 1:
+        sums = [x + y for x, y in zip(sums[::2], sums[1::2])] + sums[len(sums) // 2 * 2 :]
+    total = sums[0] + pltpu.roll(sums[0], parts // 2, 0)
+    lane = lax.broadcasted_iota(jnp.int32, total.shape, 1)
+    info = jnp.transpose(jnp.concatenate([jnp.where(lane < SHARES, tiles[0], total)] * fit, axis=0))
 
     def all_devices(shares):
         total = sum(shares[1:], shares[0])
@@ -343,7 +346,7 @@
 
     zero = jnp.zeros((8, LANES), jnp.float32)
     norm, h00, h10, h01, h11, h21 = [row(info, i) for i in range(6)]
-    last = [all_devices([row(s, SHARES + i) for s in sets]) for i in range(ITERS)]
+    last = [row(info, SHARES + i) for i in range(ITERS)]
     shares = []
     for s in sets:
         off = [last[i] - row(s, SHARES + ITERS + i) for i in range(ITERS)]
@@ -379,28 +382,25 @@
     columns = jnp.transpose(
         jnp.concatenate([y for y in coef_y] + [jnp.zeros((LANES - 8 * ITERS, LANES), jnp.float32)], axis=0)
     )[:parts]
-    size = krylov[0].shape[-1]
-    wide = [jnp.broadcast_to(columns[:, 8 * m : 8 * m + 1], (parts, size)) for m in range(ITERS)]
-    for b in range(out_ref.shape[-1] // size):
-        at = slice(b * size, (b + 1) * size)
-        x = wide[-1] * krylov[-1][:, at] + sum(y * z[b] for y, z in zip(wide[:-1], krylov[:-1]))
-        out_ref[0, :, at] = x[: parts // 2]
-        out_ref[1, :, at] = x[parts // 2 :]
-
-
-def run_final(tiles, krylov):
-    parts, rows = krylov[-1].shape
+    rows = own_ref.shape[-1]
+    x = sum(jnp.broadcast_to(columns[:, 8 * m : 8 * m + 1], (parts, rows)) * own_ref[m] for m in range(ITERS))
+    out_ref[0] = x[: parts // 2]
+    out_ref[1] = x[parts // 2 :]
+
+
+def run_final(tiles, own):
+    _, parts, rows = own.shape
     vmem = pl.BlockSpec(memory_space=pltpu.VMEM)
     return pl.pallas_call(
-        functools.partial(final_kernel, len(tiles)),
-        in_specs=[vmem] * (len(tiles) + ITERS),
+        final_kernel,
+        in_specs=[vmem] * 2,
         out_specs=[vmem] * 2,
         out_shape=[
             jax.ShapeDtypeStruct((2, parts // 2, rows), jnp.float32),
             jax.ShapeDtypeStruct((1, parts // 2), jnp.float32),
         ],
         name="final",
-    )(*tiles, *krylov)
+    )(tiles, own)
 
 
 def make_shards(line, plane, freqs):
@@ -408,11 +408,12 @@
         row_blocks, own_slots, size, _ = g_blocks.shape
         freq_count = excitation.shape[1]
         parts = 2 * freq_count
-        where = jnp.stack([lax.axis_index(name) for name in ("line", "place", "freq")]).astype(jnp.int32)
+        where = jnp.stack([lax.axis_index(name) for name in ("line", "place", "freq")])
+        scalars = jnp.concatenate([where, counts, freq_ids]).astype(jnp.int32)
         stored = (row_blocks * own_slots, size, size)
         g_own, c_own = g_blocks.reshape(stored), c_blocks.reshape(stored)
         *lists, turn, g_near, c_near = run_setup(
-            pattern, counts, where, freq_ids, g_own, c_own, line, plane, freqs
+            pattern, scalars, freq_count, g_own, c_own, line, plane, freqs
         )
         g_parts, c_parts = [g_near], [c_near]
         for d in range(1, freqs):
@@ -427,8 +428,7 @@
             lines = gather_rows(rows, line, plane)
             result = run_step(step, lists, turn, info, lines, krylov, blocks, freqs)
             if step == ITERS - 1:
-                rows, info = result
-                krylov.append(rows)
+                own, info = result
             elif step == 0:
                 z, rows, info, tiles = result
                 blocks = [tiles]
@@ -436,7 +436,7 @@
             else:
                 z, rows, info = result
                 krylov.append(z)
-        answer, residual = run_final(gather_rows(info, line, plane), krylov)
+        answer, residual = run_final(jnp.concatenate(gather_rows(info, line, plane)), own)
         return answer, residual.reshape(freq_count)
 
     return shards

time: 82.5 us -> 80.4 us (0.975)
  Pallas kernels: 19.3 us -> 17.1 us
    pallas_call x3, Pallas kernels: 15.4 us -> 13.9 us  [run_step(): pl.pallas_call(functools.partial(step_kernel, step, plane, line, freqs),...]
    unnamed x27 -> x19, local copies, waits for them, and re-layouts: 6.4 us -> 5.15 us
    ppermute x12, waiting for transfers between devices: 10.1 us -> 11.2 us  [gather_rows(): lax.ppermute(rows, 'line', perm)]
    ppermute x12, waiting for transfers between devices: 11.2 us -> 10.3 us  [gather_rows(): lax.ppermute(whole_line, 'place', perm)]
  transfers between devices with their start and end apart: 26 -> 26, of which waited for: 17 -> 17; matrix products, arithmetic and copies ran while one was open for 1% -> 2% of each run, Pallas kernels for 1% -> 1%
where the time goes in v8:
time: 80.4 us; the launch traced here: 79.9 us
  starting transfers between devices  33.6 us (42%)
  waiting for transfers between devices  21.5 us (27%)
  Pallas kernels  17.1 us (21%)
  local copies, waits for them, and re-layouts  6.75 us (8%)
  between operations  0.82 us (1%)
    ppermute x12, starting transfers between devices, gather_rows(): lax.ppermute(rows, 'line', perm)  18.9 us
    ppermute x12, starting transfers between devices, gather_rows(): lax.ppermute(whole_line, 'place', perm)  14.1 us
    pallas_call x3, Pallas kernels, run_step(): pl.pallas_call(functools.partial(step_kernel, step, plane, line, freqs),...  13.9 us
    ppermute x12, waiting for transfers between devices, gather_rows(): lax.ppermute(rows, 'line', perm)  11.2 us
    ppermute x12, waiting for transfers between devices, gather_rows(): lax.ppermute(whole_line, 'place', perm)  10.3 us
    unnamed x19, local copies, waits for them, and re-layouts  5.15 us
    pallas_call x1, Pallas kernels, run_final(): pl.pallas_call(final_kernel, in_specs=[vmem] * 2, out_specs=[vmem] * 2, o...  2.17 us
  transfers between devices with their start and end apart: 26, of which 17 were waited for; matrix products, arithmetic and copies ran while one was open for 2% of the time, Pallas kernels for 1%

profile of v8, /device:TPU:0, one launch (start us, length us, event | category | flops | bytes accessed | tf_op | source)
XLA Modules:
  0.0 79.9 jit_solution(7512769300485620129)
XLA Ops:
  0.6 0.5 collective-permute-start.6
  1.2 3.0 %collective-permute-start = (f32[2,4,1024]{2,1,0:T(4,128)}, f32[2,4,1024]{2,1,0:T(4,128)S(1)}, u32[]{:S(2)}, u32[]{:S(2)}) collective-permute-start(f32[2,4,1024]{2,1,0:T(4,128)} %param.6), channel_id=1, source_target_pairs={{0,8},{8,0},{16,24},{24,16},{1,9},{9,1},{17,25},{25,17},{2,10},{10... | collective-permute-start | bytes 98312 | tf_op jit(solution)/shard_map/ppermute | solution.py:39
  4.2 2.5 %collective-permute-start.2 = (f32[2,4,1024]{2,1,0:T(4,128)}, f32[2,4,1024]{2,1,0:T(4,128)S(1)}, u32[]{:S(2)}, u32[]{:S(2)}) collective-permute-start(f32[2,4,1024]{2,1,0:T(4,128)} %param.6), channel_id=1, source_target_pairs={{0,24},{8,16},{16,8},{24,0},{1,25},{9,17},{17,9},{25,1},{2,26},{10... | collective-permute-start | bytes 98312 | tf_op jit(solution)/shard_map/ppermute | solution.py:39
  6.8 0.8 %stack.72 = f32[1,8,1024]{2,1,0:T(8,128)S(1)} reshape(f32[2,4,1024]{2,1,0:T(4,128)} %param.6) | data formatting | bytes 65536 | tf_op jit(solution)/shard_map/stack | solution.py:40
  7.7 2.6 %collective-permute-done.2 = f32[2,4,1024]{2,1,0:T(4,128)S(1)} collective-permute-done((f32[2,4,1024]{2,1,0:T(4,128)}, f32[2,4,1024]{2,1,0:T(4,128)S(1)}, u32[]{:S(2)}, u32[]{:S(2)}) %collective-permute-start.2) | collective-permute-done | bytes 32800 | tf_op jit(solution)/shard_map/ppermute | solution.py:39
  10.3 1.8 %collective-permute-done.1 = f32[2,4,1024]{2,1,0:T(4,128)S(1)} collective-permute-done((f32[2,4,1024]{2,1,0:T(4,128)}, f32[2,4,1024]{2,1,0:T(4,128)S(1)}, u32[]{:S(2)}, u32[]{:S(2)}) %collective-permute-start.1) | collective-permute-done | bytes 32800 | tf_op jit(solution)/shard_map/ppermute | solution.py:39
  12.1 2.5 %collective-permute-start.5 = (f32[4,8,1024]{2,1,0:T(8,128)S(1)}, f32[4,8,1024]{2,1,0:T(8,128)S(1)}, u32[]{:S(2)}, u32[]{:S(2)}) collective-permute-start(f32[4,8,1024]{2,1,0:T(8,128)S(1)} %constant_dynamic-update-slice_fusion.refs_0_), channel_id=1, source_target_pairs={{0,6},{2,4},{4,2},{6,0},{1,7},{3,5},{5,3},{7,1},{8,14},{10,12},{12... | collective-permute-start | bytes 393224 | tf_op jit(solution)/shard_map/ppermute | solution.py:41
  15.2 0.5 collective-permute-start.3
  15.7 0.7 concatenate.8.scalars_ref
  16.4 1.6 %copy-done = f32[8,4,128,128]{3,2,1,0:T(8,128)S(1)} copy-done((f32[8,4,128,128]{3,2,1,0:T(8,128)S(1)}, f32[8,4,128,128]{3,2,1,0:T(8,128)}, u32[]{:S(2)}) %copy-start) | copy-done | bytes 2097176
  18.0 1.6 %copy-done.1 = f32[8,4,128,128]{3,2,1,0:T(8,128)S(1)} copy-done((f32[8,4,128,128]{3,2,1,0:T(8,128)S(1)}, f32[8,4,128,128]{3,2,1,0:T(8,128)}, u32[]{:S(2)}) %copy-start.1) | copy-done | bytes 2097176
  19.6 0.7 copy-done.3
  20.3 1.1 %setup.1 = (s32[12,128]{1,0:T(8,128)S(1)}, s32[8,8]{1,0:T(8,128)S(1)}, f32[8,128]{1,0:T(8,128)S(1)}, f32[32,128,128]{2,1,0:T(8,128)S(1)}, f32[32,128,128]{2,1,0:T(8,128)S(1)}) custom-call(s32[8,8]{1,0:T(8,128)S(1)} %copy-done.3, s32[15]{0:T(128)S(1)} %concatenate.8.scalars_ref, f32[32,128,128]{2,1,0:T(8,128)S(1)} %bitcast.23, f32[32,128,128]{2,1,0:T(8,128)S(1)} %bitcast.25), custom_call_target="tpu_custom_call" | custom-call | bytes 8388608 | tf_op jit(solution)/shard_map/setup/pallas_call | solution.py:111
  21.4 5.6 %step_0.1 = (f32[129,8,128]{2,1,0:T(8,128)S(1)}, f32[8,1024]{1,0:T(8,128)S(1)}, f32[8,128]{1,0:T(8,128)S(1)}, bf16[64,256,256]{2,1,0:T(8,128)(2,1)S(1)}) custom-call(s32[12,128]{1,0:T(8,128)S(1)} %get-tuple-element.18.items_ref, s32[8,8]{1,0:T(8,128)S(1)} %get-tuple-element.19.places_ref, f32[8,128]{1,0:T(8,128)S(1)} %get-tuple-element.20.turn_ref, ...), custom_call_target="tpu_custom_call" | custom-call | tf_op jit(solution)/shard_map/step_0/pallas_call | solution.py:313
  27.1 1.2 %collective-permute-start.10 = (f32[8,1024]{1,0:T(8,128)S(1)}, f32[8,1024]{1,0:T(8,128)S(1)}, u32[]{:S(2)}, u32[]{:S(2)}) collective-permute-start(f32[8,1024]{1,0:T(8,128)S(1)} %get-tuple-element.24), channel_id=1, source_target_pairs={{0,24},{8,16},{16,8},{24,0},{1,25},{9,17},{17,9},{25,1},{2,26},{10... | collective-permute-start | bytes 98312 | tf_op jit(solution)/shard_map/ppermute | solution.py:39
  28.3 0.7 collective-permute-start.9
  29.0 2.5 %collective-permute-start.8 = (f32[8,1024]{1,0:T(8,128)S(1)}, f32[8,1024]{1,0:T(8,128)S(1)}, u32[]{:S(2)}, u32[]{:S(2)}) collective-permute-start(f32[8,1024]{1,0:T(8,128)S(1)} %get-tuple-element.24), channel_id=1, source_target_pairs={{0,8},{8,0},{16,24},{24,16},{1,9},{9,1},{17,25},{25,17},{2,10},{10... | collective-permute-start | bytes 98312 | tf_op jit(solution)/shard_map/ppermute | solution.py:39
  31.5 1.3 %collective-permute-done.10 = f32[8,1024]{1,0:T(8,128)S(1)} collective-permute-done((f32[8,1024]{1,0:T(8,128)S(1)}, f32[8,1024]{1,0:T(8,128)S(1)}, u32[]{:S(2)}, u32[]{:S(2)}) %collective-permute-start.10) | collective-permute-done | bytes 32800 | tf_op jit(solution)/shard_map/ppermute | solution.py:39
  32.9 0.8 %collective-permute-done.9 = f32[8,1024]{1,0:T(8,128)S(1)} collective-permute-done((f32[8,1024]{1,0:T(8,128)S(1)}, f32[8,1024]{1,0:T(8,128)S(1)}, u32[]{:S(2)}, u32[]{:S(2)}) %collective-permute-start.9) | collective-permute-done | bytes 32800 | tf_op jit(solution)/shard_map/ppermute | solution.py:39
  33.8 2.0 %collective-permute-start.13 = (f32[4,8,1024]{2,1,0:T(8,128)S(1)}, f32[4,8,1024]{2,1,0:T(8,128)S(1)}, u32[]{:S(2)}, u32[]{:S(2)}) collective-permute-start(f32[4,8,1024]{2,1,0:T(8,128)S(1)} %pad_maximum_fusion.refs_0_), channel_id=1, source_target_pairs={{0,6},{2,4},{4,2},{6,0},{1,7},{3,5},{5,3},{7,1},{8,14},{10,12},{12... | collective-permute-start | bytes 393224 | tf_op jit(solution)/shard_map/ppermute | solution.py:41
  35.8 0.6 collective-permute-start.12
  36.4 0.9 %collective-permute-start.11 = (f32[4,8,1024]{2,1,0:T(8,128)S(1)}, f32[4,8,1024]{2,1,0:T(8,128)S(1)}, u32[]{:S(2)}, u32[]{:S(2)}) collective-permute-start(f32[4,8,1024]{2,1,0:T(8,128)S(1)} %pad_maximum_fusion.refs_0_), channel_id=1, source_target_pairs={{0,2},{2,0},{4,6},{6,4},{1,3},{3,1},{5,7},{7,5},{8,10},{10,8},{12,... | collective-permute-start | bytes 393224 | tf_op jit(solution)/shard_map/ppermute | solution.py:41
  37.3 2.4 %collective-permute-done.13.refs_3_ = f32[4,8,1024]{2,1,0:T(8,128)S(1)} collective-permute-done((f32[4,8,1024]{2,1,0:T(8,128)S(1)}, f32[4,8,1024]{2,1,0:T(8,128)S(1)}, u32[]{:S(2)}, u32[]{:S(2)}) %collective-permute-start.13) | collective-permute-done | bytes 131104 | tf_op jit(solution)/shard_map/ppermute | solution.py:41
  39.7 1.4 %collective-permute-done.12.refs_2_ = f32[4,8,1024]{2,1,0:T(8,128)S(1)} collective-permute-done((f32[4,8,1024]{2,1,0:T(8,128)S(1)}, f32[4,8,1024]{2,1,0:T(8,128)S(1)}, u32[]{:S(2)}, u32[]{:S(2)}) %collective-permute-start.12) | collective-permute-done | bytes 131104 | tf_op jit(solution)/shard_map/ppermute | solution.py:41
  41.4 3.9 %step_1.1 = (f32[129,8,128]{2,1,0:T(8,128)S(1)}, f32[8,1024]{1,0:T(8,128)S(1)}, f32[8,128]{1,0:T(8,128)S(1)}) custom-call(s32[12,128]{1,0:T(8,128)S(1)} %get-tuple-element.18.items_ref, s32[8,8]{1,0:T(8,128)S(1)} %get-tuple-element.19.places_ref, f32[8,128]{1,0:T(8,128)S(1)} %get-tuple-element.20.turn_ref, f32[8,128]{1,0:T(8,128)S(1)} %get-tuple-element.23.info_in_ref, ...), custom_call_target="tpu_custom_call" | custom-call | tf_op jit(solution)/shard_map/step_1/pallas_call | solution.py:313
  45.3 1.7 %collective-permute-start.16 = (f32[8,1024]{1,0:T(8,128)S(1)}, f32[8,1024]{1,0:T(8,128)S(1)}, u32[]{:S(2)}, u32[]{:S(2)}) collective-permute-start(f32[8,1024]{1,0:T(8,128)S(1)} %get-tuple-element.28), channel_id=1, source_target_pairs={{0,24},{8,16},{16,8},{24,0},{1,25},{9,17},{17,9},{25,1},{2,26},{10... | collective-permute-start | bytes 98312 | tf_op jit(solution)/shard_map/ppermute | solution.py:39
  47.0 1.6 %collective-permute-start.15 = (f32[8,1024]{1,0:T(8,128)S(1)}, f32[8,1024]{1,0:T(8,128)S(1)}, u32[]{:S(2)}, u32[]{:S(2)}) collective-permute-start(f32[8,1024]{1,0:T(8,128)S(1)} %get-tuple-element.28), channel_id=1, source_target_pairs={{0,16},{8,24},{16,0},{24,8},{1,17},{9,25},{17,1},{25,9},{2,18},{10... | collective-permute-start | bytes 98312 | tf_op jit(solution)/shard_map/ppermute | solution.py:39
  48.6 1.2 %collective-permute-start.14 = (f32[8,1024]{1,0:T(8,128)S(1)}, f32[8,1024]{1,0:T(8,128)S(1)}, u32[]{:S(2)}, u32[]{:S(2)}) collective-permute-start(f32[8,1024]{1,0:T(8,128)S(1)} %get-tuple-element.28), channel_id=1, source_target_pairs={{0,8},{8,0},{16,24},{24,16},{1,9},{9,1},{17,25},{25,17},{2,10},{10... | collective-permute-start | bytes 98312 | tf_op jit(solution)/shard_map/ppermute | solution.py:39
  49.8 1.3 %collective-permute-done.16 = f32[8,1024]{1,0:T(8,128)S(1)} collective-permute-done((f32[8,1024]{1,0:T(8,128)S(1)}, f32[8,1024]{1,0:T(8,128)S(1)}, u32[]{:S(2)}, u32[]{:S(2)}) %collective-permute-start.16) | collective-permute-done | bytes 32800 | tf_op jit(solution)/shard_map/ppermute | solution.py:39
  51.1 0.7 collective-permute-done.15
  51.8 0.7 collective-permute-done.14
  52.5 1.8 %collective-permute-start.19 = (f32[4,8,1024]{2,1,0:T(8,128)S(1)}, f32[4,8,1024]{2,1,0:T(8,128)S(1)}, u32[]{:S(2)}, u32[]{:S(2)}) collective-permute-start(f32[4,8,1024]{2,1,0:T(8,128)S(1)} %pad_maximum_fusion.1.refs_0_), channel_id=1, source_target_pairs={{0,6},{2,4},{4,2},{6,0},{1,7},{3,5},{5,3},{7,1},{8,14},{10,12},{12... | collective-permute-start | bytes 393224 | tf_op jit(solution)/shard_map/ppermute | solution.py:41
  54.5 1.5 %collective-permute-start.17 = (f32[4,8,1024]{2,1,0:T(8,128)S(1)}, f32[4,8,1024]{2,1,0:T(8,128)S(1)}, u32[]{:S(2)}, u32[]{:S(2)}) collective-permute-start(f32[4,8,1024]{2,1,0:T(8,128)S(1)} %pad_maximum_fusion.1.refs_0_), channel_id=1, source_target_pairs={{0,2},{2,0},{4,6},{6,4},{1,3},{3,1},{5,7},{7,5},{8,10},{10,8},{12,... | collective-permute-start | bytes 393224 | tf_op jit(solution)/shard_map/ppermute | solution.py:41
  56.0 2.4 %collective-permute-done.19.refs_3_ = f32[4,8,1024]{2,1,0:T(8,128)S(1)} collective-permute-done((f32[4,8,1024]{2,1,0:T(8,128)S(1)}, f32[4,8,1024]{2,1,0:T(8,128)S(1)}, u32[]{:S(2)}, u32[]{:S(2)}) %collective-permute-start.19) | collective-permute-done | bytes 131104 | tf_op jit(solution)/shard_map/ppermute | solution.py:41
  58.5 1.3 %collective-permute-done.18.refs_2_ = f32[4,8,1024]{2,1,0:T(8,128)S(1)} collective-permute-done((f32[4,8,1024]{2,1,0:T(8,128)S(1)}, f32[4,8,1024]{2,1,0:T(8,128)S(1)}, u32[]{:S(2)}, u32[]{:S(2)}) %collective-permute-start.18) | collective-permute-done | bytes 131104 | tf_op jit(solution)/shard_map/ppermute | solution.py:41
  59.8 4.3 %step_2.1 = (f32[3,8,1024]{2,1,0:T(8,128)S(1)}, f32[8,128]{1,0:T(8,128)S(1)}) custom-call(s32[12,128]{1,0:T(8,128)S(1)} %get-tuple-element.18.items_ref, s32[8,8]{1,0:T(8,128)S(1)} %get-tuple-element.19.places_ref, f32[8,128]{1,0:T(8,128)S(1)} %get-tuple-element.20.turn_ref, f32[8,128]{1,0:T(8,128)S(1)} %get-tuple-element.27.info_in_ref, ...), custom_call_target="tpu_custom_call" | custom-call | tf_op jit(solution)/shard_map/step_2/pallas_call | solution.py:313
  64.2 0.6 copy-done.2
  64.8 1.5 %collective-permute-start.22 = (f32[8,128]{1,0:T(8,128)S(1)}, f32[8,128]{1,0:T(8,128)S(1)}, u32[]{:S(2)}, u32[]{:S(2)}) collective-permute-start(f32[8,128]{1,0:T(8,128)S(1)} %get-tuple-element.30), channel_id=1, source_target_pairs={{0,24},{8,16},{16,8},{24,0},{1,25},{9,17},{17,9},{25,1},{2,26},{10... | collective-permute-start | bytes 12296 | tf_op jit(solution)/shard_map/ppermute | solution.py:39
  66.3 1.2 %collective-permute-start.21 = (f32[8,128]{1,0:T(8,128)S(1)}, f32[8,128]{1,0:T(8,128)S(1)}, u32[]{:S(2)}, u32[]{:S(2)}) collective-permute-start(f32[8,128]{1,0:T(8,128)S(1)} %get-tuple-element.30), channel_id=1, source_target_pairs={{0,16},{8,24},{16,0},{24,8},{1,17},{9,25},{17,1},{25,9},{2,18},{10... | collective-permute-start | bytes 12296 | tf_op jit(solution)/shard_map/ppermute | solution.py:39
  67.5 1.7 %collective-permute-start.20 = (f32[8,128]{1,0:T(8,128)S(1)}, f32[8,128]{1,0:T(8,128)S(1)}, u32[]{:S(2)}, u32[]{:S(2)}) collective-permute-start(f32[8,128]{1,0:T(8,128)S(1)} %get-tuple-element.30), channel_id=1, source_target_pairs={{0,8},{8,0},{16,24},{24,16},{1,9},{9,1},{17,25},{25,17},{2,10},{10... | collective-permute-start | bytes 12296 | tf_op jit(solution)/shard_map/ppermute | solution.py:39
  69.2 1.0 %collective-permute-done.22 = f32[8,128]{1,0:T(8,128)S(1)} collective-permute-done((f32[8,128]{1,0:T(8,128)S(1)}, f32[8,128]{1,0:T(8,128)S(1)}, u32[]{:S(2)}, u32[]{:S(2)}) %collective-permute-start.22) | collective-permute-done | bytes 4128 | tf_op jit(solution)/shard_map/ppermute | solution.py:39
  70.2 0.6 collective-permute-done.21
  71.1 1.6 %collective-permute-start.25 = (f32[4,8,128]{2,1,0:T(8,128)S(1)}, f32[4,8,128]{2,1,0:T(8,128)S(1)}, u32[]{:S(2)}, u32[]{:S(2)}) collective-permute-start(f32[4,8,128]{2,1,0:T(8,128)S(1)} %pad_maximum_fusion.2), channel_id=1, source_target_pairs={{0,6},{2,4},{4,2},{6,0},{1,7},{3,5},{5,3},{7,1},{8,14},{10,12},{12... | collective-permute-start | bytes 49160 | tf_op jit(solution)/shard_map/ppermute | solution.py:41
  72.7 0.6 collective-permute-start.24
  73.3 1.3 %collective-permute-start.23 = (f32[4,8,128]{2,1,0:T(8,128)S(1)}, f32[4,8,128]{2,1,0:T(8,128)S(1)}, u32[]{:S(2)}, u32[]{:S(2)}) collective-permute-start(f32[4,8,128]{2,1,0:T(8,128)S(1)} %pad_maximum_fusion.2), channel_id=1, source_target_pairs={{0,2},{2,0},{4,6},{6,4},{1,3},{3,1},{5,7},{7,5},{8,10},{10,8},{12,... | collective-permute-start | bytes 49160 | tf_op jit(solution)/shard_map/ppermute | solution.py:41
  74.6 2.5 %collective-permute-done.23 = f32[4,8,128]{2,1,0:T(8,128)S(1)} collective-permute-done((f32[4,8,128]{2,1,0:T(8,128)S(1)}, f32[4,8,128]{2,1,0:T(8,128)S(1)}, u32[]{:S(2)}, u32[]{:S(2)}) %collective-permute-start.23) | collective-permute-done | bytes 16416 | tf_op jit(solution)/shard_map/ppermute | solution.py:41
  77.1 0.6 copy-done.4
  77.7 2.2 %final.1 = (f32[2,4,1024]{2,1,0:T(4,128)}, f32[1,4]{1,0:T(1,128)}) custom-call(f32[16,8,128]{2,1,0:T(8,128)} %copy-done.4, f32[3,8,1024]{2,1,0:T(8,128)} %copy-done.2), custom_call_target="tpu_custom_call" | custom-call | tf_op jit(solution)/shard_map/final/pallas_call | solution.py:394
  (39 shorter events, 1.8 us)
Async XLA Ops:
  0.6 20.8 %collective-permute-start.6 = (f32[32,128,128]{2,1,0:T(8,128)}, f32[32,128,128]{2,1,0:T(8,128)S(1)}, u32[]{:S(2)}, u32[]{:S(2)}) collective-permute-start(f32[32,128,128]{2,1,0:T(8,128)} %bitcast.22), channel_id=1, source_target_pairs={{0,1},{1,0},{2,3},{3,2},{4,5},{5,4},{6,7},{7,6},{8,9},{9,8},{10,11... | collective-permute-start | bytes 6291464 | tf_op jit(solution)/shard_map/ppermute | solution.py:421
  1.1 20.3 %collective-permute-start.7 = (f32[32,128,128]{2,1,0:T(8,128)}, f32[32,128,128]{2,1,0:T(8,128)}, u32[]{:S(2)}, u32[]{:S(2)}) collective-permute-start(f32[32,128,128]{2,1,0:T(8,128)} %bitcast.24), channel_id=1, source_target_pairs={{0,1},{1,0},{2,3},{3,2},{4,5},{5,4},{6,7},{7,6},{8,9},{9,8},{10,11... | collective-permute-start | bytes 6291464 | tf_op jit(solution)/shard_map/ppermute | solution.py:422
  1.2 6.4 %collective-permute-start = (f32[2,4,1024]{2,1,0:T(4,128)}, f32[2,4,1024]{2,1,0:T(4,128)S(1)}, u32[]{:S(2)}, u32[]{:S(2)}) collective-permute-start(f32[2,4,1024]{2,1,0:T(4,128)} %param.6), channel_id=1, source_target_pairs={{0,8},{8,0},{16,24},{24,16},{1,9},{9,1},{17,25},{25,17},{2,10},{10... | collective-permute-start | bytes 98312 | tf_op jit(solution)/shard_map/ppermute | solution.py:39
  4.2 6.1 %collective-permute-start.2 = (f32[2,4,1024]{2,1,0:T(4,128)}, f32[2,4,1024]{2,1,0:T(4,128)S(1)}, u32[]{:S(2)}, u32[]{:S(2)}) collective-permute-start(f32[2,4,1024]{2,1,0:T(4,128)} %param.6), channel_id=1, source_target_pairs={{0,24},{8,16},{16,8},{24,0},{1,25},{9,17},{17,9},{25,1},{2,26},{10... | collective-permute-start | bytes 98312 | tf_op jit(solution)/shard_map/ppermute | solution.py:39
  6.7 5.4 %collective-permute-start.1 = (f32[2,4,1024]{2,1,0:T(4,128)}, f32[2,4,1024]{2,1,0:T(4,128)S(1)}, u32[]{:S(2)}, u32[]{:S(2)}) collective-permute-start(f32[2,4,1024]{2,1,0:T(4,128)} %param.6), channel_id=1, source_target_pairs={{0,16},{8,24},{16,0},{24,8},{1,17},{9,25},{17,1},{25,9},{2,18},{10... | collective-permute-start | bytes 98312 | tf_op jit(solution)/shard_map/ppermute | solution.py:39
  12.1 9.2 %collective-permute-start.5 = (f32[4,8,1024]{2,1,0:T(8,128)S(1)}, f32[4,8,1024]{2,1,0:T(8,128)S(1)}, u32[]{:S(2)}, u32[]{:S(2)}) collective-permute-start(f32[4,8,1024]{2,1,0:T(8,128)S(1)} %constant_dynamic-update-slice_fusion.refs_0_), channel_id=1, source_target_pairs={{0,6},{2,4},{4,2},{6,0},{1,7},{3,5},{5,3},{7,1},{8,14},{10,12},{12... | collective-permute-start | bytes 393224 | tf_op jit(solution)/shard_map/ppermute | solution.py:41
  14.6 6.7 %collective-permute-start.4 = (f32[4,8,1024]{2,1,0:T(8,128)S(1)}, f32[4,8,1024]{2,1,0:T(8,128)S(1)}, u32[]{:S(2)}, u32[]{:S(2)}) collective-permute-start(f32[4,8,1024]{2,1,0:T(8,128)S(1)} %constant_dynamic-update-slice_fusion.refs_0_), channel_id=1, source_target_pairs={{0,4},{2,6},{4,0},{6,2},{1,5},{3,7},{5,1},{7,3},{8,12},{10,14},{12... | collective-permute-start | bytes 393224 | tf_op jit(solution)/shard_map/ppermute | solution.py:41
  15.2 6.2 %collective-permute-start.3 = (f32[4,8,1024]{2,1,0:T(8,128)S(1)}, f32[4,8,1024]{2,1,0:T(8,128)S(1)}, u32[]{:S(2)}, u32[]{:S(2)}) collective-permute-start(f32[4,8,1024]{2,1,0:T(8,128)S(1)} %constant_dynamic-update-slice_fusion.refs_0_), channel_id=1, source_target_pairs={{0,2},{2,0},{4,6},{6,4},{1,3},{3,1},{5,7},{7,5},{8,10},{10,8},{12,... | collective-permute-start | bytes 393224 | tf_op jit(solution)/shard_map/ppermute | solution.py:41
  16.4 1.6 %copy-start = (f32[8,4,128,128]{3,2,1,0:T(8,128)S(1)}, f32[8,4,128,128]{3,2,1,0:T(8,128)}, u32[]{:S(2)}) copy-start(f32[8,4,128,128]{3,2,1,0:T(8,128)} %param.7) | copy-start | bytes 6291460
  18.0 1.6 %copy-start.1 = (f32[8,4,128,128]{3,2,1,0:T(8,128)S(1)}, f32[8,4,128,128]{3,2,1,0:T(8,128)}, u32[]{:S(2)}) copy-start(f32[8,4,128,128]{3,2,1,0:T(8,128)} %param.8) | copy-start | bytes 6291460
  19.6 0.7 copy-start.3
  27.1 5.8 %collective-permute-start.10 = (f32[8,1024]{1,0:T(8,128)S(1)}, f32[8,1024]{1,0:T(8,128)S(1)}, u32[]{:S(2)}, u32[]{:S(2)}) collective-permute-start(f32[8,1024]{1,0:T(8,128)S(1)} %get-tuple-element.24), channel_id=1, source_target_pairs={{0,24},{8,16},{16,8},{24,0},{1,25},{9,17},{17,9},{25,1},{2,26},{10... | collective-permute-start | bytes 98312 | tf_op jit(solution)/shard_map/ppermute | solution.py:39
  28.3 5.4 %collective-permute-start.9 = (f32[8,1024]{1,0:T(8,128)S(1)}, f32[8,1024]{1,0:T(8,128)S(1)}, u32[]{:S(2)}, u32[]{:S(2)}) collective-permute-start(f32[8,1024]{1,0:T(8,128)S(1)} %get-tuple-element.24), channel_id=1, source_target_pairs={{0,16},{8,24},{16,0},{24,8},{1,17},{9,25},{17,1},{25,9},{2,18},{10... | collective-permute-start | bytes 98312 | tf_op jit(solution)/shard_map/ppermute | solution.py:39
  29.0 4.7 %collective-permute-start.8 = (f32[8,1024]{1,0:T(8,128)S(1)}, f32[8,1024]{1,0:T(8,128)S(1)}, u32[]{:S(2)}, u32[]{:S(2)}) collective-permute-start(f32[8,1024]{1,0:T(8,128)S(1)} %get-tuple-element.24), channel_id=1, source_target_pairs={{0,8},{8,0},{16,24},{24,16},{1,9},{9,1},{17,25},{25,17},{2,10},{10... | collective-permute-start | bytes 98312 | tf_op jit(solution)/shard_map/ppermute | solution.py:39
  33.8 6.0 %collective-permute-start.13 = (f32[4,8,1024]{2,1,0:T(8,128)S(1)}, f32[4,8,1024]{2,1,0:T(8,128)S(1)}, u32[]{:S(2)}, u32[]{:S(2)}) collective-permute-start(f32[4,8,1024]{2,1,0:T(8,128)S(1)} %pad_maximum_fusion.refs_0_), channel_id=1, source_target_pairs={{0,6},{2,4},{4,2},{6,0},{1,7},{3,5},{5,3},{7,1},{8,14},{10,12},{12... | collective-permute-start | bytes 393224 | tf_op jit(solution)/shard_map/ppermute | solution.py:41
  35.8 5.3 %collective-permute-start.12 = (f32[4,8,1024]{2,1,0:T(8,128)S(1)}, f32[4,8,1024]{2,1,0:T(8,128)S(1)}, u32[]{:S(2)}, u32[]{:S(2)}) collective-permute-start(f32[4,8,1024]{2,1,0:T(8,128)S(1)} %pad_maximum_fusion.refs_0_), channel_id=1, source_target_pairs={{0,4},{2,6},{4,0},{6,2},{1,5},{3,7},{5,1},{7,3},{8,12},{10,14},{12... | collective-permute-start | bytes 393224 | tf_op jit(solution)/shard_map/ppermute | solution.py:41
  36.4 5.0 %collective-permute-start.11 = (f32[4,8,1024]{2,1,0:T(8,128)S(1)}, f32[4,8,1024]{2,1,0:T(8,128)S(1)}, u32[]{:S(2)}, u32[]{:S(2)}) collective-permute-start(f32[4,8,1024]{2,1,0:T(8,128)S(1)} %pad_maximum_fusion.refs_0_), channel_id=1, source_target_pairs={{0,2},{2,0},{4,6},{6,4},{1,3},{3,1},{5,7},{7,5},{8,10},{10,8},{12,... | collective-permute-start | bytes 393224 | tf_op jit(solution)/shard_map/ppermute | solution.py:41
  45.3 5.8 %collective-permute-start.16 = (f32[8,1024]{1,0:T(8,128)S(1)}, f32[8,1024]{1,0:T(8,128)S(1)}, u32[]{:S(2)}, u32[]{:S(2)}) collective-permute-start(f32[8,1024]{1,0:T(8,128)S(1)} %get-tuple-element.28), channel_id=1, source_target_pairs={{0,24},{8,16},{16,8},{24,0},{1,25},{9,17},{17,9},{25,1},{2,26},{10... | collective-permute-start | bytes 98312 | tf_op jit(solution)/shard_map/ppermute | solution.py:39
  47.0 4.8 %collective-permute-start.15 = (f32[8,1024]{1,0:T(8,128)S(1)}, f32[8,1024]{1,0:T(8,128)S(1)}, u32[]{:S(2)}, u32[]{:S(2)}) collective-permute-start(f32[8,1024]{1,0:T(8,128)S(1)} %get-tuple-element.28), channel_id=1, source_target_pairs={{0,16},{8,24},{16,0},{24,8},{1,17},{9,25},{17,1},{25,9},{2,18},{10... | collective-permute-start | bytes 98312 | tf_op jit(solution)/shard_map/ppermute | solution.py:39
  48.6 3.9 %collective-permute-start.14 = (f32[8,1024]{1,0:T(8,128)S(1)}, f32[8,1024]{1,0:T(8,128)S(1)}, u32[]{:S(2)}, u32[]{:S(2)}) collective-permute-start(f32[8,1024]{1,0:T(8,128)S(1)} %get-tuple-element.28), channel_id=1, source_target_pairs={{0,8},{8,0},{16,24},{24,16},{1,9},{9,1},{17,25},{25,17},{2,10},{10... | collective-permute-start | bytes 98312 | tf_op jit(solution)/shard_map/ppermute | solution.py:39
  52.5 6.0 %collective-permute-start.19 = (f32[4,8,1024]{2,1,0:T(8,128)S(1)}, f32[4,8,1024]{2,1,0:T(8,128)S(1)}, u32[]{:S(2)}, u32[]{:S(2)}) collective-permute-start(f32[4,8,1024]{2,1,0:T(8,128)S(1)} %pad_maximum_fusion.1.refs_0_), channel_id=1, source_target_pairs={{0,6},{2,4},{4,2},{6,0},{1,7},{3,5},{5,3},{7,1},{8,14},{10,12},{12... | collective-permute-start | bytes 393224 | tf_op jit(solution)/shard_map/ppermute | solution.py:41
  54.3 5.6 %collective-permute-start.18 = (f32[4,8,1024]{2,1,0:T(8,128)S(1)}, f32[4,8,1024]{2,1,0:T(8,128)S(1)}, u32[]{:S(2)}, u32[]{:S(2)}) collective-permute-start(f32[4,8,1024]{2,1,0:T(8,128)S(1)} %pad_maximum_fusion.1.refs_0_), channel_id=1, source_target_pairs={{0,4},{2,6},{4,0},{6,2},{1,5},{3,7},{5,1},{7,3},{8,12},{10,14},{12... | collective-permute-start | bytes 393224 | tf_op jit(solution)/shard_map/ppermute | solution.py:41
  54.5 5.3 %collective-permute-start.17 = (f32[4,8,1024]{2,1,0:T(8,128)S(1)}, f32[4,8,1024]{2,1,0:T(8,128)S(1)}, u32[]{:S(2)}, u32[]{:S(2)}) collective-permute-start(f32[4,8,1024]{2,1,0:T(8,128)S(1)} %pad_maximum_fusion.1.refs_0_), channel_id=1, source_target_pairs={{0,2},{2,0},{4,6},{6,4},{1,3},{3,1},{5,7},{7,5},{8,10},{10,8},{12,... | collective-permute-start | bytes 393224 | tf_op jit(solution)/shard_map/ppermute | solution.py:41
  64.2 0.6 copy-start.2
  64.8 5.4 %collective-permute-start.22 = (f32[8,128]{1,0:T(8,128)S(1)}, f32[8,128]{1,0:T(8,128)S(1)}, u32[]{:S(2)}, u32[]{:S(2)}) collective-permute-start(f32[8,128]{1,0:T(8,128)S(1)} %get-tuple-element.30), channel_id=1, source_target_pairs={{0,24},{8,16},{16,8},{24,0},{1,25},{9,17},{17,9},{25,1},{2,26},{10... | collective-permute-start | bytes 12296 | tf_op jit(solution)/shard_map/ppermute | solution.py:39
  66.3 4.5 %collective-permute-start.21 = (f32[8,128]{1,0:T(8,128)S(1)}, f32[8,128]{1,0:T(8,128)S(1)}, u32[]{:S(2)}, u32[]{:S(2)}) collective-permute-start(f32[8,128]{1,0:T(8,128)S(1)} %get-tuple-element.30), channel_id=1, source_target_pairs={{0,16},{8,24},{16,0},{24,8},{1,17},{9,25},{17,1},{25,9},{2,18},{10... | collective-permute-start | bytes 12296 | tf_op jit(solution)/shard_map/ppermute | solution.py:39
  67.5 3.6 %collective-permute-start.20 = (f32[8,128]{1,0:T(8,128)S(1)}, f32[8,128]{1,0:T(8,128)S(1)}, u32[]{:S(2)}, u32[]{:S(2)}) collective-permute-start(f32[8,128]{1,0:T(8,128)S(1)} %get-tuple-element.30), channel_id=1, source_target_pairs={{0,8},{8,0},{16,24},{24,16},{1,9},{9,1},{17,25},{25,17},{2,10},{10... | collective-permute-start | bytes 12296 | tf_op jit(solution)/shard_map/ppermute | solution.py:39
  71.1 6.0 %collective-permute-start.25 = (f32[4,8,128]{2,1,0:T(8,128)S(1)}, f32[4,8,128]{2,1,0:T(8,128)S(1)}, u32[]{:S(2)}, u32[]{:S(2)}) collective-permute-start(f32[4,8,128]{2,1,0:T(8,128)S(1)} %pad_maximum_fusion.2), channel_id=1, source_target_pairs={{0,6},{2,4},{4,2},{6,0},{1,7},{3,5},{5,3},{7,1},{8,14},{10,12},{12... | collective-permute-start | bytes 49160 | tf_op jit(solution)/shard_map/ppermute | solution.py:41
  72.7 4.4 %collective-permute-start.24 = (f32[4,8,128]{2,1,0:T(8,128)S(1)}, f32[4,8,128]{2,1,0:T(8,128)S(1)}, u32[]{:S(2)}, u32[]{:S(2)}) collective-permute-start(f32[4,8,128]{2,1,0:T(8,128)S(1)} %pad_maximum_fusion.2), channel_id=1, source_target_pairs={{0,4},{2,6},{4,0},{6,2},{1,5},{3,7},{5,1},{7,3},{8,12},{10,14},{12... | collective-permute-start | bytes 49160 | tf_op jit(solution)/shard_map/ppermute | solution.py:41
  73.3 3.7 %collective-permute-start.23 = (f32[4,8,128]{2,1,0:T(8,128)S(1)}, f32[4,8,128]{2,1,0:T(8,128)S(1)}, u32[]{:S(2)}, u32[]{:S(2)}) collective-permute-start(f32[4,8,128]{2,1,0:T(8,128)S(1)} %pad_maximum_fusion.2), channel_id=1, source_target_pairs={{0,2},{2,0},{4,6},{6,4},{1,3},{3,1},{5,7},{7,5},{8,10},{10,8},{12,... | collective-permute-start | bytes 49160 | tf_op jit(solution)/shard_map/ppermute | solution.py:41
  77.1 0.6 copy-start.4

commit v9 on v8

--- a/solution.py
+++ b/solution.py
@@ -42,10 +42,11 @@
 
 
 def setup_kernel(
-    line, plane, freqs, pattern_ref, scalars_ref, g_ref, c_ref,
+    line, plane, freqs, scalars_ref, g_ref, c_ref,
     items_ref, places_ref, turn_ref, g_out_ref, c_out_ref, sems,
 ):
-    row_blocks, slots = pattern_ref.shape
+    row_blocks, slots = places_ref.shape
+    pattern_at = 3 + row_blocks + turn_ref.shape[0] // 2
     own_slots = slots // freqs
     pieces = sems.shape[1]
     part = g_ref.shape[0] // pieces
@@ -80,13 +81,15 @@
         for i, values in enumerate((layer, block, stored, groups)):
             items_ref[4 * table + i : 4 * table + i + 1, :] = values[:1]
 
-    pattern = pattern_ref[...]
+    b_at = lax.broadcasted_iota(jnp.int32, places_ref.shape, 0)
+    k_at = lax.broadcasted_iota(jnp.int32, places_ref.shape, 1)
+    pattern = jnp.zeros(places_ref.shape, jnp.int32)
+    for i in range(row_blocks * slots):
+        pattern = jnp.where(b_at * slots + k_at == i, scalars_ref[pattern_at + i], pattern)
     owner = lax.div(pattern, row_blocks)
     far = distance(scalars_ref[0], lax.div(owner, plane), line)
     place = distance(scalars_ref[1], lax.rem(owner, plane), plane) * line + far
     place = place * row_blocks + lax.rem(pattern, row_blocks)
-    b_at = lax.broadcasted_iota(jnp.int32, pattern.shape, 0)
-    k_at = lax.broadcasted_iota(jnp.int32, pattern.shape, 1)
     count = jnp.zeros(pattern.shape, jnp.int32)
     for b in range(row_blocks):
         count = jnp.where(b_at == b, scalars_ref[3 + b], count)
@@ -103,18 +106,18 @@
         copy.wait()
 
 
-def run_setup(pattern, scalars, freq_count, g_own, c_own, line, plane, freqs):
+def run_setup(scalars, shape, freq_count, g_own, c_own, line, plane, freqs):
     smem, vmem = pl.BlockSpec(memory_space=pltpu.SMEM), pl.BlockSpec(memory_space=pltpu.VMEM)
     far = pl.BlockSpec(memory_space=pl.ANY)
     blocks = jax.ShapeDtypeStruct(g_own.shape, jnp.float32)
     pieces = math.gcd(g_own.shape[0], 8)
     return pl.pallas_call(
         functools.partial(setup_kernel, line, plane, freqs),
-        in_specs=[vmem, smem, far, far],
+        in_specs=[smem, far, far],
         out_specs=[vmem] * 5,
         out_shape=[
             jax.ShapeDtypeStruct((4 * (freqs + 1), LANES), jnp.int32),
-            jax.ShapeDtypeStruct(pattern.shape, jnp.int32),
+            jax.ShapeDtypeStruct(shape, jnp.int32),
             jax.ShapeDtypeStruct((2 * freq_count, LANES), jnp.float32),
             blocks,
             blocks,
@@ -123,7 +126,7 @@
         compiler_params=pltpu.CompilerParams(vmem_limit_bytes=VMEM_LIMIT),
         cost_estimate=pl.CostEstimate(flops=0, bytes_accessed=16 * g_own.size, transcendentals=0),
         name="setup",
-    )(pattern, scalars, g_own, c_own)
+    )(scalars, g_own, c_own)
 
 
 def lane_sum(x):
@@ -230,38 +233,44 @@
         high = chosen.astype(jnp.bfloat16).astype(jnp.float32)
         layer_ref[k] = jnp.transpose(jnp.concatenate([high, chosen - high], axis=0)).astype(jnp.bfloat16)
 
-    def product(table, t, left):
+    def add_products(totals, table, t, lefts):
         right = layer_ref[items_ref[table, t]] * mask_ref[items_ref[table + 1, t]]
         right = jnp.concatenate([right, right], axis=0)
-        return jnp.dot(left, right, preferred_element_type=jnp.float32)
+        return [
+            total + jnp.dot(left, right, preferred_element_type=jnp.float32)
+            for total, left in zip(totals, lefts)
+        ]
 
     if step == 0:
         for d in range(freqs):
 
             @pl.loop(0, items_ref[4 * d + 3, 0])
             def _(group):
-                total = acc_ref[...]
+                totals = [acc_ref[0], acc_ref[1]]
                 for u in range(GROUP):
                     t = group * GROUP + u
                     stored = items_ref[4 * d + 2, t]
                     here = stored - d * g_refs[d].shape[0]
-                    high, low = split(jnp.concatenate([g_refs[d][here], c_refs[d][here]], axis=0))
-                    left = jnp.concatenate([high, low], axis=1)
-                    split_ref[stored] = left
-                    total = total + product(4 * d, t, left)
-                acc_ref[...] = total
+                    lefts = []
+                    for m, block_refs in enumerate((g_refs, c_refs)):
+                        left = jnp.concatenate(split(block_refs[d][here]), axis=1)
+                        split_ref[stored, m] = left
+                        lefts.append(left)
+                    totals = add_products(totals, 4 * d, t, lefts)
+                acc_ref[0], acc_ref[1] = totals
     else:
 
         @pl.loop(0, items_ref[4 * freqs + 3, 0])
         def _(group):
-            total = acc_ref[...]
+            totals = [acc_ref[0], acc_ref[1]]
             for u in range(FULL_GROUP):
                 t = group * FULL_GROUP + u
-                total = total + product(4 * freqs, t, split_ref[items_ref[4 * freqs + 2, t]])
-            acc_ref[...] = total
+                stored = items_ref[4 * freqs + 2, t]
+                totals = add_products(totals, 4 * freqs, t, [split_ref[stored, m] for m in range(2)])
+            acc_ref[0], acc_ref[1] = totals
 
     half = row_blocks * parts
-    gsum, csum = jnp.transpose(acc_ref[:size]), jnp.transpose(acc_ref[size:])
+    gsum, csum = jnp.transpose(acc_ref[0]), jnp.transpose(acc_ref[1])
     gsum, csum = gsum[:half] + gsum[half:], csum[:half] + csum[half:]
     turn = turn_ref[...]
     for b in range(row_blocks):
@@ -304,10 +313,10 @@
     scratch_shapes = [
         pltpu.VMEM((slots, size, LANES), jnp.bfloat16),
         pltpu.VMEM((row_blocks + 1, size, LANES), jnp.bfloat16),
-        pltpu.VMEM((2 * size, LANES), jnp.float32),
+        pltpu.VMEM((2, size, LANES), jnp.float32),
     ]
     if step == 0:
-        out_shape.append(jax.ShapeDtypeStruct((row_blocks * slots, 2 * size, 2 * size), jnp.bfloat16))
+        out_shape.append(jax.ShapeDtypeStruct((row_blocks * slots, 2, size, 2 * size), jnp.bfloat16))
     if step == ITERS - 1:
         scratch_shapes += [pltpu.VMEM(z, jnp.float32), pltpu.VMEM((parts, rows), jnp.float32)]
     return pl.pallas_call(
@@ -409,11 +418,11 @@
         freq_count = excitation.shape[1]
         parts = 2 * freq_count
         where = jnp.stack([lax.axis_index(name) for name in ("line", "place", "freq")])
-        scalars = jnp.concatenate([where, counts, freq_ids]).astype(jnp.int32)
+        scalars = jnp.concatenate([where, counts, freq_ids, pattern.reshape(-1)]).astype(jnp.int32)
         stored = (row_blocks * own_slots, size, size)
         g_own, c_own = g_blocks.reshape(stored), c_blocks.reshape(stored)
         *lists, turn, g_near, c_near = run_setup(
-            pattern, scalars, freq_count, g_own, c_own, line, plane, freqs
+            scalars, pattern.shape, freq_count, g_own, c_own, line, plane, freqs
         )
         g_parts, c_parts = [g_near], [c_near]
         for d in range(1, freqs):

time: 80.4 us -> 79.9 us (level)
  Pallas kernels: 17.1 us -> 14.2 us
  starting transfers between devices: 33.6 us -> 35.1 us
    pallas_call x3, Pallas kernels: 13.9 us -> 11 us  [run_step(): pl.pallas_call(functools.partial(step_kernel, step, plane, line, freqs),...]
    ppermute x12, starting transfers between devices: 14.1 us -> 15.6 us  [gather_rows(): lax.ppermute(whole_line, 'place', perm)]
    ppermute x12, waiting for transfers between devices: 10.3 us -> 11.5 us  [gather_rows(): lax.ppermute(whole_line, 'place', perm)]
    unnamed x19 -> x17, local copies, waits for them, and re-layouts: 5.15 us -> 4.45 us
  transfers between devices with their start and end apart: 26 -> 26, of which waited for: 17 -> 17; matrix products, arithmetic and copies ran while one was open for 2% -> 3% of each run, Pallas kernels for 1% -> 1%
where the time goes in v9:
time: 79.9 us; the launch traced here: 79.3 us
  starting transfers between devices  35.1 us (44%)
  waiting for transfers between devices  22.2 us (28%)
  Pallas kernels  14.2 us (18%)
  local copies, waits for them, and re-layouts  6.83 us (9%)
  between operations  0.82 us (1%)
    ppermute x12, starting transfers between devices, gather_rows(): lax.ppermute(rows, 'line', perm)  18.9 us
    ppermute x12, starting transfers between devices, gather_rows(): lax.ppermute(whole_line, 'place', perm)  15.6 us
    ppermute x12, waiting for transfers between devices, gather_rows(): lax.ppermute(whole_line, 'place', perm)  11.5 us
    pallas_call x3, Pallas kernels, run_step(): pl.pallas_call(functools.partial(step_kernel, step, plane, line, freqs),...  11 us
    ppermute x12, waiting for transfers between devices, gather_rows(): lax.ppermute(rows, 'line', perm)  10.8 us
    unnamed x17, local copies, waits for them, and re-layouts  4.45 us
    pallas_call x1, Pallas kernels, run_final(): pl.pallas_call(final_kernel, in_specs=[vmem] * 2, out_specs=[vmem] * 2, o...  2.17 us
  transfers between devices with their start and end apart: 26, of which 17 were waited for; matrix products, arithmetic and copies ran while one was open for 3% of the time, Pallas kernels for 1%

profile of v9, /device:TPU:0, one launch (start us, length us, event | category | flops | bytes accessed | tf_op | source)
XLA Modules:
  0.0 79.3 jit_solution(13034426831703379699)
XLA Ops:
  0.6 0.5 collective-permute-start.6
  1.2 3.0 %collective-permute-start = (f32[2,4,1024]{2,1,0:T(4,128)}, f32[2,4,1024]{2,1,0:T(4,128)S(1)}, u32[]{:S(2)}, u32[]{:S(2)}) collective-permute-start(f32[2,4,1024]{2,1,0:T(4,128)} %param.6), channel_id=1, source_target_pairs={{0,8},{8,0},{16,24},{24,16},{1,9},{9,1},{17,25},{25,17},{2,10},{10... | collective-permute-start | bytes 98312 | tf_op jit(solution)/shard_map/ppermute | solution.py:39
  4.2 2.5 %collective-permute-start.2 = (f32[2,4,1024]{2,1,0:T(4,128)}, f32[2,4,1024]{2,1,0:T(4,128)S(1)}, u32[]{:S(2)}, u32[]{:S(2)}) collective-permute-start(f32[2,4,1024]{2,1,0:T(4,128)} %param.6), channel_id=1, source_target_pairs={{0,24},{8,16},{16,8},{24,0},{1,25},{9,17},{17,9},{25,1},{2,26},{10... | collective-permute-start | bytes 98312 | tf_op jit(solution)/shard_map/ppermute | solution.py:39
  6.8 0.8 %stack.72 = f32[1,8,1024]{2,1,0:T(8,128)S(1)} reshape(f32[2,4,1024]{2,1,0:T(4,128)} %param.6) | data formatting | bytes 65536 | tf_op jit(solution)/shard_map/stack | solution.py:40
  7.7 2.6 %collective-permute-done.2 = f32[2,4,1024]{2,1,0:T(4,128)S(1)} collective-permute-done((f32[2,4,1024]{2,1,0:T(4,128)}, f32[2,4,1024]{2,1,0:T(4,128)S(1)}, u32[]{:S(2)}, u32[]{:S(2)}) %collective-permute-start.2) | collective-permute-done | bytes 32800 | tf_op jit(solution)/shard_map/ppermute | solution.py:39
  10.3 1.8 %collective-permute-done.1 = f32[2,4,1024]{2,1,0:T(4,128)S(1)} collective-permute-done((f32[2,4,1024]{2,1,0:T(4,128)}, f32[2,4,1024]{2,1,0:T(4,128)S(1)}, u32[]{:S(2)}, u32[]{:S(2)}) %collective-permute-start.1) | collective-permute-done | bytes 32800 | tf_op jit(solution)/shard_map/ppermute | solution.py:39
  12.1 2.5 %collective-permute-start.5 = (f32[4,8,1024]{2,1,0:T(8,128)S(1)}, f32[4,8,1024]{2,1,0:T(8,128)S(1)}, u32[]{:S(2)}, u32[]{:S(2)}) collective-permute-start(f32[4,8,1024]{2,1,0:T(8,128)S(1)} %constant_dynamic-update-slice_fusion.refs_0_), channel_id=1, source_target_pairs={{0,6},{2,4},{4,2},{6,0},{1,7},{3,5},{5,3},{7,1},{8,14},{10,12},{12... | collective-permute-start | bytes 393224 | tf_op jit(solution)/shard_map/ppermute | solution.py:41
  14.6 0.5 collective-permute-start.4
  15.2 0.5 collective-permute-start.3
  15.7 0.8 reshape.25
  16.5 0.7 concatenate.8.scalars_ref
  17.2 1.6 %copy-done = f32[8,4,128,128]{3,2,1,0:T(8,128)S(1)} copy-done((f32[8,4,128,128]{3,2,1,0:T(8,128)S(1)}, f32[8,4,128,128]{3,2,1,0:T(8,128)}, u32[]{:S(2)}) %copy-start) | copy-done | bytes 2097176
  18.8 1.6 %copy-done.1 = f32[8,4,128,128]{3,2,1,0:T(8,128)S(1)} copy-done((f32[8,4,128,128]{3,2,1,0:T(8,128)S(1)}, f32[8,4,128,128]{3,2,1,0:T(8,128)}, u32[]{:S(2)}) %copy-start.1) | copy-done | bytes 2097176
  20.4 1.1 %setup.1 = (s32[12,128]{1,0:T(8,128)S(1)}, s32[8,8]{1,0:T(8,128)S(1)}, f32[8,128]{1,0:T(8,128)S(1)}, f32[32,128,128]{2,1,0:T(8,128)S(1)}, f32[32,128,128]{2,1,0:T(8,128)S(1)}) custom-call(s32[79]{0:T(128)S(1)} %concatenate.8.scalars_ref, f32[32,128,128]{2,1,0:T(8,128)S(1)} %bitcast.23, f32[32,128,128]{2,1,0:T(8,128)S(1)} %bitcast.25), custom_call_target="tpu_custom_call" | custom-call | bytes 8388608 | tf_op jit(solution)/shard_map/setup/pallas_call | solution.py:114
  21.6 4.4 %step_0.1 = (f32[129,8,128]{2,1,0:T(8,128)S(1)}, f32[8,1024]{1,0:T(8,128)S(1)}, f32[8,128]{1,0:T(8,128)S(1)}, bf16[64,2,128,256]{3,2,1,0:T(8,128)(2,1)S(1)}) custom-call(s32[12,128]{1,0:T(8,128)S(1)} %get-tuple-element.18.items_ref, s32[8,8]{1,0:T(8,128)S(1)} %get-tuple-element.19.places_ref, f32[8,128]{1,0:T(8,128)S(1)} %get-tuple-element.20.turn_ref, ...), custom_call_target="tpu_custom_call" | custom-call | tf_op jit(solution)/shard_map/step_0/pallas_call | solution.py:322
  26.0 0.9 %collective-permute-start.10 = (f32[8,1024]{1,0:T(8,128)S(1)}, f32[8,1024]{1,0:T(8,128)S(1)}, u32[]{:S(2)}, u32[]{:S(2)}) collective-permute-start(f32[8,1024]{1,0:T(8,128)S(1)} %get-tuple-element.24), channel_id=1, source_target_pairs={{0,24},{8,16},{16,8},{24,0},{1,25},{9,17},{17,9},{25,1},{2,26},{10... | collective-permute-start | bytes 98312 | tf_op jit(solution)/shard_map/ppermute | solution.py:39
  26.9 1.0 %collective-permute-start.9 = (f32[8,1024]{1,0:T(8,128)S(1)}, f32[8,1024]{1,0:T(8,128)S(1)}, u32[]{:S(2)}, u32[]{:S(2)}) collective-permute-start(f32[8,1024]{1,0:T(8,128)S(1)} %get-tuple-element.24), channel_id=1, source_target_pairs={{0,16},{8,24},{16,0},{24,8},{1,17},{9,25},{17,1},{25,9},{2,18},{10... | collective-permute-start | bytes 98312 | tf_op jit(solution)/shard_map/ppermute | solution.py:39
  27.9 2.5 %collective-permute-start.8 = (f32[8,1024]{1,0:T(8,128)S(1)}, f32[8,1024]{1,0:T(8,128)S(1)}, u32[]{:S(2)}, u32[]{:S(2)}) collective-permute-start(f32[8,1024]{1,0:T(8,128)S(1)} %get-tuple-element.24), channel_id=1, source_target_pairs={{0,8},{8,0},{16,24},{24,16},{1,9},{9,1},{17,25},{25,17},{2,10},{10... | collective-permute-start | bytes 98312 | tf_op jit(solution)/shard_map/ppermute | solution.py:39
  30.4 1.4 %collective-permute-done.10 = f32[8,1024]{1,0:T(8,128)S(1)} collective-permute-done((f32[8,1024]{1,0:T(8,128)S(1)}, f32[8,1024]{1,0:T(8,128)S(1)}, u32[]{:S(2)}, u32[]{:S(2)}) %collective-permute-start.10) | collective-permute-done | bytes 32800 | tf_op jit(solution)/shard_map/ppermute | solution.py:39
  31.9 0.7 collective-permute-done.9
  32.6 2.9 %collective-permute-start.13 = (f32[4,8,1024]{2,1,0:T(8,128)S(1)}, f32[4,8,1024]{2,1,0:T(8,128)S(1)}, u32[]{:S(2)}, u32[]{:S(2)}) collective-permute-start(f32[4,8,1024]{2,1,0:T(8,128)S(1)} %pad_maximum_fusion.refs_0_), channel_id=1, source_target_pairs={{0,6},{2,4},{4,2},{6,0},{1,7},{3,5},{5,3},{7,1},{8,14},{10,12},{12... | collective-permute-start | bytes 393224 | tf_op jit(solution)/shard_map/ppermute | solution.py:41
  36.0 0.6 collective-permute-start.11
  36.7 2.0 %collective-permute-done.13.refs_3_ = f32[4,8,1024]{2,1,0:T(8,128)S(1)} collective-permute-done((f32[4,8,1024]{2,1,0:T(8,128)S(1)}, f32[4,8,1024]{2,1,0:T(8,128)S(1)}, u32[]{:S(2)}, u32[]{:S(2)}) %collective-permute-start.13) | collective-permute-done | bytes 131104 | tf_op jit(solution)/shard_map/ppermute | solution.py:41
  38.7 1.8 %collective-permute-done.12.refs_2_ = f32[4,8,1024]{2,1,0:T(8,128)S(1)} collective-permute-done((f32[4,8,1024]{2,1,0:T(8,128)S(1)}, f32[4,8,1024]{2,1,0:T(8,128)S(1)}, u32[]{:S(2)}, u32[]{:S(2)}) %collective-permute-start.12) | collective-permute-done | bytes 131104 | tf_op jit(solution)/shard_map/ppermute | solution.py:41
  40.5 0.6 collective-permute-done.11.refs_1_
  41.0 3.0 %step_1.1 = (f32[129,8,128]{2,1,0:T(8,128)S(1)}, f32[8,1024]{1,0:T(8,128)S(1)}, f32[8,128]{1,0:T(8,128)S(1)}) custom-call(s32[12,128]{1,0:T(8,128)S(1)} %get-tuple-element.18.items_ref, s32[8,8]{1,0:T(8,128)S(1)} %get-tuple-element.19.places_ref, f32[8,128]{1,0:T(8,128)S(1)} %get-tuple-element.20.turn_ref, f32[8,128]{1,0:T(8,128)S(1)} %get-tuple-element.23.info_in_ref, ...), custom_call_target="tpu_custom_call" | custom-call | tf_op jit(solution)/shard_map/step_1/pallas_call | solution.py:322
  44.1 1.7 %collective-permute-start.16 = (f32[8,1024]{1,0:T(8,128)S(1)}, f32[8,1024]{1,0:T(8,128)S(1)}, u32[]{:S(2)}, u32[]{:S(2)}) collective-permute-start(f32[8,1024]{1,0:T(8,128)S(1)} %get-tuple-element.28), channel_id=1, source_target_pairs={{0,24},{8,16},{16,8},{24,0},{1,25},{9,17},{17,9},{25,1},{2,26},{10... | collective-permute-start | bytes 98312 | tf_op jit(solution)/shard_map/ppermute | solution.py:39
  45.8 1.5 %collective-permute-start.15 = (f32[8,1024]{1,0:T(8,128)S(1)}, f32[8,1024]{1,0:T(8,128)S(1)}, u32[]{:S(2)}, u32[]{:S(2)}) collective-permute-start(f32[8,1024]{1,0:T(8,128)S(1)} %get-tuple-element.28), channel_id=1, source_target_pairs={{0,16},{8,24},{16,0},{24,8},{1,17},{9,25},{17,1},{25,9},{2,18},{10... | collective-permute-start | bytes 98312 | tf_op jit(solution)/shard_map/ppermute | solution.py:39
  47.3 1.3 %collective-permute-start.14 = (f32[8,1024]{1,0:T(8,128)S(1)}, f32[8,1024]{1,0:T(8,128)S(1)}, u32[]{:S(2)}, u32[]{:S(2)}) collective-permute-start(f32[8,1024]{1,0:T(8,128)S(1)} %get-tuple-element.28), channel_id=1, source_target_pairs={{0,8},{8,0},{16,24},{24,16},{1,9},{9,1},{17,25},{25,17},{2,10},{10... | collective-permute-start | bytes 98312 | tf_op jit(solution)/shard_map/ppermute | solution.py:39
  48.6 1.3 %collective-permute-done.16 = f32[8,1024]{1,0:T(8,128)S(1)} collective-permute-done((f32[8,1024]{1,0:T(8,128)S(1)}, f32[8,1024]{1,0:T(8,128)S(1)}, u32[]{:S(2)}, u32[]{:S(2)}) %collective-permute-start.16) | collective-permute-done | bytes 32800 | tf_op jit(solution)/shard_map/ppermute | solution.py:39
  49.9 0.7 collective-permute-done.15
  50.6 0.6 collective-permute-done.14
  51.2 2.7 %collective-permute-start.19 = (f32[4,8,1024]{2,1,0:T(8,128)S(1)}, f32[4,8,1024]{2,1,0:T(8,128)S(1)}, u32[]{:S(2)}, u32[]{:S(2)}) collective-permute-start(f32[4,8,1024]{2,1,0:T(8,128)S(1)} %pad_maximum_fusion.1.refs_0_), channel_id=1, source_target_pairs={{0,6},{2,4},{4,2},{6,0},{1,7},{3,5},{5,3},{7,1},{8,14},{10,12},{12... | collective-permute-start | bytes 393224 | tf_op jit(solution)/shard_map/ppermute | solution.py:41
  54.4 0.6 collective-permute-start.17
  55.0 2.2 %collective-permute-done.19.refs_3_ = f32[4,8,1024]{2,1,0:T(8,128)S(1)} collective-permute-done((f32[4,8,1024]{2,1,0:T(8,128)S(1)}, f32[4,8,1024]{2,1,0:T(8,128)S(1)}, u32[]{:S(2)}, u32[]{:S(2)}) %collective-permute-start.19) | collective-permute-done | bytes 131104 | tf_op jit(solution)/shard_map/ppermute | solution.py:41
  57.2 1.7 %collective-permute-done.18.refs_2_ = f32[4,8,1024]{2,1,0:T(8,128)S(1)} collective-permute-done((f32[4,8,1024]{2,1,0:T(8,128)S(1)}, f32[4,8,1024]{2,1,0:T(8,128)S(1)}, u32[]{:S(2)}, u32[]{:S(2)}) %collective-permute-start.18) | collective-permute-done | bytes 131104 | tf_op jit(solution)/shard_map/ppermute | solution.py:41
  59.4 3.5 %step_2.1 = (f32[3,8,1024]{2,1,0:T(8,128)S(1)}, f32[8,128]{1,0:T(8,128)S(1)}) custom-call(s32[12,128]{1,0:T(8,128)S(1)} %get-tuple-element.18.items_ref, s32[8,8]{1,0:T(8,128)S(1)} %get-tuple-element.19.places_ref, f32[8,128]{1,0:T(8,128)S(1)} %get-tuple-element.20.turn_ref, f32[8,128]{1,0:T(8,128)S(1)} %get-tuple-element.27.info_in_ref, ...), custom_call_target="tpu_custom_call" | custom-call | tf_op jit(solution)/shard_map/step_2/pallas_call | solution.py:322
  62.9 0.6 copy-done.2
  63.5 1.2 %collective-permute-start.22 = (f32[8,128]{1,0:T(8,128)S(1)}, f32[8,128]{1,0:T(8,128)S(1)}, u32[]{:S(2)}, u32[]{:S(2)}) collective-permute-start(f32[8,128]{1,0:T(8,128)S(1)} %get-tuple-element.30), channel_id=1, source_target_pairs={{0,24},{8,16},{16,8},{24,0},{1,25},{9,17},{17,9},{25,1},{2,26},{10... | collective-permute-start | bytes 12296 | tf_op jit(solution)/shard_map/ppermute | solution.py:39
  64.7 1.2 %collective-permute-start.21 = (f32[8,128]{1,0:T(8,128)S(1)}, f32[8,128]{1,0:T(8,128)S(1)}, u32[]{:S(2)}, u32[]{:S(2)}) collective-permute-start(f32[8,128]{1,0:T(8,128)S(1)} %get-tuple-element.30), channel_id=1, source_target_pairs={{0,16},{8,24},{16,0},{24,8},{1,17},{9,25},{17,1},{25,9},{2,18},{10... | collective-permute-start | bytes 12296 | tf_op jit(solution)/shard_map/ppermute | solution.py:39
  65.9 2.0 %collective-permute-start.20 = (f32[8,128]{1,0:T(8,128)S(1)}, f32[8,128]{1,0:T(8,128)S(1)}, u32[]{:S(2)}, u32[]{:S(2)}) collective-permute-start(f32[8,128]{1,0:T(8,128)S(1)} %get-tuple-element.30), channel_id=1, source_target_pairs={{0,8},{8,0},{16,24},{24,16},{1,9},{9,1},{17,25},{25,17},{2,10},{10... | collective-permute-start | bytes 12296 | tf_op jit(solution)/shard_map/ppermute | solution.py:39
  67.9 1.0 %collective-permute-done.22 = f32[8,128]{1,0:T(8,128)S(1)} collective-permute-done((f32[8,128]{1,0:T(8,128)S(1)}, f32[8,128]{1,0:T(8,128)S(1)}, u32[]{:S(2)}, u32[]{:S(2)}) %collective-permute-start.22) | collective-permute-done | bytes 4128 | tf_op jit(solution)/shard_map/ppermute | solution.py:39
  69.5 2.6 %collective-permute-start.25 = (f32[4,8,128]{2,1,0:T(8,128)S(1)}, f32[4,8,128]{2,1,0:T(8,128)S(1)}, u32[]{:S(2)}, u32[]{:S(2)}) collective-permute-start(f32[4,8,128]{2,1,0:T(8,128)S(1)} %pad_maximum_fusion.2), channel_id=1, source_target_pairs={{0,6},{2,4},{4,2},{6,0},{1,7},{3,5},{5,3},{7,1},{8,14},{10,12},{12... | collective-permute-start | bytes 49160 | tf_op jit(solution)/shard_map/ppermute | solution.py:41
  72.1 0.5 collective-permute-start.24
  72.7 1.1 %collective-permute-start.23 = (f32[4,8,128]{2,1,0:T(8,128)S(1)}, f32[4,8,128]{2,1,0:T(8,128)S(1)}, u32[]{:S(2)}, u32[]{:S(2)}) collective-permute-start(f32[4,8,128]{2,1,0:T(8,128)S(1)} %pad_maximum_fusion.2), channel_id=1, source_target_pairs={{0,2},{2,0},{4,6},{6,4},{1,3},{3,1},{5,7},{7,5},{8,10},{10,8},{12,... | collective-permute-start | bytes 49160 | tf_op jit(solution)/shard_map/ppermute | solution.py:41
  73.8 2.7 %collective-permute-done.23 = f32[4,8,128]{2,1,0:T(8,128)S(1)} collective-permute-done((f32[4,8,128]{2,1,0:T(8,128)S(1)}, f32[4,8,128]{2,1,0:T(8,128)S(1)}, u32[]{:S(2)}, u32[]{:S(2)}) %collective-permute-start.23) | collective-permute-done | bytes 16416 | tf_op jit(solution)/shard_map/ppermute | solution.py:41
  76.5 0.6 copy-done.3
  77.1 2.2 %final.1 = (f32[2,4,1024]{2,1,0:T(4,128)}, f32[1,4]{1,0:T(1,128)}) custom-call(f32[16,8,128]{2,1,0:T(8,128)} %copy-done.3, f32[3,8,1024]{2,1,0:T(8,128)} %copy-done.2), custom_call_target="tpu_custom_call" | custom-call | tf_op jit(solution)/shard_map/final/pallas_call | solution.py:403
  (38 shorter events, 2.4 us)
Async XLA Ops:
  0.6 20.9 %collective-permute-start.6 = (f32[32,128,128]{2,1,0:T(8,128)}, f32[32,128,128]{2,1,0:T(8,128)S(1)}, u32[]{:S(2)}, u32[]{:S(2)}) collective-permute-start(f32[32,128,128]{2,1,0:T(8,128)} %bitcast.22), channel_id=1, source_target_pairs={{0,1},{1,0},{2,3},{3,2},{4,5},{5,4},{6,7},{7,6},{8,9},{9,8},{10,11... | collective-permute-start | bytes 6291464 | tf_op jit(solution)/shard_map/ppermute | solution.py:430
  1.1 20.4 %collective-permute-start.7 = (f32[32,128,128]{2,1,0:T(8,128)}, f32[32,128,128]{2,1,0:T(8,128)}, u32[]{:S(2)}, u32[]{:S(2)}) collective-permute-start(f32[32,128,128]{2,1,0:T(8,128)} %bitcast.24), channel_id=1, source_target_pairs={{0,1},{1,0},{2,3},{3,2},{4,5},{5,4},{6,7},{7,6},{8,9},{9,8},{10,11... | collective-permute-start | bytes 6291464 | tf_op jit(solution)/shard_map/ppermute | solution.py:431
  1.2 6.4 %collective-permute-start = (f32[2,4,1024]{2,1,0:T(4,128)}, f32[2,4,1024]{2,1,0:T(4,128)S(1)}, u32[]{:S(2)}, u32[]{:S(2)}) collective-permute-start(f32[2,4,1024]{2,1,0:T(4,128)} %param.6), channel_id=1, source_target_pairs={{0,8},{8,0},{16,24},{24,16},{1,9},{9,1},{17,25},{25,17},{2,10},{10... | collective-permute-start | bytes 98312 | tf_op jit(solution)/shard_map/ppermute | solution.py:39
  4.2 6.1 %collective-permute-start.2 = (f32[2,4,1024]{2,1,0:T(4,128)}, f32[2,4,1024]{2,1,0:T(4,128)S(1)}, u32[]{:S(2)}, u32[]{:S(2)}) collective-permute-start(f32[2,4,1024]{2,1,0:T(4,128)} %param.6), channel_id=1, source_target_pairs={{0,24},{8,16},{16,8},{24,0},{1,25},{9,17},{17,9},{25,1},{2,26},{10... | collective-permute-start | bytes 98312 | tf_op jit(solution)/shard_map/ppermute | solution.py:39
  6.7 5.4 %collective-permute-start.1 = (f32[2,4,1024]{2,1,0:T(4,128)}, f32[2,4,1024]{2,1,0:T(4,128)S(1)}, u32[]{:S(2)}, u32[]{:S(2)}) collective-permute-start(f32[2,4,1024]{2,1,0:T(4,128)} %param.6), channel_id=1, source_target_pairs={{0,16},{8,24},{16,0},{24,8},{1,17},{9,25},{17,1},{25,9},{2,18},{10... | collective-permute-start | bytes 98312 | tf_op jit(solution)/shard_map/ppermute | solution.py:39
  12.1 9.4 %collective-permute-start.5 = (f32[4,8,1024]{2,1,0:T(8,128)S(1)}, f32[4,8,1024]{2,1,0:T(8,128)S(1)}, u32[]{:S(2)}, u32[]{:S(2)}) collective-permute-start(f32[4,8,1024]{2,1,0:T(8,128)S(1)} %constant_dynamic-update-slice_fusion.refs_0_), channel_id=1, source_target_pairs={{0,6},{2,4},{4,2},{6,0},{1,7},{3,5},{5,3},{7,1},{8,14},{10,12},{12... | collective-permute-start | bytes 393224 | tf_op jit(solution)/shard_map/ppermute | solution.py:41
  14.6 6.9 %collective-permute-start.4 = (f32[4,8,1024]{2,1,0:T(8,128)S(1)}, f32[4,8,1024]{2,1,0:T(8,128)S(1)}, u32[]{:S(2)}, u32[]{:S(2)}) collective-permute-start(f32[4,8,1024]{2,1,0:T(8,128)S(1)} %constant_dynamic-update-slice_fusion.refs_0_), channel_id=1, source_target_pairs={{0,4},{2,6},{4,0},{6,2},{1,5},{3,7},{5,1},{7,3},{8,12},{10,14},{12... | collective-permute-start | bytes 393224 | tf_op jit(solution)/shard_map/ppermute | solution.py:41
  15.2 6.4 %collective-permute-start.3 = (f32[4,8,1024]{2,1,0:T(8,128)S(1)}, f32[4,8,1024]{2,1,0:T(8,128)S(1)}, u32[]{:S(2)}, u32[]{:S(2)}) collective-permute-start(f32[4,8,1024]{2,1,0:T(8,128)S(1)} %constant_dynamic-update-slice_fusion.refs_0_), channel_id=1, source_target_pairs={{0,2},{2,0},{4,6},{6,4},{1,3},{3,1},{5,7},{7,5},{8,10},{10,8},{12,... | collective-permute-start | bytes 393224 | tf_op jit(solution)/shard_map/ppermute | solution.py:41
  17.2 1.6 %copy-start = (f32[8,4,128,128]{3,2,1,0:T(8,128)S(1)}, f32[8,4,128,128]{3,2,1,0:T(8,128)}, u32[]{:S(2)}) copy-start(f32[8,4,128,128]{3,2,1,0:T(8,128)} %param.7) | copy-start | bytes 6291460
  18.8 1.6 %copy-start.1 = (f32[8,4,128,128]{3,2,1,0:T(8,128)S(1)}, f32[8,4,128,128]{3,2,1,0:T(8,128)}, u32[]{:S(2)}) copy-start(f32[8,4,128,128]{3,2,1,0:T(8,128)} %param.8) | copy-start | bytes 6291460
  26.0 5.9 %collective-permute-start.10 = (f32[8,1024]{1,0:T(8,128)S(1)}, f32[8,1024]{1,0:T(8,128)S(1)}, u32[]{:S(2)}, u32[]{:S(2)}) collective-permute-start(f32[8,1024]{1,0:T(8,128)S(1)} %get-tuple-element.24), channel_id=1, source_target_pairs={{0,24},{8,16},{16,8},{24,0},{1,25},{9,17},{17,9},{25,1},{2,26},{10... | collective-permute-start | bytes 98312 | tf_op jit(solution)/shard_map/ppermute | solution.py:39
  26.9 5.6 %collective-permute-start.9 = (f32[8,1024]{1,0:T(8,128)S(1)}, f32[8,1024]{1,0:T(8,128)S(1)}, u32[]{:S(2)}, u32[]{:S(2)}) collective-permute-start(f32[8,1024]{1,0:T(8,128)S(1)} %get-tuple-element.24), channel_id=1, source_target_pairs={{0,16},{8,24},{16,0},{24,8},{1,17},{9,25},{17,1},{25,9},{2,18},{10... | collective-permute-start | bytes 98312 | tf_op jit(solution)/shard_map/ppermute | solution.py:39
  27.9 4.6 %collective-permute-start.8 = (f32[8,1024]{1,0:T(8,128)S(1)}, f32[8,1024]{1,0:T(8,128)S(1)}, u32[]{:S(2)}, u32[]{:S(2)}) collective-permute-start(f32[8,1024]{1,0:T(8,128)S(1)} %get-tuple-element.24), channel_id=1, source_target_pairs={{0,8},{8,0},{16,24},{24,16},{1,9},{9,1},{17,25},{25,17},{2,10},{10... | collective-permute-start | bytes 98312 | tf_op jit(solution)/shard_map/ppermute | solution.py:39
  32.6 6.1 %collective-permute-start.13 = (f32[4,8,1024]{2,1,0:T(8,128)S(1)}, f32[4,8,1024]{2,1,0:T(8,128)S(1)}, u32[]{:S(2)}, u32[]{:S(2)}) collective-permute-start(f32[4,8,1024]{2,1,0:T(8,128)S(1)} %pad_maximum_fusion.refs_0_), channel_id=1, source_target_pairs={{0,6},{2,4},{4,2},{6,0},{1,7},{3,5},{5,3},{7,1},{8,14},{10,12},{12... | collective-permute-start | bytes 393224 | tf_op jit(solution)/shard_map/ppermute | solution.py:41
  35.5 5.0 %collective-permute-start.12 = (f32[4,8,1024]{2,1,0:T(8,128)S(1)}, f32[4,8,1024]{2,1,0:T(8,128)S(1)}, u32[]{:S(2)}, u32[]{:S(2)}) collective-permute-start(f32[4,8,1024]{2,1,0:T(8,128)S(1)} %pad_maximum_fusion.refs_0_), channel_id=1, source_target_pairs={{0,4},{2,6},{4,0},{6,2},{1,5},{3,7},{5,1},{7,3},{8,12},{10,14},{12... | collective-permute-start | bytes 393224 | tf_op jit(solution)/shard_map/ppermute | solution.py:41
  36.0 5.0 %collective-permute-start.11 = (f32[4,8,1024]{2,1,0:T(8,128)S(1)}, f32[4,8,1024]{2,1,0:T(8,128)S(1)}, u32[]{:S(2)}, u32[]{:S(2)}) collective-permute-start(f32[4,8,1024]{2,1,0:T(8,128)S(1)} %pad_maximum_fusion.refs_0_), channel_id=1, source_target_pairs={{0,2},{2,0},{4,6},{6,4},{1,3},{3,1},{5,7},{7,5},{8,10},{10,8},{12,... | collective-permute-start | bytes 393224 | tf_op jit(solution)/shard_map/ppermute | solution.py:41
  44.1 5.8 %collective-permute-start.16 = (f32[8,1024]{1,0:T(8,128)S(1)}, f32[8,1024]{1,0:T(8,128)S(1)}, u32[]{:S(2)}, u32[]{:S(2)}) collective-permute-start(f32[8,1024]{1,0:T(8,128)S(1)} %get-tuple-element.28), channel_id=1, source_target_pairs={{0,24},{8,16},{16,8},{24,0},{1,25},{9,17},{17,9},{25,1},{2,26},{10... | collective-permute-start | bytes 98312 | tf_op jit(solution)/shard_map/ppermute | solution.py:39
  45.8 4.8 %collective-permute-start.15 = (f32[8,1024]{1,0:T(8,128)S(1)}, f32[8,1024]{1,0:T(8,128)S(1)}, u32[]{:S(2)}, u32[]{:S(2)}) collective-permute-start(f32[8,1024]{1,0:T(8,128)S(1)} %get-tuple-element.28), channel_id=1, source_target_pairs={{0,16},{8,24},{16,0},{24,8},{1,17},{9,25},{17,1},{25,9},{2,18},{10... | collective-permute-start | bytes 98312 | tf_op jit(solution)/shard_map/ppermute | solution.py:39
  47.3 3.9 %collective-permute-start.14 = (f32[8,1024]{1,0:T(8,128)S(1)}, f32[8,1024]{1,0:T(8,128)S(1)}, u32[]{:S(2)}, u32[]{:S(2)}) collective-permute-start(f32[8,1024]{1,0:T(8,128)S(1)} %get-tuple-element.28), channel_id=1, source_target_pairs={{0,8},{8,0},{16,24},{24,16},{1,9},{9,1},{17,25},{25,17},{2,10},{10... | collective-permute-start | bytes 98312 | tf_op jit(solution)/shard_map/ppermute | solution.py:39
  51.2 5.9 %collective-permute-start.19 = (f32[4,8,1024]{2,1,0:T(8,128)S(1)}, f32[4,8,1024]{2,1,0:T(8,128)S(1)}, u32[]{:S(2)}, u32[]{:S(2)}) collective-permute-start(f32[4,8,1024]{2,1,0:T(8,128)S(1)} %pad_maximum_fusion.1.refs_0_), channel_id=1, source_target_pairs={{0,6},{2,4},{4,2},{6,0},{1,7},{3,5},{5,3},{7,1},{8,14},{10,12},{12... | collective-permute-start | bytes 393224 | tf_op jit(solution)/shard_map/ppermute | solution.py:41
  53.9 5.0 %collective-permute-start.18 = (f32[4,8,1024]{2,1,0:T(8,128)S(1)}, f32[4,8,1024]{2,1,0:T(8,128)S(1)}, u32[]{:S(2)}, u32[]{:S(2)}) collective-permute-start(f32[4,8,1024]{2,1,0:T(8,128)S(1)} %pad_maximum_fusion.1.refs_0_), channel_id=1, source_target_pairs={{0,4},{2,6},{4,0},{6,2},{1,5},{3,7},{5,1},{7,3},{8,12},{10,14},{12... | collective-permute-start | bytes 393224 | tf_op jit(solution)/shard_map/ppermute | solution.py:41
  54.4 5.0 %collective-permute-start.17 = (f32[4,8,1024]{2,1,0:T(8,128)S(1)}, f32[4,8,1024]{2,1,0:T(8,128)S(1)}, u32[]{:S(2)}, u32[]{:S(2)}) collective-permute-start(f32[4,8,1024]{2,1,0:T(8,128)S(1)} %pad_maximum_fusion.1.refs_0_), channel_id=1, source_target_pairs={{0,2},{2,0},{4,6},{6,4},{1,3},{3,1},{5,7},{7,5},{8,10},{10,8},{12,... | collective-permute-start | bytes 393224 | tf_op jit(solution)/shard_map/ppermute | solution.py:41
  62.9 0.6 copy-start.2
  63.5 5.4 %collective-permute-start.22 = (f32[8,128]{1,0:T(8,128)S(1)}, f32[8,128]{1,0:T(8,128)S(1)}, u32[]{:S(2)}, u32[]{:S(2)}) collective-permute-start(f32[8,128]{1,0:T(8,128)S(1)} %get-tuple-element.30), channel_id=1, source_target_pairs={{0,24},{8,16},{16,8},{24,0},{1,25},{9,17},{17,9},{25,1},{2,26},{10... | collective-permute-start | bytes 12296 | tf_op jit(solution)/shard_map/ppermute | solution.py:39
  64.7 4.5 %collective-permute-start.21 = (f32[8,128]{1,0:T(8,128)S(1)}, f32[8,128]{1,0:T(8,128)S(1)}, u32[]{:S(2)}, u32[]{:S(2)}) collective-permute-start(f32[8,128]{1,0:T(8,128)S(1)} %get-tuple-element.30), channel_id=1, source_target_pairs={{0,16},{8,24},{16,0},{24,8},{1,17},{9,25},{17,1},{25,9},{2,18},{10... | collective-permute-start | bytes 12296 | tf_op jit(solution)/shard_map/ppermute | solution.py:39
  65.9 3.6 %collective-permute-start.20 = (f32[8,128]{1,0:T(8,128)S(1)}, f32[8,128]{1,0:T(8,128)S(1)}, u32[]{:S(2)}, u32[]{:S(2)}) collective-permute-start(f32[8,128]{1,0:T(8,128)S(1)} %get-tuple-element.30), channel_id=1, source_target_pairs={{0,8},{8,0},{16,24},{24,16},{1,9},{9,1},{17,25},{25,17},{2,10},{10... | collective-permute-start | bytes 12296 | tf_op jit(solution)/shard_map/ppermute | solution.py:39
  69.5 6.9 %collective-permute-start.25 = (f32[4,8,128]{2,1,0:T(8,128)S(1)}, f32[4,8,128]{2,1,0:T(8,128)S(1)}, u32[]{:S(2)}, u32[]{:S(2)}) collective-permute-start(f32[4,8,128]{2,1,0:T(8,128)S(1)} %pad_maximum_fusion.2), channel_id=1, source_target_pairs={{0,6},{2,4},{4,2},{6,0},{1,7},{3,5},{5,3},{7,1},{8,14},{10,12},{12... | collective-permute-start | bytes 49160 | tf_op jit(solution)/shard_map/ppermute | solution.py:41
  72.1 4.3 %collective-permute-start.24 = (f32[4,8,128]{2,1,0:T(8,128)S(1)}, f32[4,8,128]{2,1,0:T(8,128)S(1)}, u32[]{:S(2)}, u32[]{:S(2)}) collective-permute-start(f32[4,8,128]{2,1,0:T(8,128)S(1)} %pad_maximum_fusion.2), channel_id=1, source_target_pairs={{0,4},{2,6},{4,0},{6,2},{1,5},{3,7},{5,1},{7,3},{8,12},{10,14},{12... | collective-permute-start | bytes 49160 | tf_op jit(solution)/shard_map/ppermute | solution.py:41
  72.7 3.7 %collective-permute-start.23 = (f32[4,8,128]{2,1,0:T(8,128)S(1)}, f32[4,8,128]{2,1,0:T(8,128)S(1)}, u32[]{:S(2)}, u32[]{:S(2)}) collective-permute-start(f32[4,8,128]{2,1,0:T(8,128)S(1)} %pad_maximum_fusion.2), channel_id=1, source_target_pairs={{0,2},{2,0},{4,6},{6,4},{1,3},{3,1},{5,7},{7,5},{8,10},{10,8},{12,... | collective-permute-start | bytes 49160 | tf_op jit(solution)/shard_map/ppermute | solution.py:41
  76.5 0.6 copy-start.3

commit v10 on v9

--- a/solution.py
+++ b/solution.py
@@ -233,44 +233,40 @@
         high = chosen.astype(jnp.bfloat16).astype(jnp.float32)
         layer_ref[k] = jnp.transpose(jnp.concatenate([high, chosen - high], axis=0)).astype(jnp.bfloat16)
 
-    def add_products(totals, table, t, lefts):
+    def vectors(table, t):
         right = layer_ref[items_ref[table, t]] * mask_ref[items_ref[table + 1, t]]
-        right = jnp.concatenate([right, right], axis=0)
-        return [
-            total + jnp.dot(left, right, preferred_element_type=jnp.float32)
-            for total, left in zip(totals, lefts)
-        ]
+        return jnp.concatenate([right, right], axis=0)
+
+    def add_group(lefts, rights):
+        left, right = jnp.concatenate(lefts, axis=1), jnp.concatenate(rights, axis=0)
+        acc_ref[...] += jnp.dot(left, right, preferred_element_type=jnp.float32)
 
     if step == 0:
         for d in range(freqs):
 
             @pl.loop(0, items_ref[4 * d + 3, 0])
             def _(group):
-                totals = [acc_ref[0], acc_ref[1]]
+                lefts, rights = [], []
                 for u in range(GROUP):
                     t = group * GROUP + u
                     stored = items_ref[4 * d + 2, t]
                     here = stored - d * g_refs[d].shape[0]
-                    lefts = []
-                    for m, block_refs in enumerate((g_refs, c_refs)):
-                        left = jnp.concatenate(split(block_refs[d][here]), axis=1)
-                        split_ref[stored, m] = left
-                        lefts.append(left)
-                    totals = add_products(totals, 4 * d, t, lefts)
-                acc_ref[0], acc_ref[1] = totals
+                    parts_of = split(jnp.concatenate([g_refs[d][here], c_refs[d][here]], axis=0))
+                    left = jnp.concatenate(parts_of, axis=1)
+                    split_ref[stored] = left
+                    lefts.append(left)
+                    rights.append(vectors(4 * d, t))
+                add_group(lefts, rights)
     else:
 
         @pl.loop(0, items_ref[4 * freqs + 3, 0])
         def _(group):
-            totals = [acc_ref[0], acc_ref[1]]
-            for u in range(FULL_GROUP):
-                t = group * FULL_GROUP + u
-                stored = items_ref[4 * freqs + 2, t]
-                totals = add_products(totals, 4 * freqs, t, [split_ref[stored, m] for m in range(2)])
-            acc_ref[0], acc_ref[1] = totals
+            places = [group * FULL_GROUP + u for u in range(FULL_GROUP)]
+            lefts = [split_ref[items_ref[4 * freqs + 2, t]] for t in places]
+            add_group(lefts, [vectors(4 * freqs, t) for t in places])
 
     half = row_blocks * parts
-    gsum, csum = jnp.transpose(acc_ref[0]), jnp.transpose(acc_ref[1])
+    gsum, csum = jnp.transpose(acc_ref[:size]), jnp.transpose(acc_ref[size:])
     gsum, csum = gsum[:half] + gsum[half:], csum[:half] + csum[half:]
     turn = turn_ref[...]
     for b in range(row_blocks):
@@ -313,10 +309,10 @@
     scratch_shapes = [
         pltpu.VMEM((slots, size, LANES), jnp.bfloat16),
         pltpu.VMEM((row_blocks + 1, size, LANES), jnp.bfloat16),
-        pltpu.VMEM((2, size, LANES), jnp.float32),
+        pltpu.VMEM((2 * size, LANES), jnp.float32),
     ]
     if step == 0:
-        out_shape.append(jax.ShapeDtypeStruct((row_blocks * slots, 2, size, 2 * size), jnp.bfloat16))
+        out_shape.append(jax.ShapeDtypeStruct((row_blocks * slots, 2 * size, 2 * size), jnp.bfloat16))
     if step == ITERS - 1:
         scratch_shapes += [pltpu.VMEM(z, jnp.float32), pltpu.VMEM((parts, rows), jnp.float32)]
     return pl.pallas_call(

time: 79.9 us -> 81 us (1.014)
  Pallas kernels: 14.2 us -> 15.6 us
  starting transfers between devices: 35.1 us -> 34 us
    pallas_call x3, Pallas kernels: 11 us -> 12.4 us  [run_step(): pl.pallas_call(functools.partial(step_kernel, step, plane, line, freqs),...]
    ppermute x12, starting transfers between devices: 15.6 us -> 14.5 us  [gather_rows(): lax.ppermute(whole_line, 'place', perm)]
where the time goes in v10:
time: 81 us; the launch traced here: 80.1 us
  starting transfers between devices  34 us (42%)
  waiting for transfers between devices  22.8 us (28%)
  Pallas kernels  15.6 us (19%)
  local copies, waits for them, and re-layouts  6.83 us (8%)
  between operations  0.82 us (1%)
    ppermute x12, starting transfers between devices, gather_rows(): lax.ppermute(rows, 'line', perm)  18.9 us
    ppermute x12, starting transfers between devices, gather_rows(): lax.ppermute(whole_line, 'place', perm)  14.5 us
    pallas_call x3, Pallas kernels, run_step(): pl.pallas_call(functools.partial(step_kernel, step, plane, line, freqs),...  12.4 us
    ppermute x12, waiting for transfers between devices, gather_rows(): lax.ppermute(whole_line, 'place', perm)  11.5 us
    ppermute x12, waiting for transfers between devices, gather_rows(): lax.ppermute(rows, 'line', perm)  11.3 us
    unnamed x17, local copies, waits for them, and re-layouts  4.45 us
    pallas_call x1, Pallas kernels, run_final(): pl.pallas_call(final_kernel, in_specs=[vmem] * 2, out_specs=[vmem] * 2, o...  2.17 us
  transfers between devices with their start and end apart: 26, of which 17 were waited for; matrix products, arithmetic and copies ran while one was open for 3% of the time, Pallas kernels for 1%

profile of v10, /device:TPU:0, one launch (start us, length us, event | category | flops | bytes accessed | tf_op | source)
XLA Modules:
  0.0 80.1 jit_solution(5610140035227258619)
XLA Ops:
  1.2 3.0 %collective-permute-start = (f32[2,4,1024]{2,1,0:T(4,128)}, f32[2,4,1024]{2,1,0:T(4,128)S(1)}, u32[]{:S(2)}, u32[]{:S(2)}) collective-permute-start(f32[2,4,1024]{2,1,0:T(4,128)} %param.6), channel_id=1, source_target_pairs={{0,8},{8,0},{16,24},{24,16},{1,9},{9,1},{17,25},{25,17},{2,10},{10... | collective-permute-start | bytes 98312 | tf_op jit(solution)/shard_map/ppermute | solution.py:39
  4.2 2.5 %collective-permute-start.2 = (f32[2,4,1024]{2,1,0:T(4,128)}, f32[2,4,1024]{2,1,0:T(4,128)S(1)}, u32[]{:S(2)}, u32[]{:S(2)}) collective-permute-start(f32[2,4,1024]{2,1,0:T(4,128)} %param.6), channel_id=1, source_target_pairs={{0,24},{8,16},{16,8},{24,0},{1,25},{9,17},{17,9},{25,1},{2,26},{10... | collective-permute-start | bytes 98312 | tf_op jit(solution)/shard_map/ppermute | solution.py:39
  6.8 0.8 %stack.72 = f32[1,8,1024]{2,1,0:T(8,128)S(1)} reshape(f32[2,4,1024]{2,1,0:T(4,128)} %param.6) | data formatting | bytes 65536 | tf_op jit(solution)/shard_map/stack | solution.py:40
  7.7 2.6 %collective-permute-done.2 = f32[2,4,1024]{2,1,0:T(4,128)S(1)} collective-permute-done((f32[2,4,1024]{2,1,0:T(4,128)}, f32[2,4,1024]{2,1,0:T(4,128)S(1)}, u32[]{:S(2)}, u32[]{:S(2)}) %collective-permute-start.2) | collective-permute-done | bytes 32800 | tf_op jit(solution)/shard_map/ppermute | solution.py:39
  10.3 1.8 %collective-permute-done.1 = f32[2,4,1024]{2,1,0:T(4,128)S(1)} collective-permute-done((f32[2,4,1024]{2,1,0:T(4,128)}, f32[2,4,1024]{2,1,0:T(4,128)S(1)}, u32[]{:S(2)}, u32[]{:S(2)}) %collective-permute-start.1) | collective-permute-done | bytes 32800 | tf_op jit(solution)/shard_map/ppermute | solution.py:39
  12.1 2.5 %collective-permute-start.5 = (f32[4,8,1024]{2,1,0:T(8,128)S(1)}, f32[4,8,1024]{2,1,0:T(8,128)S(1)}, u32[]{:S(2)}, u32[]{:S(2)}) collective-permute-start(f32[4,8,1024]{2,1,0:T(8,128)S(1)} %constant_dynamic-update-slice_fusion.refs_0_), channel_id=1, source_target_pairs={{0,6},{2,4},{4,2},{6,0},{1,7},{3,5},{5,3},{7,1},{8,14},{10,12},{12... | collective-permute-start | bytes 393224 | tf_op jit(solution)/shard_map/ppermute | solution.py:41
  15.2 0.5 collective-permute-start.3
  15.7 0.8 reshape.25
  16.5 0.7 concatenate.8.scalars_ref
  17.2 1.6 %copy-done = f32[8,4,128,128]{3,2,1,0:T(8,128)S(1)} copy-done((f32[8,4,128,128]{3,2,1,0:T(8,128)S(1)}, f32[8,4,128,128]{3,2,1,0:T(8,128)}, u32[]{:S(2)}) %copy-start) | copy-done | bytes 2097176
  18.8 1.6 %copy-done.1 = f32[8,4,128,128]{3,2,1,0:T(8,128)S(1)} copy-done((f32[8,4,128,128]{3,2,1,0:T(8,128)S(1)}, f32[8,4,128,128]{3,2,1,0:T(8,128)}, u32[]{:S(2)}) %copy-start.1) | copy-done | bytes 2097176
  20.4 1.1 %setup.1 = (s32[12,128]{1,0:T(8,128)S(1)}, s32[8,8]{1,0:T(8,128)S(1)}, f32[8,128]{1,0:T(8,128)S(1)}, f32[32,128,128]{2,1,0:T(8,128)S(1)}, f32[32,128,128]{2,1,0:T(8,128)S(1)}) custom-call(s32[79]{0:T(128)S(1)} %concatenate.8.scalars_ref, f32[32,128,128]{2,1,0:T(8,128)S(1)} %bitcast.23, f32[32,128,128]{2,1,0:T(8,128)S(1)} %bitcast.25), custom_call_target="tpu_custom_call" | custom-call | bytes 8388608 | tf_op jit(solution)/shard_map/setup/pallas_call | solution.py:114
  21.6 5.0 %step_0.1 = (f32[129,8,128]{2,1,0:T(8,128)S(1)}, f32[8,1024]{1,0:T(8,128)S(1)}, f32[8,128]{1,0:T(8,128)S(1)}, bf16[64,256,256]{2,1,0:T(8,128)(2,1)S(1)}) custom-call(s32[12,128]{1,0:T(8,128)S(1)} %get-tuple-element.18.items_ref, s32[8,8]{1,0:T(8,128)S(1)} %get-tuple-element.19.places_ref, f32[8,128]{1,0:T(8,128)S(1)} %get-tuple-element.20.turn_ref, ...), custom_call_target="tpu_custom_call" | custom-call | tf_op jit(solution)/shard_map/step_0/pallas_call | solution.py:318
  26.5 1.2 %collective-permute-start.10 = (f32[8,1024]{1,0:T(8,128)S(1)}, f32[8,1024]{1,0:T(8,128)S(1)}, u32[]{:S(2)}, u32[]{:S(2)}) collective-permute-start(f32[8,1024]{1,0:T(8,128)S(1)} %get-tuple-element.24), channel_id=1, source_target_pairs={{0,24},{8,16},{16,8},{24,0},{1,25},{9,17},{17,9},{25,1},{2,26},{10... | collective-permute-start | bytes 98312 | tf_op jit(solution)/shard_map/ppermute | solution.py:39
  27.8 1.1 %collective-permute-start.9 = (f32[8,1024]{1,0:T(8,128)S(1)}, f32[8,1024]{1,0:T(8,128)S(1)}, u32[]{:S(2)}, u32[]{:S(2)}) collective-permute-start(f32[8,1024]{1,0:T(8,128)S(1)} %get-tuple-element.24), channel_id=1, source_target_pairs={{0,16},{8,24},{16,0},{24,8},{1,17},{9,25},{17,1},{25,9},{2,18},{10... | collective-permute-start | bytes 98312 | tf_op jit(solution)/shard_map/ppermute | solution.py:39
  28.8 2.2 %collective-permute-start.8 = (f32[8,1024]{1,0:T(8,128)S(1)}, f32[8,1024]{1,0:T(8,128)S(1)}, u32[]{:S(2)}, u32[]{:S(2)}) collective-permute-start(f32[8,1024]{1,0:T(8,128)S(1)} %get-tuple-element.24), channel_id=1, source_target_pairs={{0,8},{8,0},{16,24},{24,16},{1,9},{9,1},{17,25},{25,17},{2,10},{10... | collective-permute-start | bytes 98312 | tf_op jit(solution)/shard_map/ppermute | solution.py:39
  31.0 1.3 %collective-permute-done.10 = f32[8,1024]{1,0:T(8,128)S(1)} collective-permute-done((f32[8,1024]{1,0:T(8,128)S(1)}, f32[8,1024]{1,0:T(8,128)S(1)}, u32[]{:S(2)}, u32[]{:S(2)}) %collective-permute-start.10) | collective-permute-done | bytes 32800 | tf_op jit(solution)/shard_map/ppermute | solution.py:39
  32.3 0.7 collective-permute-done.9
  33.0 2.9 %collective-permute-start.13 = (f32[4,8,1024]{2,1,0:T(8,128)S(1)}, f32[4,8,1024]{2,1,0:T(8,128)S(1)}, u32[]{:S(2)}, u32[]{:S(2)}) collective-permute-start(f32[4,8,1024]{2,1,0:T(8,128)S(1)} %pad_maximum_fusion.refs_0_), channel_id=1, source_target_pairs={{0,6},{2,4},{4,2},{6,0},{1,7},{3,5},{5,3},{7,1},{8,14},{10,12},{12... | collective-permute-start | bytes 393224 | tf_op jit(solution)/shard_map/ppermute | solution.py:41
  35.9 1.0 %collective-permute-start.12 = (f32[4,8,1024]{2,1,0:T(8,128)S(1)}, f32[4,8,1024]{2,1,0:T(8,128)S(1)}, u32[]{:S(2)}, u32[]{:S(2)}) collective-permute-start(f32[4,8,1024]{2,1,0:T(8,128)S(1)} %pad_maximum_fusion.refs_0_), channel_id=1, source_target_pairs={{0,4},{2,6},{4,0},{6,2},{1,5},{3,7},{5,1},{7,3},{8,12},{10,14},{12... | collective-permute-start | bytes 393224 | tf_op jit(solution)/shard_map/ppermute | solution.py:41
  36.9 2.0 %collective-permute-done.13.refs_3_ = f32[4,8,1024]{2,1,0:T(8,128)S(1)} collective-permute-done((f32[4,8,1024]{2,1,0:T(8,128)S(1)}, f32[4,8,1024]{2,1,0:T(8,128)S(1)}, u32[]{:S(2)}, u32[]{:S(2)}) %collective-permute-start.13) | collective-permute-done | bytes 131104 | tf_op jit(solution)/shard_map/ppermute | solution.py:41
  39.0 1.9 %collective-permute-done.12.refs_2_ = f32[4,8,1024]{2,1,0:T(8,128)S(1)} collective-permute-done((f32[4,8,1024]{2,1,0:T(8,128)S(1)}, f32[4,8,1024]{2,1,0:T(8,128)S(1)}, u32[]{:S(2)}, u32[]{:S(2)}) %collective-permute-start.12) | collective-permute-done | bytes 131104 | tf_op jit(solution)/shard_map/ppermute | solution.py:41
  40.9 1.0 %collective-permute-done.11.refs_1_ = f32[4,8,1024]{2,1,0:T(8,128)S(1)} collective-permute-done((f32[4,8,1024]{2,1,0:T(8,128)S(1)}, f32[4,8,1024]{2,1,0:T(8,128)S(1)}, u32[]{:S(2)}, u32[]{:S(2)}) %collective-permute-start.11) | collective-permute-done | bytes 131104 | tf_op jit(solution)/shard_map/ppermute | solution.py:41
  41.9 3.5 %step_1.1 = (f32[129,8,128]{2,1,0:T(8,128)S(1)}, f32[8,1024]{1,0:T(8,128)S(1)}, f32[8,128]{1,0:T(8,128)S(1)}) custom-call(s32[12,128]{1,0:T(8,128)S(1)} %get-tuple-element.18.items_ref, s32[8,8]{1,0:T(8,128)S(1)} %get-tuple-element.19.places_ref, f32[8,128]{1,0:T(8,128)S(1)} %get-tuple-element.20.turn_ref, f32[8,128]{1,0:T(8,128)S(1)} %get-tuple-element.23.info_in_ref, ...), custom_call_target="tpu_custom_call" | custom-call | tf_op jit(solution)/shard_map/step_1/pallas_call | solution.py:318
  45.4 1.6 %collective-permute-start.16 = (f32[8,1024]{1,0:T(8,128)S(1)}, f32[8,1024]{1,0:T(8,128)S(1)}, u32[]{:S(2)}, u32[]{:S(2)}) collective-permute-start(f32[8,1024]{1,0:T(8,128)S(1)} %get-tuple-element.28), channel_id=1, source_target_pairs={{0,24},{8,16},{16,8},{24,0},{1,25},{9,17},{17,9},{25,1},{2,26},{10... | collective-permute-start | bytes 98312 | tf_op jit(solution)/shard_map/ppermute | solution.py:39
  47.0 1.6 %collective-permute-start.15 = (f32[8,1024]{1,0:T(8,128)S(1)}, f32[8,1024]{1,0:T(8,128)S(1)}, u32[]{:S(2)}, u32[]{:S(2)}) collective-permute-start(f32[8,1024]{1,0:T(8,128)S(1)} %get-tuple-element.28), channel_id=1, source_target_pairs={{0,16},{8,24},{16,0},{24,8},{1,17},{9,25},{17,1},{25,9},{2,18},{10... | collective-permute-start | bytes 98312 | tf_op jit(solution)/shard_map/ppermute | solution.py:39
  48.6 1.3 %collective-permute-start.14 = (f32[8,1024]{1,0:T(8,128)S(1)}, f32[8,1024]{1,0:T(8,128)S(1)}, u32[]{:S(2)}, u32[]{:S(2)}) collective-permute-start(f32[8,1024]{1,0:T(8,128)S(1)} %get-tuple-element.28), channel_id=1, source_target_pairs={{0,8},{8,0},{16,24},{24,16},{1,9},{9,1},{17,25},{25,17},{2,10},{10... | collective-permute-start | bytes 98312 | tf_op jit(solution)/shard_map/ppermute | solution.py:39
  49.9 1.3 %collective-permute-done.16 = f32[8,1024]{1,0:T(8,128)S(1)} collective-permute-done((f32[8,1024]{1,0:T(8,128)S(1)}, f32[8,1024]{1,0:T(8,128)S(1)}, u32[]{:S(2)}, u32[]{:S(2)}) %collective-permute-start.16) | collective-permute-done | bytes 32800 | tf_op jit(solution)/shard_map/ppermute | solution.py:39
  51.2 0.7 collective-permute-done.15
  51.9 0.7 collective-permute-done.14
  52.5 1.6 %collective-permute-start.19 = (f32[4,8,1024]{2,1,0:T(8,128)S(1)}, f32[4,8,1024]{2,1,0:T(8,128)S(1)}, u32[]{:S(2)}, u32[]{:S(2)}) collective-permute-start(f32[4,8,1024]{2,1,0:T(8,128)S(1)} %pad_maximum_fusion.1.refs_0_), channel_id=1, source_target_pairs={{0,6},{2,4},{4,2},{6,0},{1,7},{3,5},{5,3},{7,1},{8,14},{10,12},{12... | collective-permute-start | bytes 393224 | tf_op jit(solution)/shard_map/ppermute | solution.py:41
  54.1 1.0 %collective-permute-start.18 = (f32[4,8,1024]{2,1,0:T(8,128)S(1)}, f32[4,8,1024]{2,1,0:T(8,128)S(1)}, u32[]{:S(2)}, u32[]{:S(2)}) collective-permute-start(f32[4,8,1024]{2,1,0:T(8,128)S(1)} %pad_maximum_fusion.1.refs_0_), channel_id=1, source_target_pairs={{0,4},{2,6},{4,0},{6,2},{1,5},{3,7},{5,1},{7,3},{8,12},{10,14},{12... | collective-permute-start | bytes 393224 | tf_op jit(solution)/shard_map/ppermute | solution.py:41
  55.0 1.0 %collective-permute-start.17 = (f32[4,8,1024]{2,1,0:T(8,128)S(1)}, f32[4,8,1024]{2,1,0:T(8,128)S(1)}, u32[]{:S(2)}, u32[]{:S(2)}) collective-permute-start(f32[4,8,1024]{2,1,0:T(8,128)S(1)} %pad_maximum_fusion.1.refs_0_), channel_id=1, source_target_pairs={{0,2},{2,0},{4,6},{6,4},{1,3},{3,1},{5,7},{7,5},{8,10},{10,8},{12,... | collective-permute-start | bytes 393224 | tf_op jit(solution)/shard_map/ppermute | solution.py:41
  56.1 2.5 %collective-permute-done.19.refs_3_ = f32[4,8,1024]{2,1,0:T(8,128)S(1)} collective-permute-done((f32[4,8,1024]{2,1,0:T(8,128)S(1)}, f32[4,8,1024]{2,1,0:T(8,128)S(1)}, u32[]{:S(2)}, u32[]{:S(2)}) %collective-permute-start.19) | collective-permute-done | bytes 131104 | tf_op jit(solution)/shard_map/ppermute | solution.py:41
  58.5 1.3 %collective-permute-done.18.refs_2_ = f32[4,8,1024]{2,1,0:T(8,128)S(1)} collective-permute-done((f32[4,8,1024]{2,1,0:T(8,128)S(1)}, f32[4,8,1024]{2,1,0:T(8,128)S(1)}, u32[]{:S(2)}, u32[]{:S(2)}) %collective-permute-start.18) | collective-permute-done | bytes 131104 | tf_op jit(solution)/shard_map/ppermute | solution.py:41
  60.0 3.9 %step_2.1 = (f32[3,8,1024]{2,1,0:T(8,128)S(1)}, f32[8,128]{1,0:T(8,128)S(1)}) custom-call(s32[12,128]{1,0:T(8,128)S(1)} %get-tuple-element.18.items_ref, s32[8,8]{1,0:T(8,128)S(1)} %get-tuple-element.19.places_ref, f32[8,128]{1,0:T(8,128)S(1)} %get-tuple-element.20.turn_ref, f32[8,128]{1,0:T(8,128)S(1)} %get-tuple-element.27.info_in_ref, ...), custom_call_target="tpu_custom_call" | custom-call | tf_op jit(solution)/shard_map/step_2/pallas_call | solution.py:318
  63.9 0.6 copy-done.2
  64.6 1.6 %collective-permute-start.22 = (f32[8,128]{1,0:T(8,128)S(1)}, f32[8,128]{1,0:T(8,128)S(1)}, u32[]{:S(2)}, u32[]{:S(2)}) collective-permute-start(f32[8,128]{1,0:T(8,128)S(1)} %get-tuple-element.30), channel_id=1, source_target_pairs={{0,24},{8,16},{16,8},{24,0},{1,25},{9,17},{17,9},{25,1},{2,26},{10... | collective-permute-start | bytes 12296 | tf_op jit(solution)/shard_map/ppermute | solution.py:39
  66.1 1.4 %collective-permute-start.21 = (f32[8,128]{1,0:T(8,128)S(1)}, f32[8,128]{1,0:T(8,128)S(1)}, u32[]{:S(2)}, u32[]{:S(2)}) collective-permute-start(f32[8,128]{1,0:T(8,128)S(1)} %get-tuple-element.30), channel_id=1, source_target_pairs={{0,16},{8,24},{16,0},{24,8},{1,17},{9,25},{17,1},{25,9},{2,18},{10... | collective-permute-start | bytes 12296 | tf_op jit(solution)/shard_map/ppermute | solution.py:39
  67.6 1.4 %collective-permute-start.20 = (f32[8,128]{1,0:T(8,128)S(1)}, f32[8,128]{1,0:T(8,128)S(1)}, u32[]{:S(2)}, u32[]{:S(2)}) collective-permute-start(f32[8,128]{1,0:T(8,128)S(1)} %get-tuple-element.30), channel_id=1, source_target_pairs={{0,8},{8,0},{16,24},{24,16},{1,9},{9,1},{17,25},{25,17},{2,10},{10... | collective-permute-start | bytes 12296 | tf_op jit(solution)/shard_map/ppermute | solution.py:39
  69.0 1.0 %collective-permute-done.22 = f32[8,128]{1,0:T(8,128)S(1)} collective-permute-done((f32[8,128]{1,0:T(8,128)S(1)}, f32[8,128]{1,0:T(8,128)S(1)}, u32[]{:S(2)}, u32[]{:S(2)}) %collective-permute-start.22) | collective-permute-done | bytes 4128 | tf_op jit(solution)/shard_map/ppermute | solution.py:39
  70.0 0.7 collective-permute-done.21
  71.2 1.6 %collective-permute-start.25 = (f32[4,8,128]{2,1,0:T(8,128)S(1)}, f32[4,8,128]{2,1,0:T(8,128)S(1)}, u32[]{:S(2)}, u32[]{:S(2)}) collective-permute-start(f32[4,8,128]{2,1,0:T(8,128)S(1)} %pad_maximum_fusion.2), channel_id=1, source_target_pairs={{0,6},{2,4},{4,2},{6,0},{1,7},{3,5},{5,3},{7,1},{8,14},{10,12},{12... | collective-permute-start | bytes 49160 | tf_op jit(solution)/shard_map/ppermute | solution.py:41
  72.8 0.7 collective-permute-start.24
  73.5 1.1 %collective-permute-start.23 = (f32[4,8,128]{2,1,0:T(8,128)S(1)}, f32[4,8,128]{2,1,0:T(8,128)S(1)}, u32[]{:S(2)}, u32[]{:S(2)}) collective-permute-start(f32[4,8,128]{2,1,0:T(8,128)S(1)} %pad_maximum_fusion.2), channel_id=1, source_target_pairs={{0,2},{2,0},{4,6},{6,4},{1,3},{3,1},{5,7},{7,5},{8,10},{10,8},{12,... | collective-permute-start | bytes 49160 | tf_op jit(solution)/shard_map/ppermute | solution.py:41
  74.7 2.6 %collective-permute-done.23 = f32[4,8,128]{2,1,0:T(8,128)S(1)} collective-permute-done((f32[4,8,128]{2,1,0:T(8,128)S(1)}, f32[4,8,128]{2,1,0:T(8,128)S(1)}, u32[]{:S(2)}, u32[]{:S(2)}) %collective-permute-start.23) | collective-permute-done | bytes 16416 | tf_op jit(solution)/shard_map/ppermute | solution.py:41
  77.3 0.6 copy-done.3
  77.9 2.2 %final.1 = (f32[2,4,1024]{2,1,0:T(4,128)}, f32[1,4]{1,0:T(1,128)}) custom-call(f32[16,8,128]{2,1,0:T(8,128)} %copy-done.3, f32[3,8,1024]{2,1,0:T(8,128)} %copy-done.2), custom_call_target="tpu_custom_call" | custom-call | tf_op jit(solution)/shard_map/final/pallas_call | solution.py:399
  (38 shorter events, 2.1 us)
Async XLA Ops:
  0.6 20.9 %collective-permute-start.6 = (f32[32,128,128]{2,1,0:T(8,128)}, f32[32,128,128]{2,1,0:T(8,128)S(1)}, u32[]{:S(2)}, u32[]{:S(2)}) collective-permute-start(f32[32,128,128]{2,1,0:T(8,128)} %bitcast.22), channel_id=1, source_target_pairs={{0,1},{1,0},{2,3},{3,2},{4,5},{5,4},{6,7},{7,6},{8,9},{9,8},{10,11... | collective-permute-start | bytes 6291464 | tf_op jit(solution)/shard_map/ppermute | solution.py:426
  1.1 20.4 %collective-permute-start.7 = (f32[32,128,128]{2,1,0:T(8,128)}, f32[32,128,128]{2,1,0:T(8,128)}, u32[]{:S(2)}, u32[]{:S(2)}) collective-permute-start(f32[32,128,128]{2,1,0:T(8,128)} %bitcast.24), channel_id=1, source_target_pairs={{0,1},{1,0},{2,3},{3,2},{4,5},{5,4},{6,7},{7,6},{8,9},{9,8},{10,11... | collective-permute-start | bytes 6291464 | tf_op jit(solution)/shard_map/ppermute | solution.py:427
  1.2 6.4 %collective-permute-start = (f32[2,4,1024]{2,1,0:T(4,128)}, f32[2,4,1024]{2,1,0:T(4,128)S(1)}, u32[]{:S(2)}, u32[]{:S(2)}) collective-permute-start(f32[2,4,1024]{2,1,0:T(4,128)} %param.6), channel_id=1, source_target_pairs={{0,8},{8,0},{16,24},{24,16},{1,9},{9,1},{17,25},{25,17},{2,10},{10... | collective-permute-start | bytes 98312 | tf_op jit(solution)/shard_map/ppermute | solution.py:39
  4.2 6.1 %collective-permute-start.2 = (f32[2,4,1024]{2,1,0:T(4,128)}, f32[2,4,1024]{2,1,0:T(4,128)S(1)}, u32[]{:S(2)}, u32[]{:S(2)}) collective-permute-start(f32[2,4,1024]{2,1,0:T(4,128)} %param.6), channel_id=1, source_target_pairs={{0,24},{8,16},{16,8},{24,0},{1,25},{9,17},{17,9},{25,1},{2,26},{10... | collective-permute-start | bytes 98312 | tf_op jit(solution)/shard_map/ppermute | solution.py:39
  6.7 5.4 %collective-permute-start.1 = (f32[2,4,1024]{2,1,0:T(4,128)}, f32[2,4,1024]{2,1,0:T(4,128)S(1)}, u32[]{:S(2)}, u32[]{:S(2)}) collective-permute-start(f32[2,4,1024]{2,1,0:T(4,128)} %param.6), channel_id=1, source_target_pairs={{0,16},{8,24},{16,0},{24,8},{1,17},{9,25},{17,1},{25,9},{2,18},{10... | collective-permute-start | bytes 98312 | tf_op jit(solution)/shard_map/ppermute | solution.py:39
  12.1 9.4 %collective-permute-start.5 = (f32[4,8,1024]{2,1,0:T(8,128)S(1)}, f32[4,8,1024]{2,1,0:T(8,128)S(1)}, u32[]{:S(2)}, u32[]{:S(2)}) collective-permute-start(f32[4,8,1024]{2,1,0:T(8,128)S(1)} %constant_dynamic-update-slice_fusion.refs_0_), channel_id=1, source_target_pairs={{0,6},{2,4},{4,2},{6,0},{1,7},{3,5},{5,3},{7,1},{8,14},{10,12},{12... | collective-permute-start | bytes 393224 | tf_op jit(solution)/shard_map/ppermute | solution.py:41
  14.6 6.9 %collective-permute-start.4 = (f32[4,8,1024]{2,1,0:T(8,128)S(1)}, f32[4,8,1024]{2,1,0:T(8,128)S(1)}, u32[]{:S(2)}, u32[]{:S(2)}) collective-permute-start(f32[4,8,1024]{2,1,0:T(8,128)S(1)} %constant_dynamic-update-slice_fusion.refs_0_), channel_id=1, source_target_pairs={{0,4},{2,6},{4,0},{6,2},{1,5},{3,7},{5,1},{7,3},{8,12},{10,14},{12... | collective-permute-start | bytes 393224 | tf_op jit(solution)/shard_map/ppermute | solution.py:41
  15.2 6.4 %collective-permute-start.3 = (f32[4,8,1024]{2,1,0:T(8,128)S(1)}, f32[4,8,1024]{2,1,0:T(8,128)S(1)}, u32[]{:S(2)}, u32[]{:S(2)}) collective-permute-start(f32[4,8,1024]{2,1,0:T(8,128)S(1)} %constant_dynamic-update-slice_fusion.refs_0_), channel_id=1, source_target_pairs={{0,2},{2,0},{4,6},{6,4},{1,3},{3,1},{5,7},{7,5},{8,10},{10,8},{12,... | collective-permute-start | bytes 393224 | tf_op jit(solution)/shard_map/ppermute | solution.py:41
  17.2 1.6 %copy-start = (f32[8,4,128,128]{3,2,1,0:T(8,128)S(1)}, f32[8,4,128,128]{3,2,1,0:T(8,128)}, u32[]{:S(2)}) copy-start(f32[8,4,128,128]{3,2,1,0:T(8,128)} %param.7) | copy-start | bytes 6291460
  18.8 1.6 %copy-start.1 = (f32[8,4,128,128]{3,2,1,0:T(8,128)S(1)}, f32[8,4,128,128]{3,2,1,0:T(8,128)}, u32[]{:S(2)}) copy-start(f32[8,4,128,128]{3,2,1,0:T(8,128)} %param.8) | copy-start | bytes 6291460
  26.5 5.8 %collective-permute-start.10 = (f32[8,1024]{1,0:T(8,128)S(1)}, f32[8,1024]{1,0:T(8,128)S(1)}, u32[]{:S(2)}, u32[]{:S(2)}) collective-permute-start(f32[8,1024]{1,0:T(8,128)S(1)} %get-tuple-element.24), channel_id=1, source_target_pairs={{0,24},{8,16},{16,8},{24,0},{1,25},{9,17},{17,9},{25,1},{2,26},{10... | collective-permute-start | bytes 98312 | tf_op jit(solution)/shard_map/ppermute | solution.py:39
  27.8 5.3 %collective-permute-start.9 = (f32[8,1024]{1,0:T(8,128)S(1)}, f32[8,1024]{1,0:T(8,128)S(1)}, u32[]{:S(2)}, u32[]{:S(2)}) collective-permute-start(f32[8,1024]{1,0:T(8,128)S(1)} %get-tuple-element.24), channel_id=1, source_target_pairs={{0,16},{8,24},{16,0},{24,8},{1,17},{9,25},{17,1},{25,9},{2,18},{10... | collective-permute-start | bytes 98312 | tf_op jit(solution)/shard_map/ppermute | solution.py:39
  28.8 4.2 %collective-permute-start.8 = (f32[8,1024]{1,0:T(8,128)S(1)}, f32[8,1024]{1,0:T(8,128)S(1)}, u32[]{:S(2)}, u32[]{:S(2)}) collective-permute-start(f32[8,1024]{1,0:T(8,128)S(1)} %get-tuple-element.24), channel_id=1, source_target_pairs={{0,8},{8,0},{16,24},{24,16},{1,9},{9,1},{17,25},{25,17},{2,10},{10... | collective-permute-start | bytes 98312 | tf_op jit(solution)/shard_map/ppermute | solution.py:39
  33.0 5.9 %collective-permute-start.13 = (f32[4,8,1024]{2,1,0:T(8,128)S(1)}, f32[4,8,1024]{2,1,0:T(8,128)S(1)}, u32[]{:S(2)}, u32[]{:S(2)}) collective-permute-start(f32[4,8,1024]{2,1,0:T(8,128)S(1)} %pad_maximum_fusion.refs_0_), channel_id=1, source_target_pairs={{0,6},{2,4},{4,2},{6,0},{1,7},{3,5},{5,3},{7,1},{8,14},{10,12},{12... | collective-permute-start | bytes 393224 | tf_op jit(solution)/shard_map/ppermute | solution.py:41
  35.9 5.0 %collective-permute-start.12 = (f32[4,8,1024]{2,1,0:T(8,128)S(1)}, f32[4,8,1024]{2,1,0:T(8,128)S(1)}, u32[]{:S(2)}, u32[]{:S(2)}) collective-permute-start(f32[4,8,1024]{2,1,0:T(8,128)S(1)} %pad_maximum_fusion.refs_0_), channel_id=1, source_target_pairs={{0,4},{2,6},{4,0},{6,2},{1,5},{3,7},{5,1},{7,3},{8,12},{10,14},{12... | collective-permute-start | bytes 393224 | tf_op jit(solution)/shard_map/ppermute | solution.py:41
  36.9 5.0 %collective-permute-start.11 = (f32[4,8,1024]{2,1,0:T(8,128)S(1)}, f32[4,8,1024]{2,1,0:T(8,128)S(1)}, u32[]{:S(2)}, u32[]{:S(2)}) collective-permute-start(f32[4,8,1024]{2,1,0:T(8,128)S(1)} %pad_maximum_fusion.refs_0_), channel_id=1, source_target_pairs={{0,2},{2,0},{4,6},{6,4},{1,3},{3,1},{5,7},{7,5},{8,10},{10,8},{12,... | collective-permute-start | bytes 393224 | tf_op jit(solution)/shard_map/ppermute | solution.py:41
  45.4 5.8 %collective-permute-start.16 = (f32[8,1024]{1,0:T(8,128)S(1)}, f32[8,1024]{1,0:T(8,128)S(1)}, u32[]{:S(2)}, u32[]{:S(2)}) collective-permute-start(f32[8,1024]{1,0:T(8,128)S(1)} %get-tuple-element.28), channel_id=1, source_target_pairs={{0,24},{8,16},{16,8},{24,0},{1,25},{9,17},{17,9},{25,1},{2,26},{10... | collective-permute-start | bytes 98312 | tf_op jit(solution)/shard_map/ppermute | solution.py:39
  47.0 4.8 %collective-permute-start.15 = (f32[8,1024]{1,0:T(8,128)S(1)}, f32[8,1024]{1,0:T(8,128)S(1)}, u32[]{:S(2)}, u32[]{:S(2)}) collective-permute-start(f32[8,1024]{1,0:T(8,128)S(1)} %get-tuple-element.28), channel_id=1, source_target_pairs={{0,16},{8,24},{16,0},{24,8},{1,17},{9,25},{17,1},{25,9},{2,18},{10... | collective-permute-start | bytes 98312 | tf_op jit(solution)/shard_map/ppermute | solution.py:39
  48.6 3.9 %collective-permute-start.14 = (f32[8,1024]{1,0:T(8,128)S(1)}, f32[8,1024]{1,0:T(8,128)S(1)}, u32[]{:S(2)}, u32[]{:S(2)}) collective-permute-start(f32[8,1024]{1,0:T(8,128)S(1)} %get-tuple-element.28), channel_id=1, source_target_pairs={{0,8},{8,0},{16,24},{24,16},{1,9},{9,1},{17,25},{25,17},{2,10},{10... | collective-permute-start | bytes 98312 | tf_op jit(solution)/shard_map/ppermute | solution.py:39
  52.5 6.0 %collective-permute-start.19 = (f32[4,8,1024]{2,1,0:T(8,128)S(1)}, f32[4,8,1024]{2,1,0:T(8,128)S(1)}, u32[]{:S(2)}, u32[]{:S(2)}) collective-permute-start(f32[4,8,1024]{2,1,0:T(8,128)S(1)} %pad_maximum_fusion.1.refs_0_), channel_id=1, source_target_pairs={{0,6},{2,4},{4,2},{6,0},{1,7},{3,5},{5,3},{7,1},{8,14},{10,12},{12... | collective-permute-start | bytes 393224 | tf_op jit(solution)/shard_map/ppermute | solution.py:41
  54.1 5.8 %collective-permute-start.18 = (f32[4,8,1024]{2,1,0:T(8,128)S(1)}, f32[4,8,1024]{2,1,0:T(8,128)S(1)}, u32[]{:S(2)}, u32[]{:S(2)}) collective-permute-start(f32[4,8,1024]{2,1,0:T(8,128)S(1)} %pad_maximum_fusion.1.refs_0_), channel_id=1, source_target_pairs={{0,4},{2,6},{4,0},{6,2},{1,5},{3,7},{5,1},{7,3},{8,12},{10,14},{12... | collective-permute-start | bytes 393224 | tf_op jit(solution)/shard_map/ppermute | solution.py:41
  55.0 5.0 %collective-permute-start.17 = (f32[4,8,1024]{2,1,0:T(8,128)S(1)}, f32[4,8,1024]{2,1,0:T(8,128)S(1)}, u32[]{:S(2)}, u32[]{:S(2)}) collective-permute-start(f32[4,8,1024]{2,1,0:T(8,128)S(1)} %pad_maximum_fusion.1.refs_0_), channel_id=1, source_target_pairs={{0,2},{2,0},{4,6},{6,4},{1,3},{3,1},{5,7},{7,5},{8,10},{10,8},{12,... | collective-permute-start | bytes 393224 | tf_op jit(solution)/shard_map/ppermute | solution.py:41
  63.9 0.6 copy-start.2
  64.6 5.4 %collective-permute-start.22 = (f32[8,128]{1,0:T(8,128)S(1)}, f32[8,128]{1,0:T(8,128)S(1)}, u32[]{:S(2)}, u32[]{:S(2)}) collective-permute-start(f32[8,128]{1,0:T(8,128)S(1)} %get-tuple-element.30), channel_id=1, source_target_pairs={{0,24},{8,16},{16,8},{24,0},{1,25},{9,17},{17,9},{25,1},{2,26},{10... | collective-permute-start | bytes 12296 | tf_op jit(solution)/shard_map/ppermute | solution.py:39
  66.1 4.5 %collective-permute-start.21 = (f32[8,128]{1,0:T(8,128)S(1)}, f32[8,128]{1,0:T(8,128)S(1)}, u32[]{:S(2)}, u32[]{:S(2)}) collective-permute-start(f32[8,128]{1,0:T(8,128)S(1)} %get-tuple-element.30), channel_id=1, source_target_pairs={{0,16},{8,24},{16,0},{24,8},{1,17},{9,25},{17,1},{25,9},{2,18},{10... | collective-permute-start | bytes 12296 | tf_op jit(solution)/shard_map/ppermute | solution.py:39
  67.6 3.6 %collective-permute-start.20 = (f32[8,128]{1,0:T(8,128)S(1)}, f32[8,128]{1,0:T(8,128)S(1)}, u32[]{:S(2)}, u32[]{:S(2)}) collective-permute-start(f32[8,128]{1,0:T(8,128)S(1)} %get-tuple-element.30), channel_id=1, source_target_pairs={{0,8},{8,0},{16,24},{24,16},{1,9},{9,1},{17,25},{25,17},{2,10},{10... | collective-permute-start | bytes 12296 | tf_op jit(solution)/shard_map/ppermute | solution.py:39
  71.2 6.1 %collective-permute-start.25 = (f32[4,8,128]{2,1,0:T(8,128)S(1)}, f32[4,8,128]{2,1,0:T(8,128)S(1)}, u32[]{:S(2)}, u32[]{:S(2)}) collective-permute-start(f32[4,8,128]{2,1,0:T(8,128)S(1)} %pad_maximum_fusion.2), channel_id=1, source_target_pairs={{0,6},{2,4},{4,2},{6,0},{1,7},{3,5},{5,3},{7,1},{8,14},{10,12},{12... | collective-permute-start | bytes 49160 | tf_op jit(solution)/shard_map/ppermute | solution.py:41
  72.8 4.5 %collective-permute-start.24 = (f32[4,8,128]{2,1,0:T(8,128)S(1)}, f32[4,8,128]{2,1,0:T(8,128)S(1)}, u32[]{:S(2)}, u32[]{:S(2)}) collective-permute-start(f32[4,8,128]{2,1,0:T(8,128)S(1)} %pad_maximum_fusion.2), channel_id=1, source_target_pairs={{0,4},{2,6},{4,0},{6,2},{1,5},{3,7},{5,1},{7,3},{8,12},{10,14},{12... | collective-permute-start | bytes 49160 | tf_op jit(solution)/shard_map/ppermute | solution.py:41
  73.5 3.7 %collective-permute-start.23 = (f32[4,8,128]{2,1,0:T(8,128)S(1)}, f32[4,8,128]{2,1,0:T(8,128)S(1)}, u32[]{:S(2)}, u32[]{:S(2)}) collective-permute-start(f32[4,8,128]{2,1,0:T(8,128)S(1)} %pad_maximum_fusion.2), channel_id=1, source_target_pairs={{0,2},{2,0},{4,6},{6,4},{1,3},{3,1},{5,7},{7,5},{8,10},{10,8},{12,... | collective-permute-start | bytes 49160 | tf_op jit(solution)/shard_map/ppermute | solution.py:41
  77.3 0.6 copy-start.3

commit v11 on v10

--- a/solution.py
+++ b/solution.py
@@ -12,7 +12,7 @@
 ITERS = 3
 LANES = 128
 GROUP = 4
-FULL_GROUP = 8
+FULL_GROUP = 4
 SHARES = 16
 VMEM_LIMIT = 16 * 1024 * 1024
 
@@ -154,12 +154,17 @@
     row_blocks, slots = places_ref.shape
     nodes = plane * line
     if step == 0:
-        g_refs, c_refs = refs[:freqs], refs[freqs : 2 * freqs]
-        z_ref, local_ref, info_ref, split_ref, layer_ref, mask_ref, acc_ref = refs[2 * freqs :]
+        g_refs, c_refs = refs[:freqs], list(refs[freqs : 2 * freqs])
+        z_ref, local_ref, info_ref, split_ref, layer_ref, mask_ref, acc_ref, kept_ref, sems = refs[2 * freqs :]
+        arrivals = []
+        for d in range(1, freqs):
+            arrivals.append(pltpu.make_async_copy(c_refs[d], kept_ref.at[d - 1], sems.at[d - 1]))
+            arrivals[-1].start()
+            c_refs[d] = kept_ref.at[d - 1]
     elif step < ITERS - 1:
         split_ref, z_ref, local_ref, info_ref, layer_ref, mask_ref, acc_ref = refs
     else:
-        split_ref, own_ref, info_ref, layer_ref, mask_ref, acc_ref, z_ref, local_ref = refs
+        split_ref, own_ref, info_ref, layer_ref, mask_ref, acc_ref, z_ref, local_ref, zs_ref, sem = refs
     parts, rows = local_ref.shape
     size = rows // row_blocks
 
@@ -227,6 +232,11 @@
             return carry
 
     blocks(normal, 0)
+    if step == ITERS - 1:
+        for i, p in enumerate((*prev, z_ref)):
+            zs_ref[i] = jnp.concatenate([p[b] for b in range(row_blocks)], axis=1)
+        leave = pltpu.make_async_copy(zs_ref, own_ref, sem)
+        leave.start()
 
     for k in range(slots):
         chosen = jnp.concatenate([z_ref[places_ref[b, k]] for b in range(row_blocks)], axis=0)
@@ -243,6 +253,8 @@
 
     if step == 0:
         for d in range(freqs):
+            if d:
+                arrivals[d - 1].wait()
 
             @pl.loop(0, items_ref[4 * d + 3, 0])
             def _(group):
@@ -276,9 +288,7 @@
 
     if step == ITERS - 1:
         w = local_ref[...]
-        zs = [jnp.concatenate([p[b] for b in range(row_blocks)], axis=1) for p in (*prev, z_ref)]
-        for i, z in enumerate(zs):
-            own_ref[i] = z
+        zs = [zs_ref[i] for i in range(ITERS)]
         values = [lane_sum(z * w) for z in zs]
         gram = [[lane_sum(zs[i] * zs[j]) for j in range(i + 1)] for i in range(ITERS)]
         shares = []
@@ -291,6 +301,7 @@
         values += [gram[i][j] for i in range(ITERS) for j in range(i + 1)]
         for lane_at, value in enumerate(values):
             info = put_lane(info, SHARES + lane_at, value)
+        leave.wait()
     info_ref[...] = info
 
 
@@ -311,14 +322,29 @@
         pltpu.VMEM((row_blocks + 1, size, LANES), jnp.bfloat16),
         pltpu.VMEM((2 * size, LANES), jnp.float32),
     ]
+    out_specs = [vmem] * len(out_shape)
+    far = pl.BlockSpec(memory_space=pl.ANY)
     if step == 0:
+        received = len(in_specs) - freqs + 1
+        in_specs[received:] = [far] * (freqs - 1)
+        scratch_shapes += [
+            pltpu.VMEM((freqs - 1,) + blocks[0].shape, jnp.float32),
+            pltpu.SemaphoreType.DMA((freqs - 1,)),
+        ]
+        out_specs.append(vmem)
         out_shape.append(jax.ShapeDtypeStruct((row_blocks * slots, 2 * size, 2 * size), jnp.bfloat16))
     if step == ITERS - 1:
-        scratch_shapes += [pltpu.VMEM(z, jnp.float32), pltpu.VMEM((parts, rows), jnp.float32)]
+        out_specs[0] = far
+        scratch_shapes += [
+            pltpu.VMEM(z, jnp.float32),
+            pltpu.VMEM((parts, rows), jnp.float32),
+            pltpu.VMEM(owns.shape, jnp.float32),
+            pltpu.SemaphoreType.DMA,
+        ]
     return pl.pallas_call(
         functools.partial(step_kernel, step, plane, line, freqs),
         in_specs=in_specs,
-        out_specs=[vmem] * len(out_shape),
+        out_specs=out_specs,
         out_shape=out_shape,
         scratch_shapes=scratch_shapes,
         compiler_params=pltpu.CompilerParams(vmem_limit_bytes=VMEM_LIMIT),
@@ -326,7 +352,9 @@
     )(*lists, turn, info, *lines, *prev, *blocks)
 
 
-def final_kernel(tiles_ref, own_ref, out_ref, residual_ref):
+def final_kernel(tiles_ref, far_ref, out_ref, residual_ref, own_ref, sem):
+    arrive = pltpu.make_async_copy(far_ref, own_ref, sem)
+    arrive.start()
     devices, parts, _ = tiles_ref.shape
     fit = LANES // parts
     tiles = [tiles_ref[i] for i in range(devices)]
@@ -388,6 +416,7 @@
         jnp.concatenate([y for y in coef_y] + [jnp.zeros((LANES - 8 * ITERS, LANES), jnp.float32)], axis=0)
     )[:parts]
     rows = own_ref.shape[-1]
+    arrive.wait()
     x = sum(jnp.broadcast_to(columns[:, 8 * m : 8 * m + 1], (parts, rows)) * own_ref[m] for m in range(ITERS))
     out_ref[0] = x[: parts // 2]
     out_ref[1] = x[parts // 2 :]
@@ -398,12 +427,13 @@
     vmem = pl.BlockSpec(memory_space=pltpu.VMEM)
     return pl.pallas_call(
         final_kernel,
-        in_specs=[vmem] * 2,
+        in_specs=[vmem, pl.BlockSpec(memory_space=pl.ANY)],
         out_specs=[vmem] * 2,
         out_shape=[
             jax.ShapeDtypeStruct((2, parts // 2, rows), jnp.float32),
             jax.ShapeDtypeStruct((1, parts // 2), jnp.float32),
         ],
+        scratch_shapes=[pltpu.VMEM(own.shape, jnp.float32), pltpu.SemaphoreType.DMA],
         name="final",
     )(tiles, own)
 

time: 81 us -> 81.9 us (1.011)
    ppermute x12, waiting for transfers between devices: 11.5 us -> 9.86 us  [gather_rows(): lax.ppermute(whole_line, 'place', perm)]
    ppermute x12, waiting for transfers between devices: 11.3 us -> 12.9 us  [gather_rows(): lax.ppermute(rows, 'line', perm)]
  transfers between devices with their start and end apart: 26 -> 26, of which waited for: 17 -> 16; matrix products, arithmetic and copies ran while one was open for 3% -> 3% of each run, Pallas kernels for 1% -> 1%
where the time goes in v11:
time: 81.9 us; the launch traced here: 80.3 us
  starting transfers between devices  33.6 us (41%)
  waiting for transfers between devices  22.8 us (28%)
  Pallas kernels  16.2 us (20%)
  local copies, waits for them, and re-layouts  6.83 us (8%)
  between operations  0.82 us (1%)
    ppermute x12, starting transfers between devices, gather_rows(): lax.ppermute(rows, 'line', perm)  18.9 us
    ppermute x12, starting transfers between devices, gather_rows(): lax.ppermute(whole_line, 'place', perm)  14.2 us
    ppermute x12, waiting for transfers between devices, gather_rows(): lax.ppermute(rows, 'line', perm)  12.9 us
    pallas_call x3, Pallas kernels, run_step(): pl.pallas_call(functools.partial(step_kernel, step, plane, line, freqs),...  12.7 us
    ppermute x12, waiting for transfers between devices, gather_rows(): lax.ppermute(whole_line, 'place', perm)  9.86 us
    unnamed x17, local copies, waits for them, and re-layouts  4.45 us
    pallas_call x1, Pallas kernels, run_final(): pl.pallas_call(final_kernel, in_specs=[vmem, pl.BlockSpec(memory_space=pl...  2.43 us
  transfers between devices with their start and end apart: 26, of which 16 were waited for; matrix products, arithmetic and copies ran while one was open for 3% of the time, Pallas kernels for 1%

profile of v11, /device:TPU:0, one launch (start us, length us, event | category | flops | bytes accessed | tf_op | source)
XLA Modules:
  0.0 80.3 jit_solution(5014661893819086236)
XLA Ops:
  0.6 0.5 collective-permute-start.6
  1.2 3.0 %collective-permute-start = (f32[2,4,1024]{2,1,0:T(4,128)}, f32[2,4,1024]{2,1,0:T(4,128)S(1)}, u32[]{:S(2)}, u32[]{:S(2)}) collective-permute-start(f32[2,4,1024]{2,1,0:T(4,128)} %param.6), channel_id=1, source_target_pairs={{0,8},{8,0},{16,24},{24,16},{1,9},{9,1},{17,25},{25,17},{2,10},{10... | collective-permute-start | bytes 98312 | tf_op jit(solution)/shard_map/ppermute | solution.py:39
  4.2 2.5 %collective-permute-start.2 = (f32[2,4,1024]{2,1,0:T(4,128)}, f32[2,4,1024]{2,1,0:T(4,128)S(1)}, u32[]{:S(2)}, u32[]{:S(2)}) collective-permute-start(f32[2,4,1024]{2,1,0:T(4,128)} %param.6), channel_id=1, source_target_pairs={{0,24},{8,16},{16,8},{24,0},{1,25},{9,17},{17,9},{25,1},{2,26},{10... | collective-permute-start | bytes 98312 | tf_op jit(solution)/shard_map/ppermute | solution.py:39
  6.8 0.8 %stack.72 = f32[1,8,1024]{2,1,0:T(8,128)S(1)} reshape(f32[2,4,1024]{2,1,0:T(4,128)} %param.6) | data formatting | bytes 65536 | tf_op jit(solution)/shard_map/stack | solution.py:40
  7.7 2.6 %collective-permute-done.2 = f32[2,4,1024]{2,1,0:T(4,128)S(1)} collective-permute-done((f32[2,4,1024]{2,1,0:T(4,128)}, f32[2,4,1024]{2,1,0:T(4,128)S(1)}, u32[]{:S(2)}, u32[]{:S(2)}) %collective-permute-start.2) | collective-permute-done | bytes 32800 | tf_op jit(solution)/shard_map/ppermute | solution.py:39
  10.3 1.8 %collective-permute-done.1 = f32[2,4,1024]{2,1,0:T(4,128)S(1)} collective-permute-done((f32[2,4,1024]{2,1,0:T(4,128)}, f32[2,4,1024]{2,1,0:T(4,128)S(1)}, u32[]{:S(2)}, u32[]{:S(2)}) %collective-permute-start.1) | collective-permute-done | bytes 32800 | tf_op jit(solution)/shard_map/ppermute | solution.py:39
  12.1 2.5 %collective-permute-start.5 = (f32[4,8,1024]{2,1,0:T(8,128)S(1)}, f32[4,8,1024]{2,1,0:T(8,128)S(1)}, u32[]{:S(2)}, u32[]{:S(2)}) collective-permute-start(f32[4,8,1024]{2,1,0:T(8,128)S(1)} %constant_dynamic-update-slice_fusion.refs_0_), channel_id=1, source_target_pairs={{0,6},{2,4},{4,2},{6,0},{1,7},{3,5},{5,3},{7,1},{8,14},{10,12},{12... | collective-permute-start | bytes 393224 | tf_op jit(solution)/shard_map/ppermute | solution.py:41
  14.6 0.5 collective-permute-start.4
  15.2 0.5 collective-permute-start.3
  15.7 0.8 reshape.25
  16.5 0.7 concatenate.8.scalars_ref
  17.2 1.6 %copy-done = f32[8,4,128,128]{3,2,1,0:T(8,128)S(1)} copy-done((f32[8,4,128,128]{3,2,1,0:T(8,128)S(1)}, f32[8,4,128,128]{3,2,1,0:T(8,128)}, u32[]{:S(2)}) %copy-start) | copy-done | bytes 2097176
  18.8 1.6 %copy-done.1 = f32[8,4,128,128]{3,2,1,0:T(8,128)S(1)} copy-done((f32[8,4,128,128]{3,2,1,0:T(8,128)S(1)}, f32[8,4,128,128]{3,2,1,0:T(8,128)}, u32[]{:S(2)}) %copy-start.1) | copy-done | bytes 2097176
  20.4 1.1 %setup.1 = (s32[12,128]{1,0:T(8,128)S(1)}, s32[8,8]{1,0:T(8,128)S(1)}, f32[8,128]{1,0:T(8,128)S(1)}, f32[32,128,128]{2,1,0:T(8,128)S(1)}, f32[32,128,128]{2,1,0:T(8,128)S(1)}) custom-call(s32[79]{0:T(128)S(1)} %concatenate.8.scalars_ref, f32[32,128,128]{2,1,0:T(8,128)S(1)} %bitcast.23, f32[32,128,128]{2,1,0:T(8,128)S(1)} %bitcast.25), custom_call_target="tpu_custom_call" | custom-call | bytes 8388608 | tf_op jit(solution)/shard_map/setup/pallas_call | solution.py:114
  21.6 4.1 %step_0.1 = (f32[129,8,128]{2,1,0:T(8,128)S(1)}, f32[8,1024]{1,0:T(8,128)S(1)}, f32[8,128]{1,0:T(8,128)S(1)}, bf16[64,256,256]{2,1,0:T(8,128)(2,1)S(1)}) custom-call(s32[12,128]{1,0:T(8,128)S(1)} %get-tuple-element.18.items_ref, s32[8,8]{1,0:T(8,128)S(1)} %get-tuple-element.19.places_ref, f32[8,128]{1,0:T(8,128)S(1)} %get-tuple-element.20.turn_ref, ...), custom_call_target="tpu_custom_call" | custom-call | tf_op jit(solution)/shard_map/step_0/pallas_call | solution.py:344
  25.7 1.9 %collective-permute-start.10 = (f32[8,1024]{1,0:T(8,128)S(1)}, f32[8,1024]{1,0:T(8,128)S(1)}, u32[]{:S(2)}, u32[]{:S(2)}) collective-permute-start(f32[8,1024]{1,0:T(8,128)S(1)} %get-tuple-element.24), channel_id=1, source_target_pairs={{0,24},{8,16},{16,8},{24,0},{1,25},{9,17},{17,9},{25,1},{2,26},{10... | collective-permute-start | bytes 98312 | tf_op jit(solution)/shard_map/ppermute | solution.py:39
  27.6 1.1 %collective-permute-start.9 = (f32[8,1024]{1,0:T(8,128)S(1)}, f32[8,1024]{1,0:T(8,128)S(1)}, u32[]{:S(2)}, u32[]{:S(2)}) collective-permute-start(f32[8,1024]{1,0:T(8,128)S(1)} %get-tuple-element.24), channel_id=1, source_target_pairs={{0,16},{8,24},{16,0},{24,8},{1,17},{9,25},{17,1},{25,9},{2,18},{10... | collective-permute-start | bytes 98312 | tf_op jit(solution)/shard_map/ppermute | solution.py:39
  28.6 1.5 %collective-permute-start.8 = (f32[8,1024]{1,0:T(8,128)S(1)}, f32[8,1024]{1,0:T(8,128)S(1)}, u32[]{:S(2)}, u32[]{:S(2)}) collective-permute-start(f32[8,1024]{1,0:T(8,128)S(1)} %get-tuple-element.24), channel_id=1, source_target_pairs={{0,8},{8,0},{16,24},{24,16},{1,9},{9,1},{17,25},{25,17},{2,10},{10... | collective-permute-start | bytes 98312 | tf_op jit(solution)/shard_map/ppermute | solution.py:39
  30.1 1.5 %collective-permute-done.10 = f32[8,1024]{1,0:T(8,128)S(1)} collective-permute-done((f32[8,1024]{1,0:T(8,128)S(1)}, f32[8,1024]{1,0:T(8,128)S(1)}, u32[]{:S(2)}, u32[]{:S(2)}) %collective-permute-start.10) | collective-permute-done | bytes 32800 | tf_op jit(solution)/shard_map/ppermute | solution.py:39
  31.6 0.9 %collective-permute-done.9 = f32[8,1024]{1,0:T(8,128)S(1)} collective-permute-done((f32[8,1024]{1,0:T(8,128)S(1)}, f32[8,1024]{1,0:T(8,128)S(1)}, u32[]{:S(2)}, u32[]{:S(2)}) %collective-permute-start.9) | collective-permute-done | bytes 32800 | tf_op jit(solution)/shard_map/ppermute | solution.py:39
  32.9 2.0 %collective-permute-start.13 = (f32[4,8,1024]{2,1,0:T(8,128)S(1)}, f32[4,8,1024]{2,1,0:T(8,128)S(1)}, u32[]{:S(2)}, u32[]{:S(2)}) collective-permute-start(f32[4,8,1024]{2,1,0:T(8,128)S(1)} %pad_maximum_fusion.refs_0_), channel_id=1, source_target_pairs={{0,6},{2,4},{4,2},{6,0},{1,7},{3,5},{5,3},{7,1},{8,14},{10,12},{12... | collective-permute-start | bytes 393224 | tf_op jit(solution)/shard_map/ppermute | solution.py:41
  34.9 0.4 collective-permute-start.12
  35.3 1.1 %collective-permute-start.11 = (f32[4,8,1024]{2,1,0:T(8,128)S(1)}, f32[4,8,1024]{2,1,0:T(8,128)S(1)}, u32[]{:S(2)}, u32[]{:S(2)}) collective-permute-start(f32[4,8,1024]{2,1,0:T(8,128)S(1)} %pad_maximum_fusion.refs_0_), channel_id=1, source_target_pairs={{0,2},{2,0},{4,6},{6,4},{1,3},{3,1},{5,7},{7,5},{8,10},{10,8},{12,... | collective-permute-start | bytes 393224 | tf_op jit(solution)/shard_map/ppermute | solution.py:41
  36.4 2.5 %collective-permute-done.13.refs_3_ = f32[4,8,1024]{2,1,0:T(8,128)S(1)} collective-permute-done((f32[4,8,1024]{2,1,0:T(8,128)S(1)}, f32[4,8,1024]{2,1,0:T(8,128)S(1)}, u32[]{:S(2)}, u32[]{:S(2)}) %collective-permute-start.13) | collective-permute-done | bytes 131104 | tf_op jit(solution)/shard_map/ppermute | solution.py:41
  38.9 1.4 %collective-permute-done.12.refs_2_ = f32[4,8,1024]{2,1,0:T(8,128)S(1)} collective-permute-done((f32[4,8,1024]{2,1,0:T(8,128)S(1)}, f32[4,8,1024]{2,1,0:T(8,128)S(1)}, u32[]{:S(2)}, u32[]{:S(2)}) %collective-permute-start.12) | collective-permute-done | bytes 131104 | tf_op jit(solution)/shard_map/ppermute | solution.py:41
  40.5 4.0 %step_1.1 = (f32[129,8,128]{2,1,0:T(8,128)S(1)}, f32[8,1024]{1,0:T(8,128)S(1)}, f32[8,128]{1,0:T(8,128)S(1)}) custom-call(s32[12,128]{1,0:T(8,128)S(1)} %get-tuple-element.18.items_ref, s32[8,8]{1,0:T(8,128)S(1)} %get-tuple-element.19.places_ref, f32[8,128]{1,0:T(8,128)S(1)} %get-tuple-element.20.turn_ref, f32[8,128]{1,0:T(8,128)S(1)} %get-tuple-element.23.info_in_ref, ...), custom_call_target="tpu_custom_call" | custom-call | tf_op jit(solution)/shard_map/step_1/pallas_call | solution.py:344
  44.5 2.3 %collective-permute-start.16 = (f32[8,1024]{1,0:T(8,128)S(1)}, f32[8,1024]{1,0:T(8,128)S(1)}, u32[]{:S(2)}, u32[]{:S(2)}) collective-permute-start(f32[8,1024]{1,0:T(8,128)S(1)} %get-tuple-element.28), channel_id=1, source_target_pairs={{0,24},{8,16},{16,8},{24,0},{1,25},{9,17},{17,9},{25,1},{2,26},{10... | collective-permute-start | bytes 98312 | tf_op jit(solution)/shard_map/ppermute | solution.py:39
  46.8 1.7 %collective-permute-start.15 = (f32[8,1024]{1,0:T(8,128)S(1)}, f32[8,1024]{1,0:T(8,128)S(1)}, u32[]{:S(2)}, u32[]{:S(2)}) collective-permute-start(f32[8,1024]{1,0:T(8,128)S(1)} %get-tuple-element.28), channel_id=1, source_target_pairs={{0,16},{8,24},{16,0},{24,8},{1,17},{9,25},{17,1},{25,9},{2,18},{10... | collective-permute-start | bytes 98312 | tf_op jit(solution)/shard_map/ppermute | solution.py:39
  48.5 0.5 collective-permute-start.14
  48.9 1.4 %collective-permute-done.16 = f32[8,1024]{1,0:T(8,128)S(1)} collective-permute-done((f32[8,1024]{1,0:T(8,128)S(1)}, f32[8,1024]{1,0:T(8,128)S(1)}, u32[]{:S(2)}, u32[]{:S(2)}) %collective-permute-start.16) | collective-permute-done | bytes 32800 | tf_op jit(solution)/shard_map/ppermute | solution.py:39
  50.3 1.3 %collective-permute-done.15 = f32[8,1024]{1,0:T(8,128)S(1)} collective-permute-done((f32[8,1024]{1,0:T(8,128)S(1)}, f32[8,1024]{1,0:T(8,128)S(1)}, u32[]{:S(2)}, u32[]{:S(2)}) %collective-permute-start.15) | collective-permute-done | bytes 32800 | tf_op jit(solution)/shard_map/ppermute | solution.py:39
  51.6 0.8 %collective-permute-done.14 = f32[8,1024]{1,0:T(8,128)S(1)} collective-permute-done((f32[8,1024]{1,0:T(8,128)S(1)}, f32[8,1024]{1,0:T(8,128)S(1)}, u32[]{:S(2)}, u32[]{:S(2)}) %collective-permute-start.14) | collective-permute-done | bytes 32800 | tf_op jit(solution)/shard_map/ppermute | solution.py:39
  52.4 1.5 %collective-permute-start.19 = (f32[4,8,1024]{2,1,0:T(8,128)S(1)}, f32[4,8,1024]{2,1,0:T(8,128)S(1)}, u32[]{:S(2)}, u32[]{:S(2)}) collective-permute-start(f32[4,8,1024]{2,1,0:T(8,128)S(1)} %pad_maximum_fusion.1.refs_0_), channel_id=1, source_target_pairs={{0,6},{2,4},{4,2},{6,0},{1,7},{3,5},{5,3},{7,1},{8,14},{10,12},{12... | collective-permute-start | bytes 393224 | tf_op jit(solution)/shard_map/ppermute | solution.py:41
  53.9 2.1 %collective-permute-start.17 = (f32[4,8,1024]{2,1,0:T(8,128)S(1)}, f32[4,8,1024]{2,1,0:T(8,128)S(1)}, u32[]{:S(2)}, u32[]{:S(2)}) collective-permute-start(f32[4,8,1024]{2,1,0:T(8,128)S(1)} %pad_maximum_fusion.1.refs_0_), channel_id=1, source_target_pairs={{0,2},{2,0},{4,6},{6,4},{1,3},{3,1},{5,7},{7,5},{8,10},{10,8},{12,... | collective-permute-start | bytes 393224 | tf_op jit(solution)/shard_map/ppermute | solution.py:41
  55.9 2.5 %collective-permute-done.19.refs_3_ = f32[4,8,1024]{2,1,0:T(8,128)S(1)} collective-permute-done((f32[4,8,1024]{2,1,0:T(8,128)S(1)}, f32[4,8,1024]{2,1,0:T(8,128)S(1)}, u32[]{:S(2)}, u32[]{:S(2)}) %collective-permute-start.19) | collective-permute-done | bytes 131104 | tf_op jit(solution)/shard_map/ppermute | solution.py:41
  58.4 1.3 %collective-permute-done.18.refs_2_ = f32[4,8,1024]{2,1,0:T(8,128)S(1)} collective-permute-done((f32[4,8,1024]{2,1,0:T(8,128)S(1)}, f32[4,8,1024]{2,1,0:T(8,128)S(1)}, u32[]{:S(2)}, u32[]{:S(2)}) %collective-permute-start.18) | collective-permute-done | bytes 131104 | tf_op jit(solution)/shard_map/ppermute | solution.py:41
  59.7 4.6 %step_2.1 = (f32[3,8,1024]{2,1,0:T(8,128)S(1)}, f32[8,128]{1,0:T(8,128)S(1)}) custom-call(s32[12,128]{1,0:T(8,128)S(1)} %get-tuple-element.18.items_ref, s32[8,8]{1,0:T(8,128)S(1)} %get-tuple-element.19.places_ref, f32[8,128]{1,0:T(8,128)S(1)} %get-tuple-element.20.turn_ref, f32[8,128]{1,0:T(8,128)S(1)} %get-tuple-element.27.info_in_ref, ...), custom_call_target="tpu_custom_call" | custom-call | tf_op jit(solution)/shard_map/step_2/pallas_call | solution.py:344
  64.3 0.6 copy-done.2
  64.9 2.2 %collective-permute-start.22 = (f32[8,128]{1,0:T(8,128)S(1)}, f32[8,128]{1,0:T(8,128)S(1)}, u32[]{:S(2)}, u32[]{:S(2)}) collective-permute-start(f32[8,128]{1,0:T(8,128)S(1)} %get-tuple-element.30), channel_id=1, source_target_pairs={{0,24},{8,16},{16,8},{24,0},{1,25},{9,17},{17,9},{25,1},{2,26},{10... | collective-permute-start | bytes 12296 | tf_op jit(solution)/shard_map/ppermute | solution.py:39
  67.2 0.7 collective-permute-start.21
  67.9 1.4 %collective-permute-start.20 = (f32[8,128]{1,0:T(8,128)S(1)}, f32[8,128]{1,0:T(8,128)S(1)}, u32[]{:S(2)}, u32[]{:S(2)}) collective-permute-start(f32[8,128]{1,0:T(8,128)S(1)} %get-tuple-element.30), channel_id=1, source_target_pairs={{0,8},{8,0},{16,24},{24,16},{1,9},{9,1},{17,25},{25,17},{2,10},{10... | collective-permute-start | bytes 12296 | tf_op jit(solution)/shard_map/ppermute | solution.py:39
  69.3 1.0 %collective-permute-done.22 = f32[8,128]{1,0:T(8,128)S(1)} collective-permute-done((f32[8,128]{1,0:T(8,128)S(1)}, f32[8,128]{1,0:T(8,128)S(1)}, u32[]{:S(2)}, u32[]{:S(2)}) %collective-permute-start.22) | collective-permute-done | bytes 4128 | tf_op jit(solution)/shard_map/ppermute | solution.py:39
  70.4 1.3 %collective-permute-done.21 = f32[8,128]{1,0:T(8,128)S(1)} collective-permute-done((f32[8,128]{1,0:T(8,128)S(1)}, f32[8,128]{1,0:T(8,128)S(1)}, u32[]{:S(2)}, u32[]{:S(2)}) %collective-permute-start.21) | collective-permute-done | bytes 4128 | tf_op jit(solution)/shard_map/ppermute | solution.py:39
  71.7 1.4 %collective-permute-start.25 = (f32[4,8,128]{2,1,0:T(8,128)S(1)}, f32[4,8,128]{2,1,0:T(8,128)S(1)}, u32[]{:S(2)}, u32[]{:S(2)}) collective-permute-start(f32[4,8,128]{2,1,0:T(8,128)S(1)} %pad_maximum_fusion.2), channel_id=1, source_target_pairs={{0,6},{2,4},{4,2},{6,0},{1,7},{3,5},{5,3},{7,1},{8,14},{10,12},{12... | collective-permute-start | bytes 49160 | tf_op jit(solution)/shard_map/ppermute | solution.py:41
  73.4 1.7 %collective-permute-start.23 = (f32[4,8,128]{2,1,0:T(8,128)S(1)}, f32[4,8,128]{2,1,0:T(8,128)S(1)}, u32[]{:S(2)}, u32[]{:S(2)}) collective-permute-start(f32[4,8,128]{2,1,0:T(8,128)S(1)} %pad_maximum_fusion.2), channel_id=1, source_target_pairs={{0,2},{2,0},{4,6},{6,4},{1,3},{3,1},{5,7},{7,5},{8,10},{10,8},{12,... | collective-permute-start | bytes 49160 | tf_op jit(solution)/shard_map/ppermute | solution.py:41
  75.2 2.0 %collective-permute-done.23 = f32[4,8,128]{2,1,0:T(8,128)S(1)} collective-permute-done((f32[4,8,128]{2,1,0:T(8,128)S(1)}, f32[4,8,128]{2,1,0:T(8,128)S(1)}, u32[]{:S(2)}, u32[]{:S(2)}) %collective-permute-start.23) | collective-permute-done | bytes 16416 | tf_op jit(solution)/shard_map/ppermute | solution.py:41
  77.2 0.6 copy-done.3
  77.8 2.4 %final.1 = (f32[2,4,1024]{2,1,0:T(4,128)}, f32[1,4]{1,0:T(1,128)}) custom-call(f32[16,8,128]{2,1,0:T(8,128)} %copy-done.3, f32[3,8,1024]{2,1,0:T(8,128)} %copy-done.2), custom_call_target="tpu_custom_call" | custom-call | tf_op jit(solution)/shard_map/final/pallas_call | solution.py:428
  (38 shorter events, 1.2 us)
Async XLA Ops:
  0.6 20.9 %collective-permute-start.6 = (f32[32,128,128]{2,1,0:T(8,128)}, f32[32,128,128]{2,1,0:T(8,128)S(1)}, u32[]{:S(2)}, u32[]{:S(2)}) collective-permute-start(f32[32,128,128]{2,1,0:T(8,128)} %bitcast.22), channel_id=1, source_target_pairs={{0,1},{1,0},{2,3},{3,2},{4,5},{5,4},{6,7},{7,6},{8,9},{9,8},{10,11... | collective-permute-start | bytes 6291464 | tf_op jit(solution)/shard_map/ppermute | solution.py:456
  1.1 20.4 %collective-permute-start.7 = (f32[32,128,128]{2,1,0:T(8,128)}, f32[32,128,128]{2,1,0:T(8,128)}, u32[]{:S(2)}, u32[]{:S(2)}) collective-permute-start(f32[32,128,128]{2,1,0:T(8,128)} %bitcast.24), channel_id=1, source_target_pairs={{0,1},{1,0},{2,3},{3,2},{4,5},{5,4},{6,7},{7,6},{8,9},{9,8},{10,11... | collective-permute-start | bytes 6291464 | tf_op jit(solution)/shard_map/ppermute | solution.py:457
  1.2 6.4 %collective-permute-start = (f32[2,4,1024]{2,1,0:T(4,128)}, f32[2,4,1024]{2,1,0:T(4,128)S(1)}, u32[]{:S(2)}, u32[]{:S(2)}) collective-permute-start(f32[2,4,1024]{2,1,0:T(4,128)} %param.6), channel_id=1, source_target_pairs={{0,8},{8,0},{16,24},{24,16},{1,9},{9,1},{17,25},{25,17},{2,10},{10... | collective-permute-start | bytes 98312 | tf_op jit(solution)/shard_map/ppermute | solution.py:39
  4.2 6.1 %collective-permute-start.2 = (f32[2,4,1024]{2,1,0:T(4,128)}, f32[2,4,1024]{2,1,0:T(4,128)S(1)}, u32[]{:S(2)}, u32[]{:S(2)}) collective-permute-start(f32[2,4,1024]{2,1,0:T(4,128)} %param.6), channel_id=1, source_target_pairs={{0,24},{8,16},{16,8},{24,0},{1,25},{9,17},{17,9},{25,1},{2,26},{10... | collective-permute-start | bytes 98312 | tf_op jit(solution)/shard_map/ppermute | solution.py:39
  6.7 5.4 %collective-permute-start.1 = (f32[2,4,1024]{2,1,0:T(4,128)}, f32[2,4,1024]{2,1,0:T(4,128)S(1)}, u32[]{:S(2)}, u32[]{:S(2)}) collective-permute-start(f32[2,4,1024]{2,1,0:T(4,128)} %param.6), channel_id=1, source_target_pairs={{0,16},{8,24},{16,0},{24,8},{1,17},{9,25},{17,1},{25,9},{2,18},{10... | collective-permute-start | bytes 98312 | tf_op jit(solution)/shard_map/ppermute | solution.py:39
  12.1 9.4 %collective-permute-start.5 = (f32[4,8,1024]{2,1,0:T(8,128)S(1)}, f32[4,8,1024]{2,1,0:T(8,128)S(1)}, u32[]{:S(2)}, u32[]{:S(2)}) collective-permute-start(f32[4,8,1024]{2,1,0:T(8,128)S(1)} %constant_dynamic-update-slice_fusion.refs_0_), channel_id=1, source_target_pairs={{0,6},{2,4},{4,2},{6,0},{1,7},{3,5},{5,3},{7,1},{8,14},{10,12},{12... | collective-permute-start | bytes 393224 | tf_op jit(solution)/shard_map/ppermute | solution.py:41
  14.6 6.9 %collective-permute-start.4 = (f32[4,8,1024]{2,1,0:T(8,128)S(1)}, f32[4,8,1024]{2,1,0:T(8,128)S(1)}, u32[]{:S(2)}, u32[]{:S(2)}) collective-permute-start(f32[4,8,1024]{2,1,0:T(8,128)S(1)} %constant_dynamic-update-slice_fusion.refs_0_), channel_id=1, source_target_pairs={{0,4},{2,6},{4,0},{6,2},{1,5},{3,7},{5,1},{7,3},{8,12},{10,14},{12... | collective-permute-start | bytes 393224 | tf_op jit(solution)/shard_map/ppermute | solution.py:41
  15.2 6.4 %collective-permute-start.3 = (f32[4,8,1024]{2,1,0:T(8,128)S(1)}, f32[4,8,1024]{2,1,0:T(8,128)S(1)}, u32[]{:S(2)}, u32[]{:S(2)}) collective-permute-start(f32[4,8,1024]{2,1,0:T(8,128)S(1)} %constant_dynamic-update-slice_fusion.refs_0_), channel_id=1, source_target_pairs={{0,2},{2,0},{4,6},{6,4},{1,3},{3,1},{5,7},{7,5},{8,10},{10,8},{12,... | collective-permute-start | bytes 393224 | tf_op jit(solution)/shard_map/ppermute | solution.py:41
  17.2 1.6 %copy-start = (f32[8,4,128,128]{3,2,1,0:T(8,128)S(1)}, f32[8,4,128,128]{3,2,1,0:T(8,128)}, u32[]{:S(2)}) copy-start(f32[8,4,128,128]{3,2,1,0:T(8,128)} %param.7) | copy-start | bytes 6291460
  18.8 1.6 %copy-start.1 = (f32[8,4,128,128]{3,2,1,0:T(8,128)S(1)}, f32[8,4,128,128]{3,2,1,0:T(8,128)}, u32[]{:S(2)}) copy-start(f32[8,4,128,128]{3,2,1,0:T(8,128)} %param.8) | copy-start | bytes 6291460
  25.7 5.9 %collective-permute-start.10 = (f32[8,1024]{1,0:T(8,128)S(1)}, f32[8,1024]{1,0:T(8,128)S(1)}, u32[]{:S(2)}, u32[]{:S(2)}) collective-permute-start(f32[8,1024]{1,0:T(8,128)S(1)} %get-tuple-element.24), channel_id=1, source_target_pairs={{0,24},{8,16},{16,8},{24,0},{1,25},{9,17},{17,9},{25,1},{2,26},{10... | collective-permute-start | bytes 98312 | tf_op jit(solution)/shard_map/ppermute | solution.py:39
  27.6 5.0 %collective-permute-start.9 = (f32[8,1024]{1,0:T(8,128)S(1)}, f32[8,1024]{1,0:T(8,128)S(1)}, u32[]{:S(2)}, u32[]{:S(2)}) collective-permute-start(f32[8,1024]{1,0:T(8,128)S(1)} %get-tuple-element.24), channel_id=1, source_target_pairs={{0,16},{8,24},{16,0},{24,8},{1,17},{9,25},{17,1},{25,9},{2,18},{10... | collective-permute-start | bytes 98312 | tf_op jit(solution)/shard_map/ppermute | solution.py:39
  28.6 4.2 %collective-permute-start.8 = (f32[8,1024]{1,0:T(8,128)S(1)}, f32[8,1024]{1,0:T(8,128)S(1)}, u32[]{:S(2)}, u32[]{:S(2)}) collective-permute-start(f32[8,1024]{1,0:T(8,128)S(1)} %get-tuple-element.24), channel_id=1, source_target_pairs={{0,8},{8,0},{16,24},{24,16},{1,9},{9,1},{17,25},{25,17},{2,10},{10... | collective-permute-start | bytes 98312 | tf_op jit(solution)/shard_map/ppermute | solution.py:39
  32.9 6.1 %collective-permute-start.13 = (f32[4,8,1024]{2,1,0:T(8,128)S(1)}, f32[4,8,1024]{2,1,0:T(8,128)S(1)}, u32[]{:S(2)}, u32[]{:S(2)}) collective-permute-start(f32[4,8,1024]{2,1,0:T(8,128)S(1)} %pad_maximum_fusion.refs_0_), channel_id=1, source_target_pairs={{0,6},{2,4},{4,2},{6,0},{1,7},{3,5},{5,3},{7,1},{8,14},{10,12},{12... | collective-permute-start | bytes 393224 | tf_op jit(solution)/shard_map/ppermute | solution.py:41
  34.9 5.4 %collective-permute-start.12 = (f32[4,8,1024]{2,1,0:T(8,128)S(1)}, f32[4,8,1024]{2,1,0:T(8,128)S(1)}, u32[]{:S(2)}, u32[]{:S(2)}) collective-permute-start(f32[4,8,1024]{2,1,0:T(8,128)S(1)} %pad_maximum_fusion.refs_0_), channel_id=1, source_target_pairs={{0,4},{2,6},{4,0},{6,2},{1,5},{3,7},{5,1},{7,3},{8,12},{10,14},{12... | collective-permute-start | bytes 393224 | tf_op jit(solution)/shard_map/ppermute | solution.py:41
  35.3 5.2 %collective-permute-start.11 = (f32[4,8,1024]{2,1,0:T(8,128)S(1)}, f32[4,8,1024]{2,1,0:T(8,128)S(1)}, u32[]{:S(2)}, u32[]{:S(2)}) collective-permute-start(f32[4,8,1024]{2,1,0:T(8,128)S(1)} %pad_maximum_fusion.refs_0_), channel_id=1, source_target_pairs={{0,2},{2,0},{4,6},{6,4},{1,3},{3,1},{5,7},{7,5},{8,10},{10,8},{12,... | collective-permute-start | bytes 393224 | tf_op jit(solution)/shard_map/ppermute | solution.py:41
  44.5 5.8 %collective-permute-start.16 = (f32[8,1024]{1,0:T(8,128)S(1)}, f32[8,1024]{1,0:T(8,128)S(1)}, u32[]{:S(2)}, u32[]{:S(2)}) collective-permute-start(f32[8,1024]{1,0:T(8,128)S(1)} %get-tuple-element.28), channel_id=1, source_target_pairs={{0,24},{8,16},{16,8},{24,0},{1,25},{9,17},{17,9},{25,1},{2,26},{10... | collective-permute-start | bytes 98312 | tf_op jit(solution)/shard_map/ppermute | solution.py:39
  46.8 4.8 %collective-permute-start.15 = (f32[8,1024]{1,0:T(8,128)S(1)}, f32[8,1024]{1,0:T(8,128)S(1)}, u32[]{:S(2)}, u32[]{:S(2)}) collective-permute-start(f32[8,1024]{1,0:T(8,128)S(1)} %get-tuple-element.28), channel_id=1, source_target_pairs={{0,16},{8,24},{16,0},{24,8},{1,17},{9,25},{17,1},{25,9},{2,18},{10... | collective-permute-start | bytes 98312 | tf_op jit(solution)/shard_map/ppermute | solution.py:39
  48.5 3.9 %collective-permute-start.14 = (f32[8,1024]{1,0:T(8,128)S(1)}, f32[8,1024]{1,0:T(8,128)S(1)}, u32[]{:S(2)}, u32[]{:S(2)}) collective-permute-start(f32[8,1024]{1,0:T(8,128)S(1)} %get-tuple-element.28), channel_id=1, source_target_pairs={{0,8},{8,0},{16,24},{24,16},{1,9},{9,1},{17,25},{25,17},{2,10},{10... | collective-permute-start | bytes 98312 | tf_op jit(solution)/shard_map/ppermute | solution.py:39
  52.4 6.0 %collective-permute-start.19 = (f32[4,8,1024]{2,1,0:T(8,128)S(1)}, f32[4,8,1024]{2,1,0:T(8,128)S(1)}, u32[]{:S(2)}, u32[]{:S(2)}) collective-permute-start(f32[4,8,1024]{2,1,0:T(8,128)S(1)} %pad_maximum_fusion.1.refs_0_), channel_id=1, source_target_pairs={{0,6},{2,4},{4,2},{6,0},{1,7},{3,5},{5,3},{7,1},{8,14},{10,12},{12... | collective-permute-start | bytes 393224 | tf_op jit(solution)/shard_map/ppermute | solution.py:41
  53.9 5.9 %collective-permute-start.18 = (f32[4,8,1024]{2,1,0:T(8,128)S(1)}, f32[4,8,1024]{2,1,0:T(8,128)S(1)}, u32[]{:S(2)}, u32[]{:S(2)}) collective-permute-start(f32[4,8,1024]{2,1,0:T(8,128)S(1)} %pad_maximum_fusion.1.refs_0_), channel_id=1, source_target_pairs={{0,4},{2,6},{4,0},{6,2},{1,5},{3,7},{5,1},{7,3},{8,12},{10,14},{12... | collective-permute-start | bytes 393224 | tf_op jit(solution)/shard_map/ppermute | solution.py:41
  53.9 5.9 %collective-permute-start.17 = (f32[4,8,1024]{2,1,0:T(8,128)S(1)}, f32[4,8,1024]{2,1,0:T(8,128)S(1)}, u32[]{:S(2)}, u32[]{:S(2)}) collective-permute-start(f32[4,8,1024]{2,1,0:T(8,128)S(1)} %pad_maximum_fusion.1.refs_0_), channel_id=1, source_target_pairs={{0,2},{2,0},{4,6},{6,4},{1,3},{3,1},{5,7},{7,5},{8,10},{10,8},{12,... | collective-permute-start | bytes 393224 | tf_op jit(solution)/shard_map/ppermute | solution.py:41
  64.3 0.6 copy-start.2
  64.9 5.4 %collective-permute-start.22 = (f32[8,128]{1,0:T(8,128)S(1)}, f32[8,128]{1,0:T(8,128)S(1)}, u32[]{:S(2)}, u32[]{:S(2)}) collective-permute-start(f32[8,128]{1,0:T(8,128)S(1)} %get-tuple-element.30), channel_id=1, source_target_pairs={{0,24},{8,16},{16,8},{24,0},{1,25},{9,17},{17,9},{25,1},{2,26},{10... | collective-permute-start | bytes 12296 | tf_op jit(solution)/shard_map/ppermute | solution.py:39
  67.2 4.5 %collective-permute-start.21 = (f32[8,128]{1,0:T(8,128)S(1)}, f32[8,128]{1,0:T(8,128)S(1)}, u32[]{:S(2)}, u32[]{:S(2)}) collective-permute-start(f32[8,128]{1,0:T(8,128)S(1)} %get-tuple-element.30), channel_id=1, source_target_pairs={{0,16},{8,24},{16,0},{24,8},{1,17},{9,25},{17,1},{25,9},{2,18},{10... | collective-permute-start | bytes 12296 | tf_op jit(solution)/shard_map/ppermute | solution.py:39
  67.9 3.8 %collective-permute-start.20 = (f32[8,128]{1,0:T(8,128)S(1)}, f32[8,128]{1,0:T(8,128)S(1)}, u32[]{:S(2)}, u32[]{:S(2)}) collective-permute-start(f32[8,128]{1,0:T(8,128)S(1)} %get-tuple-element.30), channel_id=1, source_target_pairs={{0,8},{8,0},{16,24},{24,16},{1,9},{9,1},{17,25},{25,17},{2,10},{10... | collective-permute-start | bytes 12296 | tf_op jit(solution)/shard_map/ppermute | solution.py:39
  71.7 5.5 %collective-permute-start.25 = (f32[4,8,128]{2,1,0:T(8,128)S(1)}, f32[4,8,128]{2,1,0:T(8,128)S(1)}, u32[]{:S(2)}, u32[]{:S(2)}) collective-permute-start(f32[4,8,128]{2,1,0:T(8,128)S(1)} %pad_maximum_fusion.2), channel_id=1, source_target_pairs={{0,6},{2,4},{4,2},{6,0},{1,7},{3,5},{5,3},{7,1},{8,14},{10,12},{12... | collective-permute-start | bytes 49160 | tf_op jit(solution)/shard_map/ppermute | solution.py:41
  73.1 4.1 %collective-permute-start.24 = (f32[4,8,128]{2,1,0:T(8,128)S(1)}, f32[4,8,128]{2,1,0:T(8,128)S(1)}, u32[]{:S(2)}, u32[]{:S(2)}) collective-permute-start(f32[4,8,128]{2,1,0:T(8,128)S(1)} %pad_maximum_fusion.2), channel_id=1, source_target_pairs={{0,4},{2,6},{4,0},{6,2},{1,5},{3,7},{5,1},{7,3},{8,12},{10,14},{12... | collective-permute-start | bytes 49160 | tf_op jit(solution)/shard_map/ppermute | solution.py:41
  73.4 3.7 %collective-permute-start.23 = (f32[4,8,128]{2,1,0:T(8,128)S(1)}, f32[4,8,128]{2,1,0:T(8,128)S(1)}, u32[]{:S(2)}, u32[]{:S(2)}) collective-permute-start(f32[4,8,128]{2,1,0:T(8,128)S(1)} %pad_maximum_fusion.2), channel_id=1, source_target_pairs={{0,2},{2,0},{4,6},{6,4},{1,3},{3,1},{5,7},{7,5},{8,10},{10,8},{12,... | collective-permute-start | bytes 49160 | tf_op jit(solution)/shard_map/ppermute | solution.py:41
  77.2 0.6 copy-start.3

commit v12 on v10

--- a/solution.py
+++ b/solution.py
@@ -154,8 +154,13 @@
     row_blocks, slots = places_ref.shape
     nodes = plane * line
     if step == 0:
-        g_refs, c_refs = refs[:freqs], refs[freqs : 2 * freqs]
-        z_ref, local_ref, info_ref, split_ref, layer_ref, mask_ref, acc_ref = refs[2 * freqs :]
+        g_refs, c_refs = refs[:freqs], list(refs[freqs : 2 * freqs])
+        z_ref, local_ref, info_ref, split_ref, layer_ref, mask_ref, acc_ref, kept_ref, sems = refs[2 * freqs :]
+        arrivals = []
+        for d in range(1, freqs):
+            arrivals.append(pltpu.make_async_copy(c_refs[d], kept_ref.at[d - 1], sems.at[d - 1]))
+            arrivals[-1].start()
+            c_refs[d] = kept_ref.at[d - 1]
     elif step < ITERS - 1:
         split_ref, z_ref, local_ref, info_ref, layer_ref, mask_ref, acc_ref = refs
     else:
@@ -241,29 +246,45 @@
         left, right = jnp.concatenate(lefts, axis=1), jnp.concatenate(rights, axis=0)
         acc_ref[...] += jnp.dot(left, right, preferred_element_type=jnp.float32)
 
+    def work_off(table, sizes, slots_of):
+        total = items_ref[4 * table + 3, 0] * sizes[-1]
+        turns = lax.div(total, sizes[0])
+
+        @pl.loop(0, turns)
+        def _(turn):
+            slots_of(turn * sizes[0], sizes[0])
+
+        start = turns * sizes[0]
+        for count in sizes[1:]:
+            fits = total - start >= count
+            pl.when(fits)(functools.partial(slots_of, start, count))
+            start = start + jnp.where(fits, count, 0)
+
     if step == 0:
         for d in range(freqs):
-
-            @pl.loop(0, items_ref[4 * d + 3, 0])
-            def _(group):
+            if d:
+                arrivals[d - 1].wait()
+
+            def split_slots(start, count, d=d):
                 lefts, rights = [], []
-                for u in range(GROUP):
-                    t = group * GROUP + u
-                    stored = items_ref[4 * d + 2, t]
+                for u in range(count):
+                    stored = items_ref[4 * d + 2, start + u]
                     here = stored - d * g_refs[d].shape[0]
                     parts_of = split(jnp.concatenate([g_refs[d][here], c_refs[d][here]], axis=0))
                     left = jnp.concatenate(parts_of, axis=1)
                     split_ref[stored] = left
                     lefts.append(left)
-                    rights.append(vectors(4 * d, t))
+                    rights.append(vectors(4 * d, start + u))
                 add_group(lefts, rights)
+
+            work_off(d, (4 * GROUP, 2 * GROUP, GROUP), split_slots)
     else:
 
-        @pl.loop(0, items_ref[4 * freqs + 3, 0])
-        def _(group):
-            places = [group * FULL_GROUP + u for u in range(FULL_GROUP)]
-            lefts = [split_ref[items_ref[4 * freqs + 2, t]] for t in places]
-            add_group(lefts, [vectors(4 * freqs, t) for t in places])
+        def kept_slots(start, count):
+            lefts = [split_ref[items_ref[4 * freqs + 2, start + u]] for u in range(count)]
+            add_group(lefts, [vectors(4 * freqs, start + u) for u in range(count)])
+
+        work_off(freqs, (4 * FULL_GROUP, 2 * FULL_GROUP, FULL_GROUP), kept_slots)
 
     half = row_blocks * parts
     gsum, csum = jnp.transpose(acc_ref[:size]), jnp.transpose(acc_ref[size:])
@@ -312,6 +333,12 @@
         pltpu.VMEM((2 * size, LANES), jnp.float32),
     ]
     if step == 0:
+        received = len(in_specs) - freqs + 1
+        in_specs[received:] = [pl.BlockSpec(memory_space=pl.ANY)] * (freqs - 1)
+        scratch_shapes += [
+            pltpu.VMEM((freqs - 1,) + blocks[0].shape, jnp.float32),
+            pltpu.SemaphoreType.DMA((freqs - 1,)),
+        ]
         out_shape.append(jax.ShapeDtypeStruct((row_blocks * slots, 2 * size, 2 * size), jnp.bfloat16))
     if step == ITERS - 1:
         scratch_shapes += [pltpu.VMEM(z, jnp.float32), pltpu.VMEM((parts, rows), jnp.float32)]

time: 81 us -> 77.4 us (0.956)
  Pallas kernels: 15.6 us -> 13.4 us
    pallas_call x3, Pallas kernels: 12.4 us -> 10.1 us  [run_step(): pl.pallas_call(functools.partial(step_kernel, step, plane, line, freqs),...]
where the time goes in v12:
time: 77.4 us; the launch traced here: 77.1 us
  starting transfers between devices  33.6 us (43%)
  waiting for transfers between devices  22.4 us (29%)
  Pallas kernels  13.4 us (17%)
  local copies, waits for them, and re-layouts  6.83 us (9%)
  between operations  0.82 us (1%)
    ppermute x12, starting transfers between devices, gather_rows(): lax.ppermute(rows, 'line', perm)  18.9 us
    ppermute x12, starting transfers between devices, gather_rows(): lax.ppermute(whole_line, 'place', perm)  14.1 us
    ppermute x12, waiting for transfers between devices, gather_rows(): lax.ppermute(whole_line, 'place', perm)  11.5 us
    ppermute x12, waiting for transfers between devices, gather_rows(): lax.ppermute(rows, 'line', perm)  10.9 us
    pallas_call x3, Pallas kernels, run_step(): pl.pallas_call(functools.partial(step_kernel, step, plane, line, freqs),...  10.1 us
    unnamed x17, local copies, waits for them, and re-layouts  4.45 us
    pallas_call x1, Pallas kernels, run_final(): pl.pallas_call(final_kernel, in_specs=[vmem] * 2, out_specs=[vmem] * 2, o...  2.17 us
  transfers between devices with their start and end apart: 26, of which 17 were waited for; matrix products, arithmetic and copies ran while one was open for 3% of the time, Pallas kernels for 1%

profile of v12, /device:TPU:0, one launch (start us, length us, event | category | flops | bytes accessed | tf_op | source)
XLA Modules:
  0.0 77.1 jit_solution(3657321949728958731)
XLA Ops:
  0.6 0.5 collective-permute-start.6
  1.2 3.0 %collective-permute-start = (f32[2,4,1024]{2,1,0:T(4,128)}, f32[2,4,1024]{2,1,0:T(4,128)S(1)}, u32[]{:S(2)}, u32[]{:S(2)}) collective-permute-start(f32[2,4,1024]{2,1,0:T(4,128)} %param.6), channel_id=1, source_target_pairs={{0,8},{8,0},{16,24},{24,16},{1,9},{9,1},{17,25},{25,17},{2,10},{10... | collective-permute-start | bytes 98312 | tf_op jit(solution)/shard_map/ppermute | solution.py:39
  4.2 2.5 %collective-permute-start.2 = (f32[2,4,1024]{2,1,0:T(4,128)}, f32[2,4,1024]{2,1,0:T(4,128)S(1)}, u32[]{:S(2)}, u32[]{:S(2)}) collective-permute-start(f32[2,4,1024]{2,1,0:T(4,128)} %param.6), channel_id=1, source_target_pairs={{0,24},{8,16},{16,8},{24,0},{1,25},{9,17},{17,9},{25,1},{2,26},{10... | collective-permute-start | bytes 98312 | tf_op jit(solution)/shard_map/ppermute | solution.py:39
  6.8 0.8 %stack.72 = f32[1,8,1024]{2,1,0:T(8,128)S(1)} reshape(f32[2,4,1024]{2,1,0:T(4,128)} %param.6) | data formatting | bytes 65536 | tf_op jit(solution)/shard_map/stack | solution.py:40
  7.7 2.6 %collective-permute-done.2 = f32[2,4,1024]{2,1,0:T(4,128)S(1)} collective-permute-done((f32[2,4,1024]{2,1,0:T(4,128)}, f32[2,4,1024]{2,1,0:T(4,128)S(1)}, u32[]{:S(2)}, u32[]{:S(2)}) %collective-permute-start.2) | collective-permute-done | bytes 32800 | tf_op jit(solution)/shard_map/ppermute | solution.py:39
  10.3 1.8 %collective-permute-done.1 = f32[2,4,1024]{2,1,0:T(4,128)S(1)} collective-permute-done((f32[2,4,1024]{2,1,0:T(4,128)}, f32[2,4,1024]{2,1,0:T(4,128)S(1)}, u32[]{:S(2)}, u32[]{:S(2)}) %collective-permute-start.1) | collective-permute-done | bytes 32800 | tf_op jit(solution)/shard_map/ppermute | solution.py:39
  12.1 2.5 %collective-permute-start.5 = (f32[4,8,1024]{2,1,0:T(8,128)S(1)}, f32[4,8,1024]{2,1,0:T(8,128)S(1)}, u32[]{:S(2)}, u32[]{:S(2)}) collective-permute-start(f32[4,8,1024]{2,1,0:T(8,128)S(1)} %constant_dynamic-update-slice_fusion.refs_0_), channel_id=1, source_target_pairs={{0,6},{2,4},{4,2},{6,0},{1,7},{3,5},{5,3},{7,1},{8,14},{10,12},{12... | collective-permute-start | bytes 393224 | tf_op jit(solution)/shard_map/ppermute | solution.py:41
  14.6 0.5 collective-permute-start.4
  15.2 0.5 collective-permute-start.3
  15.7 0.8 reshape.25
  16.5 0.7 concatenate.8.scalars_ref
  17.2 1.6 %copy-done = f32[8,4,128,128]{3,2,1,0:T(8,128)S(1)} copy-done((f32[8,4,128,128]{3,2,1,0:T(8,128)S(1)}, f32[8,4,128,128]{3,2,1,0:T(8,128)}, u32[]{:S(2)}) %copy-start) | copy-done | bytes 2097176
  18.8 1.6 %copy-done.1 = f32[8,4,128,128]{3,2,1,0:T(8,128)S(1)} copy-done((f32[8,4,128,128]{3,2,1,0:T(8,128)S(1)}, f32[8,4,128,128]{3,2,1,0:T(8,128)}, u32[]{:S(2)}) %copy-start.1) | copy-done | bytes 2097176
  20.4 1.1 %setup.1 = (s32[12,128]{1,0:T(8,128)S(1)}, s32[8,8]{1,0:T(8,128)S(1)}, f32[8,128]{1,0:T(8,128)S(1)}, f32[32,128,128]{2,1,0:T(8,128)S(1)}, f32[32,128,128]{2,1,0:T(8,128)S(1)}) custom-call(s32[79]{0:T(128)S(1)} %concatenate.8.scalars_ref, f32[32,128,128]{2,1,0:T(8,128)S(1)} %bitcast.23, f32[32,128,128]{2,1,0:T(8,128)S(1)} %bitcast.25), custom_call_target="tpu_custom_call" | custom-call | bytes 8388608 | tf_op jit(solution)/shard_map/setup/pallas_call | solution.py:114
  21.6 3.6 %step_0.1 = (f32[129,8,128]{2,1,0:T(8,128)S(1)}, f32[8,1024]{1,0:T(8,128)S(1)}, f32[8,128]{1,0:T(8,128)S(1)}, bf16[64,256,256]{2,1,0:T(8,128)(2,1)S(1)}) custom-call(s32[12,128]{1,0:T(8,128)S(1)} %get-tuple-element.18.items_ref, s32[8,8]{1,0:T(8,128)S(1)} %get-tuple-element.19.places_ref, f32[8,128]{1,0:T(8,128)S(1)} %get-tuple-element.20.turn_ref, ...), custom_call_target="tpu_custom_call" | custom-call | tf_op jit(solution)/shard_map/step_0/pallas_call | solution.py:345
  25.2 1.2 %collective-permute-start.10 = (f32[8,1024]{1,0:T(8,128)S(1)}, f32[8,1024]{1,0:T(8,128)S(1)}, u32[]{:S(2)}, u32[]{:S(2)}) collective-permute-start(f32[8,1024]{1,0:T(8,128)S(1)} %get-tuple-element.24), channel_id=1, source_target_pairs={{0,24},{8,16},{16,8},{24,0},{1,25},{9,17},{17,9},{25,1},{2,26},{10... | collective-permute-start | bytes 98312 | tf_op jit(solution)/shard_map/ppermute | solution.py:39
  26.4 0.7 collective-permute-start.9
  27.2 2.5 %collective-permute-start.8 = (f32[8,1024]{1,0:T(8,128)S(1)}, f32[8,1024]{1,0:T(8,128)S(1)}, u32[]{:S(2)}, u32[]{:S(2)}) collective-permute-start(f32[8,1024]{1,0:T(8,128)S(1)} %get-tuple-element.24), channel_id=1, source_target_pairs={{0,8},{8,0},{16,24},{24,16},{1,9},{9,1},{17,25},{25,17},{2,10},{10... | collective-permute-start | bytes 98312 | tf_op jit(solution)/shard_map/ppermute | solution.py:39
  29.7 1.7 %collective-permute-done.10 = f32[8,1024]{1,0:T(8,128)S(1)} collective-permute-done((f32[8,1024]{1,0:T(8,128)S(1)}, f32[8,1024]{1,0:T(8,128)S(1)}, u32[]{:S(2)}, u32[]{:S(2)}) %collective-permute-start.10) | collective-permute-done | bytes 32800 | tf_op jit(solution)/shard_map/ppermute | solution.py:39
  31.8 2.6 %collective-permute-start.13 = (f32[4,8,1024]{2,1,0:T(8,128)S(1)}, f32[4,8,1024]{2,1,0:T(8,128)S(1)}, u32[]{:S(2)}, u32[]{:S(2)}) collective-permute-start(f32[4,8,1024]{2,1,0:T(8,128)S(1)} %pad_maximum_fusion.refs_0_), channel_id=1, source_target_pairs={{0,6},{2,4},{4,2},{6,0},{1,7},{3,5},{5,3},{7,1},{8,14},{10,12},{12... | collective-permute-start | bytes 393224 | tf_op jit(solution)/shard_map/ppermute | solution.py:41
  34.6 0.8 collective-permute-start.11
  35.4 2.7 %collective-permute-done.13.refs_3_ = f32[4,8,1024]{2,1,0:T(8,128)S(1)} collective-permute-done((f32[4,8,1024]{2,1,0:T(8,128)S(1)}, f32[4,8,1024]{2,1,0:T(8,128)S(1)}, u32[]{:S(2)}, u32[]{:S(2)}) %collective-permute-start.13) | collective-permute-done | bytes 131104 | tf_op jit(solution)/shard_map/ppermute | solution.py:41
  38.1 1.4 %collective-permute-done.12.refs_2_ = f32[4,8,1024]{2,1,0:T(8,128)S(1)} collective-permute-done((f32[4,8,1024]{2,1,0:T(8,128)S(1)}, f32[4,8,1024]{2,1,0:T(8,128)S(1)}, u32[]{:S(2)}, u32[]{:S(2)}) %collective-permute-start.12) | collective-permute-done | bytes 131104 | tf_op jit(solution)/shard_map/ppermute | solution.py:41
  39.6 3.0 %step_1.1 = (f32[129,8,128]{2,1,0:T(8,128)S(1)}, f32[8,1024]{1,0:T(8,128)S(1)}, f32[8,128]{1,0:T(8,128)S(1)}) custom-call(s32[12,128]{1,0:T(8,128)S(1)} %get-tuple-element.18.items_ref, s32[8,8]{1,0:T(8,128)S(1)} %get-tuple-element.19.places_ref, f32[8,128]{1,0:T(8,128)S(1)} %get-tuple-element.20.turn_ref, f32[8,128]{1,0:T(8,128)S(1)} %get-tuple-element.23.info_in_ref, ...), custom_call_target="tpu_custom_call" | custom-call | tf_op jit(solution)/shard_map/step_1/pallas_call | solution.py:345
  42.6 1.5 %collective-permute-start.16 = (f32[8,1024]{1,0:T(8,128)S(1)}, f32[8,1024]{1,0:T(8,128)S(1)}, u32[]{:S(2)}, u32[]{:S(2)}) collective-permute-start(f32[8,1024]{1,0:T(8,128)S(1)} %get-tuple-element.28), channel_id=1, source_target_pairs={{0,24},{8,16},{16,8},{24,0},{1,25},{9,17},{17,9},{25,1},{2,26},{10... | collective-permute-start | bytes 98312 | tf_op jit(solution)/shard_map/ppermute | solution.py:39
  44.1 1.8 %collective-permute-start.15 = (f32[8,1024]{1,0:T(8,128)S(1)}, f32[8,1024]{1,0:T(8,128)S(1)}, u32[]{:S(2)}, u32[]{:S(2)}) collective-permute-start(f32[8,1024]{1,0:T(8,128)S(1)} %get-tuple-element.28), channel_id=1, source_target_pairs={{0,16},{8,24},{16,0},{24,8},{1,17},{9,25},{17,1},{25,9},{2,18},{10... | collective-permute-start | bytes 98312 | tf_op jit(solution)/shard_map/ppermute | solution.py:39
  45.9 1.2 %collective-permute-start.14 = (f32[8,1024]{1,0:T(8,128)S(1)}, f32[8,1024]{1,0:T(8,128)S(1)}, u32[]{:S(2)}, u32[]{:S(2)}) collective-permute-start(f32[8,1024]{1,0:T(8,128)S(1)} %get-tuple-element.28), channel_id=1, source_target_pairs={{0,8},{8,0},{16,24},{24,16},{1,9},{9,1},{17,25},{25,17},{2,10},{10... | collective-permute-start | bytes 98312 | tf_op jit(solution)/shard_map/ppermute | solution.py:39
  47.1 1.3 %collective-permute-done.16 = f32[8,1024]{1,0:T(8,128)S(1)} collective-permute-done((f32[8,1024]{1,0:T(8,128)S(1)}, f32[8,1024]{1,0:T(8,128)S(1)}, u32[]{:S(2)}, u32[]{:S(2)}) %collective-permute-start.16) | collective-permute-done | bytes 32800 | tf_op jit(solution)/shard_map/ppermute | solution.py:39
  48.4 0.5 collective-permute-done.15
  48.9 0.9 %collective-permute-done.14 = f32[8,1024]{1,0:T(8,128)S(1)} collective-permute-done((f32[8,1024]{1,0:T(8,128)S(1)}, f32[8,1024]{1,0:T(8,128)S(1)}, u32[]{:S(2)}, u32[]{:S(2)}) %collective-permute-start.14) | collective-permute-done | bytes 32800 | tf_op jit(solution)/shard_map/ppermute | solution.py:39
  49.9 1.9 %collective-permute-start.19 = (f32[4,8,1024]{2,1,0:T(8,128)S(1)}, f32[4,8,1024]{2,1,0:T(8,128)S(1)}, u32[]{:S(2)}, u32[]{:S(2)}) collective-permute-start(f32[4,8,1024]{2,1,0:T(8,128)S(1)} %pad_maximum_fusion.1.refs_0_), channel_id=1, source_target_pairs={{0,6},{2,4},{4,2},{6,0},{1,7},{3,5},{5,3},{7,1},{8,14},{10,12},{12... | collective-permute-start | bytes 393224 | tf_op jit(solution)/shard_map/ppermute | solution.py:41
  51.8 1.1 %collective-permute-start.18 = (f32[4,8,1024]{2,1,0:T(8,128)S(1)}, f32[4,8,1024]{2,1,0:T(8,128)S(1)}, u32[]{:S(2)}, u32[]{:S(2)}) collective-permute-start(f32[4,8,1024]{2,1,0:T(8,128)S(1)} %pad_maximum_fusion.1.refs_0_), channel_id=1, source_target_pairs={{0,4},{2,6},{4,0},{6,2},{1,5},{3,7},{5,1},{7,3},{8,12},{10,14},{12... | collective-permute-start | bytes 393224 | tf_op jit(solution)/shard_map/ppermute | solution.py:41
  52.9 0.5 collective-permute-start.17
  53.4 2.4 %collective-permute-done.19.refs_3_ = f32[4,8,1024]{2,1,0:T(8,128)S(1)} collective-permute-done((f32[4,8,1024]{2,1,0:T(8,128)S(1)}, f32[4,8,1024]{2,1,0:T(8,128)S(1)}, u32[]{:S(2)}, u32[]{:S(2)}) %collective-permute-start.19) | collective-permute-done | bytes 131104 | tf_op jit(solution)/shard_map/ppermute | solution.py:41
  55.8 1.4 %collective-permute-done.18.refs_2_ = f32[4,8,1024]{2,1,0:T(8,128)S(1)} collective-permute-done((f32[4,8,1024]{2,1,0:T(8,128)S(1)}, f32[4,8,1024]{2,1,0:T(8,128)S(1)}, u32[]{:S(2)}, u32[]{:S(2)}) %collective-permute-start.18) | collective-permute-done | bytes 131104 | tf_op jit(solution)/shard_map/ppermute | solution.py:41
  57.2 0.7 collective-permute-done.17.refs_1_
  57.9 3.4 %step_2.1 = (f32[3,8,1024]{2,1,0:T(8,128)S(1)}, f32[8,128]{1,0:T(8,128)S(1)}) custom-call(s32[12,128]{1,0:T(8,128)S(1)} %get-tuple-element.18.items_ref, s32[8,8]{1,0:T(8,128)S(1)} %get-tuple-element.19.places_ref, f32[8,128]{1,0:T(8,128)S(1)} %get-tuple-element.20.turn_ref, f32[8,128]{1,0:T(8,128)S(1)} %get-tuple-element.27.info_in_ref, ...), custom_call_target="tpu_custom_call" | custom-call | tf_op jit(solution)/shard_map/step_2/pallas_call | solution.py:345
  61.3 0.6 copy-done.2
  62.0 1.0 %collective-permute-start.22 = (f32[8,128]{1,0:T(8,128)S(1)}, f32[8,128]{1,0:T(8,128)S(1)}, u32[]{:S(2)}, u32[]{:S(2)}) collective-permute-start(f32[8,128]{1,0:T(8,128)S(1)} %get-tuple-element.30), channel_id=1, source_target_pairs={{0,24},{8,16},{16,8},{24,0},{1,25},{9,17},{17,9},{25,1},{2,26},{10... | collective-permute-start | bytes 12296 | tf_op jit(solution)/shard_map/ppermute | solution.py:39
  63.0 1.2 %collective-permute-start.21 = (f32[8,128]{1,0:T(8,128)S(1)}, f32[8,128]{1,0:T(8,128)S(1)}, u32[]{:S(2)}, u32[]{:S(2)}) collective-permute-start(f32[8,128]{1,0:T(8,128)S(1)} %get-tuple-element.30), channel_id=1, source_target_pairs={{0,16},{8,24},{16,0},{24,8},{1,17},{9,25},{17,1},{25,9},{2,18},{10... | collective-permute-start | bytes 12296 | tf_op jit(solution)/shard_map/ppermute | solution.py:39
  64.2 2.2 %collective-permute-start.20 = (f32[8,128]{1,0:T(8,128)S(1)}, f32[8,128]{1,0:T(8,128)S(1)}, u32[]{:S(2)}, u32[]{:S(2)}) collective-permute-start(f32[8,128]{1,0:T(8,128)S(1)} %get-tuple-element.30), channel_id=1, source_target_pairs={{0,8},{8,0},{16,24},{24,16},{1,9},{9,1},{17,25},{25,17},{2,10},{10... | collective-permute-start | bytes 12296 | tf_op jit(solution)/shard_map/ppermute | solution.py:39
  66.4 1.0 %collective-permute-done.22 = f32[8,128]{1,0:T(8,128)S(1)} collective-permute-done((f32[8,128]{1,0:T(8,128)S(1)}, f32[8,128]{1,0:T(8,128)S(1)}, u32[]{:S(2)}, u32[]{:S(2)}) %collective-permute-start.22) | collective-permute-done | bytes 4128 | tf_op jit(solution)/shard_map/ppermute | solution.py:39
  67.9 1.9 %collective-permute-start.25 = (f32[4,8,128]{2,1,0:T(8,128)S(1)}, f32[4,8,128]{2,1,0:T(8,128)S(1)}, u32[]{:S(2)}, u32[]{:S(2)}) collective-permute-start(f32[4,8,128]{2,1,0:T(8,128)S(1)} %pad_maximum_fusion.2), channel_id=1, source_target_pairs={{0,6},{2,4},{4,2},{6,0},{1,7},{3,5},{5,3},{7,1},{8,14},{10,12},{12... | collective-permute-start | bytes 49160 | tf_op jit(solution)/shard_map/ppermute | solution.py:41
  69.8 0.7 collective-permute-start.24
  70.5 0.9 %collective-permute-start.23 = (f32[4,8,128]{2,1,0:T(8,128)S(1)}, f32[4,8,128]{2,1,0:T(8,128)S(1)}, u32[]{:S(2)}, u32[]{:S(2)}) collective-permute-start(f32[4,8,128]{2,1,0:T(8,128)S(1)} %pad_maximum_fusion.2), channel_id=1, source_target_pairs={{0,2},{2,0},{4,6},{6,4},{1,3},{3,1},{5,7},{7,5},{8,10},{10,8},{12,... | collective-permute-start | bytes 49160 | tf_op jit(solution)/shard_map/ppermute | solution.py:41
  71.4 2.9 %collective-permute-done.23 = f32[4,8,128]{2,1,0:T(8,128)S(1)} collective-permute-done((f32[4,8,128]{2,1,0:T(8,128)S(1)}, f32[4,8,128]{2,1,0:T(8,128)S(1)}, u32[]{:S(2)}, u32[]{:S(2)}) %collective-permute-start.23) | collective-permute-done | bytes 16416 | tf_op jit(solution)/shard_map/ppermute | solution.py:41
  74.3 0.6 copy-done.3
  74.9 2.2 %final.1 = (f32[2,4,1024]{2,1,0:T(4,128)}, f32[1,4]{1,0:T(1,128)}) custom-call(f32[16,8,128]{2,1,0:T(8,128)} %copy-done.3, f32[3,8,1024]{2,1,0:T(8,128)} %copy-done.2), custom_call_target="tpu_custom_call" | custom-call | tf_op jit(solution)/shard_map/final/pallas_call | solution.py:426
  (38 shorter events, 1.7 us)
Async XLA Ops:
  0.6 20.9 %collective-permute-start.6 = (f32[32,128,128]{2,1,0:T(8,128)}, f32[32,128,128]{2,1,0:T(8,128)S(1)}, u32[]{:S(2)}, u32[]{:S(2)}) collective-permute-start(f32[32,128,128]{2,1,0:T(8,128)} %bitcast.22), channel_id=1, source_target_pairs={{0,1},{1,0},{2,3},{3,2},{4,5},{5,4},{6,7},{7,6},{8,9},{9,8},{10,11... | collective-permute-start | bytes 6291464 | tf_op jit(solution)/shard_map/ppermute | solution.py:453
  1.1 20.4 %collective-permute-start.7 = (f32[32,128,128]{2,1,0:T(8,128)}, f32[32,128,128]{2,1,0:T(8,128)}, u32[]{:S(2)}, u32[]{:S(2)}) collective-permute-start(f32[32,128,128]{2,1,0:T(8,128)} %bitcast.24), channel_id=1, source_target_pairs={{0,1},{1,0},{2,3},{3,2},{4,5},{5,4},{6,7},{7,6},{8,9},{9,8},{10,11... | collective-permute-start | bytes 6291464 | tf_op jit(solution)/shard_map/ppermute | solution.py:454
  1.2 6.4 %collective-permute-start = (f32[2,4,1024]{2,1,0:T(4,128)}, f32[2,4,1024]{2,1,0:T(4,128)S(1)}, u32[]{:S(2)}, u32[]{:S(2)}) collective-permute-start(f32[2,4,1024]{2,1,0:T(4,128)} %param.6), channel_id=1, source_target_pairs={{0,8},{8,0},{16,24},{24,16},{1,9},{9,1},{17,25},{25,17},{2,10},{10... | collective-permute-start | bytes 98312 | tf_op jit(solution)/shard_map/ppermute | solution.py:39
  4.2 6.1 %collective-permute-start.2 = (f32[2,4,1024]{2,1,0:T(4,128)}, f32[2,4,1024]{2,1,0:T(4,128)S(1)}, u32[]{:S(2)}, u32[]{:S(2)}) collective-permute-start(f32[2,4,1024]{2,1,0:T(4,128)} %param.6), channel_id=1, source_target_pairs={{0,24},{8,16},{16,8},{24,0},{1,25},{9,17},{17,9},{25,1},{2,26},{10... | collective-permute-start | bytes 98312 | tf_op jit(solution)/shard_map/ppermute | solution.py:39
  6.7 5.4 %collective-permute-start.1 = (f32[2,4,1024]{2,1,0:T(4,128)}, f32[2,4,1024]{2,1,0:T(4,128)S(1)}, u32[]{:S(2)}, u32[]{:S(2)}) collective-permute-start(f32[2,4,1024]{2,1,0:T(4,128)} %param.6), channel_id=1, source_target_pairs={{0,16},{8,24},{16,0},{24,8},{1,17},{9,25},{17,1},{25,9},{2,18},{10... | collective-permute-start | bytes 98312 | tf_op jit(solution)/shard_map/ppermute | solution.py:39
  12.1 9.4 %collective-permute-start.5 = (f32[4,8,1024]{2,1,0:T(8,128)S(1)}, f32[4,8,1024]{2,1,0:T(8,128)S(1)}, u32[]{:S(2)}, u32[]{:S(2)}) collective-permute-start(f32[4,8,1024]{2,1,0:T(8,128)S(1)} %constant_dynamic-update-slice_fusion.refs_0_), channel_id=1, source_target_pairs={{0,6},{2,4},{4,2},{6,0},{1,7},{3,5},{5,3},{7,1},{8,14},{10,12},{12... | collective-permute-start | bytes 393224 | tf_op jit(solution)/shard_map/ppermute | solution.py:41
  14.6 6.9 %collective-permute-start.4 = (f32[4,8,1024]{2,1,0:T(8,128)S(1)}, f32[4,8,1024]{2,1,0:T(8,128)S(1)}, u32[]{:S(2)}, u32[]{:S(2)}) collective-permute-start(f32[4,8,1024]{2,1,0:T(8,128)S(1)} %constant_dynamic-update-slice_fusion.refs_0_), channel_id=1, source_target_pairs={{0,4},{2,6},{4,0},{6,2},{1,5},{3,7},{5,1},{7,3},{8,12},{10,14},{12... | collective-permute-start | bytes 393224 | tf_op jit(solution)/shard_map/ppermute | solution.py:41
  15.2 6.4 %collective-permute-start.3 = (f32[4,8,1024]{2,1,0:T(8,128)S(1)}, f32[4,8,1024]{2,1,0:T(8,128)S(1)}, u32[]{:S(2)}, u32[]{:S(2)}) collective-permute-start(f32[4,8,1024]{2,1,0:T(8,128)S(1)} %constant_dynamic-update-slice_fusion.refs_0_), channel_id=1, source_target_pairs={{0,2},{2,0},{4,6},{6,4},{1,3},{3,1},{5,7},{7,5},{8,10},{10,8},{12,... | collective-permute-start | bytes 393224 | tf_op jit(solution)/shard_map/ppermute | solution.py:41
  17.2 1.6 %copy-start = (f32[8,4,128,128]{3,2,1,0:T(8,128)S(1)}, f32[8,4,128,128]{3,2,1,0:T(8,128)}, u32[]{:S(2)}) copy-start(f32[8,4,128,128]{3,2,1,0:T(8,128)} %param.7) | copy-start | bytes 6291460
  18.8 1.6 %copy-start.1 = (f32[8,4,128,128]{3,2,1,0:T(8,128)S(1)}, f32[8,4,128,128]{3,2,1,0:T(8,128)}, u32[]{:S(2)}) copy-start(f32[8,4,128,128]{3,2,1,0:T(8,128)} %param.8) | copy-start | bytes 6291460
  25.2 6.1 %collective-permute-start.10 = (f32[8,1024]{1,0:T(8,128)S(1)}, f32[8,1024]{1,0:T(8,128)S(1)}, u32[]{:S(2)}, u32[]{:S(2)}) collective-permute-start(f32[8,1024]{1,0:T(8,128)S(1)} %get-tuple-element.24), channel_id=1, source_target_pairs={{0,24},{8,16},{16,8},{24,0},{1,25},{9,17},{17,9},{25,1},{2,26},{10... | collective-permute-start | bytes 98312 | tf_op jit(solution)/shard_map/ppermute | solution.py:39
  26.4 5.4 %collective-permute-start.9 = (f32[8,1024]{1,0:T(8,128)S(1)}, f32[8,1024]{1,0:T(8,128)S(1)}, u32[]{:S(2)}, u32[]{:S(2)}) collective-permute-start(f32[8,1024]{1,0:T(8,128)S(1)} %get-tuple-element.24), channel_id=1, source_target_pairs={{0,16},{8,24},{16,0},{24,8},{1,17},{9,25},{17,1},{25,9},{2,18},{10... | collective-permute-start | bytes 98312 | tf_op jit(solution)/shard_map/ppermute | solution.py:39
  27.2 4.7 %collective-permute-start.8 = (f32[8,1024]{1,0:T(8,128)S(1)}, f32[8,1024]{1,0:T(8,128)S(1)}, u32[]{:S(2)}, u32[]{:S(2)}) collective-permute-start(f32[8,1024]{1,0:T(8,128)S(1)} %get-tuple-element.24), channel_id=1, source_target_pairs={{0,8},{8,0},{16,24},{24,16},{1,9},{9,1},{17,25},{25,17},{2,10},{10... | collective-permute-start | bytes 98312 | tf_op jit(solution)/shard_map/ppermute | solution.py:39
  31.8 6.3 %collective-permute-start.13 = (f32[4,8,1024]{2,1,0:T(8,128)S(1)}, f32[4,8,1024]{2,1,0:T(8,128)S(1)}, u32[]{:S(2)}, u32[]{:S(2)}) collective-permute-start(f32[4,8,1024]{2,1,0:T(8,128)S(1)} %pad_maximum_fusion.refs_0_), channel_id=1, source_target_pairs={{0,6},{2,4},{4,2},{6,0},{1,7},{3,5},{5,3},{7,1},{8,14},{10,12},{12... | collective-permute-start | bytes 393224 | tf_op jit(solution)/shard_map/ppermute | solution.py:41
  34.4 5.1 %collective-permute-start.12 = (f32[4,8,1024]{2,1,0:T(8,128)S(1)}, f32[4,8,1024]{2,1,0:T(8,128)S(1)}, u32[]{:S(2)}, u32[]{:S(2)}) collective-permute-start(f32[4,8,1024]{2,1,0:T(8,128)S(1)} %pad_maximum_fusion.refs_0_), channel_id=1, source_target_pairs={{0,4},{2,6},{4,0},{6,2},{1,5},{3,7},{5,1},{7,3},{8,12},{10,14},{12... | collective-permute-start | bytes 393224 | tf_op jit(solution)/shard_map/ppermute | solution.py:41
  34.6 5.0 %collective-permute-start.11 = (f32[4,8,1024]{2,1,0:T(8,128)S(1)}, f32[4,8,1024]{2,1,0:T(8,128)S(1)}, u32[]{:S(2)}, u32[]{:S(2)}) collective-permute-start(f32[4,8,1024]{2,1,0:T(8,128)S(1)} %pad_maximum_fusion.refs_0_), channel_id=1, source_target_pairs={{0,2},{2,0},{4,6},{6,4},{1,3},{3,1},{5,7},{7,5},{8,10},{10,8},{12,... | collective-permute-start | bytes 393224 | tf_op jit(solution)/shard_map/ppermute | solution.py:41
  42.6 5.8 %collective-permute-start.16 = (f32[8,1024]{1,0:T(8,128)S(1)}, f32[8,1024]{1,0:T(8,128)S(1)}, u32[]{:S(2)}, u32[]{:S(2)}) collective-permute-start(f32[8,1024]{1,0:T(8,128)S(1)} %get-tuple-element.28), channel_id=1, source_target_pairs={{0,24},{8,16},{16,8},{24,0},{1,25},{9,17},{17,9},{25,1},{2,26},{10... | collective-permute-start | bytes 98312 | tf_op jit(solution)/shard_map/ppermute | solution.py:39
  44.1 4.8 %collective-permute-start.15 = (f32[8,1024]{1,0:T(8,128)S(1)}, f32[8,1024]{1,0:T(8,128)S(1)}, u32[]{:S(2)}, u32[]{:S(2)}) collective-permute-start(f32[8,1024]{1,0:T(8,128)S(1)} %get-tuple-element.28), channel_id=1, source_target_pairs={{0,16},{8,24},{16,0},{24,8},{1,17},{9,25},{17,1},{25,9},{2,18},{10... | collective-permute-start | bytes 98312 | tf_op jit(solution)/shard_map/ppermute | solution.py:39
  45.9 3.9 %collective-permute-start.14 = (f32[8,1024]{1,0:T(8,128)S(1)}, f32[8,1024]{1,0:T(8,128)S(1)}, u32[]{:S(2)}, u32[]{:S(2)}) collective-permute-start(f32[8,1024]{1,0:T(8,128)S(1)} %get-tuple-element.28), channel_id=1, source_target_pairs={{0,8},{8,0},{16,24},{24,16},{1,9},{9,1},{17,25},{25,17},{2,10},{10... | collective-permute-start | bytes 98312 | tf_op jit(solution)/shard_map/ppermute | solution.py:39
  49.9 6.0 %collective-permute-start.19 = (f32[4,8,1024]{2,1,0:T(8,128)S(1)}, f32[4,8,1024]{2,1,0:T(8,128)S(1)}, u32[]{:S(2)}, u32[]{:S(2)}) collective-permute-start(f32[4,8,1024]{2,1,0:T(8,128)S(1)} %pad_maximum_fusion.1.refs_0_), channel_id=1, source_target_pairs={{0,6},{2,4},{4,2},{6,0},{1,7},{3,5},{5,3},{7,1},{8,14},{10,12},{12... | collective-permute-start | bytes 393224 | tf_op jit(solution)/shard_map/ppermute | solution.py:41
  51.8 5.4 %collective-permute-start.18 = (f32[4,8,1024]{2,1,0:T(8,128)S(1)}, f32[4,8,1024]{2,1,0:T(8,128)S(1)}, u32[]{:S(2)}, u32[]{:S(2)}) collective-permute-start(f32[4,8,1024]{2,1,0:T(8,128)S(1)} %pad_maximum_fusion.1.refs_0_), channel_id=1, source_target_pairs={{0,4},{2,6},{4,0},{6,2},{1,5},{3,7},{5,1},{7,3},{8,12},{10,14},{12... | collective-permute-start | bytes 393224 | tf_op jit(solution)/shard_map/ppermute | solution.py:41
  52.9 5.0 %collective-permute-start.17 = (f32[4,8,1024]{2,1,0:T(8,128)S(1)}, f32[4,8,1024]{2,1,0:T(8,128)S(1)}, u32[]{:S(2)}, u32[]{:S(2)}) collective-permute-start(f32[4,8,1024]{2,1,0:T(8,128)S(1)} %pad_maximum_fusion.1.refs_0_), channel_id=1, source_target_pairs={{0,2},{2,0},{4,6},{6,4},{1,3},{3,1},{5,7},{7,5},{8,10},{10,8},{12,... | collective-permute-start | bytes 393224 | tf_op jit(solution)/shard_map/ppermute | solution.py:41
  61.3 0.6 copy-start.2
  62.0 5.4 %collective-permute-start.22 = (f32[8,128]{1,0:T(8,128)S(1)}, f32[8,128]{1,0:T(8,128)S(1)}, u32[]{:S(2)}, u32[]{:S(2)}) collective-permute-start(f32[8,128]{1,0:T(8,128)S(1)} %get-tuple-element.30), channel_id=1, source_target_pairs={{0,24},{8,16},{16,8},{24,0},{1,25},{9,17},{17,9},{25,1},{2,26},{10... | collective-permute-start | bytes 12296 | tf_op jit(solution)/shard_map/ppermute | solution.py:39
  63.0 4.5 %collective-permute-start.21 = (f32[8,128]{1,0:T(8,128)S(1)}, f32[8,128]{1,0:T(8,128)S(1)}, u32[]{:S(2)}, u32[]{:S(2)}) collective-permute-start(f32[8,128]{1,0:T(8,128)S(1)} %get-tuple-element.30), channel_id=1, source_target_pairs={{0,16},{8,24},{16,0},{24,8},{1,17},{9,25},{17,1},{25,9},{2,18},{10... | collective-permute-start | bytes 12296 | tf_op jit(solution)/shard_map/ppermute | solution.py:39
  64.2 3.8 %collective-permute-start.20 = (f32[8,128]{1,0:T(8,128)S(1)}, f32[8,128]{1,0:T(8,128)S(1)}, u32[]{:S(2)}, u32[]{:S(2)}) collective-permute-start(f32[8,128]{1,0:T(8,128)S(1)} %get-tuple-element.30), channel_id=1, source_target_pairs={{0,8},{8,0},{16,24},{24,16},{1,9},{9,1},{17,25},{25,17},{2,10},{10... | collective-permute-start | bytes 12296 | tf_op jit(solution)/shard_map/ppermute | solution.py:39
  67.9 6.4 %collective-permute-start.25 = (f32[4,8,128]{2,1,0:T(8,128)S(1)}, f32[4,8,128]{2,1,0:T(8,128)S(1)}, u32[]{:S(2)}, u32[]{:S(2)}) collective-permute-start(f32[4,8,128]{2,1,0:T(8,128)S(1)} %pad_maximum_fusion.2), channel_id=1, source_target_pairs={{0,6},{2,4},{4,2},{6,0},{1,7},{3,5},{5,3},{7,1},{8,14},{10,12},{12... | collective-permute-start | bytes 49160 | tf_op jit(solution)/shard_map/ppermute | solution.py:41
  69.8 4.5 %collective-permute-start.24 = (f32[4,8,128]{2,1,0:T(8,128)S(1)}, f32[4,8,128]{2,1,0:T(8,128)S(1)}, u32[]{:S(2)}, u32[]{:S(2)}) collective-permute-start(f32[4,8,128]{2,1,0:T(8,128)S(1)} %pad_maximum_fusion.2), channel_id=1, source_target_pairs={{0,4},{2,6},{4,0},{6,2},{1,5},{3,7},{5,1},{7,3},{8,12},{10,14},{12... | collective-permute-start | bytes 49160 | tf_op jit(solution)/shard_map/ppermute | solution.py:41
  70.5 3.7 %collective-permute-start.23 = (f32[4,8,128]{2,1,0:T(8,128)S(1)}, f32[4,8,128]{2,1,0:T(8,128)S(1)}, u32[]{:S(2)}, u32[]{:S(2)}) collective-permute-start(f32[4,8,128]{2,1,0:T(8,128)S(1)} %pad_maximum_fusion.2), channel_id=1, source_target_pairs={{0,2},{2,0},{4,6},{6,4},{1,3},{3,1},{5,7},{7,5},{8,10},{10,8},{12,... | collective-permute-start | bytes 49160 | tf_op jit(solution)/shard_map/ppermute | solution.py:41
  74.3 0.6 copy-start.3

commit v13 on v12

--- a/solution.py
+++ b/solution.py
@@ -34,20 +34,16 @@
     return lax.rem(me - other + size, size)
 
 
-def gather_rows(rows, line, plane):
+def gather_rows(rows, line, plane, between=None):
     parts = rows.size // rows.shape[-1]
     held = [rows] + [lax.ppermute(rows, "line", perm) for perm in partner_steps(line)]
     whole_line = jnp.stack(held).reshape(line, parts, rows.shape[-1])
+    if between is not None:
+        whole_line = whole_line + between[:1, :1]
     return [whole_line] + [lax.ppermute(whole_line, "place", perm) for perm in partner_steps(plane)]
 
 
-def setup_kernel(
-    line, plane, freqs, scalars_ref, g_ref, c_ref,
-    items_ref, places_ref, turn_ref, g_out_ref, c_out_ref, sems,
-):
-    row_blocks, slots = places_ref.shape
-    pattern_at = 3 + row_blocks + turn_ref.shape[0] // 2
-    own_slots = slots // freqs
+def near_kernel(g_ref, c_ref, g_out_ref, c_out_ref, done_ref, sems):
     pieces = sems.shape[1]
     part = g_ref.shape[0] // pieces
     copies = []
@@ -56,7 +52,30 @@
             at = pl.ds(i * part, part)
             copies.append(pltpu.make_async_copy(source.at[at], target.at[at], sems.at[m, i]))
             copies[-1].start()
-
+    for copy in copies:
+        copy.wait()
+    done_ref[...] = jnp.zeros_like(done_ref)
+
+
+def bring_near(g_own, c_own):
+    vmem, far = pl.BlockSpec(memory_space=pltpu.VMEM), pl.BlockSpec(memory_space=pl.ANY)
+    blocks = jax.ShapeDtypeStruct(g_own.shape, jnp.float32)
+    return pl.pallas_call(
+        near_kernel,
+        in_specs=[far] * 2,
+        out_specs=[vmem] * 3,
+        out_shape=[blocks] * 2 + [jax.ShapeDtypeStruct((8, LANES), jnp.float32)],
+        scratch_shapes=[pltpu.SemaphoreType.DMA((2, math.gcd(g_own.shape[0], 8)))],
+        compiler_params=pltpu.CompilerParams(vmem_limit_bytes=VMEM_LIMIT),
+        cost_estimate=pl.CostEstimate(flops=0, bytes_accessed=16 * g_own.size, transcendentals=0),
+        name="near",
+    )(g_own, c_own)
+
+
+def setup_kernel(line, plane, freqs, scalars_ref, items_ref, places_ref, turn_ref):
+    row_blocks, slots = places_ref.shape
+    pattern_at = 3 + row_blocks + turn_ref.shape[0] // 2
+    own_slots = slots // freqs
     order = lax.broadcasted_iota(jnp.int32, (8, LANES), 1)
     freq = scalars_ref[2]
     for table, d in enumerate(list(range(freqs)) + [None]):
@@ -102,31 +121,20 @@
         ids = jnp.where(lax.rem(row_at, half) == f, scalars_ref[3 + row_blocks + f], ids)
     angular = 0.2 * jnp.exp(ids.astype(jnp.float32) * (math.log(8.0) / 1000.0))
     turn_ref[...] = jnp.where(row_at < half, -angular, angular)
-    for copy in copies:
-        copy.wait()
-
-
-def run_setup(scalars, shape, freq_count, g_own, c_own, line, plane, freqs):
-    smem, vmem = pl.BlockSpec(memory_space=pltpu.SMEM), pl.BlockSpec(memory_space=pltpu.VMEM)
-    far = pl.BlockSpec(memory_space=pl.ANY)
-    blocks = jax.ShapeDtypeStruct(g_own.shape, jnp.float32)
-    pieces = math.gcd(g_own.shape[0], 8)
+
+
+def run_setup(scalars, shape, freq_count, line, plane, freqs):
     return pl.pallas_call(
         functools.partial(setup_kernel, line, plane, freqs),
-        in_specs=[smem, far, far],
-        out_specs=[vmem] * 5,
+        in_specs=[pl.BlockSpec(memory_space=pltpu.SMEM)],
+        out_specs=[pl.BlockSpec(memory_space=pltpu.VMEM)] * 3,
         out_shape=[
             jax.ShapeDtypeStruct((4 * (freqs + 1), LANES), jnp.int32),
             jax.ShapeDtypeStruct(shape, jnp.int32),
             jax.ShapeDtypeStruct((2 * freq_count, LANES), jnp.float32),
-            blocks,
-            blocks,
         ],
-        scratch_shapes=[pltpu.SemaphoreType.DMA((2, pieces))],
-        compiler_params=pltpu.CompilerParams(vmem_limit_bytes=VMEM_LIMIT),
-        cost_estimate=pl.CostEstimate(flops=0, bytes_accessed=16 * g_own.size, transcendentals=0),
         name="setup",
-    )(scalars, g_own, c_own)
+    )(scalars)
 
 
 def lane_sum(x):
@@ -444,9 +452,8 @@
         scalars = jnp.concatenate([where, counts, freq_ids, pattern.reshape(-1)]).astype(jnp.int32)
         stored = (row_blocks * own_slots, size, size)
         g_own, c_own = g_blocks.reshape(stored), c_blocks.reshape(stored)
-        *lists, turn, g_near, c_near = run_setup(
-            scalars, pattern.shape, freq_count, g_own, c_own, line, plane, freqs
-        )
+        *lists, turn = run_setup(scalars, pattern.shape, freq_count, line, plane, freqs)
+        g_near, c_near, near = bring_near(g_own, c_own)
         g_parts, c_parts = [g_near], [c_near]
         for d in range(1, freqs):
             perm = [(i, (i + d) % freqs) for i in range(freqs)]
@@ -457,7 +464,7 @@
         rows = excitation
         blocks = g_parts + c_parts
         for step in range(ITERS):
-            lines = gather_rows(rows, line, plane)
+            lines = gather_rows(rows, line, plane, None if step else near)
             result = run_step(step, lists, turn, info, lines, krylov, blocks, freqs)
             if step == ITERS - 1:
                 own, info = result

time: 77.4 us -> 87 us (1.12)
  local copies, waits for them, and re-layouts: 6.83 us -> 14.4 us
    unnamed x17 -> x34, local copies, waits for them, and re-layouts: 4.45 us -> 12.4 us
    ppermute x12, waiting for transfers between devices: 11.5 us -> 13.8 us  [gather_rows(): lax.ppermute(whole_line, 'place', perm)]
    ppermute x12, waiting for transfers between devices: 10.9 us -> 9.18 us  [gather_rows(): lax.ppermute(rows, 'line', perm)]
  transfers between devices with their start and end apart: 26 -> 26, of which waited for: 17 -> 15; matrix products, arithmetic and copies ran while one was open for 3% -> 3% of each run, Pallas kernels for 1% -> 2%
where the time goes in v13:
time: 87 us; the launch traced here: 86.4 us
  starting transfers between devices  33.6 us (39%)
  waiting for transfers between devices  23 us (26%)
  local copies, waits for them, and re-layouts  14.4 us (17%)
  Pallas kernels  13.9 us (16%)
    ppermute x12, starting transfers between devices, gather_rows(): lax.ppermute(rows, 'line', perm)  18.9 us
    ppermute x12, starting transfers between devices, gather_rows(): lax.ppermute(whole_line, 'place', perm)  14.2 us
    ppermute x12, waiting for transfers between devices, gather_rows(): lax.ppermute(whole_line, 'place', perm)  13.8 us
    unnamed x34, local copies, waits for them, and re-layouts  12.4 us
    pallas_call x3, Pallas kernels, run_step(): pl.pallas_call(functools.partial(step_kernel, step, plane, line, freqs),...  9.9 us
    ppermute x12, waiting for transfers between devices, gather_rows(): lax.ppermute(rows, 'line', perm)  9.18 us
    pallas_call x1, Pallas kernels, run_final(): pl.pallas_call(final_kernel, in_specs=[vmem] * 2, out_specs=[vmem] * 2, o...  2.17 us
  transfers between devices with their start and end apart: 26, of which 15 were waited for; matrix products, arithmetic and copies ran while one was open for 3% of the time, Pallas kernels for 2%

profile of v13, /device:TPU:0, one launch (start us, length us, event | category | flops | bytes accessed | tf_op | source)
XLA Modules:
  0.0 86.4 jit_solution(8795575151782465520)
XLA Ops:
  1.2 3.0 %collective-permute-start = (f32[2,4,1024]{2,1,0:T(4,128)}, f32[2,4,1024]{2,1,0:T(4,128)S(1)}, u32[]{:S(2)}, u32[]{:S(2)}) collective-permute-start(f32[2,4,1024]{2,1,0:T(4,128)} %param.6), channel_id=1, source_target_pairs={{0,8},{8,0},{16,24},{24,16},{1,9},{9,1},{17,25},{25,17},{2,10},{10... | collective-permute-start | bytes 98312 | tf_op jit(solution)/shard_map/ppermute | solution.py:39
  4.2 2.5 %collective-permute-start.2 = (f32[2,4,1024]{2,1,0:T(4,128)}, f32[2,4,1024]{2,1,0:T(4,128)S(1)}, u32[]{:S(2)}, u32[]{:S(2)}) collective-permute-start(f32[2,4,1024]{2,1,0:T(4,128)} %param.6), channel_id=1, source_target_pairs={{0,24},{8,16},{16,8},{24,0},{1,25},{9,17},{17,9},{25,1},{2,26},{10... | collective-permute-start | bytes 98312 | tf_op jit(solution)/shard_map/ppermute | solution.py:39
  6.8 0.8 stack.72
  7.6 1.6 %copy-done = f32[8,4,128,128]{3,2,1,0:T(8,128)S(1)} copy-done((f32[8,4,128,128]{3,2,1,0:T(8,128)S(1)}, f32[8,4,128,128]{3,2,1,0:T(8,128)}, u32[]{:S(2)}) %copy-start) | copy-done | bytes 2097176
  9.2 1.6 %copy-done.1 = f32[8,4,128,128]{3,2,1,0:T(8,128)S(1)} copy-done((f32[8,4,128,128]{3,2,1,0:T(8,128)S(1)}, f32[8,4,128,128]{3,2,1,0:T(8,128)}, u32[]{:S(2)}) %copy-start.1) | copy-done | bytes 2097176
  11.3 1.3 %copy-done.2 = f32[32,128,128]{2,1,0:T(8,128)} copy-done((f32[32,128,128]{2,1,0:T(8,128)}, f32[32,128,128]{2,1,0:T(8,128)S(1)}, u32[]{:S(2)}) %copy-start.2) | copy-done | bytes 2097176
  12.6 1.4 %copy-done.4 = f32[32,128,128]{2,1,0:T(8,128)} copy-done((f32[32,128,128]{2,1,0:T(8,128)}, f32[32,128,128]{2,1,0:T(8,128)S(1)}, u32[]{:S(2)}) %copy-start.4) | copy-done | bytes 2097176
  14.6 0.7 maximum_add_fusion.refs_0_
  15.3 2.5 %collective-permute-start.5 = (f32[4,8,1024]{2,1,0:T(8,128)S(1)}, f32[4,8,1024]{2,1,0:T(8,128)S(1)}, u32[]{:S(2)}, u32[]{:S(2)}) collective-permute-start(f32[4,8,1024]{2,1,0:T(8,128)S(1)} %maximum_add_fusion.refs_0_), channel_id=1, source_target_pairs={{0,6},{2,4},{4,2},{6,0},{1,7},{3,5},{5,3},{7,1},{8,14},{10,12},{12... | collective-permute-start | bytes 393224 | tf_op jit(solution)/shard_map/ppermute | solution.py:43
  18.9 0.6 concatenate.8.scalars_ref
  19.5 1.4 %setup.1 = (s32[12,128]{1,0:T(8,128)}, s32[8,8]{1,0:T(8,128)}, f32[8,128]{1,0:T(8,128)}) custom-call(s32[79]{0:T(128)} %concatenate.8.scalars_ref), custom_call_target="tpu_custom_call" | custom-call | tf_op jit(solution)/shard_map/setup/pallas_call | solution.py:127
  20.9 0.8 collective-permute-done.5.refs_3_
  21.7 2.3 %collective-permute-done.4.refs_2_ = f32[4,8,1024]{2,1,0:T(8,128)S(1)} collective-permute-done((f32[4,8,1024]{2,1,0:T(8,128)S(1)}, f32[4,8,1024]{2,1,0:T(8,128)S(1)}, u32[]{:S(2)}, u32[]{:S(2)}) %collective-permute-start.4) | collective-permute-done | bytes 131104 | tf_op jit(solution)/shard_map/ppermute | solution.py:43
  24.1 1.6 %copy-done.3 = f32[32,128,128]{2,1,0:T(8,128)S(1)} copy-done((f32[32,128,128]{2,1,0:T(8,128)S(1)}, f32[32,128,128]{2,1,0:T(8,128)}, u32[]{:S(2)}) %copy-start.3) | copy-done | bytes 2097176
  25.7 1.6 %copy-done.5 = f32[32,128,128]{2,1,0:T(8,128)S(1)} copy-done((f32[32,128,128]{2,1,0:T(8,128)S(1)}, f32[32,128,128]{2,1,0:T(8,128)}, u32[]{:S(2)}) %copy-start.5) | copy-done | bytes 2097176
  27.2 0.7 copy-done.7
  27.9 0.7 copy-done.8
  28.6 0.7 copy-done.9
  29.3 3.4 %step_0.1 = (f32[129,8,128]{2,1,0:T(8,128)S(1)}, f32[8,1024]{1,0:T(8,128)S(1)}, f32[8,128]{1,0:T(8,128)S(1)}, bf16[64,256,256]{2,1,0:T(8,128)(2,1)S(1)}) custom-call(s32[12,128]{1,0:T(8,128)S(1)} %copy-done.7, s32[8,8]{1,0:T(8,128)S(1)} %copy-done.8, f32[8,128]{1,0:T(8,128)S(1)} %copy-done.9, f32[8,128]{1,0:T(8,128)S(1)} %broadcast_in_dim.4.info_in_ref, ...), custom_call_target="tpu_custom_call" | custom-call | tf_op jit(solution)/shard_map/step_0/pallas_call | solution.py:353
  32.8 2.8 %collective-permute-start.10 = (f32[8,1024]{1,0:T(8,128)S(1)}, f32[8,1024]{1,0:T(8,128)S(1)}, u32[]{:S(2)}, u32[]{:S(2)}) collective-permute-start(f32[8,1024]{1,0:T(8,128)S(1)} %get-tuple-element.26), channel_id=1, source_target_pairs={{0,24},{8,16},{16,8},{24,0},{1,25},{9,17},{17,9},{25,1},{2,26},{10... | collective-permute-start | bytes 98312 | tf_op jit(solution)/shard_map/ppermute | solution.py:39
  35.6 1.6 %collective-permute-start.8 = (f32[8,1024]{1,0:T(8,128)S(1)}, f32[8,1024]{1,0:T(8,128)S(1)}, u32[]{:S(2)}, u32[]{:S(2)}) collective-permute-start(f32[8,1024]{1,0:T(8,128)S(1)} %get-tuple-element.26), channel_id=1, source_target_pairs={{0,8},{8,0},{16,24},{24,16},{1,9},{9,1},{17,25},{25,17},{2,10},{10... | collective-permute-start | bytes 98312 | tf_op jit(solution)/shard_map/ppermute | solution.py:39
  37.2 1.4 %collective-permute-done.10 = f32[8,1024]{1,0:T(8,128)S(1)} collective-permute-done((f32[8,1024]{1,0:T(8,128)S(1)}, f32[8,1024]{1,0:T(8,128)S(1)}, u32[]{:S(2)}, u32[]{:S(2)}) %collective-permute-start.10) | collective-permute-done | bytes 32800 | tf_op jit(solution)/shard_map/ppermute | solution.py:39
  38.6 1.9 %collective-permute-done.9 = f32[8,1024]{1,0:T(8,128)S(1)} collective-permute-done((f32[8,1024]{1,0:T(8,128)S(1)}, f32[8,1024]{1,0:T(8,128)S(1)}, u32[]{:S(2)}, u32[]{:S(2)}) %collective-permute-start.9) | collective-permute-done | bytes 32800 | tf_op jit(solution)/shard_map/ppermute | solution.py:39
  40.4 1.5 %collective-permute-start.13 = (f32[4,8,1024]{2,1,0:T(8,128)S(1)}, f32[4,8,1024]{2,1,0:T(8,128)S(1)}, u32[]{:S(2)}, u32[]{:S(2)}) collective-permute-start(f32[4,8,1024]{2,1,0:T(8,128)S(1)} %pad_maximum_fusion.refs_0_), channel_id=1, source_target_pairs={{0,6},{2,4},{4,2},{6,0},{1,7},{3,5},{5,3},{7,1},{8,14},{10,12},{12... | collective-permute-start | bytes 393224 | tf_op jit(solution)/shard_map/ppermute | solution.py:43
  41.9 1.4 %collective-permute-start.12 = (f32[4,8,1024]{2,1,0:T(8,128)S(1)}, f32[4,8,1024]{2,1,0:T(8,128)S(1)}, u32[]{:S(2)}, u32[]{:S(2)}) collective-permute-start(f32[4,8,1024]{2,1,0:T(8,128)S(1)} %pad_maximum_fusion.refs_0_), channel_id=1, source_target_pairs={{0,4},{2,6},{4,0},{6,2},{1,5},{3,7},{5,1},{7,3},{8,12},{10,14},{12... | collective-permute-start | bytes 393224 | tf_op jit(solution)/shard_map/ppermute | solution.py:43
  43.3 0.6 collective-permute-start.11
  44.0 3.0 %collective-permute-done.13.refs_3_ = f32[4,8,1024]{2,1,0:T(8,128)S(1)} collective-permute-done((f32[4,8,1024]{2,1,0:T(8,128)S(1)}, f32[4,8,1024]{2,1,0:T(8,128)S(1)}, u32[]{:S(2)}, u32[]{:S(2)}) %collective-permute-start.13) | collective-permute-done | bytes 131104 | tf_op jit(solution)/shard_map/ppermute | solution.py:43
  47.0 1.3 %collective-permute-done.12.refs_2_ = f32[4,8,1024]{2,1,0:T(8,128)S(1)} collective-permute-done((f32[4,8,1024]{2,1,0:T(8,128)S(1)}, f32[4,8,1024]{2,1,0:T(8,128)S(1)}, u32[]{:S(2)}, u32[]{:S(2)}) %collective-permute-start.12) | collective-permute-done | bytes 131104 | tf_op jit(solution)/shard_map/ppermute | solution.py:43
  48.5 3.0 %step_1.1 = (f32[129,8,128]{2,1,0:T(8,128)S(1)}, f32[8,1024]{1,0:T(8,128)S(1)}, f32[8,128]{1,0:T(8,128)S(1)}) custom-call(s32[12,128]{1,0:T(8,128)S(1)} %copy-done.7, s32[8,8]{1,0:T(8,128)S(1)} %copy-done.8, f32[8,128]{1,0:T(8,128)S(1)} %copy-done.9, f32[8,128]{1,0:T(8,128)S(1)} %get-tuple-element.25.info_in_ref, f32[4,8,1024]{2,1,0:T(8,128)S(1)} %pad_maximum_fusion.refs_0_, ...), custom_call_target="tpu_custom_call" | custom-call | tf_op jit(solution)/shard_map/step_1/pallas_call | solution.py:353
  51.6 3.4 %collective-permute-start.16 = (f32[8,1024]{1,0:T(8,128)S(1)}, f32[8,1024]{1,0:T(8,128)S(1)}, u32[]{:S(2)}, u32[]{:S(2)}) collective-permute-start(f32[8,1024]{1,0:T(8,128)S(1)} %get-tuple-element.30), channel_id=1, source_target_pairs={{0,24},{8,16},{16,8},{24,0},{1,25},{9,17},{17,9},{25,1},{2,26},{10... | collective-permute-start | bytes 98312 | tf_op jit(solution)/shard_map/ppermute | solution.py:39
  55.0 1.0 %collective-permute-start.14 = (f32[8,1024]{1,0:T(8,128)S(1)}, f32[8,1024]{1,0:T(8,128)S(1)}, u32[]{:S(2)}, u32[]{:S(2)}) collective-permute-start(f32[8,1024]{1,0:T(8,128)S(1)} %get-tuple-element.30), channel_id=1, source_target_pairs={{0,8},{8,0},{16,24},{24,16},{1,9},{9,1},{17,25},{25,17},{2,10},{10... | collective-permute-start | bytes 98312 | tf_op jit(solution)/shard_map/ppermute | solution.py:39
  56.0 1.4 %collective-permute-done.16 = f32[8,1024]{1,0:T(8,128)S(1)} collective-permute-done((f32[8,1024]{1,0:T(8,128)S(1)}, f32[8,1024]{1,0:T(8,128)S(1)}, u32[]{:S(2)}, u32[]{:S(2)}) %collective-permute-start.16) | collective-permute-done | bytes 32800 | tf_op jit(solution)/shard_map/ppermute | solution.py:39
  57.4 2.4 %collective-permute-done.15 = f32[8,1024]{1,0:T(8,128)S(1)} collective-permute-done((f32[8,1024]{1,0:T(8,128)S(1)}, f32[8,1024]{1,0:T(8,128)S(1)}, u32[]{:S(2)}, u32[]{:S(2)}) %collective-permute-start.15) | collective-permute-done | bytes 32800 | tf_op jit(solution)/shard_map/ppermute | solution.py:39
  59.8 0.9 collective-permute-start.19
  60.7 1.4 %collective-permute-start.18 = (f32[4,8,1024]{2,1,0:T(8,128)S(1)}, f32[4,8,1024]{2,1,0:T(8,128)S(1)}, u32[]{:S(2)}, u32[]{:S(2)}) collective-permute-start(f32[4,8,1024]{2,1,0:T(8,128)S(1)} %pad_maximum_fusion.1.refs_0_), channel_id=1, source_target_pairs={{0,4},{2,6},{4,0},{6,2},{1,5},{3,7},{5,1},{7,3},{8,12},{10,14},{12... | collective-permute-start | bytes 393224 | tf_op jit(solution)/shard_map/ppermute | solution.py:43
  62.0 1.3 %collective-permute-start.17 = (f32[4,8,1024]{2,1,0:T(8,128)S(1)}, f32[4,8,1024]{2,1,0:T(8,128)S(1)}, u32[]{:S(2)}, u32[]{:S(2)}) collective-permute-start(f32[4,8,1024]{2,1,0:T(8,128)S(1)} %pad_maximum_fusion.1.refs_0_), channel_id=1, source_target_pairs={{0,2},{2,0},{4,6},{6,4},{1,3},{3,1},{5,7},{7,5},{8,10},{10,8},{12,... | collective-permute-start | bytes 393224 | tf_op jit(solution)/shard_map/ppermute | solution.py:43
  63.4 2.5 %collective-permute-done.19.refs_3_ = f32[4,8,1024]{2,1,0:T(8,128)S(1)} collective-permute-done((f32[4,8,1024]{2,1,0:T(8,128)S(1)}, f32[4,8,1024]{2,1,0:T(8,128)S(1)}, u32[]{:S(2)}, u32[]{:S(2)}) %collective-permute-start.19) | collective-permute-done | bytes 131104 | tf_op jit(solution)/shard_map/ppermute | solution.py:43
  65.9 1.2 %collective-permute-done.18.refs_2_ = f32[4,8,1024]{2,1,0:T(8,128)S(1)} collective-permute-done((f32[4,8,1024]{2,1,0:T(8,128)S(1)}, f32[4,8,1024]{2,1,0:T(8,128)S(1)}, u32[]{:S(2)}, u32[]{:S(2)}) %collective-permute-start.18) | collective-permute-done | bytes 131104 | tf_op jit(solution)/shard_map/ppermute | solution.py:43
  67.1 3.4 %step_2.1 = (f32[3,8,1024]{2,1,0:T(8,128)S(1)}, f32[8,128]{1,0:T(8,128)S(1)}) custom-call(s32[12,128]{1,0:T(8,128)S(1)} %copy-done.7, s32[8,8]{1,0:T(8,128)S(1)} %copy-done.8, f32[8,128]{1,0:T(8,128)S(1)} %copy-done.9, f32[8,128]{1,0:T(8,128)S(1)} %get-tuple-element.29.info_in_ref, f32[4,8,1024]{2,1,0:T(8,128)S(1)} %pad_maximum_fusion.1.refs_0_, ...), custom_call_target="tpu_custom_call" | custom-call | tf_op jit(solution)/shard_map/step_2/pallas_call | solution.py:353
  71.1 2.1 %collective-permute-start.22 = (f32[8,128]{1,0:T(8,128)S(1)}, f32[8,128]{1,0:T(8,128)S(1)}, u32[]{:S(2)}, u32[]{:S(2)}) collective-permute-start(f32[8,128]{1,0:T(8,128)S(1)} %get-tuple-element.32), channel_id=1, source_target_pairs={{0,24},{8,16},{16,8},{24,0},{1,25},{9,17},{17,9},{25,1},{2,26},{10... | collective-permute-start | bytes 12296 | tf_op jit(solution)/shard_map/ppermute | solution.py:39
  73.4 2.1 %collective-permute-start.20 = (f32[8,128]{1,0:T(8,128)S(1)}, f32[8,128]{1,0:T(8,128)S(1)}, u32[]{:S(2)}, u32[]{:S(2)}) collective-permute-start(f32[8,128]{1,0:T(8,128)S(1)} %get-tuple-element.32), channel_id=1, source_target_pairs={{0,8},{8,0},{16,24},{24,16},{1,9},{9,1},{17,25},{25,17},{2,10},{10... | collective-permute-start | bytes 12296 | tf_op jit(solution)/shard_map/ppermute | solution.py:39
  75.5 1.0 %collective-permute-done.22 = f32[8,128]{1,0:T(8,128)S(1)} collective-permute-done((f32[8,128]{1,0:T(8,128)S(1)}, f32[8,128]{1,0:T(8,128)S(1)}, u32[]{:S(2)}, u32[]{:S(2)}) %collective-permute-start.22) | collective-permute-done | bytes 4128 | tf_op jit(solution)/shard_map/ppermute | solution.py:39
  76.5 1.2 %collective-permute-done.21 = f32[8,128]{1,0:T(8,128)S(1)} collective-permute-done((f32[8,128]{1,0:T(8,128)S(1)}, f32[8,128]{1,0:T(8,128)S(1)}, u32[]{:S(2)}, u32[]{:S(2)}) %collective-permute-start.21) | collective-permute-done | bytes 4128 | tf_op jit(solution)/shard_map/ppermute | solution.py:39
  77.7 1.5 %collective-permute-start.25 = (f32[4,8,128]{2,1,0:T(8,128)S(1)}, f32[4,8,128]{2,1,0:T(8,128)S(1)}, u32[]{:S(2)}, u32[]{:S(2)}) collective-permute-start(f32[4,8,128]{2,1,0:T(8,128)S(1)} %pad_maximum_fusion.2), channel_id=1, source_target_pairs={{0,6},{2,4},{4,2},{6,0},{1,7},{3,5},{5,3},{7,1},{8,14},{10,12},{12... | collective-permute-start | bytes 49160 | tf_op jit(solution)/shard_map/ppermute | solution.py:43
  79.2 0.6 collective-permute-start.24
  79.9 1.4 %collective-permute-start.23 = (f32[4,8,128]{2,1,0:T(8,128)S(1)}, f32[4,8,128]{2,1,0:T(8,128)S(1)}, u32[]{:S(2)}, u32[]{:S(2)}) collective-permute-start(f32[4,8,128]{2,1,0:T(8,128)S(1)} %pad_maximum_fusion.2), channel_id=1, source_target_pairs={{0,2},{2,0},{4,6},{6,4},{1,3},{3,1},{5,7},{7,5},{8,10},{10,8},{12,... | collective-permute-start | bytes 49160 | tf_op jit(solution)/shard_map/ppermute | solution.py:43
  81.2 2.4 %collective-permute-done.23 = f32[4,8,128]{2,1,0:T(8,128)S(1)} collective-permute-done((f32[4,8,128]{2,1,0:T(8,128)S(1)}, f32[4,8,128]{2,1,0:T(8,128)S(1)}, u32[]{:S(2)}, u32[]{:S(2)}) %collective-permute-start.23) | collective-permute-done | bytes 16416 | tf_op jit(solution)/shard_map/ppermute | solution.py:43
  84.2 2.2 %final.1 = (f32[2,4,1024]{2,1,0:T(4,128)}, f32[1,4]{1,0:T(1,128)}) custom-call(f32[16,8,128]{2,1,0:T(8,128)} %copy-done.10, f32[3,8,1024]{2,1,0:T(8,128)} %copy-done.6), custom_call_target="tpu_custom_call" | custom-call | tf_op jit(solution)/shard_map/final/pallas_call | solution.py:434
  (57 shorter events, 4.7 us)
Async XLA Ops:
  0.6 23.4 %collective-permute-start.6 = (f32[32,128,128]{2,1,0:T(8,128)}, f32[32,128,128]{2,1,0:T(8,128)S(1)}, u32[]{:S(2)}, u32[]{:S(2)}) collective-permute-start(f32[32,128,128]{2,1,0:T(8,128)} %bitcast.23), channel_id=1, source_target_pairs={{0,1},{1,0},{2,3},{3,2},{4,5},{5,4},{6,7},{7,6},{8,9},{9,8},{10,11... | collective-permute-start | bytes 6291464 | tf_op jit(solution)/shard_map/ppermute | solution.py:460
  1.1 22.9 %collective-permute-start.7 = (f32[32,128,128]{2,1,0:T(8,128)}, f32[32,128,128]{2,1,0:T(8,128)}, u32[]{:S(2)}, u32[]{:S(2)}) collective-permute-start(f32[32,128,128]{2,1,0:T(8,128)} %bitcast.25), channel_id=1, source_target_pairs={{0,1},{1,0},{2,3},{3,2},{4,5},{5,4},{6,7},{7,6},{8,9},{9,8},{10,11... | collective-permute-start | bytes 6291464 | tf_op jit(solution)/shard_map/ppermute | solution.py:461
  1.2 13.3 %collective-permute-start = (f32[2,4,1024]{2,1,0:T(4,128)}, f32[2,4,1024]{2,1,0:T(4,128)S(1)}, u32[]{:S(2)}, u32[]{:S(2)}) collective-permute-start(f32[2,4,1024]{2,1,0:T(4,128)} %param.6), channel_id=1, source_target_pairs={{0,8},{8,0},{16,24},{24,16},{1,9},{9,1},{17,25},{25,17},{2,10},{10... | collective-permute-start | bytes 98312 | tf_op jit(solution)/shard_map/ppermute | solution.py:39
  4.2 10.3 %collective-permute-start.2 = (f32[2,4,1024]{2,1,0:T(4,128)}, f32[2,4,1024]{2,1,0:T(4,128)S(1)}, u32[]{:S(2)}, u32[]{:S(2)}) collective-permute-start(f32[2,4,1024]{2,1,0:T(4,128)} %param.6), channel_id=1, source_target_pairs={{0,24},{8,16},{16,8},{24,0},{1,25},{9,17},{17,9},{25,1},{2,26},{10... | collective-permute-start | bytes 98312 | tf_op jit(solution)/shard_map/ppermute | solution.py:39
  6.7 7.9 %collective-permute-start.1 = (f32[2,4,1024]{2,1,0:T(4,128)}, f32[2,4,1024]{2,1,0:T(4,128)S(1)}, u32[]{:S(2)}, u32[]{:S(2)}) collective-permute-start(f32[2,4,1024]{2,1,0:T(4,128)} %param.6), channel_id=1, source_target_pairs={{0,16},{8,24},{16,0},{24,8},{1,17},{9,25},{17,1},{25,9},{2,18},{10... | collective-permute-start | bytes 98312 | tf_op jit(solution)/shard_map/ppermute | solution.py:39
  7.6 1.6 %copy-start = (f32[8,4,128,128]{3,2,1,0:T(8,128)S(1)}, f32[8,4,128,128]{3,2,1,0:T(8,128)}, u32[]{:S(2)}) copy-start(f32[8,4,128,128]{3,2,1,0:T(8,128)} %param.7) | copy-start | bytes 6291460
  9.2 1.6 %copy-start.1 = (f32[8,4,128,128]{3,2,1,0:T(8,128)S(1)}, f32[8,4,128,128]{3,2,1,0:T(8,128)}, u32[]{:S(2)}) copy-start(f32[8,4,128,128]{3,2,1,0:T(8,128)} %param.8) | copy-start | bytes 6291460
  10.8 8.0 %copy-start.11 = (s32[8,8]{1,0:T(8,128)S(1)}, s32[8,8]{1,0:T(8,128)}, u32[]{:S(2)}) copy-start(s32[8,8]{1,0:T(8,128)} %param.9) | copy-start | bytes 772
  10.8 8.1 %copy-start.12 = (s32[8]{0:T(128)S(1)}, s32[8]{0:T(128)}, u32[]{:S(2)}) copy-start(s32[8]{0:T(128)} %param.10) | copy-start | bytes 100
  10.8 8.1 %copy-start.13 = (s32[4]{0:T(128)S(1)}, s32[4]{0:T(128)}, u32[]{:S(2)}) copy-start(s32[4]{0:T(128)} %param.11) | copy-start | bytes 52
  11.3 1.3 %copy-start.2 = (f32[32,128,128]{2,1,0:T(8,128)}, f32[32,128,128]{2,1,0:T(8,128)S(1)}, u32[]{:S(2)}) copy-start(f32[32,128,128]{2,1,0:T(8,128)S(1)} %get-tuple-element.23.refs_4_) | copy-start | bytes 6291460
  12.6 1.4 %copy-start.4 = (f32[32,128,128]{2,1,0:T(8,128)}, f32[32,128,128]{2,1,0:T(8,128)S(1)}, u32[]{:S(2)}) copy-start(f32[32,128,128]{2,1,0:T(8,128)S(1)} %get-tuple-element.24.refs_6_) | copy-start | bytes 6291460
  15.3 6.4 %collective-permute-start.5 = (f32[4,8,1024]{2,1,0:T(8,128)S(1)}, f32[4,8,1024]{2,1,0:T(8,128)S(1)}, u32[]{:S(2)}, u32[]{:S(2)}) collective-permute-start(f32[4,8,1024]{2,1,0:T(8,128)S(1)} %maximum_add_fusion.refs_0_), channel_id=1, source_target_pairs={{0,6},{2,4},{4,2},{6,0},{1,7},{3,5},{5,3},{7,1},{8,14},{10,12},{12... | collective-permute-start | bytes 393224 | tf_op jit(solution)/shard_map/ppermute | solution.py:43
  17.8 6.2 %collective-permute-start.4 = (f32[4,8,1024]{2,1,0:T(8,128)S(1)}, f32[4,8,1024]{2,1,0:T(8,128)S(1)}, u32[]{:S(2)}, u32[]{:S(2)}) collective-permute-start(f32[4,8,1024]{2,1,0:T(8,128)S(1)} %maximum_add_fusion.refs_0_), channel_id=1, source_target_pairs={{0,4},{2,6},{4,0},{6,2},{1,5},{3,7},{5,1},{7,3},{8,12},{10,14},{12... | collective-permute-start | bytes 393224 | tf_op jit(solution)/shard_map/ppermute | solution.py:43
  18.3 5.8 %collective-permute-start.3 = (f32[4,8,1024]{2,1,0:T(8,128)S(1)}, f32[4,8,1024]{2,1,0:T(8,128)S(1)}, u32[]{:S(2)}, u32[]{:S(2)}) collective-permute-start(f32[4,8,1024]{2,1,0:T(8,128)S(1)} %maximum_add_fusion.refs_0_), channel_id=1, source_target_pairs={{0,2},{2,0},{4,6},{6,4},{1,3},{3,1},{5,7},{7,5},{8,10},{10,8},{12,... | collective-permute-start | bytes 393224 | tf_op jit(solution)/shard_map/ppermute | solution.py:43
  24.1 1.6 %copy-start.3 = (f32[32,128,128]{2,1,0:T(8,128)S(1)}, f32[32,128,128]{2,1,0:T(8,128)}, u32[]{:S(2)}) copy-start(f32[32,128,128]{2,1,0:T(8,128)} %copy-done.2) | copy-start | bytes 6291460
  25.7 1.6 %copy-start.5 = (f32[32,128,128]{2,1,0:T(8,128)S(1)}, f32[32,128,128]{2,1,0:T(8,128)}, u32[]{:S(2)}) copy-start(f32[32,128,128]{2,1,0:T(8,128)} %copy-done.4) | copy-start | bytes 6291460
  27.2 0.7 copy-start.7
  27.9 0.7 copy-start.8
  28.6 0.7 copy-start.9
  32.8 5.8 %collective-permute-start.10 = (f32[8,1024]{1,0:T(8,128)S(1)}, f32[8,1024]{1,0:T(8,128)S(1)}, u32[]{:S(2)}, u32[]{:S(2)}) collective-permute-start(f32[8,1024]{1,0:T(8,128)S(1)} %get-tuple-element.26), channel_id=1, source_target_pairs={{0,24},{8,16},{16,8},{24,0},{1,25},{9,17},{17,9},{25,1},{2,26},{10... | collective-permute-start | bytes 98312 | tf_op jit(solution)/shard_map/ppermute | solution.py:39
  35.6 4.8 %collective-permute-start.9 = (f32[8,1024]{1,0:T(8,128)S(1)}, f32[8,1024]{1,0:T(8,128)S(1)}, u32[]{:S(2)}, u32[]{:S(2)}) collective-permute-start(f32[8,1024]{1,0:T(8,128)S(1)} %get-tuple-element.26), channel_id=1, source_target_pairs={{0,16},{8,24},{16,0},{24,8},{1,17},{9,25},{17,1},{25,9},{2,18},{10... | collective-permute-start | bytes 98312 | tf_op jit(solution)/shard_map/ppermute | solution.py:39
  35.6 4.8 %collective-permute-start.8 = (f32[8,1024]{1,0:T(8,128)S(1)}, f32[8,1024]{1,0:T(8,128)S(1)}, u32[]{:S(2)}, u32[]{:S(2)}) collective-permute-start(f32[8,1024]{1,0:T(8,128)S(1)} %get-tuple-element.26), channel_id=1, source_target_pairs={{0,8},{8,0},{16,24},{24,16},{1,9},{9,1},{17,25},{25,17},{2,10},{10... | collective-permute-start | bytes 98312 | tf_op jit(solution)/shard_map/ppermute | solution.py:39
  40.4 6.6 %collective-permute-start.13 = (f32[4,8,1024]{2,1,0:T(8,128)S(1)}, f32[4,8,1024]{2,1,0:T(8,128)S(1)}, u32[]{:S(2)}, u32[]{:S(2)}) collective-permute-start(f32[4,8,1024]{2,1,0:T(8,128)S(1)} %pad_maximum_fusion.refs_0_), channel_id=1, source_target_pairs={{0,6},{2,4},{4,2},{6,0},{1,7},{3,5},{5,3},{7,1},{8,14},{10,12},{12... | collective-permute-start | bytes 393224 | tf_op jit(solution)/shard_map/ppermute | solution.py:43
  41.9 6.4 %collective-permute-start.12 = (f32[4,8,1024]{2,1,0:T(8,128)S(1)}, f32[4,8,1024]{2,1,0:T(8,128)S(1)}, u32[]{:S(2)}, u32[]{:S(2)}) collective-permute-start(f32[4,8,1024]{2,1,0:T(8,128)S(1)} %pad_maximum_fusion.refs_0_), channel_id=1, source_target_pairs={{0,4},{2,6},{4,0},{6,2},{1,5},{3,7},{5,1},{7,3},{8,12},{10,14},{12... | collective-permute-start | bytes 393224 | tf_op jit(solution)/shard_map/ppermute | solution.py:43
  43.3 5.2 %collective-permute-start.11 = (f32[4,8,1024]{2,1,0:T(8,128)S(1)}, f32[4,8,1024]{2,1,0:T(8,128)S(1)}, u32[]{:S(2)}, u32[]{:S(2)}) collective-permute-start(f32[4,8,1024]{2,1,0:T(8,128)S(1)} %pad_maximum_fusion.refs_0_), channel_id=1, source_target_pairs={{0,2},{2,0},{4,6},{6,4},{1,3},{3,1},{5,7},{7,5},{8,10},{10,8},{12,... | collective-permute-start | bytes 393224 | tf_op jit(solution)/shard_map/ppermute | solution.py:43
  51.6 5.9 %collective-permute-start.16 = (f32[8,1024]{1,0:T(8,128)S(1)}, f32[8,1024]{1,0:T(8,128)S(1)}, u32[]{:S(2)}, u32[]{:S(2)}) collective-permute-start(f32[8,1024]{1,0:T(8,128)S(1)} %get-tuple-element.30), channel_id=1, source_target_pairs={{0,24},{8,16},{16,8},{24,0},{1,25},{9,17},{17,9},{25,1},{2,26},{10... | collective-permute-start | bytes 98312 | tf_op jit(solution)/shard_map/ppermute | solution.py:39
  55.0 4.8 %collective-permute-start.15 = (f32[8,1024]{1,0:T(8,128)S(1)}, f32[8,1024]{1,0:T(8,128)S(1)}, u32[]{:S(2)}, u32[]{:S(2)}) collective-permute-start(f32[8,1024]{1,0:T(8,128)S(1)} %get-tuple-element.30), channel_id=1, source_target_pairs={{0,16},{8,24},{16,0},{24,8},{1,17},{9,25},{17,1},{25,9},{2,18},{10... | collective-permute-start | bytes 98312 | tf_op jit(solution)/shard_map/ppermute | solution.py:39
  55.0 4.8 %collective-permute-start.14 = (f32[8,1024]{1,0:T(8,128)S(1)}, f32[8,1024]{1,0:T(8,128)S(1)}, u32[]{:S(2)}, u32[]{:S(2)}) collective-permute-start(f32[8,1024]{1,0:T(8,128)S(1)} %get-tuple-element.30), channel_id=1, source_target_pairs={{0,8},{8,0},{16,24},{24,16},{1,9},{9,1},{17,25},{25,17},{2,10},{10... | collective-permute-start | bytes 98312 | tf_op jit(solution)/shard_map/ppermute | solution.py:39
  59.8 6.0 %collective-permute-start.19 = (f32[4,8,1024]{2,1,0:T(8,128)S(1)}, f32[4,8,1024]{2,1,0:T(8,128)S(1)}, u32[]{:S(2)}, u32[]{:S(2)}) collective-permute-start(f32[4,8,1024]{2,1,0:T(8,128)S(1)} %pad_maximum_fusion.1.refs_0_), channel_id=1, source_target_pairs={{0,6},{2,4},{4,2},{6,0},{1,7},{3,5},{5,3},{7,1},{8,14},{10,12},{12... | collective-permute-start | bytes 393224 | tf_op jit(solution)/shard_map/ppermute | solution.py:43
  60.7 6.4 %collective-permute-start.18 = (f32[4,8,1024]{2,1,0:T(8,128)S(1)}, f32[4,8,1024]{2,1,0:T(8,128)S(1)}, u32[]{:S(2)}, u32[]{:S(2)}) collective-permute-start(f32[4,8,1024]{2,1,0:T(8,128)S(1)} %pad_maximum_fusion.1.refs_0_), channel_id=1, source_target_pairs={{0,4},{2,6},{4,0},{6,2},{1,5},{3,7},{5,1},{7,3},{8,12},{10,14},{12... | collective-permute-start | bytes 393224 | tf_op jit(solution)/shard_map/ppermute | solution.py:43
  62.0 5.0 %collective-permute-start.17 = (f32[4,8,1024]{2,1,0:T(8,128)S(1)}, f32[4,8,1024]{2,1,0:T(8,128)S(1)}, u32[]{:S(2)}, u32[]{:S(2)}) collective-permute-start(f32[4,8,1024]{2,1,0:T(8,128)S(1)} %pad_maximum_fusion.1.refs_0_), channel_id=1, source_target_pairs={{0,2},{2,0},{4,6},{6,4},{1,3},{3,1},{5,7},{7,5},{8,10},{10,8},{12,... | collective-permute-start | bytes 393224 | tf_op jit(solution)/shard_map/ppermute | solution.py:43
  70.5 0.6 copy-start.6
  71.1 5.4 %collective-permute-start.22 = (f32[8,128]{1,0:T(8,128)S(1)}, f32[8,128]{1,0:T(8,128)S(1)}, u32[]{:S(2)}, u32[]{:S(2)}) collective-permute-start(f32[8,128]{1,0:T(8,128)S(1)} %get-tuple-element.32), channel_id=1, source_target_pairs={{0,24},{8,16},{16,8},{24,0},{1,25},{9,17},{17,9},{25,1},{2,26},{10... | collective-permute-start | bytes 12296 | tf_op jit(solution)/shard_map/ppermute | solution.py:39
  73.2 4.5 %collective-permute-start.21 = (f32[8,128]{1,0:T(8,128)S(1)}, f32[8,128]{1,0:T(8,128)S(1)}, u32[]{:S(2)}, u32[]{:S(2)}) collective-permute-start(f32[8,128]{1,0:T(8,128)S(1)} %get-tuple-element.32), channel_id=1, source_target_pairs={{0,16},{8,24},{16,0},{24,8},{1,17},{9,25},{17,1},{25,9},{2,18},{10... | collective-permute-start | bytes 12296 | tf_op jit(solution)/shard_map/ppermute | solution.py:39
  73.4 4.3 %collective-permute-start.20 = (f32[8,128]{1,0:T(8,128)S(1)}, f32[8,128]{1,0:T(8,128)S(1)}, u32[]{:S(2)}, u32[]{:S(2)}) collective-permute-start(f32[8,128]{1,0:T(8,128)S(1)} %get-tuple-element.32), channel_id=1, source_target_pairs={{0,8},{8,0},{16,24},{24,16},{1,9},{9,1},{17,25},{25,17},{2,10},{10... | collective-permute-start | bytes 12296 | tf_op jit(solution)/shard_map/ppermute | solution.py:39
  77.7 5.9 %collective-permute-start.25 = (f32[4,8,128]{2,1,0:T(8,128)S(1)}, f32[4,8,128]{2,1,0:T(8,128)S(1)}, u32[]{:S(2)}, u32[]{:S(2)}) collective-permute-start(f32[4,8,128]{2,1,0:T(8,128)S(1)} %pad_maximum_fusion.2), channel_id=1, source_target_pairs={{0,6},{2,4},{4,2},{6,0},{1,7},{3,5},{5,3},{7,1},{8,14},{10,12},{12... | collective-permute-start | bytes 49160 | tf_op jit(solution)/shard_map/ppermute | solution.py:43
  79.2 4.4 %collective-permute-start.24 = (f32[4,8,128]{2,1,0:T(8,128)S(1)}, f32[4,8,128]{2,1,0:T(8,128)S(1)}, u32[]{:S(2)}, u32[]{:S(2)}) collective-permute-start(f32[4,8,128]{2,1,0:T(8,128)S(1)} %pad_maximum_fusion.2), channel_id=1, source_target_pairs={{0,4},{2,6},{4,0},{6,2},{1,5},{3,7},{5,1},{7,3},{8,12},{10,14},{12... | collective-permute-start | bytes 49160 | tf_op jit(solution)/shard_map/ppermute | solution.py:43
  79.9 3.7 %collective-permute-start.23 = (f32[4,8,128]{2,1,0:T(8,128)S(1)}, f32[4,8,128]{2,1,0:T(8,128)S(1)}, u32[]{:S(2)}, u32[]{:S(2)}) collective-permute-start(f32[4,8,128]{2,1,0:T(8,128)S(1)} %pad_maximum_fusion.2), channel_id=1, source_target_pairs={{0,2},{2,0},{4,6},{6,4},{1,3},{3,1},{5,7},{7,5},{8,10},{10,8},{12,... | collective-permute-start | bytes 49160 | tf_op jit(solution)/shard_map/ppermute | solution.py:43
  83.6 0.6 copy-start.10

commit v14 on v12

--- a/solution.py
+++ b/solution.py
@@ -46,7 +46,6 @@
     items_ref, places_ref, turn_ref, g_out_ref, c_out_ref, sems,
 ):
     row_blocks, slots = places_ref.shape
-    pattern_at = 3 + row_blocks + turn_ref.shape[0] // 2
     own_slots = slots // freqs
     pieces = sems.shape[1]
     part = g_ref.shape[0] // pieces
@@ -58,7 +57,7 @@
             copies[-1].start()
 
     order = lax.broadcasted_iota(jnp.int32, (8, LANES), 1)
-    freq = scalars_ref[2]
+    freq = scalars_ref[row_blocks, 2]
     for table, d in enumerate(list(range(freqs)) + [None]):
         first = 0 if d is None else lax.rem(freq + (freqs - d), freqs) * own_slots
         group = FULL_GROUP if d is None else GROUP
@@ -67,7 +66,7 @@
         home = jnp.zeros((8, LANES), jnp.int32)
         used = jnp.int32(0)
         for b in range(row_blocks):
-            here = scalars_ref[3 + b] if d is None else jnp.clip(scalars_ref[3 + b] - first, 0, own_slots)
+            here = scalars_ref[row_blocks, 3 + b] if d is None else jnp.clip(scalars_ref[row_blocks, 3 + b] - first, 0, own_slots)
             inside = order - used
             hit = (inside >= 0) & (inside < here)
             layer = jnp.where(hit, first + inside, layer)
@@ -85,21 +84,21 @@
     k_at = lax.broadcasted_iota(jnp.int32, places_ref.shape, 1)
     pattern = jnp.zeros(places_ref.shape, jnp.int32)
     for i in range(row_blocks * slots):
-        pattern = jnp.where(b_at * slots + k_at == i, scalars_ref[pattern_at + i], pattern)
+        pattern = jnp.where(b_at * slots + k_at == i, scalars_ref[i // slots, i % slots], pattern)
     owner = lax.div(pattern, row_blocks)
-    far = distance(scalars_ref[0], lax.div(owner, plane), line)
-    place = distance(scalars_ref[1], lax.rem(owner, plane), plane) * line + far
+    far = distance(scalars_ref[row_blocks, 0], lax.div(owner, plane), line)
+    place = distance(scalars_ref[row_blocks, 1], lax.rem(owner, plane), plane) * line + far
     place = place * row_blocks + lax.rem(pattern, row_blocks)
     count = jnp.zeros(pattern.shape, jnp.int32)
     for b in range(row_blocks):
-        count = jnp.where(b_at == b, scalars_ref[3 + b], count)
+        count = jnp.where(b_at == b, scalars_ref[row_blocks, 3 + b], count)
     places_ref[...] = jnp.where(k_at < count, place, line * plane * row_blocks)
 
     half = turn_ref.shape[0] // 2
     row_at = lax.broadcasted_iota(jnp.int32, turn_ref.shape, 0)
     ids = jnp.zeros(turn_ref.shape, jnp.int32)
     for f in range(half):
-        ids = jnp.where(lax.rem(row_at, half) == f, scalars_ref[3 + row_blocks + f], ids)
+        ids = jnp.where(lax.rem(row_at, half) == f, scalars_ref[row_blocks, 3 + row_blocks + f], ids)
     angular = 0.2 * jnp.exp(ids.astype(jnp.float32) * (math.log(8.0) / 1000.0))
     turn_ref[...] = jnp.where(row_at < half, -angular, angular)
     for copy in copies:
@@ -441,7 +440,13 @@
         freq_count = excitation.shape[1]
         parts = 2 * freq_count
         where = jnp.stack([lax.axis_index(name) for name in ("line", "place", "freq")])
-        scalars = jnp.concatenate([where, counts, freq_ids, pattern.reshape(-1)]).astype(jnp.int32)
+        last_row = jnp.concatenate([where, counts, freq_ids])
+        scalars = jnp.concatenate(
+            [
+                jnp.pad(pattern, ((0, 0), (0, LANES - pattern.shape[1]))),
+                jnp.pad(last_row, (0, LANES - last_row.size))[None],
+            ]
+        ).astype(jnp.int32)
         stored = (row_blocks * own_slots, size, size)
         g_own, c_own = g_blocks.reshape(stored), c_blocks.reshape(stored)
         *lists, turn, g_near, c_near = run_setup(

time: 77.4 us -> 77.3 us (level)
    ppermute x12, waiting for transfers between devices: 10.9 us -> 9.42 us  [gather_rows(): lax.ppermute(rows, 'line', perm)]
    ppermute x12, waiting for transfers between devices: 11.5 us -> 12.6 us  [gather_rows(): lax.ppermute(whole_line, 'place', perm)]
  transfers between devices with their start and end apart: 26 -> 26, of which waited for: 17 -> 17; matrix products, arithmetic and copies ran while one was open for 3% -> 3% of each run, Pallas kernels for 1% -> 2%
where the time goes in v14:
time: 77.3 us
  starting transfers between devices  33.6 us (43%)
  waiting for transfers between devices  22 us (28%)
  Pallas kernels  14.1 us (18%)
  local copies, waits for them, and re-layouts  6.06 us (8%)
  between operations  0.82 us (1%)
    ppermute x12, starting transfers between devices, gather_rows(): lax.ppermute(rows, 'line', perm)  18.9 us
    ppermute x12, starting transfers between devices, gather_rows(): lax.ppermute(whole_line, 'place', perm)  14.1 us
    ppermute x12, waiting for transfers between devices, gather_rows(): lax.ppermute(whole_line, 'place', perm)  12.6 us
    pallas_call x3, Pallas kernels, run_step(): pl.pallas_call(functools.partial(step_kernel, step, plane, line, freqs),...  10.7 us
    ppermute x12, waiting for transfers between devices, gather_rows(): lax.ppermute(rows, 'line', perm)  9.42 us
    unnamed x17, local copies, waits for them, and re-layouts  4.45 us
    pallas_call x1, Pallas kernels, run_final(): pl.pallas_call(final_kernel, in_specs=[vmem] * 2, out_specs=[vmem] * 2, o...  2.17 us
  transfers between devices with their start and end apart: 26, of which 17 were waited for; matrix products, arithmetic and copies ran while one was open for 3% of the time, Pallas kernels for 2%

profile of v14, /device:TPU:0, one launch (start us, length us, event | category | flops | bytes accessed | tf_op | source)
XLA Modules:
  0.0 77.3 jit_solution(8121077655852723937)
XLA Ops:
  0.6 0.5 collective-permute-start.6
  1.2 3.0 %collective-permute-start = (f32[2,4,1024]{2,1,0:T(4,128)}, f32[2,4,1024]{2,1,0:T(4,128)S(1)}, u32[]{:S(2)}, u32[]{:S(2)}) collective-permute-start(f32[2,4,1024]{2,1,0:T(4,128)} %param.6), channel_id=1, source_target_pairs={{0,8},{8,0},{16,24},{24,16},{1,9},{9,1},{17,25},{25,17},{2,10},{10... | collective-permute-start | bytes 98312 | tf_op jit(solution)/shard_map/ppermute | solution.py:39
  4.2 2.5 %collective-permute-start.2 = (f32[2,4,1024]{2,1,0:T(4,128)}, f32[2,4,1024]{2,1,0:T(4,128)S(1)}, u32[]{:S(2)}, u32[]{:S(2)}) collective-permute-start(f32[2,4,1024]{2,1,0:T(4,128)} %param.6), channel_id=1, source_target_pairs={{0,24},{8,16},{16,8},{24,0},{1,25},{9,17},{17,9},{25,1},{2,26},{10... | collective-permute-start | bytes 98312 | tf_op jit(solution)/shard_map/ppermute | solution.py:39
  6.8 0.8 %stack.72 = f32[1,8,1024]{2,1,0:T(8,128)S(1)} reshape(f32[2,4,1024]{2,1,0:T(4,128)} %param.6) | data formatting | bytes 65536 | tf_op jit(solution)/shard_map/stack | solution.py:40
  7.6 0.7 concatenate.11
  8.4 1.9 %collective-permute-done.2 = f32[2,4,1024]{2,1,0:T(4,128)S(1)} collective-permute-done((f32[2,4,1024]{2,1,0:T(4,128)}, f32[2,4,1024]{2,1,0:T(4,128)S(1)}, u32[]{:S(2)}, u32[]{:S(2)}) %collective-permute-start.2) | collective-permute-done | bytes 32800 | tf_op jit(solution)/shard_map/ppermute | solution.py:39
  10.3 1.8 %collective-permute-done.1 = f32[2,4,1024]{2,1,0:T(4,128)S(1)} collective-permute-done((f32[2,4,1024]{2,1,0:T(4,128)}, f32[2,4,1024]{2,1,0:T(4,128)S(1)}, u32[]{:S(2)}, u32[]{:S(2)}) %collective-permute-start.1) | collective-permute-done | bytes 32800 | tf_op jit(solution)/shard_map/ppermute | solution.py:39
  12.1 2.5 %collective-permute-start.5 = (f32[4,8,1024]{2,1,0:T(8,128)S(1)}, f32[4,8,1024]{2,1,0:T(8,128)S(1)}, u32[]{:S(2)}, u32[]{:S(2)}) collective-permute-start(f32[4,8,1024]{2,1,0:T(8,128)S(1)} %constant_dynamic-update-slice_fusion.refs_0_), channel_id=1, source_target_pairs={{0,6},{2,4},{4,2},{6,0},{1,7},{3,5},{5,3},{7,1},{8,14},{10,12},{12... | collective-permute-start | bytes 393224 | tf_op jit(solution)/shard_map/ppermute | solution.py:41
  14.6 0.5 collective-permute-start.4
  15.2 0.5 collective-permute-start.3
  15.7 0.7 pad_add_fusion.scalars_ref
  16.4 1.6 %copy-done = f32[8,4,128,128]{3,2,1,0:T(8,128)S(1)} copy-done((f32[8,4,128,128]{3,2,1,0:T(8,128)S(1)}, f32[8,4,128,128]{3,2,1,0:T(8,128)}, u32[]{:S(2)}) %copy-start) | copy-done | bytes 2097176
  18.0 1.6 %copy-done.1 = f32[8,4,128,128]{3,2,1,0:T(8,128)S(1)} copy-done((f32[8,4,128,128]{3,2,1,0:T(8,128)S(1)}, f32[8,4,128,128]{3,2,1,0:T(8,128)}, u32[]{:S(2)}) %copy-start.1) | copy-done | bytes 2097176
  19.6 1.2 %setup.1 = (s32[12,128]{1,0:T(8,128)S(1)}, s32[8,8]{1,0:T(8,128)S(1)}, f32[8,128]{1,0:T(8,128)S(1)}, f32[32,128,128]{2,1,0:T(8,128)S(1)}, f32[32,128,128]{2,1,0:T(8,128)S(1)}) custom-call(s32[9,128]{1,0:T(8,128)S(1)} %pad_add_fusion.scalars_ref, f32[32,128,128]{2,1,0:T(8,128)S(1)} %bitcast.25, f32[32,128,128]{2,1,0:T(8,128)S(1)} %bitcast.27), custom_call_target="tpu_custom_call" | custom-call | bytes 8388608 | tf_op jit(solution)/shard_map/setup/pallas_call | solution.py:113
  20.9 3.7 %step_0.1 = (f32[129,8,128]{2,1,0:T(8,128)S(1)}, f32[8,1024]{1,0:T(8,128)S(1)}, f32[8,128]{1,0:T(8,128)S(1)}, bf16[64,256,256]{2,1,0:T(8,128)(2,1)S(1)}) custom-call(s32[12,128]{1,0:T(8,128)S(1)} %get-tuple-element.18.items_ref, s32[8,8]{1,0:T(8,128)S(1)} %get-tuple-element.19.places_ref, f32[8,128]{1,0:T(8,128)S(1)} %get-tuple-element.20.turn_ref, ...), custom_call_target="tpu_custom_call" | custom-call | tf_op jit(solution)/shard_map/step_0/pallas_call | solution.py:344
  24.5 0.9 %collective-permute-start.10 = (f32[8,1024]{1,0:T(8,128)S(1)}, f32[8,1024]{1,0:T(8,128)S(1)}, u32[]{:S(2)}, u32[]{:S(2)}) collective-permute-start(f32[8,1024]{1,0:T(8,128)S(1)} %get-tuple-element.24), channel_id=1, source_target_pairs={{0,24},{8,16},{16,8},{24,0},{1,25},{9,17},{17,9},{25,1},{2,26},{10... | collective-permute-start | bytes 98312 | tf_op jit(solution)/shard_map/ppermute | solution.py:39
  25.4 1.1 %collective-permute-start.9 = (f32[8,1024]{1,0:T(8,128)S(1)}, f32[8,1024]{1,0:T(8,128)S(1)}, u32[]{:S(2)}, u32[]{:S(2)}) collective-permute-start(f32[8,1024]{1,0:T(8,128)S(1)} %get-tuple-element.24), channel_id=1, source_target_pairs={{0,16},{8,24},{16,0},{24,8},{1,17},{9,25},{17,1},{25,9},{2,18},{10... | collective-permute-start | bytes 98312 | tf_op jit(solution)/shard_map/ppermute | solution.py:39
  26.5 2.5 %collective-permute-start.8 = (f32[8,1024]{1,0:T(8,128)S(1)}, f32[8,1024]{1,0:T(8,128)S(1)}, u32[]{:S(2)}, u32[]{:S(2)}) collective-permute-start(f32[8,1024]{1,0:T(8,128)S(1)} %get-tuple-element.24), channel_id=1, source_target_pairs={{0,8},{8,0},{16,24},{24,16},{1,9},{9,1},{17,25},{25,17},{2,10},{10... | collective-permute-start | bytes 98312 | tf_op jit(solution)/shard_map/ppermute | solution.py:39
  29.0 1.4 %collective-permute-done.10 = f32[8,1024]{1,0:T(8,128)S(1)} collective-permute-done((f32[8,1024]{1,0:T(8,128)S(1)}, f32[8,1024]{1,0:T(8,128)S(1)}, u32[]{:S(2)}, u32[]{:S(2)}) %collective-permute-start.10) | collective-permute-done | bytes 32800 | tf_op jit(solution)/shard_map/ppermute | solution.py:39
  31.0 2.8 %collective-permute-start.13 = (f32[4,8,1024]{2,1,0:T(8,128)S(1)}, f32[4,8,1024]{2,1,0:T(8,128)S(1)}, u32[]{:S(2)}, u32[]{:S(2)}) collective-permute-start(f32[4,8,1024]{2,1,0:T(8,128)S(1)} %pad_maximum_fusion.refs_0_), channel_id=1, source_target_pairs={{0,6},{2,4},{4,2},{6,0},{1,7},{3,5},{5,3},{7,1},{8,14},{10,12},{12... | collective-permute-start | bytes 393224 | tf_op jit(solution)/shard_map/ppermute | solution.py:41
  34.1 0.5 collective-permute-start.11
  34.5 3.4 %collective-permute-done.13.refs_3_ = f32[4,8,1024]{2,1,0:T(8,128)S(1)} collective-permute-done((f32[4,8,1024]{2,1,0:T(8,128)S(1)}, f32[4,8,1024]{2,1,0:T(8,128)S(1)}, u32[]{:S(2)}, u32[]{:S(2)}) %collective-permute-start.13) | collective-permute-done | bytes 131104 | tf_op jit(solution)/shard_map/ppermute | solution.py:41
  38.0 1.2 %collective-permute-done.12.refs_2_ = f32[4,8,1024]{2,1,0:T(8,128)S(1)} collective-permute-done((f32[4,8,1024]{2,1,0:T(8,128)S(1)}, f32[4,8,1024]{2,1,0:T(8,128)S(1)}, u32[]{:S(2)}, u32[]{:S(2)}) %collective-permute-start.12) | collective-permute-done | bytes 131104 | tf_op jit(solution)/shard_map/ppermute | solution.py:41
  39.6 3.3 %step_1.1 = (f32[129,8,128]{2,1,0:T(8,128)S(1)}, f32[8,1024]{1,0:T(8,128)S(1)}, f32[8,128]{1,0:T(8,128)S(1)}) custom-call(s32[12,128]{1,0:T(8,128)S(1)} %get-tuple-element.18.items_ref, s32[8,8]{1,0:T(8,128)S(1)} %get-tuple-element.19.places_ref, f32[8,128]{1,0:T(8,128)S(1)} %get-tuple-element.20.turn_ref, f32[8,128]{1,0:T(8,128)S(1)} %get-tuple-element.23.info_in_ref, ...), custom_call_target="tpu_custom_call" | custom-call | tf_op jit(solution)/shard_map/step_1/pallas_call | solution.py:344
  42.9 0.8 %collective-permute-start.16 = (f32[8,1024]{1,0:T(8,128)S(1)}, f32[8,1024]{1,0:T(8,128)S(1)}, u32[]{:S(2)}, u32[]{:S(2)}) collective-permute-start(f32[8,1024]{1,0:T(8,128)S(1)} %get-tuple-element.28), channel_id=1, source_target_pairs={{0,24},{8,16},{16,8},{24,0},{1,25},{9,17},{17,9},{25,1},{2,26},{10... | collective-permute-start | bytes 98312 | tf_op jit(solution)/shard_map/ppermute | solution.py:39
  43.7 1.6 %collective-permute-start.15 = (f32[8,1024]{1,0:T(8,128)S(1)}, f32[8,1024]{1,0:T(8,128)S(1)}, u32[]{:S(2)}, u32[]{:S(2)}) collective-permute-start(f32[8,1024]{1,0:T(8,128)S(1)} %get-tuple-element.28), channel_id=1, source_target_pairs={{0,16},{8,24},{16,0},{24,8},{1,17},{9,25},{17,1},{25,9},{2,18},{10... | collective-permute-start | bytes 98312 | tf_op jit(solution)/shard_map/ppermute | solution.py:39
  45.3 2.1 %collective-permute-start.14 = (f32[8,1024]{1,0:T(8,128)S(1)}, f32[8,1024]{1,0:T(8,128)S(1)}, u32[]{:S(2)}, u32[]{:S(2)}) collective-permute-start(f32[8,1024]{1,0:T(8,128)S(1)} %get-tuple-element.28), channel_id=1, source_target_pairs={{0,8},{8,0},{16,24},{24,16},{1,9},{9,1},{17,25},{25,17},{2,10},{10... | collective-permute-start | bytes 98312 | tf_op jit(solution)/shard_map/ppermute | solution.py:39
  47.4 1.4 %collective-permute-done.16 = f32[8,1024]{1,0:T(8,128)S(1)} collective-permute-done((f32[8,1024]{1,0:T(8,128)S(1)}, f32[8,1024]{1,0:T(8,128)S(1)}, u32[]{:S(2)}, u32[]{:S(2)}) %collective-permute-start.16) | collective-permute-done | bytes 32800 | tf_op jit(solution)/shard_map/ppermute | solution.py:39
  48.8 0.5 collective-permute-done.15
  49.4 1.8 %collective-permute-start.19 = (f32[4,8,1024]{2,1,0:T(8,128)S(1)}, f32[4,8,1024]{2,1,0:T(8,128)S(1)}, u32[]{:S(2)}, u32[]{:S(2)}) collective-permute-start(f32[4,8,1024]{2,1,0:T(8,128)S(1)} %pad_maximum_fusion.1.refs_0_), channel_id=1, source_target_pairs={{0,6},{2,4},{4,2},{6,0},{1,7},{3,5},{5,3},{7,1},{8,14},{10,12},{12... | collective-permute-start | bytes 393224 | tf_op jit(solution)/shard_map/ppermute | solution.py:41
  51.2 1.0 %collective-permute-start.18 = (f32[4,8,1024]{2,1,0:T(8,128)S(1)}, f32[4,8,1024]{2,1,0:T(8,128)S(1)}, u32[]{:S(2)}, u32[]{:S(2)}) collective-permute-start(f32[4,8,1024]{2,1,0:T(8,128)S(1)} %pad_maximum_fusion.1.refs_0_), channel_id=1, source_target_pairs={{0,4},{2,6},{4,0},{6,2},{1,5},{3,7},{5,1},{7,3},{8,12},{10,14},{12... | collective-permute-start | bytes 393224 | tf_op jit(solution)/shard_map/ppermute | solution.py:41
  52.1 0.8 %collective-permute-start.17 = (f32[4,8,1024]{2,1,0:T(8,128)S(1)}, f32[4,8,1024]{2,1,0:T(8,128)S(1)}, u32[]{:S(2)}, u32[]{:S(2)}) collective-permute-start(f32[4,8,1024]{2,1,0:T(8,128)S(1)} %pad_maximum_fusion.1.refs_0_), channel_id=1, source_target_pairs={{0,2},{2,0},{4,6},{6,4},{1,3},{3,1},{5,7},{7,5},{8,10},{10,8},{12,... | collective-permute-start | bytes 393224 | tf_op jit(solution)/shard_map/ppermute | solution.py:41
  52.9 2.4 %collective-permute-done.19.refs_3_ = f32[4,8,1024]{2,1,0:T(8,128)S(1)} collective-permute-done((f32[4,8,1024]{2,1,0:T(8,128)S(1)}, f32[4,8,1024]{2,1,0:T(8,128)S(1)}, u32[]{:S(2)}, u32[]{:S(2)}) %collective-permute-start.19) | collective-permute-done | bytes 131104 | tf_op jit(solution)/shard_map/ppermute | solution.py:41
  55.3 1.3 %collective-permute-done.18.refs_2_ = f32[4,8,1024]{2,1,0:T(8,128)S(1)} collective-permute-done((f32[4,8,1024]{2,1,0:T(8,128)S(1)}, f32[4,8,1024]{2,1,0:T(8,128)S(1)}, u32[]{:S(2)}, u32[]{:S(2)}) %collective-permute-start.18) | collective-permute-done | bytes 131104 | tf_op jit(solution)/shard_map/ppermute | solution.py:41
  56.7 0.5 collective-permute-done.17.refs_1_
  57.2 3.7 %step_2.1 = (f32[3,8,1024]{2,1,0:T(8,128)S(1)}, f32[8,128]{1,0:T(8,128)S(1)}) custom-call(s32[12,128]{1,0:T(8,128)S(1)} %get-tuple-element.18.items_ref, s32[8,8]{1,0:T(8,128)S(1)} %get-tuple-element.19.places_ref, f32[8,128]{1,0:T(8,128)S(1)} %get-tuple-element.20.turn_ref, f32[8,128]{1,0:T(8,128)S(1)} %get-tuple-element.27.info_in_ref, ...), custom_call_target="tpu_custom_call" | custom-call | tf_op jit(solution)/shard_map/step_2/pallas_call | solution.py:344
  60.9 0.6 copy-done.2
  61.6 1.1 %collective-permute-start.22 = (f32[8,128]{1,0:T(8,128)S(1)}, f32[8,128]{1,0:T(8,128)S(1)}, u32[]{:S(2)}, u32[]{:S(2)}) collective-permute-start(f32[8,128]{1,0:T(8,128)S(1)} %get-tuple-element.30), channel_id=1, source_target_pairs={{0,24},{8,16},{16,8},{24,0},{1,25},{9,17},{17,9},{25,1},{2,26},{10... | collective-permute-start | bytes 12296 | tf_op jit(solution)/shard_map/ppermute | solution.py:39
  62.6 1.5 %collective-permute-start.21 = (f32[8,128]{1,0:T(8,128)S(1)}, f32[8,128]{1,0:T(8,128)S(1)}, u32[]{:S(2)}, u32[]{:S(2)}) collective-permute-start(f32[8,128]{1,0:T(8,128)S(1)} %get-tuple-element.30), channel_id=1, source_target_pairs={{0,16},{8,24},{16,0},{24,8},{1,17},{9,25},{17,1},{25,9},{2,18},{10... | collective-permute-start | bytes 12296 | tf_op jit(solution)/shard_map/ppermute | solution.py:39
  64.2 1.8 %collective-permute-start.20 = (f32[8,128]{1,0:T(8,128)S(1)}, f32[8,128]{1,0:T(8,128)S(1)}, u32[]{:S(2)}, u32[]{:S(2)}) collective-permute-start(f32[8,128]{1,0:T(8,128)S(1)} %get-tuple-element.30), channel_id=1, source_target_pairs={{0,8},{8,0},{16,24},{24,16},{1,9},{9,1},{17,25},{25,17},{2,10},{10... | collective-permute-start | bytes 12296 | tf_op jit(solution)/shard_map/ppermute | solution.py:39
  66.0 1.0 %collective-permute-done.22 = f32[8,128]{1,0:T(8,128)S(1)} collective-permute-done((f32[8,128]{1,0:T(8,128)S(1)}, f32[8,128]{1,0:T(8,128)S(1)}, u32[]{:S(2)}, u32[]{:S(2)}) %collective-permute-start.22) | collective-permute-done | bytes 4128 | tf_op jit(solution)/shard_map/ppermute | solution.py:39
  67.1 0.7 collective-permute-done.20
  67.8 1.8 %collective-permute-start.25 = (f32[4,8,128]{2,1,0:T(8,128)S(1)}, f32[4,8,128]{2,1,0:T(8,128)S(1)}, u32[]{:S(2)}, u32[]{:S(2)}) collective-permute-start(f32[4,8,128]{2,1,0:T(8,128)S(1)} %pad_maximum_fusion.2), channel_id=1, source_target_pairs={{0,6},{2,4},{4,2},{6,0},{1,7},{3,5},{5,3},{7,1},{8,14},{10,12},{12... | collective-permute-start | bytes 49160 | tf_op jit(solution)/shard_map/ppermute | solution.py:41
  69.6 1.1 %collective-permute-start.24 = (f32[4,8,128]{2,1,0:T(8,128)S(1)}, f32[4,8,128]{2,1,0:T(8,128)S(1)}, u32[]{:S(2)}, u32[]{:S(2)}) collective-permute-start(f32[4,8,128]{2,1,0:T(8,128)S(1)} %pad_maximum_fusion.2), channel_id=1, source_target_pairs={{0,4},{2,6},{4,0},{6,2},{1,5},{3,7},{5,1},{7,3},{8,12},{10,14},{12... | collective-permute-start | bytes 49160 | tf_op jit(solution)/shard_map/ppermute | solution.py:41
  70.7 0.6 collective-permute-start.23
  71.3 3.2 %collective-permute-done.23 = f32[4,8,128]{2,1,0:T(8,128)S(1)} collective-permute-done((f32[4,8,128]{2,1,0:T(8,128)S(1)}, f32[4,8,128]{2,1,0:T(8,128)S(1)}, u32[]{:S(2)}, u32[]{:S(2)}) %collective-permute-start.23) | collective-permute-done | bytes 16416 | tf_op jit(solution)/shard_map/ppermute | solution.py:41
  74.5 0.6 copy-done.3
  75.1 2.2 %final.1 = (f32[2,4,1024]{2,1,0:T(4,128)}, f32[1,4]{1,0:T(1,128)}) custom-call(f32[16,8,128]{2,1,0:T(8,128)} %copy-done.3, f32[3,8,1024]{2,1,0:T(8,128)} %copy-done.2), custom_call_target="tpu_custom_call" | custom-call | tf_op jit(solution)/shard_map/final/pallas_call | solution.py:425
  (39 shorter events, 1.8 us)
Async XLA Ops:
  0.6 20.2 %collective-permute-start.6 = (f32[32,128,128]{2,1,0:T(8,128)}, f32[32,128,128]{2,1,0:T(8,128)S(1)}, u32[]{:S(2)}, u32[]{:S(2)}) collective-permute-start(f32[32,128,128]{2,1,0:T(8,128)} %bitcast.24), channel_id=1, source_target_pairs={{0,1},{1,0},{2,3},{3,2},{4,5},{5,4},{6,7},{7,6},{8,9},{9,8},{10,11... | collective-permute-start | bytes 6291464 | tf_op jit(solution)/shard_map/ppermute | solution.py:458
  1.1 19.7 %collective-permute-start.7 = (f32[32,128,128]{2,1,0:T(8,128)}, f32[32,128,128]{2,1,0:T(8,128)}, u32[]{:S(2)}, u32[]{:S(2)}) collective-permute-start(f32[32,128,128]{2,1,0:T(8,128)} %bitcast.26), channel_id=1, source_target_pairs={{0,1},{1,0},{2,3},{3,2},{4,5},{5,4},{6,7},{7,6},{8,9},{9,8},{10,11... | collective-permute-start | bytes 6291464 | tf_op jit(solution)/shard_map/ppermute | solution.py:459
  1.2 7.2 %collective-permute-start = (f32[2,4,1024]{2,1,0:T(4,128)}, f32[2,4,1024]{2,1,0:T(4,128)S(1)}, u32[]{:S(2)}, u32[]{:S(2)}) collective-permute-start(f32[2,4,1024]{2,1,0:T(4,128)} %param.6), channel_id=1, source_target_pairs={{0,8},{8,0},{16,24},{24,16},{1,9},{9,1},{17,25},{25,17},{2,10},{10... | collective-permute-start | bytes 98312 | tf_op jit(solution)/shard_map/ppermute | solution.py:39
  4.2 6.1 %collective-permute-start.2 = (f32[2,4,1024]{2,1,0:T(4,128)}, f32[2,4,1024]{2,1,0:T(4,128)S(1)}, u32[]{:S(2)}, u32[]{:S(2)}) collective-permute-start(f32[2,4,1024]{2,1,0:T(4,128)} %param.6), channel_id=1, source_target_pairs={{0,24},{8,16},{16,8},{24,0},{1,25},{9,17},{17,9},{25,1},{2,26},{10... | collective-permute-start | bytes 98312 | tf_op jit(solution)/shard_map/ppermute | solution.py:39
  6.7 5.4 %collective-permute-start.1 = (f32[2,4,1024]{2,1,0:T(4,128)}, f32[2,4,1024]{2,1,0:T(4,128)S(1)}, u32[]{:S(2)}, u32[]{:S(2)}) collective-permute-start(f32[2,4,1024]{2,1,0:T(4,128)} %param.6), channel_id=1, source_target_pairs={{0,16},{8,24},{16,0},{24,8},{1,17},{9,25},{17,1},{25,9},{2,18},{10... | collective-permute-start | bytes 98312 | tf_op jit(solution)/shard_map/ppermute | solution.py:39
  12.1 8.7 %collective-permute-start.5 = (f32[4,8,1024]{2,1,0:T(8,128)S(1)}, f32[4,8,1024]{2,1,0:T(8,128)S(1)}, u32[]{:S(2)}, u32[]{:S(2)}) collective-permute-start(f32[4,8,1024]{2,1,0:T(8,128)S(1)} %constant_dynamic-update-slice_fusion.refs_0_), channel_id=1, source_target_pairs={{0,6},{2,4},{4,2},{6,0},{1,7},{3,5},{5,3},{7,1},{8,14},{10,12},{12... | collective-permute-start | bytes 393224 | tf_op jit(solution)/shard_map/ppermute | solution.py:41
  14.6 6.2 %collective-permute-start.4 = (f32[4,8,1024]{2,1,0:T(8,128)S(1)}, f32[4,8,1024]{2,1,0:T(8,128)S(1)}, u32[]{:S(2)}, u32[]{:S(2)}) collective-permute-start(f32[4,8,1024]{2,1,0:T(8,128)S(1)} %constant_dynamic-update-slice_fusion.refs_0_), channel_id=1, source_target_pairs={{0,4},{2,6},{4,0},{6,2},{1,5},{3,7},{5,1},{7,3},{8,12},{10,14},{12... | collective-permute-start | bytes 393224 | tf_op jit(solution)/shard_map/ppermute | solution.py:41
  15.2 5.7 %collective-permute-start.3 = (f32[4,8,1024]{2,1,0:T(8,128)S(1)}, f32[4,8,1024]{2,1,0:T(8,128)S(1)}, u32[]{:S(2)}, u32[]{:S(2)}) collective-permute-start(f32[4,8,1024]{2,1,0:T(8,128)S(1)} %constant_dynamic-update-slice_fusion.refs_0_), channel_id=1, source_target_pairs={{0,2},{2,0},{4,6},{6,4},{1,3},{3,1},{5,7},{7,5},{8,10},{10,8},{12,... | collective-permute-start | bytes 393224 | tf_op jit(solution)/shard_map/ppermute | solution.py:41
  16.4 1.6 %copy-start = (f32[8,4,128,128]{3,2,1,0:T(8,128)S(1)}, f32[8,4,128,128]{3,2,1,0:T(8,128)}, u32[]{:S(2)}) copy-start(f32[8,4,128,128]{3,2,1,0:T(8,128)} %param.7) | copy-start | bytes 6291460
  18.0 1.6 %copy-start.1 = (f32[8,4,128,128]{3,2,1,0:T(8,128)S(1)}, f32[8,4,128,128]{3,2,1,0:T(8,128)}, u32[]{:S(2)}) copy-start(f32[8,4,128,128]{3,2,1,0:T(8,128)} %param.8) | copy-start | bytes 6291460
  24.5 5.9 %collective-permute-start.10 = (f32[8,1024]{1,0:T(8,128)S(1)}, f32[8,1024]{1,0:T(8,128)S(1)}, u32[]{:S(2)}, u32[]{:S(2)}) collective-permute-start(f32[8,1024]{1,0:T(8,128)S(1)} %get-tuple-element.24), channel_id=1, source_target_pairs={{0,24},{8,16},{16,8},{24,0},{1,25},{9,17},{17,9},{25,1},{2,26},{10... | collective-permute-start | bytes 98312 | tf_op jit(solution)/shard_map/ppermute | solution.py:39
  25.4 5.3 %collective-permute-start.9 = (f32[8,1024]{1,0:T(8,128)S(1)}, f32[8,1024]{1,0:T(8,128)S(1)}, u32[]{:S(2)}, u32[]{:S(2)}) collective-permute-start(f32[8,1024]{1,0:T(8,128)S(1)} %get-tuple-element.24), channel_id=1, source_target_pairs={{0,16},{8,24},{16,0},{24,8},{1,17},{9,25},{17,1},{25,9},{2,18},{10... | collective-permute-start | bytes 98312 | tf_op jit(solution)/shard_map/ppermute | solution.py:39
  26.5 4.5 %collective-permute-start.8 = (f32[8,1024]{1,0:T(8,128)S(1)}, f32[8,1024]{1,0:T(8,128)S(1)}, u32[]{:S(2)}, u32[]{:S(2)}) collective-permute-start(f32[8,1024]{1,0:T(8,128)S(1)} %get-tuple-element.24), channel_id=1, source_target_pairs={{0,8},{8,0},{16,24},{24,16},{1,9},{9,1},{17,25},{25,17},{2,10},{10... | collective-permute-start | bytes 98312 | tf_op jit(solution)/shard_map/ppermute | solution.py:39
  31.0 7.0 %collective-permute-start.13 = (f32[4,8,1024]{2,1,0:T(8,128)S(1)}, f32[4,8,1024]{2,1,0:T(8,128)S(1)}, u32[]{:S(2)}, u32[]{:S(2)}) collective-permute-start(f32[4,8,1024]{2,1,0:T(8,128)S(1)} %pad_maximum_fusion.refs_0_), channel_id=1, source_target_pairs={{0,6},{2,4},{4,2},{6,0},{1,7},{3,5},{5,3},{7,1},{8,14},{10,12},{12... | collective-permute-start | bytes 393224 | tf_op jit(solution)/shard_map/ppermute | solution.py:41
  33.8 5.4 %collective-permute-start.12 = (f32[4,8,1024]{2,1,0:T(8,128)S(1)}, f32[4,8,1024]{2,1,0:T(8,128)S(1)}, u32[]{:S(2)}, u32[]{:S(2)}) collective-permute-start(f32[4,8,1024]{2,1,0:T(8,128)S(1)} %pad_maximum_fusion.refs_0_), channel_id=1, source_target_pairs={{0,4},{2,6},{4,0},{6,2},{1,5},{3,7},{5,1},{7,3},{8,12},{10,14},{12... | collective-permute-start | bytes 393224 | tf_op jit(solution)/shard_map/ppermute | solution.py:41
  34.1 5.5 %collective-permute-start.11 = (f32[4,8,1024]{2,1,0:T(8,128)S(1)}, f32[4,8,1024]{2,1,0:T(8,128)S(1)}, u32[]{:S(2)}, u32[]{:S(2)}) collective-permute-start(f32[4,8,1024]{2,1,0:T(8,128)S(1)} %pad_maximum_fusion.refs_0_), channel_id=1, source_target_pairs={{0,2},{2,0},{4,6},{6,4},{1,3},{3,1},{5,7},{7,5},{8,10},{10,8},{12,... | collective-permute-start | bytes 393224 | tf_op jit(solution)/shard_map/ppermute | solution.py:41
  42.9 5.9 %collective-permute-start.16 = (f32[8,1024]{1,0:T(8,128)S(1)}, f32[8,1024]{1,0:T(8,128)S(1)}, u32[]{:S(2)}, u32[]{:S(2)}) collective-permute-start(f32[8,1024]{1,0:T(8,128)S(1)} %get-tuple-element.28), channel_id=1, source_target_pairs={{0,24},{8,16},{16,8},{24,0},{1,25},{9,17},{17,9},{25,1},{2,26},{10... | collective-permute-start | bytes 98312 | tf_op jit(solution)/shard_map/ppermute | solution.py:39
  43.7 5.6 %collective-permute-start.15 = (f32[8,1024]{1,0:T(8,128)S(1)}, f32[8,1024]{1,0:T(8,128)S(1)}, u32[]{:S(2)}, u32[]{:S(2)}) collective-permute-start(f32[8,1024]{1,0:T(8,128)S(1)} %get-tuple-element.28), channel_id=1, source_target_pairs={{0,16},{8,24},{16,0},{24,8},{1,17},{9,25},{17,1},{25,9},{2,18},{10... | collective-permute-start | bytes 98312 | tf_op jit(solution)/shard_map/ppermute | solution.py:39
  45.3 4.1 %collective-permute-start.14 = (f32[8,1024]{1,0:T(8,128)S(1)}, f32[8,1024]{1,0:T(8,128)S(1)}, u32[]{:S(2)}, u32[]{:S(2)}) collective-permute-start(f32[8,1024]{1,0:T(8,128)S(1)} %get-tuple-element.28), channel_id=1, source_target_pairs={{0,8},{8,0},{16,24},{24,16},{1,9},{9,1},{17,25},{25,17},{2,10},{10... | collective-permute-start | bytes 98312 | tf_op jit(solution)/shard_map/ppermute | solution.py:39
  49.4 6.0 %collective-permute-start.19 = (f32[4,8,1024]{2,1,0:T(8,128)S(1)}, f32[4,8,1024]{2,1,0:T(8,128)S(1)}, u32[]{:S(2)}, u32[]{:S(2)}) collective-permute-start(f32[4,8,1024]{2,1,0:T(8,128)S(1)} %pad_maximum_fusion.1.refs_0_), channel_id=1, source_target_pairs={{0,6},{2,4},{4,2},{6,0},{1,7},{3,5},{5,3},{7,1},{8,14},{10,12},{12... | collective-permute-start | bytes 393224 | tf_op jit(solution)/shard_map/ppermute | solution.py:41
  51.2 5.5 %collective-permute-start.18 = (f32[4,8,1024]{2,1,0:T(8,128)S(1)}, f32[4,8,1024]{2,1,0:T(8,128)S(1)}, u32[]{:S(2)}, u32[]{:S(2)}) collective-permute-start(f32[4,8,1024]{2,1,0:T(8,128)S(1)} %pad_maximum_fusion.1.refs_0_), channel_id=1, source_target_pairs={{0,4},{2,6},{4,0},{6,2},{1,5},{3,7},{5,1},{7,3},{8,12},{10,14},{12... | collective-permute-start | bytes 393224 | tf_op jit(solution)/shard_map/ppermute | solution.py:41
  52.1 5.1 %collective-permute-start.17 = (f32[4,8,1024]{2,1,0:T(8,128)S(1)}, f32[4,8,1024]{2,1,0:T(8,128)S(1)}, u32[]{:S(2)}, u32[]{:S(2)}) collective-permute-start(f32[4,8,1024]{2,1,0:T(8,128)S(1)} %pad_maximum_fusion.1.refs_0_), channel_id=1, source_target_pairs={{0,2},{2,0},{4,6},{6,4},{1,3},{3,1},{5,7},{7,5},{8,10},{10,8},{12,... | collective-permute-start | bytes 393224 | tf_op jit(solution)/shard_map/ppermute | solution.py:41
  60.9 0.6 copy-start.2
  61.6 5.4 %collective-permute-start.22 = (f32[8,128]{1,0:T(8,128)S(1)}, f32[8,128]{1,0:T(8,128)S(1)}, u32[]{:S(2)}, u32[]{:S(2)}) collective-permute-start(f32[8,128]{1,0:T(8,128)S(1)} %get-tuple-element.30), channel_id=1, source_target_pairs={{0,24},{8,16},{16,8},{24,0},{1,25},{9,17},{17,9},{25,1},{2,26},{10... | collective-permute-start | bytes 12296 | tf_op jit(solution)/shard_map/ppermute | solution.py:39
  62.6 4.5 %collective-permute-start.21 = (f32[8,128]{1,0:T(8,128)S(1)}, f32[8,128]{1,0:T(8,128)S(1)}, u32[]{:S(2)}, u32[]{:S(2)}) collective-permute-start(f32[8,128]{1,0:T(8,128)S(1)} %get-tuple-element.30), channel_id=1, source_target_pairs={{0,16},{8,24},{16,0},{24,8},{1,17},{9,25},{17,1},{25,9},{2,18},{10... | collective-permute-start | bytes 12296 | tf_op jit(solution)/shard_map/ppermute | solution.py:39
  64.2 3.6 %collective-permute-start.20 = (f32[8,128]{1,0:T(8,128)S(1)}, f32[8,128]{1,0:T(8,128)S(1)}, u32[]{:S(2)}, u32[]{:S(2)}) collective-permute-start(f32[8,128]{1,0:T(8,128)S(1)} %get-tuple-element.30), channel_id=1, source_target_pairs={{0,8},{8,0},{16,24},{24,16},{1,9},{9,1},{17,25},{25,17},{2,10},{10... | collective-permute-start | bytes 12296 | tf_op jit(solution)/shard_map/ppermute | solution.py:39
  67.8 6.7 %collective-permute-start.25 = (f32[4,8,128]{2,1,0:T(8,128)S(1)}, f32[4,8,128]{2,1,0:T(8,128)S(1)}, u32[]{:S(2)}, u32[]{:S(2)}) collective-permute-start(f32[4,8,128]{2,1,0:T(8,128)S(1)} %pad_maximum_fusion.2), channel_id=1, source_target_pairs={{0,6},{2,4},{4,2},{6,0},{1,7},{3,5},{5,3},{7,1},{8,14},{10,12},{12... | collective-permute-start | bytes 49160 | tf_op jit(solution)/shard_map/ppermute | solution.py:41
  69.6 4.9 %collective-permute-start.24 = (f32[4,8,128]{2,1,0:T(8,128)S(1)}, f32[4,8,128]{2,1,0:T(8,128)S(1)}, u32[]{:S(2)}, u32[]{:S(2)}) collective-permute-start(f32[4,8,128]{2,1,0:T(8,128)S(1)} %pad_maximum_fusion.2), channel_id=1, source_target_pairs={{0,4},{2,6},{4,0},{6,2},{1,5},{3,7},{5,1},{7,3},{8,12},{10,14},{12... | collective-permute-start | bytes 49160 | tf_op jit(solution)/shard_map/ppermute | solution.py:41
  70.7 3.7 %collective-permute-start.23 = (f32[4,8,128]{2,1,0:T(8,128)S(1)}, f32[4,8,128]{2,1,0:T(8,128)S(1)}, u32[]{:S(2)}, u32[]{:S(2)}) collective-permute-start(f32[4,8,128]{2,1,0:T(8,128)S(1)} %pad_maximum_fusion.2), channel_id=1, source_target_pairs={{0,2},{2,0},{4,6},{6,4},{1,3},{3,1},{5,7},{7,5},{8,10},{10,8},{12,... | collective-permute-start | bytes 49160 | tf_op jit(solution)/shard_map/ppermute | solution.py:41
  74.5 0.6 copy-start.3

commit v15 on v14

--- a/solution.py
+++ b/solution.py
@@ -41,21 +41,9 @@
     return [whole_line] + [lax.ppermute(whole_line, "place", perm) for perm in partner_steps(plane)]
 
 
-def setup_kernel(
-    line, plane, freqs, scalars_ref, g_ref, c_ref,
-    items_ref, places_ref, turn_ref, g_out_ref, c_out_ref, sems,
-):
+def setup_kernel(line, plane, freqs, scalars_ref, items_ref, places_ref, turn_ref):
     row_blocks, slots = places_ref.shape
     own_slots = slots // freqs
-    pieces = sems.shape[1]
-    part = g_ref.shape[0] // pieces
-    copies = []
-    for m, (source, target) in enumerate(((g_ref, g_out_ref), (c_ref, c_out_ref))):
-        for i in range(pieces):
-            at = pl.ds(i * part, part)
-            copies.append(pltpu.make_async_copy(source.at[at], target.at[at], sems.at[m, i]))
-            copies[-1].start()
-
     order = lax.broadcasted_iota(jnp.int32, (8, LANES), 1)
     freq = scalars_ref[row_blocks, 2]
     for table, d in enumerate(list(range(freqs)) + [None]):
@@ -101,31 +89,20 @@
         ids = jnp.where(lax.rem(row_at, half) == f, scalars_ref[row_blocks, 3 + row_blocks + f], ids)
     angular = 0.2 * jnp.exp(ids.astype(jnp.float32) * (math.log(8.0) / 1000.0))
     turn_ref[...] = jnp.where(row_at < half, -angular, angular)
-    for copy in copies:
-        copy.wait()
-
-
-def run_setup(scalars, shape, freq_count, g_own, c_own, line, plane, freqs):
-    smem, vmem = pl.BlockSpec(memory_space=pltpu.SMEM), pl.BlockSpec(memory_space=pltpu.VMEM)
-    far = pl.BlockSpec(memory_space=pl.ANY)
-    blocks = jax.ShapeDtypeStruct(g_own.shape, jnp.float32)
-    pieces = math.gcd(g_own.shape[0], 8)
+
+
+def run_setup(scalars, shape, freq_count, line, plane, freqs):
     return pl.pallas_call(
         functools.partial(setup_kernel, line, plane, freqs),
-        in_specs=[smem, far, far],
-        out_specs=[vmem] * 5,
+        in_specs=[pl.BlockSpec(memory_space=pltpu.SMEM)],
+        out_specs=[pl.BlockSpec(memory_space=pltpu.VMEM)] * 3,
         out_shape=[
             jax.ShapeDtypeStruct((4 * (freqs + 1), LANES), jnp.int32),
             jax.ShapeDtypeStruct(shape, jnp.int32),
             jax.ShapeDtypeStruct((2 * freq_count, LANES), jnp.float32),
-            blocks,
-            blocks,
         ],
-        scratch_shapes=[pltpu.SemaphoreType.DMA((2, pieces))],
-        compiler_params=pltpu.CompilerParams(vmem_limit_bytes=VMEM_LIMIT),
-        cost_estimate=pl.CostEstimate(flops=0, bytes_accessed=16 * g_own.size, transcendentals=0),
         name="setup",
-    )(scalars, g_own, c_own)
+    )(scalars)
 
 
 def lane_sum(x):
@@ -153,13 +130,13 @@
     row_blocks, slots = places_ref.shape
     nodes = plane * line
     if step == 0:
-        g_refs, c_refs = refs[:freqs], list(refs[freqs : 2 * freqs])
+        g_refs, c_refs = list(refs[:freqs]), list(refs[freqs : 2 * freqs])
         z_ref, local_ref, info_ref, split_ref, layer_ref, mask_ref, acc_ref, kept_ref, sems = refs[2 * freqs :]
         arrivals = []
-        for d in range(1, freqs):
-            arrivals.append(pltpu.make_async_copy(c_refs[d], kept_ref.at[d - 1], sems.at[d - 1]))
+        for at, (held, d) in enumerate([(c_refs, d) for d in range(1, freqs)] + [(g_refs, 0), (c_refs, 0)]):
+            arrivals.append(pltpu.make_async_copy(held[d], kept_ref.at[at], sems.at[at]))
             arrivals[-1].start()
-            c_refs[d] = kept_ref.at[d - 1]
+            held[d] = kept_ref.at[at]
     elif step < ITERS - 1:
         split_ref, z_ref, local_ref, info_ref, layer_ref, mask_ref, acc_ref = refs
     else:
@@ -260,9 +237,9 @@
             start = start + jnp.where(fits, count, 0)
 
     if step == 0:
-        for d in range(freqs):
-            if d:
-                arrivals[d - 1].wait()
+        for d in (*range(1, freqs), 0):
+            for arrival in [arrivals[d - 1]] if d else arrivals[freqs - 1 :]:
+                arrival.wait()
 
             def split_slots(start, count, d=d):
                 lefts, rights = [], []
@@ -333,10 +310,12 @@
     ]
     if step == 0:
         received = len(in_specs) - freqs + 1
-        in_specs[received:] = [pl.BlockSpec(memory_space=pl.ANY)] * (freqs - 1)
+        far = pl.BlockSpec(memory_space=pl.ANY)
+        in_specs[received - 1 :] = [far] * freqs
+        in_specs[received - 1 - freqs] = far
         scratch_shapes += [
-            pltpu.VMEM((freqs - 1,) + blocks[0].shape, jnp.float32),
-            pltpu.SemaphoreType.DMA((freqs - 1,)),
+            pltpu.VMEM((freqs + 1,) + blocks[0].shape, jnp.float32),
+            pltpu.SemaphoreType.DMA((freqs + 1,)),
         ]
         out_shape.append(jax.ShapeDtypeStruct((row_blocks * slots, 2 * size, 2 * size), jnp.bfloat16))
     if step == ITERS - 1:
@@ -449,10 +428,8 @@
         ).astype(jnp.int32)
         stored = (row_blocks * own_slots, size, size)
         g_own, c_own = g_blocks.reshape(stored), c_blocks.reshape(stored)
-        *lists, turn, g_near, c_near = run_setup(
-            scalars, pattern.shape, freq_count, g_own, c_own, line, plane, freqs
-        )
-        g_parts, c_parts = [g_near], [c_near]
+        *lists, turn = run_setup(scalars, pattern.shape, freq_count, line, plane, freqs)
+        g_parts, c_parts = [g_own], [c_own]
         for d in range(1, freqs):
             perm = [(i, (i + d) % freqs) for i in range(freqs)]
             g_parts.append(lax.ppermute(g_own, "freq", perm))

time: 77.3 us -> 82.9 us (1.072)
  local copies, waits for them, and re-layouts: 6.06 us -> 8.09 us
  waiting for transfers between devices: 22 us -> 23.4 us
  Pallas kernels: 14.1 us -> 15.1 us
    unnamed x17 -> x23, local copies, waits for them, and re-layouts: 4.45 us -> 6.48 us
    ppermute x12, waiting for transfers between devices: 9.42 us -> 11.3 us  [gather_rows(): lax.ppermute(rows, 'line', perm)]
  transfers between devices with their start and end apart: 26 -> 26, of which waited for: 17 -> 18; matrix products, arithmetic and copies ran while one was open for 3% -> 4% of each run, Pallas kernels for 2% -> 2%
where the time goes in v15:
time: 82.9 us; the launch traced here: 82.3 us
  starting transfers between devices  33.6 us (41%)
  waiting for transfers between devices  23.4 us (28%)
  Pallas kernels  15.1 us (18%)
  local copies, waits for them, and re-layouts  8.09 us (10%)
  other arithmetic  1.31 us (2%)
    ppermute x12, starting transfers between devices, gather_rows(): lax.ppermute(rows, 'line', perm)  18.9 us
    ppermute x12, starting transfers between devices, gather_rows(): lax.ppermute(whole_line, 'place', perm)  14.1 us
    ppermute x12, waiting for transfers between devices, gather_rows(): lax.ppermute(whole_line, 'place', perm)  12.1 us
    pallas_call x3, Pallas kernels, run_step(): pl.pallas_call(functools.partial(step_kernel, step, plane, line, freqs),...  11.4 us
    ppermute x12, waiting for transfers between devices, gather_rows(): lax.ppermute(rows, 'line', perm)  11.3 us
    unnamed x23, local copies, waits for them, and re-layouts  6.48 us
    pallas_call x1, Pallas kernels, run_final(): pl.pallas_call(final_kernel, in_specs=[vmem] * 2, out_specs=[vmem] * 2, o...  2.17 us
  transfers between devices with their start and end apart: 26, of which 18 were waited for; matrix products, arithmetic and copies ran while one was open for 4% of the time, Pallas kernels for 2%

profile of v15, /device:TPU:0, one launch (start us, length us, event | category | flops | bytes accessed | tf_op | source)
XLA Modules:
  0.0 82.3 jit_solution(2575043884979588797)
XLA Ops:
  1.2 3.0 %collective-permute-start = (f32[2,4,1024]{2,1,0:T(4,128)}, f32[2,4,1024]{2,1,0:T(4,128)S(1)}, u32[]{:S(2)}, u32[]{:S(2)}) collective-permute-start(f32[2,4,1024]{2,1,0:T(4,128)} %param.6), channel_id=1, source_target_pairs={{0,8},{8,0},{16,24},{24,16},{1,9},{9,1},{17,25},{25,17},{2,10},{10... | collective-permute-start | bytes 98312 | tf_op jit(solution)/shard_map/ppermute | solution.py:39
  4.2 2.5 %collective-permute-start.2 = (f32[2,4,1024]{2,1,0:T(4,128)}, f32[2,4,1024]{2,1,0:T(4,128)S(1)}, u32[]{:S(2)}, u32[]{:S(2)}) collective-permute-start(f32[2,4,1024]{2,1,0:T(4,128)} %param.6), channel_id=1, source_target_pairs={{0,24},{8,16},{16,8},{24,0},{1,25},{9,17},{17,9},{25,1},{2,26},{10... | collective-permute-start | bytes 98312 | tf_op jit(solution)/shard_map/ppermute | solution.py:39
  6.8 0.8 stack.72
  7.6 0.7 concatenate.11
  8.4 1.9 %collective-permute-done.2 = f32[2,4,1024]{2,1,0:T(4,128)S(1)} collective-permute-done((f32[2,4,1024]{2,1,0:T(4,128)}, f32[2,4,1024]{2,1,0:T(4,128)S(1)}, u32[]{:S(2)}, u32[]{:S(2)}) %collective-permute-start.2) | collective-permute-done | bytes 32800 | tf_op jit(solution)/shard_map/ppermute | solution.py:39
  10.3 1.8 %collective-permute-done.1 = f32[2,4,1024]{2,1,0:T(4,128)S(1)} collective-permute-done((f32[2,4,1024]{2,1,0:T(4,128)}, f32[2,4,1024]{2,1,0:T(4,128)S(1)}, u32[]{:S(2)}, u32[]{:S(2)}) %collective-permute-start.1) | collective-permute-done | bytes 32800 | tf_op jit(solution)/shard_map/ppermute | solution.py:39
  12.1 2.5 %collective-permute-start.5 = (f32[4,8,1024]{2,1,0:T(8,128)S(1)}, f32[4,8,1024]{2,1,0:T(8,128)S(1)}, u32[]{:S(2)}, u32[]{:S(2)}) collective-permute-start(f32[4,8,1024]{2,1,0:T(8,128)S(1)} %constant_dynamic-update-slice_fusion.refs_0_), channel_id=1, source_target_pairs={{0,6},{2,4},{4,2},{6,0},{1,7},{3,5},{5,3},{7,1},{8,14},{10,12},{12... | collective-permute-start | bytes 393224 | tf_op jit(solution)/shard_map/ppermute | solution.py:41
  15.7 1.3 %pad_add_fusion.scalars_ref = s32[9,128]{1,0:T(8,128)} fusion(s32[8,8]{1,0:T(8,128)} %param.9, s32[1,128]{1,0:T(1,128)S(1)} %pad_bitcast_fusion), kind=kLoop, calls=%fused_computation.14 | loop fusion | flops 1152 | bytes 5376 | tf_op jit(solution)/shard_map/concatenate | solution.py:423
  17.0 1.5 %setup.1 = (s32[12,128]{1,0:T(8,128)}, s32[8,8]{1,0:T(8,128)}, f32[8,128]{1,0:T(8,128)}) custom-call(s32[9,128]{1,0:T(8,128)} %pad_add_fusion.scalars_ref), custom_call_target="tpu_custom_call" | custom-call | tf_op jit(solution)/shard_map/setup/pallas_call | solution.py:95
  18.5 0.9 %collective-permute-done.5.refs_3_ = f32[4,8,1024]{2,1,0:T(8,128)S(1)} collective-permute-done((f32[4,8,1024]{2,1,0:T(8,128)S(1)}, f32[4,8,1024]{2,1,0:T(8,128)S(1)}, u32[]{:S(2)}, u32[]{:S(2)}) %collective-permute-start.5) | collective-permute-done | bytes 131104 | tf_op jit(solution)/shard_map/ppermute | solution.py:41
  19.4 0.8 collective-permute-done.4.refs_2_
  20.2 1.6 %copy-done = f32[8,4,128,128]{3,2,1,0:T(8,128)S(1)} copy-done((f32[8,4,128,128]{3,2,1,0:T(8,128)S(1)}, f32[8,4,128,128]{3,2,1,0:T(8,128)}, u32[]{:S(2)}) %copy-start) | copy-done | bytes 2097176
  21.8 1.6 %copy-done.1 = f32[8,4,128,128]{3,2,1,0:T(8,128)S(1)} copy-done((f32[8,4,128,128]{3,2,1,0:T(8,128)S(1)}, f32[8,4,128,128]{3,2,1,0:T(8,128)}, u32[]{:S(2)}) %copy-start.1) | copy-done | bytes 2097176
  23.4 0.7 copy-done.3
  24.1 0.7 copy-done.4
  24.8 0.7 copy-done.5
  25.5 5.0 %step_0.1 = (f32[129,8,128]{2,1,0:T(8,128)S(1)}, f32[8,1024]{1,0:T(8,128)S(1)}, f32[8,128]{1,0:T(8,128)S(1)}, bf16[64,256,256]{2,1,0:T(8,128)(2,1)S(1)}) custom-call(s32[12,128]{1,0:T(8,128)S(1)} %copy-done.3, s32[8,8]{1,0:T(8,128)S(1)} %copy-done.4, f32[8,128]{1,0:T(8,128)S(1)} %copy-done.5, f32[8,128]{1,0:T(8,128)S(1)} %broadcast_in_dim.7.info_in_ref, ...), custom_call_target="tpu_custom_call" | custom-call | tf_op jit(solution)/shard_map/step_0/pallas_call | solution.py:323
  30.4 2.2 %collective-permute-start.10 = (f32[8,1024]{1,0:T(8,128)S(1)}, f32[8,1024]{1,0:T(8,128)S(1)}, u32[]{:S(2)}, u32[]{:S(2)}) collective-permute-start(f32[8,1024]{1,0:T(8,128)S(1)} %get-tuple-element.20), channel_id=1, source_target_pairs={{0,24},{8,16},{16,8},{24,0},{1,25},{9,17},{17,9},{25,1},{2,26},{10... | collective-permute-start | bytes 98312 | tf_op jit(solution)/shard_map/ppermute | solution.py:39
  32.6 2.3 %collective-permute-start.8 = (f32[8,1024]{1,0:T(8,128)S(1)}, f32[8,1024]{1,0:T(8,128)S(1)}, u32[]{:S(2)}, u32[]{:S(2)}) collective-permute-start(f32[8,1024]{1,0:T(8,128)S(1)} %get-tuple-element.20), channel_id=1, source_target_pairs={{0,8},{8,0},{16,24},{24,16},{1,9},{9,1},{17,25},{25,17},{2,10},{10... | collective-permute-start | bytes 98312 | tf_op jit(solution)/shard_map/ppermute | solution.py:39
  34.9 1.3 %collective-permute-done.10 = f32[8,1024]{1,0:T(8,128)S(1)} collective-permute-done((f32[8,1024]{1,0:T(8,128)S(1)}, f32[8,1024]{1,0:T(8,128)S(1)}, u32[]{:S(2)}, u32[]{:S(2)}) %collective-permute-start.10) | collective-permute-done | bytes 32800 | tf_op jit(solution)/shard_map/ppermute | solution.py:39
  36.2 1.2 %collective-permute-done.9 = f32[8,1024]{1,0:T(8,128)S(1)} collective-permute-done((f32[8,1024]{1,0:T(8,128)S(1)}, f32[8,1024]{1,0:T(8,128)S(1)}, u32[]{:S(2)}, u32[]{:S(2)}) %collective-permute-start.9) | collective-permute-done | bytes 32800 | tf_op jit(solution)/shard_map/ppermute | solution.py:39
  37.4 1.7 %collective-permute-start.13 = (f32[4,8,1024]{2,1,0:T(8,128)S(1)}, f32[4,8,1024]{2,1,0:T(8,128)S(1)}, u32[]{:S(2)}, u32[]{:S(2)}) collective-permute-start(f32[4,8,1024]{2,1,0:T(8,128)S(1)} %pad_maximum_fusion.refs_0_), channel_id=1, source_target_pairs={{0,6},{2,4},{4,2},{6,0},{1,7},{3,5},{5,3},{7,1},{8,14},{10,12},{12... | collective-permute-start | bytes 393224 | tf_op jit(solution)/shard_map/ppermute | solution.py:41
  39.2 0.8 collective-permute-start.12
  40.0 1.0 %collective-permute-start.11 = (f32[4,8,1024]{2,1,0:T(8,128)S(1)}, f32[4,8,1024]{2,1,0:T(8,128)S(1)}, u32[]{:S(2)}, u32[]{:S(2)}) collective-permute-start(f32[4,8,1024]{2,1,0:T(8,128)S(1)} %pad_maximum_fusion.refs_0_), channel_id=1, source_target_pairs={{0,2},{2,0},{4,6},{6,4},{1,3},{3,1},{5,7},{7,5},{8,10},{10,8},{12,... | collective-permute-start | bytes 393224 | tf_op jit(solution)/shard_map/ppermute | solution.py:41
  41.0 2.4 %collective-permute-done.13.refs_3_ = f32[4,8,1024]{2,1,0:T(8,128)S(1)} collective-permute-done((f32[4,8,1024]{2,1,0:T(8,128)S(1)}, f32[4,8,1024]{2,1,0:T(8,128)S(1)}, u32[]{:S(2)}, u32[]{:S(2)}) %collective-permute-start.13) | collective-permute-done | bytes 131104 | tf_op jit(solution)/shard_map/ppermute | solution.py:41
  43.4 1.3 %collective-permute-done.12.refs_2_ = f32[4,8,1024]{2,1,0:T(8,128)S(1)} collective-permute-done((f32[4,8,1024]{2,1,0:T(8,128)S(1)}, f32[4,8,1024]{2,1,0:T(8,128)S(1)}, u32[]{:S(2)}, u32[]{:S(2)}) %collective-permute-start.12) | collective-permute-done | bytes 131104 | tf_op jit(solution)/shard_map/ppermute | solution.py:41
  44.9 3.0 %step_1.1 = (f32[129,8,128]{2,1,0:T(8,128)S(1)}, f32[8,1024]{1,0:T(8,128)S(1)}, f32[8,128]{1,0:T(8,128)S(1)}) custom-call(s32[12,128]{1,0:T(8,128)S(1)} %copy-done.3, s32[8,8]{1,0:T(8,128)S(1)} %copy-done.4, f32[8,128]{1,0:T(8,128)S(1)} %copy-done.5, f32[8,128]{1,0:T(8,128)S(1)} %get-tuple-element.19.info_in_ref, f32[4,8,1024]{2,1,0:T(8,128)S(1)} %pad_maximum_fusion.refs_0_, ...), custom_call_target="tpu_custom_call" | custom-call | tf_op jit(solution)/shard_map/step_1/pallas_call | solution.py:323
  48.0 2.1 %collective-permute-start.16 = (f32[8,1024]{1,0:T(8,128)S(1)}, f32[8,1024]{1,0:T(8,128)S(1)}, u32[]{:S(2)}, u32[]{:S(2)}) collective-permute-start(f32[8,1024]{1,0:T(8,128)S(1)} %get-tuple-element.24), channel_id=1, source_target_pairs={{0,24},{8,16},{16,8},{24,0},{1,25},{9,17},{17,9},{25,1},{2,26},{10... | collective-permute-start | bytes 98312 | tf_op jit(solution)/shard_map/ppermute | solution.py:39
  50.1 1.4 %collective-permute-start.15 = (f32[8,1024]{1,0:T(8,128)S(1)}, f32[8,1024]{1,0:T(8,128)S(1)}, u32[]{:S(2)}, u32[]{:S(2)}) collective-permute-start(f32[8,1024]{1,0:T(8,128)S(1)} %get-tuple-element.24), channel_id=1, source_target_pairs={{0,16},{8,24},{16,0},{24,8},{1,17},{9,25},{17,1},{25,9},{2,18},{10... | collective-permute-start | bytes 98312 | tf_op jit(solution)/shard_map/ppermute | solution.py:39
  51.5 1.0 %collective-permute-start.14 = (f32[8,1024]{1,0:T(8,128)S(1)}, f32[8,1024]{1,0:T(8,128)S(1)}, u32[]{:S(2)}, u32[]{:S(2)}) collective-permute-start(f32[8,1024]{1,0:T(8,128)S(1)} %get-tuple-element.24), channel_id=1, source_target_pairs={{0,8},{8,0},{16,24},{24,16},{1,9},{9,1},{17,25},{25,17},{2,10},{10... | collective-permute-start | bytes 98312 | tf_op jit(solution)/shard_map/ppermute | solution.py:39
  52.4 1.3 %collective-permute-done.16 = f32[8,1024]{1,0:T(8,128)S(1)} collective-permute-done((f32[8,1024]{1,0:T(8,128)S(1)}, f32[8,1024]{1,0:T(8,128)S(1)}, u32[]{:S(2)}, u32[]{:S(2)}) %collective-permute-start.16) | collective-permute-done | bytes 32800 | tf_op jit(solution)/shard_map/ppermute | solution.py:39
  53.8 1.6 %collective-permute-done.15 = f32[8,1024]{1,0:T(8,128)S(1)} collective-permute-done((f32[8,1024]{1,0:T(8,128)S(1)}, f32[8,1024]{1,0:T(8,128)S(1)}, u32[]{:S(2)}, u32[]{:S(2)}) %collective-permute-start.15) | collective-permute-done | bytes 32800 | tf_op jit(solution)/shard_map/ppermute | solution.py:39
  55.5 1.6 %collective-permute-start.19 = (f32[4,8,1024]{2,1,0:T(8,128)S(1)}, f32[4,8,1024]{2,1,0:T(8,128)S(1)}, u32[]{:S(2)}, u32[]{:S(2)}) collective-permute-start(f32[4,8,1024]{2,1,0:T(8,128)S(1)} %pad_maximum_fusion.1.refs_0_), channel_id=1, source_target_pairs={{0,6},{2,4},{4,2},{6,0},{1,7},{3,5},{5,3},{7,1},{8,14},{10,12},{12... | collective-permute-start | bytes 393224 | tf_op jit(solution)/shard_map/ppermute | solution.py:41
  57.1 0.7 collective-permute-start.18
  57.8 1.3 %collective-permute-start.17 = (f32[4,8,1024]{2,1,0:T(8,128)S(1)}, f32[4,8,1024]{2,1,0:T(8,128)S(1)}, u32[]{:S(2)}, u32[]{:S(2)}) collective-permute-start(f32[4,8,1024]{2,1,0:T(8,128)S(1)} %pad_maximum_fusion.1.refs_0_), channel_id=1, source_target_pairs={{0,2},{2,0},{4,6},{6,4},{1,3},{3,1},{5,7},{7,5},{8,10},{10,8},{12,... | collective-permute-start | bytes 393224 | tf_op jit(solution)/shard_map/ppermute | solution.py:41
  59.1 2.5 %collective-permute-done.19.refs_3_ = f32[4,8,1024]{2,1,0:T(8,128)S(1)} collective-permute-done((f32[4,8,1024]{2,1,0:T(8,128)S(1)}, f32[4,8,1024]{2,1,0:T(8,128)S(1)}, u32[]{:S(2)}, u32[]{:S(2)}) %collective-permute-start.19) | collective-permute-done | bytes 131104 | tf_op jit(solution)/shard_map/ppermute | solution.py:41
  61.5 1.3 %collective-permute-done.18.refs_2_ = f32[4,8,1024]{2,1,0:T(8,128)S(1)} collective-permute-done((f32[4,8,1024]{2,1,0:T(8,128)S(1)}, f32[4,8,1024]{2,1,0:T(8,128)S(1)}, u32[]{:S(2)}, u32[]{:S(2)}) %collective-permute-start.18) | collective-permute-done | bytes 131104 | tf_op jit(solution)/shard_map/ppermute | solution.py:41
  62.9 3.4 %step_2.1 = (f32[3,8,1024]{2,1,0:T(8,128)S(1)}, f32[8,128]{1,0:T(8,128)S(1)}) custom-call(s32[12,128]{1,0:T(8,128)S(1)} %copy-done.3, s32[8,8]{1,0:T(8,128)S(1)} %copy-done.4, f32[8,128]{1,0:T(8,128)S(1)} %copy-done.5, f32[8,128]{1,0:T(8,128)S(1)} %get-tuple-element.23.info_in_ref, f32[4,8,1024]{2,1,0:T(8,128)S(1)} %pad_maximum_fusion.1.refs_0_, ...), custom_call_target="tpu_custom_call" | custom-call | tf_op jit(solution)/shard_map/step_2/pallas_call | solution.py:323
  66.9 1.8 %collective-permute-start.22 = (f32[8,128]{1,0:T(8,128)S(1)}, f32[8,128]{1,0:T(8,128)S(1)}, u32[]{:S(2)}, u32[]{:S(2)}) collective-permute-start(f32[8,128]{1,0:T(8,128)S(1)} %get-tuple-element.26), channel_id=1, source_target_pairs={{0,24},{8,16},{16,8},{24,0},{1,25},{9,17},{17,9},{25,1},{2,26},{10... | collective-permute-start | bytes 12296 | tf_op jit(solution)/shard_map/ppermute | solution.py:39
  68.7 1.0 %collective-permute-start.21 = (f32[8,128]{1,0:T(8,128)S(1)}, f32[8,128]{1,0:T(8,128)S(1)}, u32[]{:S(2)}, u32[]{:S(2)}) collective-permute-start(f32[8,128]{1,0:T(8,128)S(1)} %get-tuple-element.26), channel_id=1, source_target_pairs={{0,16},{8,24},{16,0},{24,8},{1,17},{9,25},{17,1},{25,9},{2,18},{10... | collective-permute-start | bytes 12296 | tf_op jit(solution)/shard_map/ppermute | solution.py:39
  69.7 1.6 %collective-permute-start.20 = (f32[8,128]{1,0:T(8,128)S(1)}, f32[8,128]{1,0:T(8,128)S(1)}, u32[]{:S(2)}, u32[]{:S(2)}) collective-permute-start(f32[8,128]{1,0:T(8,128)S(1)} %get-tuple-element.26), channel_id=1, source_target_pairs={{0,8},{8,0},{16,24},{24,16},{1,9},{9,1},{17,25},{25,17},{2,10},{10... | collective-permute-start | bytes 12296 | tf_op jit(solution)/shard_map/ppermute | solution.py:39
  71.3 1.0 %collective-permute-done.22 = f32[8,128]{1,0:T(8,128)S(1)} collective-permute-done((f32[8,128]{1,0:T(8,128)S(1)}, f32[8,128]{1,0:T(8,128)S(1)}, u32[]{:S(2)}, u32[]{:S(2)}) %collective-permute-start.22) | collective-permute-done | bytes 4128 | tf_op jit(solution)/shard_map/ppermute | solution.py:39
  72.3 0.9 %collective-permute-done.21 = f32[8,128]{1,0:T(8,128)S(1)} collective-permute-done((f32[8,128]{1,0:T(8,128)S(1)}, f32[8,128]{1,0:T(8,128)S(1)}, u32[]{:S(2)}, u32[]{:S(2)}) %collective-permute-start.21) | collective-permute-done | bytes 4128 | tf_op jit(solution)/shard_map/ppermute | solution.py:39
  73.3 1.7 %collective-permute-start.25 = (f32[4,8,128]{2,1,0:T(8,128)S(1)}, f32[4,8,128]{2,1,0:T(8,128)S(1)}, u32[]{:S(2)}, u32[]{:S(2)}) collective-permute-start(f32[4,8,128]{2,1,0:T(8,128)S(1)} %pad_maximum_fusion.2), channel_id=1, source_target_pairs={{0,6},{2,4},{4,2},{6,0},{1,7},{3,5},{5,3},{7,1},{8,14},{10,12},{12... | collective-permute-start | bytes 49160 | tf_op jit(solution)/shard_map/ppermute | solution.py:41
  75.0 0.7 collective-permute-start.24
  75.8 1.1 %collective-permute-start.23 = (f32[4,8,128]{2,1,0:T(8,128)S(1)}, f32[4,8,128]{2,1,0:T(8,128)S(1)}, u32[]{:S(2)}, u32[]{:S(2)}) collective-permute-start(f32[4,8,128]{2,1,0:T(8,128)S(1)} %pad_maximum_fusion.2), channel_id=1, source_target_pairs={{0,2},{2,0},{4,6},{6,4},{1,3},{3,1},{5,7},{7,5},{8,10},{10,8},{12,... | collective-permute-start | bytes 49160 | tf_op jit(solution)/shard_map/ppermute | solution.py:41
  76.8 2.7 %collective-permute-done.23 = f32[4,8,128]{2,1,0:T(8,128)S(1)} collective-permute-done((f32[4,8,128]{2,1,0:T(8,128)S(1)}, f32[4,8,128]{2,1,0:T(8,128)S(1)}, u32[]{:S(2)}, u32[]{:S(2)}) %collective-permute-start.23) | collective-permute-done | bytes 16416 | tf_op jit(solution)/shard_map/ppermute | solution.py:41
  80.1 2.2 %final.1 = (f32[2,4,1024]{2,1,0:T(4,128)}, f32[1,4]{1,0:T(1,128)}) custom-call(f32[16,8,128]{2,1,0:T(8,128)} %copy-done.6, f32[3,8,1024]{2,1,0:T(8,128)} %copy-done.2), custom_call_target="tpu_custom_call" | custom-call | tf_op jit(solution)/shard_map/final/pallas_call | solution.py:404
  (45 shorter events, 3.6 us)
Async XLA Ops:
  0.6 19.6 %collective-permute-start.6 = (f32[32,128,128]{2,1,0:T(8,128)}, f32[32,128,128]{2,1,0:T(8,128)S(1)}, u32[]{:S(2)}, u32[]{:S(2)}) collective-permute-start(f32[32,128,128]{2,1,0:T(8,128)} %bitcast.24), channel_id=1, source_target_pairs={{0,1},{1,0},{2,3},{3,2},{4,5},{5,4},{6,7},{7,6},{8,9},{9,8},{10,11... | collective-permute-start | bytes 6291464 | tf_op jit(solution)/shard_map/ppermute | solution.py:435
  1.1 19.1 %collective-permute-start.7 = (f32[32,128,128]{2,1,0:T(8,128)}, f32[32,128,128]{2,1,0:T(8,128)}, u32[]{:S(2)}, u32[]{:S(2)}) collective-permute-start(f32[32,128,128]{2,1,0:T(8,128)} %bitcast.26), channel_id=1, source_target_pairs={{0,1},{1,0},{2,3},{3,2},{4,5},{5,4},{6,7},{7,6},{8,9},{9,8},{10,11... | collective-permute-start | bytes 6291464 | tf_op jit(solution)/shard_map/ppermute | solution.py:436
  1.2 7.2 %collective-permute-start = (f32[2,4,1024]{2,1,0:T(4,128)}, f32[2,4,1024]{2,1,0:T(4,128)S(1)}, u32[]{:S(2)}, u32[]{:S(2)}) collective-permute-start(f32[2,4,1024]{2,1,0:T(4,128)} %param.6), channel_id=1, source_target_pairs={{0,8},{8,0},{16,24},{24,16},{1,9},{9,1},{17,25},{25,17},{2,10},{10... | collective-permute-start | bytes 98312 | tf_op jit(solution)/shard_map/ppermute | solution.py:39
  4.2 6.1 %collective-permute-start.2 = (f32[2,4,1024]{2,1,0:T(4,128)}, f32[2,4,1024]{2,1,0:T(4,128)S(1)}, u32[]{:S(2)}, u32[]{:S(2)}) collective-permute-start(f32[2,4,1024]{2,1,0:T(4,128)} %param.6), channel_id=1, source_target_pairs={{0,24},{8,16},{16,8},{24,0},{1,25},{9,17},{17,9},{25,1},{2,26},{10... | collective-permute-start | bytes 98312 | tf_op jit(solution)/shard_map/ppermute | solution.py:39
  6.7 5.4 %collective-permute-start.1 = (f32[2,4,1024]{2,1,0:T(4,128)}, f32[2,4,1024]{2,1,0:T(4,128)S(1)}, u32[]{:S(2)}, u32[]{:S(2)}) collective-permute-start(f32[2,4,1024]{2,1,0:T(4,128)} %param.6), channel_id=1, source_target_pairs={{0,16},{8,24},{16,0},{24,8},{1,17},{9,25},{17,1},{25,9},{2,18},{10... | collective-permute-start | bytes 98312 | tf_op jit(solution)/shard_map/ppermute | solution.py:39
  12.1 7.3 %collective-permute-start.5 = (f32[4,8,1024]{2,1,0:T(8,128)S(1)}, f32[4,8,1024]{2,1,0:T(8,128)S(1)}, u32[]{:S(2)}, u32[]{:S(2)}) collective-permute-start(f32[4,8,1024]{2,1,0:T(8,128)S(1)} %constant_dynamic-update-slice_fusion.refs_0_), channel_id=1, source_target_pairs={{0,6},{2,4},{4,2},{6,0},{1,7},{3,5},{5,3},{7,1},{8,14},{10,12},{12... | collective-permute-start | bytes 393224 | tf_op jit(solution)/shard_map/ppermute | solution.py:41
  14.6 5.6 %collective-permute-start.4 = (f32[4,8,1024]{2,1,0:T(8,128)S(1)}, f32[4,8,1024]{2,1,0:T(8,128)S(1)}, u32[]{:S(2)}, u32[]{:S(2)}) collective-permute-start(f32[4,8,1024]{2,1,0:T(8,128)S(1)} %constant_dynamic-update-slice_fusion.refs_0_), channel_id=1, source_target_pairs={{0,4},{2,6},{4,0},{6,2},{1,5},{3,7},{5,1},{7,3},{8,12},{10,14},{12... | collective-permute-start | bytes 393224 | tf_op jit(solution)/shard_map/ppermute | solution.py:41
  15.2 5.1 %collective-permute-start.3 = (f32[4,8,1024]{2,1,0:T(8,128)S(1)}, f32[4,8,1024]{2,1,0:T(8,128)S(1)}, u32[]{:S(2)}, u32[]{:S(2)}) collective-permute-start(f32[4,8,1024]{2,1,0:T(8,128)S(1)} %constant_dynamic-update-slice_fusion.refs_0_), channel_id=1, source_target_pairs={{0,2},{2,0},{4,6},{6,4},{1,3},{3,1},{5,7},{7,5},{8,10},{10,8},{12,... | collective-permute-start | bytes 393224 | tf_op jit(solution)/shard_map/ppermute | solution.py:41
  20.2 1.6 %copy-start = (f32[8,4,128,128]{3,2,1,0:T(8,128)S(1)}, f32[8,4,128,128]{3,2,1,0:T(8,128)}, u32[]{:S(2)}) copy-start(f32[8,4,128,128]{3,2,1,0:T(8,128)} %param.7) | copy-start | bytes 6291460
  21.8 1.6 %copy-start.1 = (f32[8,4,128,128]{3,2,1,0:T(8,128)S(1)}, f32[8,4,128,128]{3,2,1,0:T(8,128)}, u32[]{:S(2)}) copy-start(f32[8,4,128,128]{3,2,1,0:T(8,128)} %param.8) | copy-start | bytes 6291460
  23.4 0.7 copy-start.3
  24.1 0.7 copy-start.4
  24.8 0.7 copy-start.5
  30.4 5.8 %collective-permute-start.10 = (f32[8,1024]{1,0:T(8,128)S(1)}, f32[8,1024]{1,0:T(8,128)S(1)}, u32[]{:S(2)}, u32[]{:S(2)}) collective-permute-start(f32[8,1024]{1,0:T(8,128)S(1)} %get-tuple-element.20), channel_id=1, source_target_pairs={{0,24},{8,16},{16,8},{24,0},{1,25},{9,17},{17,9},{25,1},{2,26},{10... | collective-permute-start | bytes 98312 | tf_op jit(solution)/shard_map/ppermute | solution.py:39
  32.6 4.8 %collective-permute-start.9 = (f32[8,1024]{1,0:T(8,128)S(1)}, f32[8,1024]{1,0:T(8,128)S(1)}, u32[]{:S(2)}, u32[]{:S(2)}) collective-permute-start(f32[8,1024]{1,0:T(8,128)S(1)} %get-tuple-element.20), channel_id=1, source_target_pairs={{0,16},{8,24},{16,0},{24,8},{1,17},{9,25},{17,1},{25,9},{2,18},{10... | collective-permute-start | bytes 98312 | tf_op jit(solution)/shard_map/ppermute | solution.py:39
  32.6 4.8 %collective-permute-start.8 = (f32[8,1024]{1,0:T(8,128)S(1)}, f32[8,1024]{1,0:T(8,128)S(1)}, u32[]{:S(2)}, u32[]{:S(2)}) collective-permute-start(f32[8,1024]{1,0:T(8,128)S(1)} %get-tuple-element.20), channel_id=1, source_target_pairs={{0,8},{8,0},{16,24},{24,16},{1,9},{9,1},{17,25},{25,17},{2,10},{10... | collective-permute-start | bytes 98312 | tf_op jit(solution)/shard_map/ppermute | solution.py:39
  37.4 6.0 %collective-permute-start.13 = (f32[4,8,1024]{2,1,0:T(8,128)S(1)}, f32[4,8,1024]{2,1,0:T(8,128)S(1)}, u32[]{:S(2)}, u32[]{:S(2)}) collective-permute-start(f32[4,8,1024]{2,1,0:T(8,128)S(1)} %pad_maximum_fusion.refs_0_), channel_id=1, source_target_pairs={{0,6},{2,4},{4,2},{6,0},{1,7},{3,5},{5,3},{7,1},{8,14},{10,12},{12... | collective-permute-start | bytes 393224 | tf_op jit(solution)/shard_map/ppermute | solution.py:41
  39.2 5.6 %collective-permute-start.12 = (f32[4,8,1024]{2,1,0:T(8,128)S(1)}, f32[4,8,1024]{2,1,0:T(8,128)S(1)}, u32[]{:S(2)}, u32[]{:S(2)}) collective-permute-start(f32[4,8,1024]{2,1,0:T(8,128)S(1)} %pad_maximum_fusion.refs_0_), channel_id=1, source_target_pairs={{0,4},{2,6},{4,0},{6,2},{1,5},{3,7},{5,1},{7,3},{8,12},{10,14},{12... | collective-permute-start | bytes 393224 | tf_op jit(solution)/shard_map/ppermute | solution.py:41
  40.0 5.0 %collective-permute-start.11 = (f32[4,8,1024]{2,1,0:T(8,128)S(1)}, f32[4,8,1024]{2,1,0:T(8,128)S(1)}, u32[]{:S(2)}, u32[]{:S(2)}) collective-permute-start(f32[4,8,1024]{2,1,0:T(8,128)S(1)} %pad_maximum_fusion.refs_0_), channel_id=1, source_target_pairs={{0,2},{2,0},{4,6},{6,4},{1,3},{3,1},{5,7},{7,5},{8,10},{10,8},{12,... | collective-permute-start | bytes 393224 | tf_op jit(solution)/shard_map/ppermute | solution.py:41
  48.0 5.8 %collective-permute-start.16 = (f32[8,1024]{1,0:T(8,128)S(1)}, f32[8,1024]{1,0:T(8,128)S(1)}, u32[]{:S(2)}, u32[]{:S(2)}) collective-permute-start(f32[8,1024]{1,0:T(8,128)S(1)} %get-tuple-element.24), channel_id=1, source_target_pairs={{0,24},{8,16},{16,8},{24,0},{1,25},{9,17},{17,9},{25,1},{2,26},{10... | collective-permute-start | bytes 98312 | tf_op jit(solution)/shard_map/ppermute | solution.py:39
  50.1 5.3 %collective-permute-start.15 = (f32[8,1024]{1,0:T(8,128)S(1)}, f32[8,1024]{1,0:T(8,128)S(1)}, u32[]{:S(2)}, u32[]{:S(2)}) collective-permute-start(f32[8,1024]{1,0:T(8,128)S(1)} %get-tuple-element.24), channel_id=1, source_target_pairs={{0,16},{8,24},{16,0},{24,8},{1,17},{9,25},{17,1},{25,9},{2,18},{10... | collective-permute-start | bytes 98312 | tf_op jit(solution)/shard_map/ppermute | solution.py:39
  51.5 4.0 %collective-permute-start.14 = (f32[8,1024]{1,0:T(8,128)S(1)}, f32[8,1024]{1,0:T(8,128)S(1)}, u32[]{:S(2)}, u32[]{:S(2)}) collective-permute-start(f32[8,1024]{1,0:T(8,128)S(1)} %get-tuple-element.24), channel_id=1, source_target_pairs={{0,8},{8,0},{16,24},{24,16},{1,9},{9,1},{17,25},{25,17},{2,10},{10... | collective-permute-start | bytes 98312 | tf_op jit(solution)/shard_map/ppermute | solution.py:39
  55.5 6.0 %collective-permute-start.19 = (f32[4,8,1024]{2,1,0:T(8,128)S(1)}, f32[4,8,1024]{2,1,0:T(8,128)S(1)}, u32[]{:S(2)}, u32[]{:S(2)}) collective-permute-start(f32[4,8,1024]{2,1,0:T(8,128)S(1)} %pad_maximum_fusion.1.refs_0_), channel_id=1, source_target_pairs={{0,6},{2,4},{4,2},{6,0},{1,7},{3,5},{5,3},{7,1},{8,14},{10,12},{12... | collective-permute-start | bytes 393224 | tf_op jit(solution)/shard_map/ppermute | solution.py:41
  57.1 5.8 %collective-permute-start.18 = (f32[4,8,1024]{2,1,0:T(8,128)S(1)}, f32[4,8,1024]{2,1,0:T(8,128)S(1)}, u32[]{:S(2)}, u32[]{:S(2)}) collective-permute-start(f32[4,8,1024]{2,1,0:T(8,128)S(1)} %pad_maximum_fusion.1.refs_0_), channel_id=1, source_target_pairs={{0,4},{2,6},{4,0},{6,2},{1,5},{3,7},{5,1},{7,3},{8,12},{10,14},{12... | collective-permute-start | bytes 393224 | tf_op jit(solution)/shard_map/ppermute | solution.py:41
  57.8 5.1 %collective-permute-start.17 = (f32[4,8,1024]{2,1,0:T(8,128)S(1)}, f32[4,8,1024]{2,1,0:T(8,128)S(1)}, u32[]{:S(2)}, u32[]{:S(2)}) collective-permute-start(f32[4,8,1024]{2,1,0:T(8,128)S(1)} %pad_maximum_fusion.1.refs_0_), channel_id=1, source_target_pairs={{0,2},{2,0},{4,6},{6,4},{1,3},{3,1},{5,7},{7,5},{8,10},{10,8},{12,... | collective-permute-start | bytes 393224 | tf_op jit(solution)/shard_map/ppermute | solution.py:41
  66.3 0.6 copy-start.2
  66.9 5.4 %collective-permute-start.22 = (f32[8,128]{1,0:T(8,128)S(1)}, f32[8,128]{1,0:T(8,128)S(1)}, u32[]{:S(2)}, u32[]{:S(2)}) collective-permute-start(f32[8,128]{1,0:T(8,128)S(1)} %get-tuple-element.26), channel_id=1, source_target_pairs={{0,24},{8,16},{16,8},{24,0},{1,25},{9,17},{17,9},{25,1},{2,26},{10... | collective-permute-start | bytes 12296 | tf_op jit(solution)/shard_map/ppermute | solution.py:39
  68.7 4.5 %collective-permute-start.21 = (f32[8,128]{1,0:T(8,128)S(1)}, f32[8,128]{1,0:T(8,128)S(1)}, u32[]{:S(2)}, u32[]{:S(2)}) collective-permute-start(f32[8,128]{1,0:T(8,128)S(1)} %get-tuple-element.26), channel_id=1, source_target_pairs={{0,16},{8,24},{16,0},{24,8},{1,17},{9,25},{17,1},{25,9},{2,18},{10... | collective-permute-start | bytes 12296 | tf_op jit(solution)/shard_map/ppermute | solution.py:39
  69.7 3.6 %collective-permute-start.20 = (f32[8,128]{1,0:T(8,128)S(1)}, f32[8,128]{1,0:T(8,128)S(1)}, u32[]{:S(2)}, u32[]{:S(2)}) collective-permute-start(f32[8,128]{1,0:T(8,128)S(1)} %get-tuple-element.26), channel_id=1, source_target_pairs={{0,8},{8,0},{16,24},{24,16},{1,9},{9,1},{17,25},{25,17},{2,10},{10... | collective-permute-start | bytes 12296 | tf_op jit(solution)/shard_map/ppermute | solution.py:39
  73.3 6.2 %collective-permute-start.25 = (f32[4,8,128]{2,1,0:T(8,128)S(1)}, f32[4,8,128]{2,1,0:T(8,128)S(1)}, u32[]{:S(2)}, u32[]{:S(2)}) collective-permute-start(f32[4,8,128]{2,1,0:T(8,128)S(1)} %pad_maximum_fusion.2), channel_id=1, source_target_pairs={{0,6},{2,4},{4,2},{6,0},{1,7},{3,5},{5,3},{7,1},{8,14},{10,12},{12... | collective-permute-start | bytes 49160 | tf_op jit(solution)/shard_map/ppermute | solution.py:41
  75.0 4.5 %collective-permute-start.24 = (f32[4,8,128]{2,1,0:T(8,128)S(1)}, f32[4,8,128]{2,1,0:T(8,128)S(1)}, u32[]{:S(2)}, u32[]{:S(2)}) collective-permute-start(f32[4,8,128]{2,1,0:T(8,128)S(1)} %pad_maximum_fusion.2), channel_id=1, source_target_pairs={{0,4},{2,6},{4,0},{6,2},{1,5},{3,7},{5,1},{7,3},{8,12},{10,14},{12... | collective-permute-start | bytes 49160 | tf_op jit(solution)/shard_map/ppermute | solution.py:41
  75.8 3.7 %collective-permute-start.23 = (f32[4,8,128]{2,1,0:T(8,128)S(1)}, f32[4,8,128]{2,1,0:T(8,128)S(1)}, u32[]{:S(2)}, u32[]{:S(2)}) collective-permute-start(f32[4,8,128]{2,1,0:T(8,128)S(1)} %pad_maximum_fusion.2), channel_id=1, source_target_pairs={{0,2},{2,0},{4,6},{6,4},{1,3},{3,1},{5,7},{7,5},{8,10},{10,8},{12,... | collective-permute-start | bytes 49160 | tf_op jit(solution)/shard_map/ppermute | solution.py:41
  79.5 0.6 copy-start.6

commit v16 on v14

--- a/solution.py
+++ b/solution.py
@@ -14,7 +14,7 @@
 GROUP = 4
 FULL_GROUP = 8
 SHARES = 16
-VMEM_LIMIT = 16 * 1024 * 1024
+VMEM_LIMIT = 8 * 1024 * 1024
 
 
 def split_nodes(nodes):

time: 77.3 us -> 77.4 us (level)
  waiting for transfers between devices: 22 us -> 22.8 us
  transfers between devices with their start and end apart: 26 -> 26, of which waited for: 17 -> 18; matrix products, arithmetic and copies ran while one was open for 3% -> 3% of each run, Pallas kernels for 2% -> 2%
where the time goes in v16:
time: 77.4 us; the launch traced here: 77.6 us
  starting transfers between devices  33.6 us (43%)
  waiting for transfers between devices  22.8 us (29%)
  Pallas kernels  13.5 us (17%)
  local copies, waits for them, and re-layouts  6.06 us (8%)
  between operations  0.82 us (1%)
    ppermute x12, starting transfers between devices, gather_rows(): lax.ppermute(rows, 'line', perm)  18.9 us
    ppermute x12, starting transfers between devices, gather_rows(): lax.ppermute(whole_line, 'place', perm)  14.1 us
    ppermute x12, waiting for transfers between devices, gather_rows(): lax.ppermute(whole_line, 'place', perm)  12.7 us
    pallas_call x3, Pallas kernels, run_step(): pl.pallas_call(functools.partial(step_kernel, step, plane, line, freqs),...  10.1 us
    ppermute x12, waiting for transfers between devices, gather_rows(): lax.ppermute(rows, 'line', perm)  10.1 us
    unnamed x17, local copies, waits for them, and re-layouts  4.45 us
    pallas_call x1, Pallas kernels, run_final(): pl.pallas_call(final_kernel, in_specs=[vmem] * 2, out_specs=[vmem] * 2, o...  2.17 us
  transfers between devices with their start and end apart: 26, of which 18 were waited for; matrix products, arithmetic and copies ran while one was open for 3% of the time, Pallas kernels for 2%

profile of v16, /device:TPU:0, one launch (start us, length us, event | category | flops | bytes accessed | tf_op | source)
XLA Modules:
  0.0 77.6 jit_solution(7487594016317300512)
XLA Ops:
  0.6 0.5 collective-permute-start.6
  1.2 3.0 %collective-permute-start = (f32[2,4,1024]{2,1,0:T(4,128)}, f32[2,4,1024]{2,1,0:T(4,128)S(1)}, u32[]{:S(2)}, u32[]{:S(2)}) collective-permute-start(f32[2,4,1024]{2,1,0:T(4,128)} %param.6), channel_id=1, source_target_pairs={{0,8},{8,0},{16,24},{24,16},{1,9},{9,1},{17,25},{25,17},{2,10},{10... | collective-permute-start | bytes 98312 | tf_op jit(solution)/shard_map/ppermute | solution.py:39
  4.2 2.5 %collective-permute-start.2 = (f32[2,4,1024]{2,1,0:T(4,128)}, f32[2,4,1024]{2,1,0:T(4,128)S(1)}, u32[]{:S(2)}, u32[]{:S(2)}) collective-permute-start(f32[2,4,1024]{2,1,0:T(4,128)} %param.6), channel_id=1, source_target_pairs={{0,24},{8,16},{16,8},{24,0},{1,25},{9,17},{17,9},{25,1},{2,26},{10... | collective-permute-start | bytes 98312 | tf_op jit(solution)/shard_map/ppermute | solution.py:39
  6.8 0.8 %stack.72 = f32[1,8,1024]{2,1,0:T(8,128)S(1)} reshape(f32[2,4,1024]{2,1,0:T(4,128)} %param.6) | data formatting | bytes 65536 | tf_op jit(solution)/shard_map/stack | solution.py:40
  7.6 0.7 concatenate.11
  8.4 1.9 %collective-permute-done.2 = f32[2,4,1024]{2,1,0:T(4,128)S(1)} collective-permute-done((f32[2,4,1024]{2,1,0:T(4,128)}, f32[2,4,1024]{2,1,0:T(4,128)S(1)}, u32[]{:S(2)}, u32[]{:S(2)}) %collective-permute-start.2) | collective-permute-done | bytes 32800 | tf_op jit(solution)/shard_map/ppermute | solution.py:39
  10.3 1.8 %collective-permute-done.1 = f32[2,4,1024]{2,1,0:T(4,128)S(1)} collective-permute-done((f32[2,4,1024]{2,1,0:T(4,128)}, f32[2,4,1024]{2,1,0:T(4,128)S(1)}, u32[]{:S(2)}, u32[]{:S(2)}) %collective-permute-start.1) | collective-permute-done | bytes 32800 | tf_op jit(solution)/shard_map/ppermute | solution.py:39
  12.1 2.5 %collective-permute-start.5 = (f32[4,8,1024]{2,1,0:T(8,128)S(1)}, f32[4,8,1024]{2,1,0:T(8,128)S(1)}, u32[]{:S(2)}, u32[]{:S(2)}) collective-permute-start(f32[4,8,1024]{2,1,0:T(8,128)S(1)} %constant_dynamic-update-slice_fusion.refs_0_), channel_id=1, source_target_pairs={{0,6},{2,4},{4,2},{6,0},{1,7},{3,5},{5,3},{7,1},{8,14},{10,12},{12... | collective-permute-start | bytes 393224 | tf_op jit(solution)/shard_map/ppermute | solution.py:41
  14.6 0.5 collective-permute-start.4
  15.2 0.5 collective-permute-start.3
  15.7 0.7 pad_add_fusion.scalars_ref
  16.4 1.6 %copy-done = f32[8,4,128,128]{3,2,1,0:T(8,128)S(1)} copy-done((f32[8,4,128,128]{3,2,1,0:T(8,128)S(1)}, f32[8,4,128,128]{3,2,1,0:T(8,128)}, u32[]{:S(2)}) %copy-start) | copy-done | bytes 2097176
  18.0 1.6 %copy-done.1 = f32[8,4,128,128]{3,2,1,0:T(8,128)S(1)} copy-done((f32[8,4,128,128]{3,2,1,0:T(8,128)S(1)}, f32[8,4,128,128]{3,2,1,0:T(8,128)}, u32[]{:S(2)}) %copy-start.1) | copy-done | bytes 2097176
  19.6 1.2 %setup.1 = (s32[12,128]{1,0:T(8,128)S(1)}, s32[8,8]{1,0:T(8,128)S(1)}, f32[8,128]{1,0:T(8,128)S(1)}, f32[32,128,128]{2,1,0:T(8,128)S(1)}, f32[32,128,128]{2,1,0:T(8,128)S(1)}) custom-call(s32[9,128]{1,0:T(8,128)S(1)} %pad_add_fusion.scalars_ref, f32[32,128,128]{2,1,0:T(8,128)S(1)} %bitcast.25, f32[32,128,128]{2,1,0:T(8,128)S(1)} %bitcast.27), custom_call_target="tpu_custom_call" | custom-call | bytes 8388608 | tf_op jit(solution)/shard_map/setup/pallas_call | solution.py:113
  20.9 3.7 %step_0.1 = (f32[129,8,128]{2,1,0:T(8,128)S(1)}, f32[8,1024]{1,0:T(8,128)S(1)}, f32[8,128]{1,0:T(8,128)S(1)}, bf16[64,256,256]{2,1,0:T(8,128)(2,1)S(1)}) custom-call(s32[12,128]{1,0:T(8,128)S(1)} %get-tuple-element.18.items_ref, s32[8,8]{1,0:T(8,128)S(1)} %get-tuple-element.19.places_ref, f32[8,128]{1,0:T(8,128)S(1)} %get-tuple-element.20.turn_ref, ...), custom_call_target="tpu_custom_call" | custom-call | tf_op jit(solution)/shard_map/step_0/pallas_call | solution.py:344
  24.5 1.2 %collective-permute-start.10 = (f32[8,1024]{1,0:T(8,128)S(1)}, f32[8,1024]{1,0:T(8,128)S(1)}, u32[]{:S(2)}, u32[]{:S(2)}) collective-permute-start(f32[8,1024]{1,0:T(8,128)S(1)} %get-tuple-element.24), channel_id=1, source_target_pairs={{0,24},{8,16},{16,8},{24,0},{1,25},{9,17},{17,9},{25,1},{2,26},{10... | collective-permute-start | bytes 98312 | tf_op jit(solution)/shard_map/ppermute | solution.py:39
  25.7 0.4 collective-permute-start.9
  26.2 2.8 %collective-permute-start.8 = (f32[8,1024]{1,0:T(8,128)S(1)}, f32[8,1024]{1,0:T(8,128)S(1)}, u32[]{:S(2)}, u32[]{:S(2)}) collective-permute-start(f32[8,1024]{1,0:T(8,128)S(1)} %get-tuple-element.24), channel_id=1, source_target_pairs={{0,8},{8,0},{16,24},{24,16},{1,9},{9,1},{17,25},{25,17},{2,10},{10... | collective-permute-start | bytes 98312 | tf_op jit(solution)/shard_map/ppermute | solution.py:39
  29.0 1.3 %collective-permute-done.10 = f32[8,1024]{1,0:T(8,128)S(1)} collective-permute-done((f32[8,1024]{1,0:T(8,128)S(1)}, f32[8,1024]{1,0:T(8,128)S(1)}, u32[]{:S(2)}, u32[]{:S(2)}) %collective-permute-start.10) | collective-permute-done | bytes 32800 | tf_op jit(solution)/shard_map/ppermute | solution.py:39
  30.3 0.8 collective-permute-done.9
  31.2 2.5 %collective-permute-start.13 = (f32[4,8,1024]{2,1,0:T(8,128)S(1)}, f32[4,8,1024]{2,1,0:T(8,128)S(1)}, u32[]{:S(2)}, u32[]{:S(2)}) collective-permute-start(f32[4,8,1024]{2,1,0:T(8,128)S(1)} %pad_maximum_fusion.refs_0_), channel_id=1, source_target_pairs={{0,6},{2,4},{4,2},{6,0},{1,7},{3,5},{5,3},{7,1},{8,14},{10,12},{12... | collective-permute-start | bytes 393224 | tf_op jit(solution)/shard_map/ppermute | solution.py:41
  33.7 0.7 collective-permute-start.12
  34.8 2.8 %collective-permute-done.13.refs_3_ = f32[4,8,1024]{2,1,0:T(8,128)S(1)} collective-permute-done((f32[4,8,1024]{2,1,0:T(8,128)S(1)}, f32[4,8,1024]{2,1,0:T(8,128)S(1)}, u32[]{:S(2)}, u32[]{:S(2)}) %collective-permute-start.13) | collective-permute-done | bytes 131104 | tf_op jit(solution)/shard_map/ppermute | solution.py:41
  37.6 1.4 %collective-permute-done.12.refs_2_ = f32[4,8,1024]{2,1,0:T(8,128)S(1)} collective-permute-done((f32[4,8,1024]{2,1,0:T(8,128)S(1)}, f32[4,8,1024]{2,1,0:T(8,128)S(1)}, u32[]{:S(2)}, u32[]{:S(2)}) %collective-permute-start.12) | collective-permute-done | bytes 131104 | tf_op jit(solution)/shard_map/ppermute | solution.py:41
  39.4 3.0 %step_1.1 = (f32[129,8,128]{2,1,0:T(8,128)S(1)}, f32[8,1024]{1,0:T(8,128)S(1)}, f32[8,128]{1,0:T(8,128)S(1)}) custom-call(s32[12,128]{1,0:T(8,128)S(1)} %get-tuple-element.18.items_ref, s32[8,8]{1,0:T(8,128)S(1)} %get-tuple-element.19.places_ref, f32[8,128]{1,0:T(8,128)S(1)} %get-tuple-element.20.turn_ref, f32[8,128]{1,0:T(8,128)S(1)} %get-tuple-element.23.info_in_ref, ...), custom_call_target="tpu_custom_call" | custom-call | tf_op jit(solution)/shard_map/step_1/pallas_call | solution.py:344
  42.4 1.5 %collective-permute-start.16 = (f32[8,1024]{1,0:T(8,128)S(1)}, f32[8,1024]{1,0:T(8,128)S(1)}, u32[]{:S(2)}, u32[]{:S(2)}) collective-permute-start(f32[8,1024]{1,0:T(8,128)S(1)} %get-tuple-element.28), channel_id=1, source_target_pairs={{0,24},{8,16},{16,8},{24,0},{1,25},{9,17},{17,9},{25,1},{2,26},{10... | collective-permute-start | bytes 98312 | tf_op jit(solution)/shard_map/ppermute | solution.py:39
  43.9 1.6 %collective-permute-start.15 = (f32[8,1024]{1,0:T(8,128)S(1)}, f32[8,1024]{1,0:T(8,128)S(1)}, u32[]{:S(2)}, u32[]{:S(2)}) collective-permute-start(f32[8,1024]{1,0:T(8,128)S(1)} %get-tuple-element.28), channel_id=1, source_target_pairs={{0,16},{8,24},{16,0},{24,8},{1,17},{9,25},{17,1},{25,9},{2,18},{10... | collective-permute-start | bytes 98312 | tf_op jit(solution)/shard_map/ppermute | solution.py:39
  45.4 1.4 %collective-permute-start.14 = (f32[8,1024]{1,0:T(8,128)S(1)}, f32[8,1024]{1,0:T(8,128)S(1)}, u32[]{:S(2)}, u32[]{:S(2)}) collective-permute-start(f32[8,1024]{1,0:T(8,128)S(1)} %get-tuple-element.28), channel_id=1, source_target_pairs={{0,8},{8,0},{16,24},{24,16},{1,9},{9,1},{17,25},{25,17},{2,10},{10... | collective-permute-start | bytes 98312 | tf_op jit(solution)/shard_map/ppermute | solution.py:39
  46.9 1.3 %collective-permute-done.16 = f32[8,1024]{1,0:T(8,128)S(1)} collective-permute-done((f32[8,1024]{1,0:T(8,128)S(1)}, f32[8,1024]{1,0:T(8,128)S(1)}, u32[]{:S(2)}, u32[]{:S(2)}) %collective-permute-start.16) | collective-permute-done | bytes 32800 | tf_op jit(solution)/shard_map/ppermute | solution.py:39
  48.2 0.5 collective-permute-done.15
  48.7 0.7 collective-permute-done.14
  49.4 1.7 %collective-permute-start.19 = (f32[4,8,1024]{2,1,0:T(8,128)S(1)}, f32[4,8,1024]{2,1,0:T(8,128)S(1)}, u32[]{:S(2)}, u32[]{:S(2)}) collective-permute-start(f32[4,8,1024]{2,1,0:T(8,128)S(1)} %pad_maximum_fusion.1.refs_0_), channel_id=1, source_target_pairs={{0,6},{2,4},{4,2},{6,0},{1,7},{3,5},{5,3},{7,1},{8,14},{10,12},{12... | collective-permute-start | bytes 393224 | tf_op jit(solution)/shard_map/ppermute | solution.py:41
  51.1 1.4 %collective-permute-start.18 = (f32[4,8,1024]{2,1,0:T(8,128)S(1)}, f32[4,8,1024]{2,1,0:T(8,128)S(1)}, u32[]{:S(2)}, u32[]{:S(2)}) collective-permute-start(f32[4,8,1024]{2,1,0:T(8,128)S(1)} %pad_maximum_fusion.1.refs_0_), channel_id=1, source_target_pairs={{0,4},{2,6},{4,0},{6,2},{1,5},{3,7},{5,1},{7,3},{8,12},{10,14},{12... | collective-permute-start | bytes 393224 | tf_op jit(solution)/shard_map/ppermute | solution.py:41
  52.9 2.4 %collective-permute-done.19.refs_3_ = f32[4,8,1024]{2,1,0:T(8,128)S(1)} collective-permute-done((f32[4,8,1024]{2,1,0:T(8,128)S(1)}, f32[4,8,1024]{2,1,0:T(8,128)S(1)}, u32[]{:S(2)}, u32[]{:S(2)}) %collective-permute-start.19) | collective-permute-done | bytes 131104 | tf_op jit(solution)/shard_map/ppermute | solution.py:41
  55.4 1.3 %collective-permute-done.18.refs_2_ = f32[4,8,1024]{2,1,0:T(8,128)S(1)} collective-permute-done((f32[4,8,1024]{2,1,0:T(8,128)S(1)}, f32[4,8,1024]{2,1,0:T(8,128)S(1)}, u32[]{:S(2)}, u32[]{:S(2)}) %collective-permute-start.18) | collective-permute-done | bytes 131104 | tf_op jit(solution)/shard_map/ppermute | solution.py:41
  56.7 0.8 collective-permute-done.17.refs_1_
  57.5 3.5 %step_2.1 = (f32[3,8,1024]{2,1,0:T(8,128)S(1)}, f32[8,128]{1,0:T(8,128)S(1)}) custom-call(s32[12,128]{1,0:T(8,128)S(1)} %get-tuple-element.18.items_ref, s32[8,8]{1,0:T(8,128)S(1)} %get-tuple-element.19.places_ref, f32[8,128]{1,0:T(8,128)S(1)} %get-tuple-element.20.turn_ref, f32[8,128]{1,0:T(8,128)S(1)} %get-tuple-element.27.info_in_ref, ...), custom_call_target="tpu_custom_call" | custom-call | tf_op jit(solution)/shard_map/step_2/pallas_call | solution.py:344
  60.9 0.6 copy-done.2
  61.6 1.5 %collective-permute-start.22 = (f32[8,128]{1,0:T(8,128)S(1)}, f32[8,128]{1,0:T(8,128)S(1)}, u32[]{:S(2)}, u32[]{:S(2)}) collective-permute-start(f32[8,128]{1,0:T(8,128)S(1)} %get-tuple-element.30), channel_id=1, source_target_pairs={{0,24},{8,16},{16,8},{24,0},{1,25},{9,17},{17,9},{25,1},{2,26},{10... | collective-permute-start | bytes 12296 | tf_op jit(solution)/shard_map/ppermute | solution.py:39
  63.1 1.1 %collective-permute-start.21 = (f32[8,128]{1,0:T(8,128)S(1)}, f32[8,128]{1,0:T(8,128)S(1)}, u32[]{:S(2)}, u32[]{:S(2)}) collective-permute-start(f32[8,128]{1,0:T(8,128)S(1)} %get-tuple-element.30), channel_id=1, source_target_pairs={{0,16},{8,24},{16,0},{24,8},{1,17},{9,25},{17,1},{25,9},{2,18},{10... | collective-permute-start | bytes 12296 | tf_op jit(solution)/shard_map/ppermute | solution.py:39
  64.2 1.8 %collective-permute-start.20 = (f32[8,128]{1,0:T(8,128)S(1)}, f32[8,128]{1,0:T(8,128)S(1)}, u32[]{:S(2)}, u32[]{:S(2)}) collective-permute-start(f32[8,128]{1,0:T(8,128)S(1)} %get-tuple-element.30), channel_id=1, source_target_pairs={{0,8},{8,0},{16,24},{24,16},{1,9},{9,1},{17,25},{25,17},{2,10},{10... | collective-permute-start | bytes 12296 | tf_op jit(solution)/shard_map/ppermute | solution.py:39
  66.0 1.0 %collective-permute-done.22 = f32[8,128]{1,0:T(8,128)S(1)} collective-permute-done((f32[8,128]{1,0:T(8,128)S(1)}, f32[8,128]{1,0:T(8,128)S(1)}, u32[]{:S(2)}, u32[]{:S(2)}) %collective-permute-start.22) | collective-permute-done | bytes 4128 | tf_op jit(solution)/shard_map/ppermute | solution.py:39
  67.0 0.6 collective-permute-done.21
  67.8 2.2 %collective-permute-start.25 = (f32[4,8,128]{2,1,0:T(8,128)S(1)}, f32[4,8,128]{2,1,0:T(8,128)S(1)}, u32[]{:S(2)}, u32[]{:S(2)}) collective-permute-start(f32[4,8,128]{2,1,0:T(8,128)S(1)} %pad_maximum_fusion.2), channel_id=1, source_target_pairs={{0,6},{2,4},{4,2},{6,0},{1,7},{3,5},{5,3},{7,1},{8,14},{10,12},{12... | collective-permute-start | bytes 49160 | tf_op jit(solution)/shard_map/ppermute | solution.py:41
  69.9 1.1 %collective-permute-start.24 = (f32[4,8,128]{2,1,0:T(8,128)S(1)}, f32[4,8,128]{2,1,0:T(8,128)S(1)}, u32[]{:S(2)}, u32[]{:S(2)}) collective-permute-start(f32[4,8,128]{2,1,0:T(8,128)S(1)} %pad_maximum_fusion.2), channel_id=1, source_target_pairs={{0,4},{2,6},{4,0},{6,2},{1,5},{3,7},{5,1},{7,3},{8,12},{10,14},{12... | collective-permute-start | bytes 49160 | tf_op jit(solution)/shard_map/ppermute | solution.py:41
  71.3 3.5 %collective-permute-done.23 = f32[4,8,128]{2,1,0:T(8,128)S(1)} collective-permute-done((f32[4,8,128]{2,1,0:T(8,128)S(1)}, f32[4,8,128]{2,1,0:T(8,128)S(1)}, u32[]{:S(2)}, u32[]{:S(2)}) %collective-permute-start.23) | collective-permute-done | bytes 16416 | tf_op jit(solution)/shard_map/ppermute | solution.py:41
  74.8 0.6 copy-done.3
  75.4 2.2 %final.1 = (f32[2,4,1024]{2,1,0:T(4,128)}, f32[1,4]{1,0:T(1,128)}) custom-call(f32[16,8,128]{2,1,0:T(8,128)} %copy-done.3, f32[3,8,1024]{2,1,0:T(8,128)} %copy-done.2), custom_call_target="tpu_custom_call" | custom-call | tf_op jit(solution)/shard_map/final/pallas_call | solution.py:425
  (39 shorter events, 2.0 us)
Async XLA Ops:
  0.6 20.2 %collective-permute-start.6 = (f32[32,128,128]{2,1,0:T(8,128)}, f32[32,128,128]{2,1,0:T(8,128)S(1)}, u32[]{:S(2)}, u32[]{:S(2)}) collective-permute-start(f32[32,128,128]{2,1,0:T(8,128)} %bitcast.24), channel_id=1, source_target_pairs={{0,1},{1,0},{2,3},{3,2},{4,5},{5,4},{6,7},{7,6},{8,9},{9,8},{10,11... | collective-permute-start | bytes 6291464 | tf_op jit(solution)/shard_map/ppermute | solution.py:458
  1.1 19.7 %collective-permute-start.7 = (f32[32,128,128]{2,1,0:T(8,128)}, f32[32,128,128]{2,1,0:T(8,128)}, u32[]{:S(2)}, u32[]{:S(2)}) collective-permute-start(f32[32,128,128]{2,1,0:T(8,128)} %bitcast.26), channel_id=1, source_target_pairs={{0,1},{1,0},{2,3},{3,2},{4,5},{5,4},{6,7},{7,6},{8,9},{9,8},{10,11... | collective-permute-start | bytes 6291464 | tf_op jit(solution)/shard_map/ppermute | solution.py:459
  1.2 7.2 %collective-permute-start = (f32[2,4,1024]{2,1,0:T(4,128)}, f32[2,4,1024]{2,1,0:T(4,128)S(1)}, u32[]{:S(2)}, u32[]{:S(2)}) collective-permute-start(f32[2,4,1024]{2,1,0:T(4,128)} %param.6), channel_id=1, source_target_pairs={{0,8},{8,0},{16,24},{24,16},{1,9},{9,1},{17,25},{25,17},{2,10},{10... | collective-permute-start | bytes 98312 | tf_op jit(solution)/shard_map/ppermute | solution.py:39
  4.2 6.1 %collective-permute-start.2 = (f32[2,4,1024]{2,1,0:T(4,128)}, f32[2,4,1024]{2,1,0:T(4,128)S(1)}, u32[]{:S(2)}, u32[]{:S(2)}) collective-permute-start(f32[2,4,1024]{2,1,0:T(4,128)} %param.6), channel_id=1, source_target_pairs={{0,24},{8,16},{16,8},{24,0},{1,25},{9,17},{17,9},{25,1},{2,26},{10... | collective-permute-start | bytes 98312 | tf_op jit(solution)/shard_map/ppermute | solution.py:39
  6.7 5.4 %collective-permute-start.1 = (f32[2,4,1024]{2,1,0:T(4,128)}, f32[2,4,1024]{2,1,0:T(4,128)S(1)}, u32[]{:S(2)}, u32[]{:S(2)}) collective-permute-start(f32[2,4,1024]{2,1,0:T(4,128)} %param.6), channel_id=1, source_target_pairs={{0,16},{8,24},{16,0},{24,8},{1,17},{9,25},{17,1},{25,9},{2,18},{10... | collective-permute-start | bytes 98312 | tf_op jit(solution)/shard_map/ppermute | solution.py:39
  12.1 8.7 %collective-permute-start.5 = (f32[4,8,1024]{2,1,0:T(8,128)S(1)}, f32[4,8,1024]{2,1,0:T(8,128)S(1)}, u32[]{:S(2)}, u32[]{:S(2)}) collective-permute-start(f32[4,8,1024]{2,1,0:T(8,128)S(1)} %constant_dynamic-update-slice_fusion.refs_0_), channel_id=1, source_target_pairs={{0,6},{2,4},{4,2},{6,0},{1,7},{3,5},{5,3},{7,1},{8,14},{10,12},{12... | collective-permute-start | bytes 393224 | tf_op jit(solution)/shard_map/ppermute | solution.py:41
  14.6 6.2 %collective-permute-start.4 = (f32[4,8,1024]{2,1,0:T(8,128)S(1)}, f32[4,8,1024]{2,1,0:T(8,128)S(1)}, u32[]{:S(2)}, u32[]{:S(2)}) collective-permute-start(f32[4,8,1024]{2,1,0:T(8,128)S(1)} %constant_dynamic-update-slice_fusion.refs_0_), channel_id=1, source_target_pairs={{0,4},{2,6},{4,0},{6,2},{1,5},{3,7},{5,1},{7,3},{8,12},{10,14},{12... | collective-permute-start | bytes 393224 | tf_op jit(solution)/shard_map/ppermute | solution.py:41
  15.2 5.7 %collective-permute-start.3 = (f32[4,8,1024]{2,1,0:T(8,128)S(1)}, f32[4,8,1024]{2,1,0:T(8,128)S(1)}, u32[]{:S(2)}, u32[]{:S(2)}) collective-permute-start(f32[4,8,1024]{2,1,0:T(8,128)S(1)} %constant_dynamic-update-slice_fusion.refs_0_), channel_id=1, source_target_pairs={{0,2},{2,0},{4,6},{6,4},{1,3},{3,1},{5,7},{7,5},{8,10},{10,8},{12,... | collective-permute-start | bytes 393224 | tf_op jit(solution)/shard_map/ppermute | solution.py:41
  16.4 1.6 %copy-start = (f32[8,4,128,128]{3,2,1,0:T(8,128)S(1)}, f32[8,4,128,128]{3,2,1,0:T(8,128)}, u32[]{:S(2)}) copy-start(f32[8,4,128,128]{3,2,1,0:T(8,128)} %param.7) | copy-start | bytes 6291460
  18.0 1.6 %copy-start.1 = (f32[8,4,128,128]{3,2,1,0:T(8,128)S(1)}, f32[8,4,128,128]{3,2,1,0:T(8,128)}, u32[]{:S(2)}) copy-start(f32[8,4,128,128]{3,2,1,0:T(8,128)} %param.8) | copy-start | bytes 6291460
  24.5 5.8 %collective-permute-start.10 = (f32[8,1024]{1,0:T(8,128)S(1)}, f32[8,1024]{1,0:T(8,128)S(1)}, u32[]{:S(2)}, u32[]{:S(2)}) collective-permute-start(f32[8,1024]{1,0:T(8,128)S(1)} %get-tuple-element.24), channel_id=1, source_target_pairs={{0,24},{8,16},{16,8},{24,0},{1,25},{9,17},{17,9},{25,1},{2,26},{10... | collective-permute-start | bytes 98312 | tf_op jit(solution)/shard_map/ppermute | solution.py:39
  25.7 5.4 %collective-permute-start.9 = (f32[8,1024]{1,0:T(8,128)S(1)}, f32[8,1024]{1,0:T(8,128)S(1)}, u32[]{:S(2)}, u32[]{:S(2)}) collective-permute-start(f32[8,1024]{1,0:T(8,128)S(1)} %get-tuple-element.24), channel_id=1, source_target_pairs={{0,16},{8,24},{16,0},{24,8},{1,17},{9,25},{17,1},{25,9},{2,18},{10... | collective-permute-start | bytes 98312 | tf_op jit(solution)/shard_map/ppermute | solution.py:39
  26.2 5.0 %collective-permute-start.8 = (f32[8,1024]{1,0:T(8,128)S(1)}, f32[8,1024]{1,0:T(8,128)S(1)}, u32[]{:S(2)}, u32[]{:S(2)}) collective-permute-start(f32[8,1024]{1,0:T(8,128)S(1)} %get-tuple-element.24), channel_id=1, source_target_pairs={{0,8},{8,0},{16,24},{24,16},{1,9},{9,1},{17,25},{25,17},{2,10},{10... | collective-permute-start | bytes 98312 | tf_op jit(solution)/shard_map/ppermute | solution.py:39
  31.2 6.4 %collective-permute-start.13 = (f32[4,8,1024]{2,1,0:T(8,128)S(1)}, f32[4,8,1024]{2,1,0:T(8,128)S(1)}, u32[]{:S(2)}, u32[]{:S(2)}) collective-permute-start(f32[4,8,1024]{2,1,0:T(8,128)S(1)} %pad_maximum_fusion.refs_0_), channel_id=1, source_target_pairs={{0,6},{2,4},{4,2},{6,0},{1,7},{3,5},{5,3},{7,1},{8,14},{10,12},{12... | collective-permute-start | bytes 393224 | tf_op jit(solution)/shard_map/ppermute | solution.py:41
  33.7 5.2 %collective-permute-start.12 = (f32[4,8,1024]{2,1,0:T(8,128)S(1)}, f32[4,8,1024]{2,1,0:T(8,128)S(1)}, u32[]{:S(2)}, u32[]{:S(2)}) collective-permute-start(f32[4,8,1024]{2,1,0:T(8,128)S(1)} %pad_maximum_fusion.refs_0_), channel_id=1, source_target_pairs={{0,4},{2,6},{4,0},{6,2},{1,5},{3,7},{5,1},{7,3},{8,12},{10,14},{12... | collective-permute-start | bytes 393224 | tf_op jit(solution)/shard_map/ppermute | solution.py:41
  34.4 5.0 %collective-permute-start.11 = (f32[4,8,1024]{2,1,0:T(8,128)S(1)}, f32[4,8,1024]{2,1,0:T(8,128)S(1)}, u32[]{:S(2)}, u32[]{:S(2)}) collective-permute-start(f32[4,8,1024]{2,1,0:T(8,128)S(1)} %pad_maximum_fusion.refs_0_), channel_id=1, source_target_pairs={{0,2},{2,0},{4,6},{6,4},{1,3},{3,1},{5,7},{7,5},{8,10},{10,8},{12,... | collective-permute-start | bytes 393224 | tf_op jit(solution)/shard_map/ppermute | solution.py:41
  42.4 5.8 %collective-permute-start.16 = (f32[8,1024]{1,0:T(8,128)S(1)}, f32[8,1024]{1,0:T(8,128)S(1)}, u32[]{:S(2)}, u32[]{:S(2)}) collective-permute-start(f32[8,1024]{1,0:T(8,128)S(1)} %get-tuple-element.28), channel_id=1, source_target_pairs={{0,24},{8,16},{16,8},{24,0},{1,25},{9,17},{17,9},{25,1},{2,26},{10... | collective-permute-start | bytes 98312 | tf_op jit(solution)/shard_map/ppermute | solution.py:39
  43.9 4.8 %collective-permute-start.15 = (f32[8,1024]{1,0:T(8,128)S(1)}, f32[8,1024]{1,0:T(8,128)S(1)}, u32[]{:S(2)}, u32[]{:S(2)}) collective-permute-start(f32[8,1024]{1,0:T(8,128)S(1)} %get-tuple-element.28), channel_id=1, source_target_pairs={{0,16},{8,24},{16,0},{24,8},{1,17},{9,25},{17,1},{25,9},{2,18},{10... | collective-permute-start | bytes 98312 | tf_op jit(solution)/shard_map/ppermute | solution.py:39
  45.4 3.9 %collective-permute-start.14 = (f32[8,1024]{1,0:T(8,128)S(1)}, f32[8,1024]{1,0:T(8,128)S(1)}, u32[]{:S(2)}, u32[]{:S(2)}) collective-permute-start(f32[8,1024]{1,0:T(8,128)S(1)} %get-tuple-element.28), channel_id=1, source_target_pairs={{0,8},{8,0},{16,24},{24,16},{1,9},{9,1},{17,25},{25,17},{2,10},{10... | collective-permute-start | bytes 98312 | tf_op jit(solution)/shard_map/ppermute | solution.py:39
  49.4 6.0 %collective-permute-start.19 = (f32[4,8,1024]{2,1,0:T(8,128)S(1)}, f32[4,8,1024]{2,1,0:T(8,128)S(1)}, u32[]{:S(2)}, u32[]{:S(2)}) collective-permute-start(f32[4,8,1024]{2,1,0:T(8,128)S(1)} %pad_maximum_fusion.1.refs_0_), channel_id=1, source_target_pairs={{0,6},{2,4},{4,2},{6,0},{1,7},{3,5},{5,3},{7,1},{8,14},{10,12},{12... | collective-permute-start | bytes 393224 | tf_op jit(solution)/shard_map/ppermute | solution.py:41
  51.1 5.6 %collective-permute-start.18 = (f32[4,8,1024]{2,1,0:T(8,128)S(1)}, f32[4,8,1024]{2,1,0:T(8,128)S(1)}, u32[]{:S(2)}, u32[]{:S(2)}) collective-permute-start(f32[4,8,1024]{2,1,0:T(8,128)S(1)} %pad_maximum_fusion.1.refs_0_), channel_id=1, source_target_pairs={{0,4},{2,6},{4,0},{6,2},{1,5},{3,7},{5,1},{7,3},{8,12},{10,14},{12... | collective-permute-start | bytes 393224 | tf_op jit(solution)/shard_map/ppermute | solution.py:41
  52.5 5.0 %collective-permute-start.17 = (f32[4,8,1024]{2,1,0:T(8,128)S(1)}, f32[4,8,1024]{2,1,0:T(8,128)S(1)}, u32[]{:S(2)}, u32[]{:S(2)}) collective-permute-start(f32[4,8,1024]{2,1,0:T(8,128)S(1)} %pad_maximum_fusion.1.refs_0_), channel_id=1, source_target_pairs={{0,2},{2,0},{4,6},{6,4},{1,3},{3,1},{5,7},{7,5},{8,10},{10,8},{12,... | collective-permute-start | bytes 393224 | tf_op jit(solution)/shard_map/ppermute | solution.py:41
  60.9 0.6 copy-start.2
  61.6 5.4 %collective-permute-start.22 = (f32[8,128]{1,0:T(8,128)S(1)}, f32[8,128]{1,0:T(8,128)S(1)}, u32[]{:S(2)}, u32[]{:S(2)}) collective-permute-start(f32[8,128]{1,0:T(8,128)S(1)} %get-tuple-element.30), channel_id=1, source_target_pairs={{0,24},{8,16},{16,8},{24,0},{1,25},{9,17},{17,9},{25,1},{2,26},{10... | collective-permute-start | bytes 12296 | tf_op jit(solution)/shard_map/ppermute | solution.py:39
  63.1 4.5 %collective-permute-start.21 = (f32[8,128]{1,0:T(8,128)S(1)}, f32[8,128]{1,0:T(8,128)S(1)}, u32[]{:S(2)}, u32[]{:S(2)}) collective-permute-start(f32[8,128]{1,0:T(8,128)S(1)} %get-tuple-element.30), channel_id=1, source_target_pairs={{0,16},{8,24},{16,0},{24,8},{1,17},{9,25},{17,1},{25,9},{2,18},{10... | collective-permute-start | bytes 12296 | tf_op jit(solution)/shard_map/ppermute | solution.py:39
  64.2 3.6 %collective-permute-start.20 = (f32[8,128]{1,0:T(8,128)S(1)}, f32[8,128]{1,0:T(8,128)S(1)}, u32[]{:S(2)}, u32[]{:S(2)}) collective-permute-start(f32[8,128]{1,0:T(8,128)S(1)} %get-tuple-element.30), channel_id=1, source_target_pairs={{0,8},{8,0},{16,24},{24,16},{1,9},{9,1},{17,25},{25,17},{2,10},{10... | collective-permute-start | bytes 12296 | tf_op jit(solution)/shard_map/ppermute | solution.py:39
  67.8 7.0 %collective-permute-start.25 = (f32[4,8,128]{2,1,0:T(8,128)S(1)}, f32[4,8,128]{2,1,0:T(8,128)S(1)}, u32[]{:S(2)}, u32[]{:S(2)}) collective-permute-start(f32[4,8,128]{2,1,0:T(8,128)S(1)} %pad_maximum_fusion.2), channel_id=1, source_target_pairs={{0,6},{2,4},{4,2},{6,0},{1,7},{3,5},{5,3},{7,1},{8,14},{10,12},{12... | collective-permute-start | bytes 49160 | tf_op jit(solution)/shard_map/ppermute | solution.py:41
  69.9 4.8 %collective-permute-start.24 = (f32[4,8,128]{2,1,0:T(8,128)S(1)}, f32[4,8,128]{2,1,0:T(8,128)S(1)}, u32[]{:S(2)}, u32[]{:S(2)}) collective-permute-start(f32[4,8,128]{2,1,0:T(8,128)S(1)} %pad_maximum_fusion.2), channel_id=1, source_target_pairs={{0,4},{2,6},{4,0},{6,2},{1,5},{3,7},{5,1},{7,3},{8,12},{10,14},{12... | collective-permute-start | bytes 49160 | tf_op jit(solution)/shard_map/ppermute | solution.py:41
  71.0 3.7 %collective-permute-start.23 = (f32[4,8,128]{2,1,0:T(8,128)S(1)}, f32[4,8,128]{2,1,0:T(8,128)S(1)}, u32[]{:S(2)}, u32[]{:S(2)}) collective-permute-start(f32[4,8,128]{2,1,0:T(8,128)S(1)} %pad_maximum_fusion.2), channel_id=1, source_target_pairs={{0,2},{2,0},{4,6},{6,4},{1,3},{3,1},{5,7},{7,5},{8,10},{10,8},{12,... | collective-permute-start | bytes 49160 | tf_op jit(solution)/shard_map/ppermute | solution.py:41
  74.8 0.6 copy-start.3
